TPU v7x, 32 devices: a whole 2x2x4 slice. The times are simulated.
32 devices in a mesh: groups: 2 (over y), loc: 4 (over z), date: 2 (over x), mp: 2 (over core).
Axes of the slice: x: 2, y: 2, z: 4, core: 2. Of those that a mesh axis runs over, the one named last changes fastest.
Arguments:
- optical: bfloat16 [8, 48, 12, 1024], P(('groups', 'loc'), None, 'date'), parts along dimension 0, may hold values from -6 to 6
- radar: bfloat16 [8, 48, 12, 1024], P(('groups', 'loc'), None, 'date'), parts along dimension 0, may hold values from -6 to 6
- cloud: int32 [8, 12], P(('groups', 'loc')), parts along dimension 0, may hold values 0 or 1
- radar_drop: int32 [8, 12], P(('groups', 'loc')), parts along dimension 0, may hold values 0 or 1
- keep_index: int32 [8, 48], P(('groups', 'loc')), parts along dimension 0, may hold values from 0 to 195, as said below
- place_table: bfloat16 [196, 1024], replicated, may hold values from -3 to 3
- date_table: bfloat16 [12, 1024], replicated, may hold values from -3 to 3
- spatial_gain: float32 [1024], replicated, may hold values from 0.25 to 1.75
- spatial_weights: bfloat16 [1024, 4, 1024], P('date', None, 'mp')
- temporal_gain: float32 [1024], replicated, may hold values from 0.25 to 1.75
- temporal_weights: bfloat16 [1024, 4, 1024], P('date', None, 'mp')
- cotangent: bfloat16 [8, 48, 12, 1024], P(('groups', 'loc'), 'date'), parts along dimension 0, may hold values from -0.5 to 0.5
Outputs:
- encoded: bfloat16 [8, 48, 12, 1024], P(('groups', 'loc'), 'date'), parts along dimension 0
- spatial_grads: float32 [2048, 4, 1024], P(('groups', 'loc', 'date'), None, 'mp'), parts along dimension 0
- temporal_grads: float32 [2048, 4, 1024], P(('groups', 'loc', 'date'), None, 'mp'), parts along dimension 0
There are 2 independent parts, one for each index of `groups`. A program takes and returns all parts, laid end to end along the dimension named above; an argument that names none is the same for every part. Nothing has to cross between parts.
Inputs may be any that keep to these rules, and one draw needn't show every extreme that they name: `keep_index`: the 48 patch numbers of one location are distinct.
All inputs are finite; a program needn't handle non-finite values. No bound on the sum of `cloud` or of `radar_drop` on one device may be relied on, other than what follows from the above.
Results may differ from a plain program's by a relative error of at most 0.02.
Values may be sent and summed in bfloat16 or wider, within the bound.
No kernel may reach another device: no remote copies, remote signals or barrier semaphores. Data moves between devices by JAX's collectives and lax.ppermute only.
A program may use at most 128 MiB of HBM per device.

v0:
```python
import functools

import jax
import jax.numpy as jnp
from jax import lax
from jax.experimental import pallas as pl
from jax.experimental.pallas import tpu as pltpu
from jax.sharding import PartitionSpec as P

HEAD_DIM = 64
EPSILON = 1e-05
CROSS = -1e30
BF = jnp.bfloat16
F32 = jnp.float32
NN = (((1,), (0,)), ((), ()))
NT = (((1,), (1,)), ((), ()))
TN = (((0,), (0,)), ((), ()))
VMEM_LIMIT = 56 * 1024 * 1024


def dot(left, right, dims):
    return lax.dot_general(left, right, dims, preferred_element_type=F32)


def statistics(rows):
    values = rows.astype(F32)
    centred = values - jnp.mean(values, -1, keepdims=True)
    inv_scale = lax.rsqrt(jnp.mean(centred * centred, -1, keepdims=True) + EPSILON)
    return centred * inv_scale, inv_scale


class Heads:
    def __init__(self, width):
        self.lanes = min(width, 256)
        self.count = self.lanes // HEAD_DIM
        owner = lax.broadcasted_iota(jnp.int32, (1, self.lanes), 1) // HEAD_DIM
        self.masks = [(owner == head).astype(F32) for head in range(self.count)]

    def stack(self, block):
        return jnp.concatenate([block * mask.astype(BF) for mask in self.masks], axis=0)

    def unstack(self, tall):
        rows = tall.shape[0] // self.count
        total = tall[0:rows] * self.masks[0]
        for head in range(1, self.count):
            total = total + tall[head * rows : (head + 1) * rows] * self.masks[head]
        return total


class Weights:
    def __init__(self, arrays, table, offsets):
        self.arrays, self.table, self.offsets = list(arrays), table, offsets

    def only(self, kinds):
        used = sorted({entry[0] for kind in kinds for entry in self.table[kind]})
        table = {
            kind: [(used.index(array), at, place) for array, at, place in self.table[kind]]
            for kind in kinds
        }
        return Weights([self.arrays[number] for number in used], table, self.offsets)


def views(table, refs, offsets, kind):
    found = []
    for array, at, place in table[kind]:
        part = refs[array].at[at]
        found.append((part, pl.ds(pl.multiple_of(offsets[place], 128), part.shape[0])))
    return found


def rows_times(rows_ref, parts, out_ref, column):
    width = parts[0][0].shape[1]
    step = min(width, 256)
    for at in range(0, width, step):
        total = None
        for part, columns in parts:
            term = dot(rows_ref[:, columns], part[:, at : at + step], NN)
            total = term if total is None else total + term
        out_ref[:, column + at : column + at + step] = total.astype(out_ref.dtype)


def emit_columns(rows_ref, outs, place, date_count, loc_count):
    block = rows_ref.shape[1] // (date_count * loc_count)
    for number, out in enumerate(outs):
        date = place if number == 0 else 1 - place
        for loc in range(loc_count):
            at = pl.multiple_of((loc * date_count + date) * block, block)
            out[:, loc * block : (loc + 1) * block] = rows_ref[:, pl.ds(at, block)]


def attention(triple_ref, bias_ref, attend_ref, mixed_ref, blocks):
    width = triple_ref.shape[1] // 3
    heads = Heads(width)
    rows = triple_ref.shape[0] // blocks
    groups = width // heads.lanes
    bias = jnp.concatenate([bias_ref[...]] * heads.count, axis=0)
    for block in range(blocks):
        at = slice(block * rows, (block + 1) * rows)
        for group in range(groups):
            lane = group * heads.lanes
            queries = heads.stack(triple_ref[at, lane : lane + heads.lanes])
            keys = triple_ref[at, width + lane : width + lane + heads.lanes]
            values = triple_ref[at, 2 * width + lane : 2 * width + lane + heads.lanes]
            scores = dot(queries, keys, NT) * HEAD_DIM ** (-0.5) + bias
            raised = jnp.exp(scores - jnp.max(scores, -1, keepdims=True))
            attend = raised * (1.0 / jnp.sum(raised, -1, keepdims=True))
            attend_ref[block * groups + group] = attend
            mixed = heads.unstack(dot(attend.astype(BF), values, NN))
            mixed_ref[at, lane : lane + heads.lanes] = mixed.astype(BF)


def attention_back(triple_ref, attend_ref, back_mixed_ref, back_triple_ref, blocks):
    width = triple_ref.shape[1] // 3
    heads = Heads(width)
    rows = triple_ref.shape[0] // blocks
    groups = width // heads.lanes
    for block in range(blocks):
        at = slice(block * rows, (block + 1) * rows)
        for group in range(groups):
            lane = group * heads.lanes
            queries = heads.stack(triple_ref[at, lane : lane + heads.lanes])
            keys = triple_ref[at, width + lane : width + lane + heads.lanes]
            values = triple_ref[at, 2 * width + lane : 2 * width + lane + heads.lanes]
            back = heads.stack(back_mixed_ref[at, lane : lane + heads.lanes])
            attend = attend_ref[block * groups + group]
            back_attend = dot(back, values, NT)
            back_values = dot(attend.astype(BF), back, TN)
            inner = back_attend - jnp.sum(back_attend * attend, -1, keepdims=True)
            back_scores = (attend * inner * HEAD_DIM ** (-0.5)).astype(BF)
            back_queries = heads.unstack(dot(back_scores, keys, NN))
            back_keys = dot(back_scores, queries, TN)
            for number, term in enumerate((back_queries, back_keys, back_values)):
                first = number * width + lane
                back_triple_ref[at, first : first + heads.lanes] = term.astype(BF)


def normalize_into(rows_ref, gain_ref, hidden_ref, blocks):
    rows = rows_ref.shape[0] // blocks
    for block in range(blocks):
        at = slice(block * rows, (block + 1) * rows)
        normed, _ = statistics(rows_ref[at, :])
        hidden_ref[at, :] = (normed * gain_ref[...]).astype(BF)


def spatial_forward_kernel(plan, place, offsets, gain, bias, *refs):
    sources, refs = refs[: plan.origins], refs[plan.origins :]
    arrays, refs = refs[: plan.arrays], refs[plan.arrays :]
    partials, refs = refs[: plan.origins], refs[plan.origins :]
    columns, refs = refs[: plan.columns], refs[plan.columns :]
    triple, attend, mixed, start, hidden, whole = refs
    for source, at, to, size in plan.moves:
        start[to : to + size, :] = sources[source][at : at + size, :]
    normalize_into(start, gain, hidden, plan.blocks)
    plan.emit(hidden, columns, place[0])
    for kind in range(3):
        rows_times(hidden, views(plan.table, arrays, offsets, kind), triple, kind * mixed.shape[1])
    attention(triple, bias, attend, mixed, plan.blocks)
    for part, features in views(plan.table, arrays, offsets, 3):
        whole[:, features] = dot(mixed[...], part[...], NT).astype(BF)
    for source, at, to, size in plan.moves:
        partials[source][at : at + size, :] = whole[to : to + size, :]


def temporal_kernel(plan, place, offsets, gain, bias, date_rows, cotangent, *refs):
    sources, refs = refs[: plan.sources], refs[plan.sources :]
    arrays, refs = refs[: plan.arrays], refs[plan.arrays :]
    hidden_columns, refs = refs[: plan.columns], refs[plan.columns :]
    upstream_columns, refs = refs[: plan.columns], refs[plan.columns :]
    joined, mixed, partial, back_triple, back_part, hidden, triple, attend, back_mixed = refs
    rows = date_rows.shape[0]
    for source, at, to, size in plan.moves:
        if source == 0 and plan.sources > 1:
            total = sources[1][at : at + size, :].astype(F32) + sources[2][at : at + size, :].astype(F32)
            out = (sources[0][at : at + size, :].astype(F32) + total).astype(BF)
        else:
            out = sources[-1][at : at + size, :]
        dated = out.astype(F32) + date_rows[to % rows : to % rows + size, :].astype(F32)
        joined[to : to + size, :] = dated.astype(BF)
    normalize_into(joined, gain, hidden, plan.blocks)
    plan.emit(hidden, hidden_columns, place[0])
    plan.emit(cotangent, upstream_columns, place[0])
    width = mixed.shape[1]
    for kind in range(3):
        rows_times(hidden, views(plan.table, arrays, offsets, kind), triple, kind * width)
    outlet = views(plan.table, arrays, offsets, 3)
    rows_times(cotangent, outlet, back_mixed, 0)
    attention(triple, bias, attend, mixed, plan.blocks)
    for part, features in outlet:
        partial[:, features] = dot(mixed[...], part[...], NT).astype(BF)
    attention_back(triple, attend, back_mixed, back_triple, plan.blocks)
    intakes = [views(plan.table, arrays, offsets, kind) for kind in range(3)]
    for entries in zip(*intakes):
        total = None
        for kind, (part, features) in enumerate(entries):
            term = dot(back_triple[:, kind * width : (kind + 1) * width], part[...], NT)
            total = term if total is None else total + term
        back_part[:, features] = total.astype(BF)


def norm_back_kernel(moves, step, gain, here, there, joined, cotangent, *outs):
    for at in range(0, joined.shape[0], step):
        span_here = slice(at, at + step)
        normed, inv_scale = statistics(joined[span_here, :])
        total = here[span_here, :].astype(F32) + there[span_here, :].astype(F32)
        scaled = total * gain[...]
        inner = (
            scaled
            - jnp.mean(scaled, -1, keepdims=True)
            - normed * jnp.mean(scaled * normed, -1, keepdims=True)
        )
        back = (cotangent[span_here, :].astype(F32) + inv_scale * inner).astype(BF)
        for target, to, first, size in moves:
            if at <= first < at + step:
                outs[target][to : to + size, :] = back[first - at : first - at + size]


def spatial_backward_kernel(plan, place, offsets, triple, attend, *refs):
    sources, refs = refs[: plan.origins], refs[plan.origins :]
    arrays, refs = refs[: plan.arrays], refs[plan.arrays :]
    columns, refs = refs[: plan.columns], refs[plan.columns :]
    back_triple, upstream, back_mixed = refs
    for source, at, to, size in plan.moves:
        upstream[to : to + size, :] = sources[source][at : at + size, :]
    plan.emit(upstream, columns, place[0])
    rows_times(upstream, views(plan.table, arrays, offsets, 3), back_mixed, 0)
    attention_back(triple, attend, back_mixed, back_triple, plan.blocks)


def grad_kernel(loc_count, loc, left_own, left_other, right_own, right_other, first, rest):
    block = first.shape[0]
    for step in range(loc_count):
        at = lax.rem(loc[0] + (2 * loc_count - 1 - step), loc_count) * block
        columns = pl.ds(pl.multiple_of(at, block), block)
        total = dot(left_own[:, columns], right_own[...], TN)
        total = total + dot(left_other[:, columns], right_other[...], TN)
        if step == 0:
            first[...] = total.astype(BF)
        else:
            rest[step - 1] = total


def finish_kernel(*refs):
    out = refs[-1]
    column = 0
    for arrived, rest in zip(refs[0:-1:2], refs[1:-1:2]):
        for at in range(0, rest.shape[1], 256):
            total = arrived[:, at : at + 256].astype(F32) + rest[:, at : at + 256]
            kind, lane = (column + at) // out.shape[2], (column + at) % out.shape[2]
            out[:, kind, lane : lane + 256] = total
        column += rest.shape[1]


class Plan:
    def __init__(self, blocks, moves, origins, weights, emit, columns, sources=0):
        self.blocks, self.moves, self.origins = blocks, moves, origins
        self.arrays, self.table = len(weights.arrays), weights.table
        self.emit, self.columns, self.sources = emit, columns, sources


def call(body, outs, args, scratch=(), flops=0):
    smem = pl.BlockSpec(memory_space=pltpu.SMEM)
    vmem = pl.BlockSpec(memory_space=pltpu.VMEM)
    specs = [smem if arg.dtype == jnp.int32 else vmem for arg in args]
    moved = sum(arg.size * arg.dtype.itemsize for arg in args)
    moved = moved + sum(out.size * out.dtype.itemsize for out in outs)
    return pl.pallas_call(
        body,
        out_shape=list(outs),
        in_specs=specs,
        out_specs=[vmem] * len(outs),
        scratch_shapes=list(scratch),
        compiler_params=pltpu.CompilerParams(vmem_limit_bytes=VMEM_LIMIT),
        cost_estimate=pl.CostEstimate(flops=flops, bytes_accessed=moved, transcendentals=0),
    )(*args)


def swap(array, axis):
    return lax.ppermute(array, axis, [(0, 1), (1, 0)])


def gather_weights(weights, sizes):
    rows = weights.shape[0]
    own = weights.transpose(1, 0, 2)
    if sizes["date"] != 2 or sizes["groups"] != 2 or sizes["loc"] % 2 or rows % 512:
        whole = lax.all_gather(own, "date", axis=1, tiled=True)
        table = {kind: [(0, kind, 0)] for kind in range(4)}
        return Weights([whole], table, jnp.zeros((1,), jnp.int32))
    side, here = lax.axis_index("groups"), lax.axis_index("date")
    even = lax.axis_index("loc") % 2
    quarter = rows // 4
    pairs = [(at, at ^ 1) for at in range(sizes["loc"])]

    def place(group, loc):
        return (1 - here) * rows + (group * 2 + loc) * quarter

    offsets = [here * rows, place(side, even), place(1 - side, even), place(side, 1 - even)]
    offsets = jnp.stack(offsets + [place(1 - side, 1 - even)]).astype(jnp.int32)
    sent = lax.dynamic_slice_in_dim(weights, (side * 2 + even) * quarter, quarter, 0)
    sent = sent.transpose(1, 0, 2)
    arrays, table = [own], {}
    for kinds in ((0, 1), (2, 3)):
        across = swap(sent[kinds[0] : kinds[1] + 1], "date")
        group = swap(across, "groups")
        loc = lax.ppermute(across, "loc", pairs)
        far = (swap(loc[0:1], "groups"), lax.ppermute(group[1:2], "loc", pairs))
        first = len(arrays)
        arrays += [across, group, loc, *far]
        for number, kind in enumerate(kinds):
            table[kind] = [
                (0, kind, 0),
                (first, number, 1),
                (first + 1, number, 2),
                (first + 2, number, 3),
                (first + 3 + number, 0, 4),
            ]
    return Weights(arrays, table, offsets)


def add_over_heads(partial, sizes):
    if sizes["mp"] == 2:
        return partial.astype(F32) + swap(partial, "mp").astype(F32)
    return lax.psum(partial.astype(F32), "mp")


def whole_grads(hidden, back_triple, upstream, mixed):
    width = mixed.shape[1]
    intake = dot(hidden, back_triple, TN)
    outlet = dot(upstream, mixed, TN)
    whole = jnp.concatenate([intake, outlet], axis=1).reshape(-1, 4, width)
    part = lax.psum_scatter(whole.astype(BF), ("loc", "date"), scatter_dimension=0, tiled=True)
    return part.astype(F32)


def ring_terms(left, right, other_left, other_right, sizes):
    count = sizes["loc"]
    loc = lax.axis_index("loc").astype(jnp.int32)[None]
    block, width = left.shape[1] // count, right.shape[1]
    return call(
        functools.partial(grad_kernel, count),
        (
            jax.ShapeDtypeStruct((block, width), BF),
            jax.ShapeDtypeStruct((count - 1, block, width), F32),
        ),
        (loc, left, other_left, right, other_right),
        flops=4 * left.shape[0] * left.shape[1] * width,
    )


def ring_sum(terms, sizes):
    count = sizes["loc"]
    ring = [(at, (at + 1) % count) for at in range(count)]
    total, rest = terms
    for step in range(count - 1):
        arrived = lax.ppermute(total, "loc", ring)
        if step < count - 2:
            total = (arrived.astype(F32) + rest[step]).astype(BF)
    return arrived, rest[count - 2]


def weight_grads(hidden, back_triple, upstream, mixed, sizes):
    width = mixed.shape[1]
    block = hidden[0].shape[1] // sizes["loc"]
    half = back_triple.shape[1] // 2
    other_hidden, other_upstream = swap(hidden[1], "date"), swap(upstream[1], "date")
    outlet = ring_terms(upstream[0], mixed, other_upstream, swap(mixed, "date"), sizes)
    outlet = ring_sum(outlet, sizes)
    intakes = []
    for at in (0, half):
        right = back_triple[:, at : at + half]
        terms = ring_terms(hidden[0], right, other_hidden, swap(right, "date"), sizes)
        intakes += ring_sum(terms, sizes)
    return call(
        finish_kernel,
        (jax.ShapeDtypeStruct((block, 4, width), F32),),
        (*intakes, *outlet),
    )[0]


def per_device(
    sizes,
    optical,
    radar,
    cloud,
    radar_drop,
    keep_index,
    place_table,
    date_table,
    spatial_gain,
    spatial_weights,
    temporal_gain,
    temporal_weights,
    cotangent,
):
    spatial = gather_weights(spatial_weights, sizes)
    temporal = gather_weights(temporal_weights, sizes)
    _, patches, dates_here, model = optical.shape
    patches_here, dates = cotangent.shape[1:3]
    width = spatial_weights.shape[2]
    rows = patches * dates_here
    here = lax.axis_index("date")
    first = here * dates_here
    paired = sizes["date"] == 2 and dates_here % 2 == 0 and patches_here % 8 == 0

    if paired:
        pairs, eights = dates_here // 2, patches_here // 8
        spatial_blocks, temporal_blocks = pairs, eights
        half_rows = eights * 16

        def own_first(array, axis):
            return jnp.where(here == 0, array, jnp.flip(array, axis))

        def spatial_rows(array):
            array = array.reshape(pairs, 2, 2, eights, 8, -1)
            return own_first(array, 2).transpose(0, 2, 3, 1, 4, 5).reshape(rows, -1)

        def temporal_rows(array):
            array = array.reshape(2, pairs, 2, eights, 8, -1)
            return own_first(array, 0).transpose(3, 0, 1, 2, 4, 5).reshape(rows, -1)

        def temporal_whole(array):
            array = array.reshape(eights, 2, pairs, 2, 8, -1).transpose(1, 2, 3, 0, 4, 5)
            return own_first(array, 0).reshape(dates, patches_here, -1)

    else:
        spatial_blocks = 1 if rows <= 192 else dates_here
        temporal_blocks = patches_here // 8 if patches_here % 8 == 0 else 1

        def spatial_rows(array):
            return array.reshape(rows, -1)

        def temporal_rows(array):
            array = array.reshape(dates, temporal_blocks, patches_here // temporal_blocks, -1)
            return array.transpose(1, 0, 2, 3).reshape(rows, -1)

        def temporal_whole(array):
            array = array.reshape(temporal_blocks, dates, patches_here // temporal_blocks, -1)
            return array.transpose(1, 0, 2, 3).reshape(dates, patches_here, -1)

    cloud_here = lax.dynamic_slice_in_dim(cloud, first, dates_here, 1)[0]
    drop_here = lax.dynamic_slice_in_dim(radar_drop, first, dates_here, 1)[0]
    optical_keep = (1 - cloud_here).astype(F32)[:, None, None]
    radar_keep = (1 - drop_here).astype(F32)[:, None, None]
    places = jnp.take(place_table, keep_index[0], axis=0).astype(F32)[None]
    start = (
        optical[0].transpose(1, 0, 2).astype(F32) * optical_keep
        + radar[0].transpose(1, 0, 2).astype(F32) * radar_keep
        + places
    ).astype(BF)
    start = spatial_rows(start)

    dates_at = jnp.arange(dates, dtype=jnp.int32)
    patches_at = jnp.arange(patches_here, dtype=jnp.int32)
    ones_here = jnp.ones((dates, patches_here, 1), jnp.int32)
    temporal_size = rows // temporal_blocks
    date_at = temporal_rows(ones_here * dates_at[:, None, None])[:temporal_size, 0]
    patch_at = temporal_rows(ones_here * patches_at[None, :, None])[:temporal_size, 0]
    spatial_size = rows // spatial_blocks
    spatial_date = jnp.ones((dates_here, patches, 1), jnp.int32) * dates_at[:dates_here, None, None]
    spatial_date = spatial_rows(spatial_date)[:spatial_size, 0]
    spatial_bias = jnp.where(spatial_date[:, None] == spatial_date[None, :], 0.0, CROSS).astype(F32)
    survive = 1 - cloud[0] * radar_drop[0]
    same_date = date_at[:, None] == date_at[None, :]
    survive_at = temporal_rows(ones_here * survive[:, None, None])[:temporal_size, 0]
    allowed = (survive_at[None, :] == 1) | same_date
    temporal_bias = jnp.where(
        patch_at[:, None] == patch_at[None, :], jnp.where(allowed, 0.0, -1000000000.0), CROSS
    ).astype(F32)
    date_rows = jnp.broadcast_to(date_table[:, None], (dates, patches_here, model))
    date_rows = temporal_rows(date_rows)[:temporal_size]
    cotangent_rows = temporal_rows(cotangent[0].transpose(1, 0, 2))

    spatial_gain = spatial_gain[None]
    temporal_gain = temporal_gain[None]
    lanes = min(width, 256)

    def shape(*dims, dtype=BF):
        return jax.ShapeDtypeStruct(dims, dtype)

    def attend_dims(blocks):
        return (blocks * (width // lanes), lanes // HEAD_DIM * (rows // blocks), rows // blocks)

    layer_flops = 2 * rows * model * width * 4
    place = here.astype(jnp.int32)[None]
    if paired:
        half = rows // 2

        def emit(rows_ref, outs, at):
            emit_columns(rows_ref, outs, at, 2, sizes["loc"])

        column_shapes = (shape(rows, model // 2), shape(rows, model // 2))
        blocked = start.reshape(pairs, 2, half_rows, model)
        origins = (blocked[:, 0].reshape(half, model), blocked[:, 1].reshape(half, model))
        spatial_moves = [
            (side, pair * half_rows, (pair * 2 + side) * half_rows, half_rows)
            for side in range(2)
            for pair in range(pairs)
        ]
        temporal_moves = [
            (side, pair * half_rows + eight * 16, (eight * 2 + side) * pairs * 16 + pair * 16, 16)
            for side in range(2)
            for pair in range(pairs)
            for eight in range(eights)
        ]
        half_shapes = (shape(half, model), shape(half, model))
    else:

        def emit(rows_ref, outs, at):
            outs[0][...] = rows_ref[...]

        column_shapes = (shape(rows, model),)
        origins = (start,)
        spatial_moves = [(0, at * spatial_size, at * spatial_size, spatial_size) for at in range(spatial_blocks)]
        temporal_moves = [(0, at * temporal_size, at * temporal_size, temporal_size) for at in range(temporal_blocks)]
        half_shapes = (shape(rows, model),)
    columns = len(column_shapes)
    origins, spatial_bias, temporal_bias, date_rows, cotangent_rows = lax.optimization_barrier(
        (origins, spatial_bias, temporal_bias, date_rows, cotangent_rows)
    )

    plan = Plan(spatial_blocks, spatial_moves, len(origins), spatial, emit, columns)
    outs = call(
        functools.partial(spatial_forward_kernel, plan),
        (
            *half_shapes,
            *column_shapes,
            shape(rows, 3 * width),
            shape(*attend_dims(spatial_blocks), dtype=F32),
            shape(rows, width),
        ),
        (place, spatial.offsets, spatial_gain, spatial_bias, *origins, *spatial.arrays),
        scratch=(
            pltpu.VMEM((rows, model), BF),
            pltpu.VMEM((rows, model), BF),
            pltpu.VMEM((rows, model), BF),
        ),
        flops=layer_flops,
    )
    partials, outs = outs[: len(origins)], outs[len(origins) :]
    hidden, (triple, attend, mixed) = outs[:columns], outs[columns:]
    if paired:
        there = (origins[1].astype(F32) + add_over_heads(partials[1], sizes)).astype(BF)
        sources = (origins[0], partials[0], swap(partials[0], "mp"), swap(there, "date"))
    else:
        spatial_out = (start.astype(F32) + add_over_heads(partials[0], sizes)).astype(BF)
        moved = lax.all_to_all(
            spatial_out.reshape(dates_here, patches, model),
            "date",
            split_axis=1,
            concat_axis=0,
            tiled=True,
        )
        sources = (temporal_rows(moved),)
    plan = Plan(
        temporal_blocks, temporal_moves, len(origins), temporal, emit, columns, len(sources)
    )
    outs = call(
        functools.partial(temporal_kernel, plan),
        (
            *column_shapes,
            *column_shapes,
            shape(rows, model),
            shape(rows, width),
            shape(rows, model),
            shape(rows, 3 * width),
            shape(rows, model),
        ),
        (
            place,
            temporal.offsets,
            temporal_gain,
            temporal_bias,
            date_rows,
            cotangent_rows,
            *sources,
            *temporal.arrays,
        ),
        scratch=(
            pltpu.VMEM((rows, model), BF),
            pltpu.VMEM((rows, 3 * width), BF),
            pltpu.VMEM(attend_dims(temporal_blocks), F32),
            pltpu.VMEM((rows, width), BF),
        ),
        flops=2 * layer_flops,
    )
    temporal_hidden, temporal_upstream = outs[:columns], outs[columns : 2 * columns]
    joined, temporal_mixed, temporal_partial, temporal_triple, back_part = outs[2 * columns :]

    if sizes["mp"] == 2:
        others = swap(back_part, "mp")
    else:
        others = (lax.psum(back_part.astype(F32), "mp") - back_part.astype(F32)).astype(BF)
    backs = call(
        functools.partial(norm_back_kernel, temporal_moves, temporal_size),
        half_shapes,
        (temporal_gain, back_part, others, joined, cotangent_rows),
    )
    if paired:
        back_origins = (backs[0], swap(backs[1], "date"))
    else:
        back = lax.all_to_all(
            temporal_whole(backs[0]), "date", split_axis=0, concat_axis=1, tiled=True
        )
        back_origins = (back.reshape(rows, model),)
    outlet = spatial.only((3,))
    plan = Plan(spatial_blocks, spatial_moves, len(origins), outlet, emit, columns)
    outs = call(
        functools.partial(spatial_backward_kernel, plan),
        (*column_shapes, shape(rows, 3 * width)),
        (place, outlet.offsets, triple, attend, *back_origins, *outlet.arrays),
        scratch=(pltpu.VMEM((rows, model), BF), pltpu.VMEM((rows, width), BF)),
        flops=layer_flops,
    )
    upstream, back_triple = outs[:columns], outs[columns]
    encoded = (joined.astype(F32) + add_over_heads(temporal_partial, sizes)).astype(BF)
    encoded = temporal_whole(encoded).transpose(1, 0, 2)[None]
    if paired:
        temporal_grads = weight_grads(
            temporal_hidden, temporal_triple, temporal_upstream, temporal_mixed, sizes
        )
        spatial_grads = weight_grads(hidden, back_triple, upstream, mixed, sizes)
    else:
        temporal_grads = whole_grads(
            temporal_hidden[0], temporal_triple, temporal_upstream[0], temporal_mixed
        )
        spatial_grads = whole_grads(hidden[0], back_triple, upstream[0], mixed)
    return (encoded, spatial_grads, temporal_grads)


def solution(mesh):
    in_specs = (
        P(("groups", "loc"), None, "date", None),
        P(("groups", "loc"), None, "date", None),
        P(("groups", "loc"), None),
        P(("groups", "loc"), None),
        P(("groups", "loc"), None),
        P(),
        P(),
        P(),
        P("date", None, "mp"),
        P(),
        P("date", None, "mp"),
        P(("groups", "loc"), "date", None, None),
    )
    out_specs = (
        P(("groups", "loc"), "date", None, None),
        P(("groups", "loc", "date"), None, "mp"),
        P(("groups", "loc", "date"), None, "mp"),
    )
    return jax.shard_map(
        functools.partial(per_device, dict(mesh.shape)),
        mesh=mesh,
        in_specs=in_specs,
        out_specs=out_specs,
        check_vma=False,
    )
```

profile of v0, /device:TPU:0, one launch (start us, length us, event | category | flops | bytes accessed | tf_op | source)
XLA Modules:
  0.0 238.7 jit_solution(4232292235908396081)
XLA Ops:
  0.7 2.1 copy.36
  2.9 2.1 copy.35
  6.2 3.0 %collective-permute-start.5 = (bf16[2,128,512]{2,1,0:T(8,128)(2,1)S(1)}, bf16[2,128,512]{2,1,0:T(8,128)(2,1)S(1)}, u32[]{:S(2)}, u32[]{:S(2)}) collective-permute-start(bf16[2,128,512]{2,1,0:T(8,128)(2,1)S(1)} %get-tuple-element.93), channel_id=1, source_target_pairs={{0,2},{2,0},{1,3},{3,1},{4,6},{6,4},{5,7},{7,5},{8,10},{10,8},{9,1... | collective-permute-start | bytes 786440 | tf_op jit(solution)/shard_map/ppermute | solution.py:278
  17.5 2.1 collective-permute-start.7
  21.3 1.8 collective-permute-start.2
  26.8 2.0 collective-permute-start.8
  30.5 1.8 collective-permute-done.2.refs_5_
  32.3 1.7 collective-permute-start.3
  40.1 7.3 %shard_map.139 = (bf16[144,1024]{1,0:T(8,128)(2,1)}, bf16[144,1024]{1,0:T(8,128)(2,1)}, bf16[288,512]{1,0:T(8,128)(2,1)}, bf16[288,512]{1,0:T(8,128)(2,1)}, bf16...) custom-call(s32[1]{0:T(128)} %bitcast.place, s32[5]{0:T(128)} %stack.29.offsets, ...), custom_call_target="tpu_custom_call" | custom-call | flops 1207959552 | bytes 8069144 | tf_op jit(solution)/shard_map/pallas_call | solution.py:266
  49.6 7.1 %collective-permute-done.18.refs_10_ = bf16[2,128,512]{2,1,0:T(8,128)(2,1)S(1)} collective-permute-done((bf16[2,128,512]{2,1,0:T(8,128)(2,1)S(1)}, bf16[2,128,512]{2,1,0:T(8,128)(2,1)S(1)}, u32[]{:S(2)}, u32[]{:S(2)}) %collective-permute-start.18) | collective-permute-done | bytes 262176 | tf_op jit(solution)/shard_map/ppermute | solution.py:278
  58.5 3.4 %collective-permute-done.13.refs_5_ = bf16[2,128,512]{2,1,0:T(8,128)(2,1)S(1)} collective-permute-done((bf16[2,128,512]{2,1,0:T(8,128)(2,1)S(1)}, bf16[2,128,512]{2,1,0:T(8,128)(2,1)S(1)}, u32[]{:S(2)}, u32[]{:S(2)}) %collective-permute-start.13) | collective-permute-done | bytes 262176 | tf_op jit(solution)/shard_map/ppermute | solution.py:278
  67.4 2.5 %collective-permute-done.15.refs_7_ = bf16[2,128,512]{2,1,0:T(8,128)(2,1)S(1)} collective-permute-done((bf16[2,128,512]{2,1,0:T(8,128)(2,1)S(1)}, bf16[2,128,512]{2,1,0:T(8,128)(2,1)S(1)}, u32[]{:S(2)}, u32[]{:S(2)}) %collective-permute-start.15) | collective-permute-done | bytes 262176 | tf_op jit(solution)/shard_map/ppermute | solution.py:304
  72.8 2.0 collective-permute-done.21.refs_13_
  77.2 2.6 %collective-permute-done.17.refs_9_ = bf16[1,128,512]{2,1,0:T(8,128)(2,1)S(1)} collective-permute-done((bf16[1,128,512]{2,1,0:T(8,128)(2,1)S(1)}, bf16[1,128,512]{2,1,0:T(8,128)(2,1)S(1)}, u32[]{:S(2)}, u32[]{:S(2)}) %collective-permute-start.17) | collective-permute-done | bytes 131104 | tf_op jit(solution)/shard_map/ppermute | solution.py:305
  80.7 12.7 %shard_map.140 = (bf16[288,512]{1,0:T(8,128)(2,1)}, bf16[288,512]{1,0:T(8,128)(2,1)}, bf16[288,512]{1,0:T(8,128)(2,1)}, bf16[288,512]{1,0:T(8,128)(2,1)}, bf16[2...) custom-call(s32[1]{0:T(128)} %bitcast.place, ...), custom_call_target="tpu_custom_call" | custom-call | flops 2415919104 | bytes 10330136 | tf_op jit(solution)/shard_map/pallas_call | solution.py:266
  98.8 4.9 %collective-permute-done.49.left_other = bf16[288,512]{1,0:T(8,128)(2,1)S(1)} collective-permute-done((bf16[288,512]{1,0:T(8,128)(2,1)}, bf16[288,512]{1,0:T(8,128)(2,1)S(1)}, u32[]{:S(2)}, u32[]{:S(2)}) %collective-permute-start.49) | collective-permute-done | bytes 294944 | tf_op jit(solution)/shard_map/ppermute | solution.py:278
  105.1 4.8 %collective-permute-done.50.right_other = bf16[288,512]{1,0:T(8,128)(2,1)S(1)} collective-permute-done((bf16[288,512]{1,0:T(8,128)(2,1)}, bf16[288,512]{1,0:T(8,128)(2,1)S(1)}, u32[]{:S(2)}, u32[]{:S(2)}) %collective-permute-start.50) | collective-permute-done | bytes 294944 | tf_op jit(solution)/shard_map/ppermute | solution.py:278
  110.7 2.9 %shard_map.149 = (bf16[128,512]{1,0:T(8,128)(2,1)}, f32[3,128,512]{2,1,0:T(8,128)}) custom-call(s32[1]{0:T(128)} %bitcast.43.loc, bf16[288,512]{1,0:T(8,128)(2,1)} %get-tuple-element.76.left_own, bf16[288,512]{1,0:T(8,128)(2,1)} %copy-done.30, bf16[288,512]{1,0:T(8,128)(2,1)} %get-tuple-element.78.right_own, bf16[288,512]{1,0:T(8,128)(2,1)} %copy-done.31), custom_call_target="tpu_custom_call" | custom-call | flops 301989888 | bytes 2097156 | tf_op jit(solution)/shard_map/pallas_call | solution.py:266
  114.3 1.7 slice_bitcast_fusion.4.refs_5_
  116.0 4.5 %collective-permute-done.51 = bf16[128,512]{1,0:T(8,128)(2,1)S(1)} collective-permute-done((bf16[128,512]{1,0:T(8,128)(2,1)}, bf16[128,512]{1,0:T(8,128)(2,1)S(1)}, u32[]{:S(2)}, u32[]{:S(2)}) %collective-permute-start.51) | collective-permute-done | bytes 131104 | tf_op jit(solution)/shard_map/ppermute | solution.py:354
  123.1 9.0 %collective-permute-done.41.right_other = bf16[288,768]{1,0:T(8,128)(2,1)S(1)} collective-permute-done((bf16[288,768]{1,0:T(8,128)(2,1)S(1)}, bf16[288,768]{1,0:T(8,128)(2,1)S(1)}, u32[]{:S(2)}, u32[]{:S(2)}) %collective-permute-start.41) | collective-permute-done | bytes 442400 | tf_op jit(solution)/shard_map/ppermute | solution.py:278
  132.9 3.4 %shard_map.147 = (bf16[128,768]{1,0:T(8,128)(2,1)}, f32[3,128,768]{2,1,0:T(8,128)}) custom-call(s32[1]{0:T(128)} %bitcast.43.loc, bf16[288,512]{1,0:T(8,128)(2,1)} %get-tuple-element.69.left_own, bf16[288,512]{1,0:T(8,128)(2,1)} %copy-done.56, bf16[288,768]{1,0:T(8,128)(2,1)} %copy-done.24, bf16[288,768]{1,0:T(8,128)(2,1)} %copy-done.51), custom_call_target="tpu_custom_call" | custom-call | flops 452984832 | bytes 2850820 | tf_op jit(solution)/shard_map/pallas_call | solution.py:266
  136.3 1.8 slice_bitcast_fusion.1.refs_1_
  138.1 2.4 %collective-permute-start.42 = (bf16[128,768]{1,0:T(8,128)(2,1)}, bf16[128,768]{1,0:T(8,128)(2,1)S(1)}, u32[]{:S(2)}, u32[]{:S(2)}) collective-permute-start(bf16[128,768]{1,0:T(8,128)(2,1)} %get-tuple-element.72), channel_id=1, source_target_pairs={{0,4},{4,8},{8,12},{12,0},{1,5},{5,9},{9,13},{13,1},{2,6},{6,10},{... | collective-permute-start | bytes 589832 | tf_op jit(solution)/shard_map/ppermute | solution.py:354
  140.5 3.4 %shard_map.148 = (bf16[128,768]{1,0:T(8,128)(2,1)}, f32[3,128,768]{2,1,0:T(8,128)}) custom-call(s32[1]{0:T(128)} %bitcast.43.loc, bf16[288,512]{1,0:T(8,128)(2,1)} %get-tuple-element.69.left_own, bf16[288,512]{1,0:T(8,128)(2,1)} %copy-done.56, bf16[288,768]{1,0:T(8,128)(2,1)} %copy-done.23, bf16[288,768]{1,0:T(8,128)(2,1)} %copy-done.52), custom_call_target="tpu_custom_call" | custom-call | flops 452984832 | bytes 2850820 | tf_op jit(solution)/shard_map/pallas_call | solution.py:266
  143.9 1.8 slice_bitcast_fusion.refs_3_
  150.7 3.4 %shard_map.141 = (bf16[144,1024]{1,0:T(8,128)(2,1)}, bf16[144,1024]{1,0:T(8,128)(2,1)}) custom-call(f32[1,1024]{1,0:T(1,128)} %bitcast.154, bf16[288,1024]{1,0:T(8,128)(2,1)} %get-tuple-element.56.here, bf16[288,1024]{1,0:T(8,128)(2,1)} %copy-done.19, bf16[288,1024]{1,0:T(8,128)(2,1)} %get-tuple-element.50.joined, bf16[288,1024]{1,0:T(8,128)(2,1)} %bitcast.144), custom_call_target="tpu_custom_call" | custom-call | bytes 2953216 | tf_op jit(solution)/shard_map/pallas_call | solution.py:266
  156.5 2.4 %collective-permute-start.47 = (bf16[128,768]{1,0:T(8,128)(2,1)S(1)}, bf16[128,768]{1,0:T(8,128)(2,1)S(1)}, u32[]{:S(2)}, u32[]{:S(2)}) collective-permute-start(bf16[128,768]{1,0:T(8,128)(2,1)S(1)} %fusion.5), channel_id=1, source_target_pairs={{0,4},{4,8},{8,12},{12,0},{1,5},{5,9},{9,13},{13,1},{2,6},{6,10},{... | collective-permute-start | bytes 589832 | tf_op jit(solution)/shard_map/ppermute | solution.py:354
  158.9 6.1 %collective-permute-done.43 = bf16[128,768]{1,0:T(8,128)(2,1)S(1)} collective-permute-done((bf16[128,768]{1,0:T(8,128)(2,1)S(1)}, bf16[128,768]{1,0:T(8,128)(2,1)S(1)}, u32[]{:S(2)}, u32[]{:S(2)}) %collective-permute-start.43) | collective-permute-done | bytes 196640 | tf_op jit(solution)/shard_map/ppermute | solution.py:354
  165.9 6.6 %shard_map.142 = (bf16[288,512]{1,0:T(8,128)(2,1)}, bf16[288,512]{1,0:T(8,128)(2,1)}, bf16[288,1536]{1,0:T(8,128)(2,1)}) custom-call(s32[1]{0:T(128)} %bitcast.place, s32[5]{0:T(128)} %stack.29.offsets, bf16[288,1536]{1,0:T(8,128)(2,1)} %get-tuple-element.54.triple, f32[6,384,96]{2,1,0:T(8,128)} %get-tuple-element.55.attend, ...), custom_call_target="tpu_custom_call" | custom-call | flops 1207959552 | bytes 6848536 | tf_op jit(solution)/shard_map/pallas_call | solution.py:266
  174.1 2.1 collective-permute-start.24
  176.3 4.0 %collective-permute-done.48.refs_2_ = bf16[128,768]{1,0:T(8,128)(2,1)S(1)} collective-permute-done((bf16[128,768]{1,0:T(8,128)(2,1)S(1)}, bf16[128,768]{1,0:T(8,128)(2,1)S(1)}, u32[]{:S(2)}, u32[]{:S(2)}) %collective-permute-start.48) | collective-permute-done | bytes 196640 | tf_op jit(solution)/shard_map/ppermute | solution.py:354
  180.3 2.0 collective-permute-start.27
  182.3 2.7 %shard_map.150 = f32[128,4,512]{2,1,0:T(4,128)} custom-call(bf16[128,768]{1,0:T(8,128)(2,1)} %copy-done.32, f32[128,768]{1,0:T(8,128)} %slice_bitcast_fusion.1.refs_1_, bf16[128,768]{1,0:T(8,128)(2,1)} %copy-done.33, f32[128,768]{1,0:T(8,128)} %slice_bitcast_fusion.refs_3_, bf16[128,512]{1,0:T(8,128)(2,1)} %copy-done.36, f32[128,512]{1,0:T(8,128)} %slice_bitcast_fusion.4.refs_5_), custom_call_target="tpu_custom_call" | custom-call | bytes 2621440 | tf_op jit(solution)/shard_map/pallas_call | solution.py:266
  185.8 2.9 %shard_map.145 = (bf16[128,512]{1,0:T(8,128)(2,1)}, f32[3,128,512]{2,1,0:T(8,128)}) custom-call(s32[1]{0:T(128)} %bitcast.43.loc, bf16[288,512]{1,0:T(8,128)(2,1)} %get-tuple-element.64.left_own, bf16[288,512]{1,0:T(8,128)(2,1)} %copy-done.29, bf16[288,512]{1,0:T(8,128)(2,1)} %get-tuple-element.66.right_own, bf16[288,512]{1,0:T(8,128)(2,1)} %copy-done.27), custom_call_target="tpu_custom_call" | custom-call | flops 301989888 | bytes 2097156 | tf_op jit(solution)/shard_map/pallas_call | solution.py:266
  190.4 5.3 %collective-permute-done.37 = bf16[128,512]{1,0:T(8,128)(2,1)S(1)} collective-permute-done((bf16[128,512]{1,0:T(8,128)(2,1)}, bf16[128,512]{1,0:T(8,128)(2,1)S(1)}, u32[]{:S(2)}, u32[]{:S(2)}) %collective-permute-start.37) | collective-permute-done | bytes 131104 | tf_op jit(solution)/shard_map/ppermute | solution.py:354
  196.7 1.8 collective-permute-done.27.right_other
  199.3 3.4 %shard_map.143 = (bf16[128,768]{1,0:T(8,128)(2,1)}, f32[3,128,768]{2,1,0:T(8,128)}) custom-call(s32[1]{0:T(128)} %bitcast.43.loc, bf16[288,512]{1,0:T(8,128)(2,1)} %get-tuple-element.52.left_own, bf16[288,512]{1,0:T(8,128)(2,1)} %copy-done.55, bf16[288,768]{1,0:T(8,128)(2,1)} %copy-done.22, bf16[288,768]{1,0:T(8,128)(2,1)} %copy-done.50), custom_call_target="tpu_custom_call" | custom-call | flops 452984832 | bytes 2850820 | tf_op jit(solution)/shard_map/pallas_call | solution.py:266
  203.8 3.4 %shard_map.144 = (bf16[128,768]{1,0:T(8,128)(2,1)}, f32[3,128,768]{2,1,0:T(8,128)}) custom-call(s32[1]{0:T(128)} %bitcast.43.loc, bf16[288,512]{1,0:T(8,128)(2,1)} %get-tuple-element.52.left_own, bf16[288,512]{1,0:T(8,128)(2,1)} %copy-done.55, bf16[288,768]{1,0:T(8,128)(2,1)} %copy-done.21, bf16[288,768]{1,0:T(8,128)(2,1)} %copy-done.49), custom_call_target="tpu_custom_call" | custom-call | flops 452984832 | bytes 2850820 | tf_op jit(solution)/shard_map/pallas_call | solution.py:266
  207.2 3.5 %collective-permute-start.32 = (bf16[128,768]{1,0:T(8,128)(2,1)}, bf16[128,768]{1,0:T(8,128)(2,1)S(1)}, u32[]{:S(2)}, u32[]{:S(2)}) collective-permute-start(bf16[128,768]{1,0:T(8,128)(2,1)} %get-tuple-element.62), channel_id=1, source_target_pairs={{0,4},{4,8},{8,12},{12,0},{1,5},{5,9},{9,13},{13,1},{2,6},{6,10},{... | collective-permute-start | bytes 589832 | tf_op jit(solution)/shard_map/ppermute | solution.py:354
  213.7 3.3 %collective-permute-done.32 = bf16[128,768]{1,0:T(8,128)(2,1)S(1)} collective-permute-done((bf16[128,768]{1,0:T(8,128)(2,1)}, bf16[128,768]{1,0:T(8,128)(2,1)S(1)}, u32[]{:S(2)}, u32[]{:S(2)}) %collective-permute-start.32) | collective-permute-done | bytes 196640 | tf_op jit(solution)/shard_map/ppermute | solution.py:354
  217.1 1.8 collective-permute-start.33
  218.8 4.7 %collective-permute-done.29 = bf16[128,768]{1,0:T(8,128)(2,1)S(1)} collective-permute-done((bf16[128,768]{1,0:T(8,128)(2,1)S(1)}, bf16[128,768]{1,0:T(8,128)(2,1)S(1)}, u32[]{:S(2)}, u32[]{:S(2)}) %collective-permute-start.29) | collective-permute-done | bytes 196640 | tf_op jit(solution)/shard_map/ppermute | solution.py:354
  223.6 2.2 collective-permute-start.30
  225.9 1.9 collective-permute-done.33
  229.4 1.7 collective-permute-done.30.refs_0_
  231.1 4.2 %collective-permute-done.34.refs_2_ = bf16[128,768]{1,0:T(8,128)(2,1)S(1)} collective-permute-done((bf16[128,768]{1,0:T(8,128)(2,1)S(1)}, bf16[128,768]{1,0:T(8,128)(2,1)S(1)}, u32[]{:S(2)}, u32[]{:S(2)}) %collective-permute-start.34) | collective-permute-done | bytes 196640 | tf_op jit(solution)/shard_map/ppermute | solution.py:354
  236.0 2.7 %shard_map.146 = f32[128,4,512]{2,1,0:T(4,128)} custom-call(bf16[128,768]{1,0:T(8,128)(2,1)} %copy-done.34, f32[128,768]{1,0:T(8,128)} %slice_bitcast_fusion.3.refs_1_, bf16[128,768]{1,0:T(8,128)(2,1)} %copy-done.35, f32[128,768]{1,0:T(8,128)} %slice_bitcast_fusion.2.refs_3_, bf16[128,512]{1,0:T(8,128)(2,1)} %copy-done.38, ...), custom_call_target="tpu_custom_call" | custom-call | bytes 2621440 | tf_op jit(solution)/shard_map/pallas_call | solution.py:266
  (276 shorter events, 70.1 us)
Async XLA Ops:
  6.2 11.2 %collective-permute-start.5 = (bf16[2,128,512]{2,1,0:T(8,128)(2,1)S(1)}, bf16[2,128,512]{2,1,0:T(8,128)(2,1)S(1)}, u32[]{:S(2)}, u32[]{:S(2)}) collective-permute-start(bf16[2,128,512]{2,1,0:T(8,128)(2,1)S(1)} %get-tuple-element.93), channel_id=1, source_target_pairs={{0,2},{2,0},{1,3},{3,1},{4,6},{6,4},{5,7},{7,5},{8,10},{10,8},{9,1... | collective-permute-start | bytes 786440 | tf_op jit(solution)/shard_map/ppermute | solution.py:278
  9.2 12.0 %collective-permute-start = (bf16[2,128,512]{2,1,0:T(8,128)(2,1)S(1)}, bf16[2,128,512]{2,1,0:T(8,128)(2,1)}, u32[]{:S(2)}, u32[]{:S(2)}) collective-permute-start(bf16[2,128,512]{2,1,0:T(8,128)(2,1)S(1)} %get-tuple-element.94), channel_id=1, source_target_pairs={{0,2},{2,0},{1,3},{3,1},{4,6},{6,4},{5,7},{7,5},{8,10},{10,8},{9,1... | collective-permute-start | bytes 786440 | tf_op jit(solution)/shard_map/ppermute | solution.py:278
  17.5 9.3 %collective-permute-start.7 = (bf16[2,128,512]{2,1,0:T(8,128)(2,1)S(1)}, bf16[2,128,512]{2,1,0:T(8,128)(2,1)S(1)}, u32[]{:S(2)}, u32[]{:S(2)}) collective-permute-start(bf16[2,128,512]{2,1,0:T(8,128)(2,1)S(1)} %collective-permute-done.5.refs_8_.refs_3_), channel_id=1, source_target_pairs={{0,4},{4,0},{8,12},{12,8},{1,5},{5,1},{9,13},{13,9},{2,6},{6,2},{1... | collective-permute-start | bytes 786440 | tf_op jit(solution)/shard_map/ppermute | solution.py:304
  19.6 9.3 %collective-permute-start.6 = (bf16[2,128,512]{2,1,0:T(8,128)(2,1)S(1)}, bf16[2,128,512]{2,1,0:T(8,128)(2,1)S(1)}, u32[]{:S(2)}, u32[]{:S(2)}) collective-permute-start(bf16[2,128,512]{2,1,0:T(8,128)(2,1)S(1)} %collective-permute-done.5.refs_8_.refs_3_), channel_id=1, source_target_pairs={{0,16},{16,0},{1,17},{17,1},{2,18},{18,2},{3,19},{19,3},{4,20},{20... | collective-permute-start | bytes 786440 | tf_op jit(solution)/shard_map/ppermute | solution.py:278
  21.3 11.1 %collective-permute-start.2 = (bf16[2,128,512]{2,1,0:T(8,128)(2,1)}, bf16[2,128,512]{2,1,0:T(8,128)(2,1)S(1)}, u32[]{:S(2)}, u32[]{:S(2)}) collective-permute-start(bf16[2,128,512]{2,1,0:T(8,128)(2,1)} %collective-permute-done.refs_3_), channel_id=1, source_target_pairs={{0,4},{4,0},{8,12},{12,8},{1,5},{5,1},{9,13},{13,9},{2,6},{6,2},{1... | collective-permute-start | bytes 786440 | tf_op jit(solution)/shard_map/ppermute | solution.py:304
  23.1 11.3 %collective-permute-start.1 = (bf16[2,128,512]{2,1,0:T(8,128)(2,1)}, bf16[2,128,512]{2,1,0:T(8,128)(2,1)S(1)}, u32[]{:S(2)}, u32[]{:S(2)}) collective-permute-start(bf16[2,128,512]{2,1,0:T(8,128)(2,1)} %collective-permute-done.refs_3_), channel_id=1, source_target_pairs={{0,16},{16,0},{1,17},{17,1},{2,18},{18,2},{3,19},{19,3},{4,20},{20... | collective-permute-start | bytes 786440 | tf_op jit(solution)/shard_map/ppermute | solution.py:278
  26.8 10.3 %collective-permute-start.8 = (bf16[1,128,512]{2,1,0:T(8,128)(2,1)S(1)}, bf16[1,128,512]{2,1,0:T(8,128)(2,1)S(1)}, u32[]{:S(2)}, u32[]{:S(2)}) collective-permute-start(bf16[1,128,512]{2,1,0:T(8,128)(2,1)S(1)} %slice.197), channel_id=1, source_target_pairs={{0,16},{16,0},{1,17},{17,1},{2,18},{18,2},{3,19},{19,3},{4,20},{20... | collective-permute-start | bytes 393224 | tf_op jit(solution)/shard_map/ppermute | solution.py:278
  28.9 8.3 %collective-permute-start.9 = (bf16[1,128,512]{2,1,0:T(8,128)(2,1)S(1)}, bf16[1,128,512]{2,1,0:T(8,128)(2,1)S(1)}, u32[]{:S(2)}, u32[]{:S(2)}) collective-permute-start(bf16[1,128,512]{2,1,0:T(8,128)(2,1)S(1)} %slice.198), channel_id=1, source_target_pairs={{0,4},{4,0},{8,12},{12,8},{1,5},{5,1},{9,13},{13,9},{2,6},{6,2},{1... | collective-permute-start | bytes 393224 | tf_op jit(solution)/shard_map/ppermute | solution.py:305
  47.4 16.3 %collective-permute-start.11 = (bf16[144,1024]{1,0:T(8,128)(2,1)}, bf16[144,1024]{1,0:T(8,128)(2,1)S(1)}, u32[]{:S(2)}, u32[]{:S(2)}) collective-permute-start(bf16[144,1024]{1,0:T(8,128)(2,1)} %get-tuple-element.49), channel_id=1, source_target_pairs={{0,1},{1,0},{2,3},{3,2},{4,5},{5,4},{6,7},{7,6},{8,9},{9,8},{10,11... | collective-permute-start | bytes 884744 | tf_op jit(solution)/shard_map/ppermute | solution.py:278
  47.6 9.2 %collective-permute-start.18 = (bf16[2,128,512]{2,1,0:T(8,128)(2,1)S(1)}, bf16[2,128,512]{2,1,0:T(8,128)(2,1)S(1)}, u32[]{:S(2)}, u32[]{:S(2)}) collective-permute-start(bf16[2,128,512]{2,1,0:T(8,128)(2,1)S(1)} %get-tuple-element.91), channel_id=1, source_target_pairs={{0,2},{2,0},{1,3},{3,1},{4,6},{6,4},{5,7},{7,5},{8,10},{10,8},{9,1... | collective-permute-start | bytes 786440 | tf_op jit(solution)/shard_map/ppermute | solution.py:278
  49.1 12.8 %collective-permute-start.13 = (bf16[2,128,512]{2,1,0:T(8,128)(2,1)S(1)}, bf16[2,128,512]{2,1,0:T(8,128)(2,1)S(1)}, u32[]{:S(2)}, u32[]{:S(2)}) collective-permute-start(bf16[2,128,512]{2,1,0:T(8,128)(2,1)S(1)} %get-tuple-element.92), channel_id=1, source_target_pairs={{0,2},{2,0},{1,3},{3,1},{4,6},{6,4},{5,7},{7,5},{8,10},{10,8},{9,1... | collective-permute-start | bytes 786440 | tf_op jit(solution)/shard_map/ppermute | solution.py:278
  56.7 7.5 %collective-permute-start.20 = (bf16[2,128,512]{2,1,0:T(8,128)(2,1)S(1)}, bf16[2,128,512]{2,1,0:T(8,128)(2,1)S(1)}, u32[]{:S(2)}, u32[]{:S(2)}) collective-permute-start(bf16[2,128,512]{2,1,0:T(8,128)(2,1)S(1)} %collective-permute-done.18.refs_10_), channel_id=1, source_target_pairs={{0,4},{4,0},{8,12},{12,8},{1,5},{5,1},{9,13},{13,9},{2,6},{6,2},{1... | collective-permute-start | bytes 786440 | tf_op jit(solution)/shard_map/ppermute | solution.py:304
  58.0 7.8 %collective-permute-start.19 = (bf16[2,128,512]{2,1,0:T(8,128)(2,1)S(1)}, bf16[2,128,512]{2,1,0:T(8,128)(2,1)S(1)}, u32[]{:S(2)}, u32[]{:S(2)}) collective-permute-start(bf16[2,128,512]{2,1,0:T(8,128)(2,1)S(1)} %collective-permute-done.18.refs_10_), channel_id=1, source_target_pairs={{0,16},{16,0},{1,17},{17,1},{2,18},{18,2},{3,19},{19,3},{4,20},{20... | collective-permute-start | bytes 786440 | tf_op jit(solution)/shard_map/ppermute | solution.py:278
  61.9 7.9 %collective-permute-start.15 = (bf16[2,128,512]{2,1,0:T(8,128)(2,1)S(1)}, bf16[2,128,512]{2,1,0:T(8,128)(2,1)S(1)}, u32[]{:S(2)}, u32[]{:S(2)}) collective-permute-start(bf16[2,128,512]{2,1,0:T(8,128)(2,1)S(1)} %collective-permute-done.13.refs_5_), channel_id=1, source_target_pairs={{0,4},{4,0},{8,12},{12,8},{1,5},{5,1},{9,13},{13,9},{2,6},{6,2},{1... | collective-permute-start | bytes 786440 | tf_op jit(solution)/shard_map/ppermute | solution.py:304
  63.2 9.0 %collective-permute-start.14 = (bf16[2,128,512]{2,1,0:T(8,128)(2,1)S(1)}, bf16[2,128,512]{2,1,0:T(8,128)(2,1)S(1)}, u32[]{:S(2)}, u32[]{:S(2)}) collective-permute-start(bf16[2,128,512]{2,1,0:T(8,128)(2,1)S(1)} %collective-permute-done.13.refs_5_), channel_id=1, source_target_pairs={{0,16},{16,0},{1,17},{17,1},{2,18},{18,2},{3,19},{19,3},{4,20},{20... | collective-permute-start | bytes 786440 | tf_op jit(solution)/shard_map/ppermute | solution.py:278
  63.8 16.1 %collective-permute-start.10 = (bf16[144,1024]{1,0:T(8,128)(2,1)}, bf16[144,1024]{1,0:T(8,128)(2,1)S(1)}, u32[]{:S(2)}, u32[]{:S(2)}) collective-permute-start(bf16[144,1024]{1,0:T(8,128)(2,1)} %get-tuple-element.48.refs_1_), channel_id=1, source_target_pairs={{0,1},{1,0},{2,3},{3,2},{4,5},{5,4},{6,7},{7,6},{8,9},{9,8},{10,11... | collective-permute-start | bytes 884744 | tf_op jit(solution)/shard_map/ppermute | solution.py:278
  64.3 15.6 %collective-permute-start.12 = (bf16[144,1024]{1,0:T(8,128)(2,1)S(1)}, bf16[144,1024]{1,0:T(8,128)(2,1)S(1)}, u32[]{:S(2)}, u32[]{:S(2)}) collective-permute-start(bf16[144,1024]{1,0:T(8,128)(2,1)S(1)} %add_convert_fusion.1), channel_id=1, source_target_pairs={{0,2},{2,0},{1,3},{3,1},{4,6},{6,4},{5,7},{7,5},{8,10},{10,8},{9,1... | collective-permute-start | bytes 884744 | tf_op jit(solution)/shard_map/ppermute | solution.py:278
  65.8 9.1 %collective-permute-start.21 = (bf16[1,128,512]{2,1,0:T(8,128)(2,1)S(1)}, bf16[1,128,512]{2,1,0:T(8,128)(2,1)S(1)}, u32[]{:S(2)}, u32[]{:S(2)}) collective-permute-start(bf16[1,128,512]{2,1,0:T(8,128)(2,1)S(1)} %slice.203), channel_id=1, source_target_pairs={{0,16},{16,0},{1,17},{17,1},{2,18},{18,2},{3,19},{19,3},{4,20},{20... | collective-permute-start | bytes 393224 | tf_op jit(solution)/shard_map/ppermute | solution.py:278
  93.4 10.2 %collective-permute-start.49 = (bf16[288,512]{1,0:T(8,128)(2,1)}, bf16[288,512]{1,0:T(8,128)(2,1)S(1)}, u32[]{:S(2)}, u32[]{:S(2)}) collective-permute-start(bf16[288,512]{1,0:T(8,128)(2,1)} %get-tuple-element.77), channel_id=1, source_target_pairs={{0,2},{2,0},{1,3},{3,1},{4,6},{6,4},{5,7},{7,5},{8,10},{10,8},{9,1... | collective-permute-start | bytes 884744 | tf_op jit(solution)/shard_map/ppermute | solution.py:278
  95.0 15.0 %collective-permute-start.50 = (bf16[288,512]{1,0:T(8,128)(2,1)}, bf16[288,512]{1,0:T(8,128)(2,1)S(1)}, u32[]{:S(2)}, u32[]{:S(2)}) collective-permute-start(bf16[288,512]{1,0:T(8,128)(2,1)} %get-tuple-element.78.right_own), channel_id=1, source_target_pairs={{0,2},{2,0},{1,3},{3,1},{4,6},{6,4},{5,7},{7,5},{8,10},{10,8},{9,1... | collective-permute-start | bytes 884744 | tf_op jit(solution)/shard_map/ppermute | solution.py:278
  95.5 89.5 %collective-permute-start.36 = (bf16[288,512]{1,0:T(8,128)(2,1)S(1)}, bf16[288,512]{1,0:T(8,128)(2,1)S(1)}, u32[]{:S(2)}, u32[]{:S(2)}) collective-permute-start(bf16[288,512]{1,0:T(8,128)(2,1)S(1)} %copy-done.26), channel_id=1, source_target_pairs={{0,2},{2,0},{1,3},{3,1},{4,6},{6,4},{5,7},{7,5},{8,10},{10,8},{9,1... | collective-permute-start | bytes 884744 | tf_op jit(solution)/shard_map/ppermute | solution.py:278
  97.0 26.0 %collective-permute-start.40 = (bf16[288,512]{1,0:T(8,128)(2,1)}, bf16[288,512]{1,0:T(8,128)(2,1)S(1)}, u32[]{:S(2)}, u32[]{:S(2)}) collective-permute-start(bf16[288,512]{1,0:T(8,128)(2,1)} %get-tuple-element.70), channel_id=1, source_target_pairs={{0,2},{2,0},{1,3},{3,1},{4,6},{6,4},{5,7},{7,5},{8,10},{10,8},{9,1... | collective-permute-start | bytes 884744 | tf_op jit(solution)/shard_map/ppermute | solution.py:278
  97.5 49.9 %collective-permute-start.23 = (bf16[288,1024]{1,0:T(8,128)(2,1)}, bf16[288,1024]{1,0:T(8,128)(2,1)S(1)}, u32[]{:S(2)}, u32[]{:S(2)}) collective-permute-start(bf16[288,1024]{1,0:T(8,128)(2,1)} %get-tuple-element.51), channel_id=1, source_target_pairs={{0,1},{1,0},{2,3},{3,2},{4,5},{5,4},{6,7},{7,6},{8,9},{9,8},{10,11... | collective-permute-start | bytes 1769480 | tf_op jit(solution)/shard_map/ppermute | solution.py:278
  103.6 28.4 %collective-permute-start.41 = (bf16[288,768]{1,0:T(8,128)(2,1)S(1)}, bf16[288,768]{1,0:T(8,128)(2,1)S(1)}, u32[]{:S(2)}, u32[]{:S(2)}) collective-permute-start(bf16[288,768]{1,0:T(8,128)(2,1)S(1)} %get-tuple-element.86.right_own), channel_id=1, source_target_pairs={{0,2},{2,0},{1,3},{3,1},{4,6},{6,4},{5,7},{7,5},{8,10},{10,8},{9,1... | collective-permute-start | bytes 1327112 | tf_op jit(solution)/shard_map/ppermute | solution.py:278
  113.6 7.0 %collective-permute-start.51 = (bf16[128,512]{1,0:T(8,128)(2,1)}, bf16[128,512]{1,0:T(8,128)(2,1)S(1)}, u32[]{:S(2)}, u32[]{:S(2)}) collective-permute-start(bf16[128,512]{1,0:T(8,128)(2,1)} %get-tuple-element.79), channel_id=1, source_target_pairs={{0,4},{4,8},{8,12},{12,0},{1,5},{5,9},{9,13},{13,1},{2,6},{6,10},{... | collective-permute-start | bytes 393224 | tf_op jit(solution)/shard_map/ppermute | solution.py:354
  120.5 17.5 %collective-permute-start.45 = (bf16[288,768]{1,0:T(8,128)(2,1)S(1)}, bf16[288,768]{1,0:T(8,128)(2,1)S(1)}, u32[]{:S(2)}, u32[]{:S(2)}) collective-permute-start(bf16[288,768]{1,0:T(8,128)(2,1)S(1)} %get-tuple-element.85.right_own), channel_id=1, source_target_pairs={{0,2},{2,0},{1,3},{3,1},{4,6},{6,4},{5,7},{7,5},{8,10},{10,8},{9,1... | collective-permute-start | bytes 1327112 | tf_op jit(solution)/shard_map/ppermute | solution.py:278
  123.0 26.8 %collective-permute-start.25 = (bf16[288,1024]{1,0:T(8,128)(2,1)S(1)}, bf16[288,1024]{1,0:T(8,128)(2,1)S(1)}, u32[]{:S(2)}, u32[]{:S(2)}) collective-permute-start(bf16[288,1024]{1,0:T(8,128)(2,1)S(1)} %copy-done.17), channel_id=1, source_target_pairs={{0,1},{1,0},{2,3},{3,2},{4,5},{5,4},{6,7},{7,6},{8,9},{9,8},{10,11... | collective-permute-start | bytes 1769480 | tf_op jit(solution)/shard_map/ppermute | solution.py:278
  132.1 13.6 %collective-permute-start.52 = (bf16[128,512]{1,0:T(8,128)(2,1)S(1)}, bf16[128,512]{1,0:T(8,128)(2,1)S(1)}, u32[]{:S(2)}, u32[]{:S(2)}) collective-permute-start(bf16[128,512]{1,0:T(8,128)(2,1)S(1)} %fusion.13), channel_id=1, source_target_pairs={{0,4},{4,8},{8,12},{12,0},{1,5},{5,9},{9,13},{13,1},{2,6},{6,10},{... | collective-permute-start | bytes 393224 | tf_op jit(solution)/shard_map/ppermute | solution.py:354
  138.1 17.5 %collective-permute-start.42 = (bf16[128,768]{1,0:T(8,128)(2,1)}, bf16[128,768]{1,0:T(8,128)(2,1)S(1)}, u32[]{:S(2)}, u32[]{:S(2)}) collective-permute-start(bf16[128,768]{1,0:T(8,128)(2,1)} %get-tuple-element.72), channel_id=1, source_target_pairs={{0,4},{4,8},{8,12},{12,0},{1,5},{5,9},{9,13},{13,1},{2,6},{6,10},{... | collective-permute-start | bytes 589832 | tf_op jit(solution)/shard_map/ppermute | solution.py:354
  145.7 10.7 %collective-permute-start.46 = (bf16[128,768]{1,0:T(8,128)(2,1)}, bf16[128,768]{1,0:T(8,128)(2,1)S(1)}, u32[]{:S(2)}, u32[]{:S(2)}) collective-permute-start(bf16[128,768]{1,0:T(8,128)(2,1)} %get-tuple-element.74), channel_id=1, source_target_pairs={{0,4},{4,8},{8,12},{12,0},{1,5},{5,9},{9,13},{13,1},{2,6},{6,10},{... | collective-permute-start | bytes 589832 | tf_op jit(solution)/shard_map/ppermute | solution.py:354
  147.5 26.6 %collective-permute-start.53 = (bf16[128,512]{1,0:T(8,128)(2,1)S(1)}, bf16[128,512]{1,0:T(8,128)(2,1)S(1)}, u32[]{:S(2)}, u32[]{:S(2)}) collective-permute-start(bf16[128,512]{1,0:T(8,128)(2,1)S(1)} %fusion.12), channel_id=1, source_target_pairs={{0,4},{4,8},{8,12},{12,0},{1,5},{5,9},{9,13},{13,1},{2,6},{6,10},{... | collective-permute-start | bytes 393224 | tf_op jit(solution)/shard_map/ppermute | solution.py:354
  154.0 11.1 %collective-permute-start.26 = (bf16[144,1024]{1,0:T(8,128)(2,1)}, bf16[144,1024]{1,0:T(8,128)(2,1)S(1)}, u32[]{:S(2)}, u32[]{:S(2)}) collective-permute-start(bf16[144,1024]{1,0:T(8,128)(2,1)} %get-tuple-element.58), channel_id=1, source_target_pairs={{0,2},{2,0},{1,3},{3,1},{4,6},{6,4},{5,7},{7,5},{8,10},{10,8},{9,1... | collective-permute-start | bytes 884744 | tf_op jit(solution)/shard_map/ppermute | solution.py:278
  155.6 9.4 %collective-permute-start.43 = (bf16[128,768]{1,0:T(8,128)(2,1)S(1)}, bf16[128,768]{1,0:T(8,128)(2,1)S(1)}, u32[]{:S(2)}, u32[]{:S(2)}) collective-permute-start(bf16[128,768]{1,0:T(8,128)(2,1)S(1)} %fusion.7), channel_id=1, source_target_pairs={{0,4},{4,8},{8,12},{12,0},{1,5},{5,9},{9,13},{13,1},{2,6},{6,10},{... | collective-permute-start | bytes 589832 | tf_op jit(solution)/shard_map/ppermute | solution.py:354
  156.5 16.0 %collective-permute-start.47 = (bf16[128,768]{1,0:T(8,128)(2,1)S(1)}, bf16[128,768]{1,0:T(8,128)(2,1)S(1)}, u32[]{:S(2)}, u32[]{:S(2)}) collective-permute-start(bf16[128,768]{1,0:T(8,128)(2,1)S(1)} %fusion.5), channel_id=1, source_target_pairs={{0,4},{4,8},{8,12},{12,0},{1,5},{5,9},{9,13},{13,1},{2,6},{6,10},{... | collective-permute-start | bytes 589832 | tf_op jit(solution)/shard_map/ppermute | solution.py:354
  165.1 11.1 %collective-permute-start.44 = (bf16[128,768]{1,0:T(8,128)(2,1)S(1)}, bf16[128,768]{1,0:T(8,128)(2,1)S(1)}, u32[]{:S(2)}, u32[]{:S(2)}) collective-permute-start(bf16[128,768]{1,0:T(8,128)(2,1)S(1)} %fusion.6), channel_id=1, source_target_pairs={{0,4},{4,8},{8,12},{12,0},{1,5},{5,9},{9,13},{13,1},{2,6},{6,10},{... | collective-permute-start | bytes 589832 | tf_op jit(solution)/shard_map/ppermute | solution.py:354
  172.5 12.6 %collective-permute-start.35 = (bf16[288,512]{1,0:T(8,128)(2,1)}, bf16[288,512]{1,0:T(8,128)(2,1)S(1)}, u32[]{:S(2)}, u32[]{:S(2)}) collective-permute-start(bf16[288,512]{1,0:T(8,128)(2,1)} %get-tuple-element.65), channel_id=1, source_target_pairs={{0,2},{2,0},{1,3},{3,1},{4,6},{6,4},{5,7},{7,5},{8,10},{10,8},{9,1... | collective-permute-start | bytes 884744 | tf_op jit(solution)/shard_map/ppermute | solution.py:278
  172.5 7.7 %collective-permute-start.48 = (bf16[128,768]{1,0:T(8,128)(2,1)S(1)}, bf16[128,768]{1,0:T(8,128)(2,1)S(1)}, u32[]{:S(2)}, u32[]{:S(2)}) collective-permute-start(bf16[128,768]{1,0:T(8,128)(2,1)S(1)} %fusion.4), channel_id=1, source_target_pairs={{0,4},{4,8},{8,12},{12,0},{1,5},{5,9},{9,13},{13,1},{2,6},{6,10},{... | collective-permute-start | bytes 589832 | tf_op jit(solution)/shard_map/ppermute | solution.py:354
  174.1 22.6 %collective-permute-start.24 = (bf16[288,512]{1,0:T(8,128)(2,1)S(1)}, bf16[288,512]{1,0:T(8,128)(2,1)S(1)}, u32[]{:S(2)}, u32[]{:S(2)}) collective-permute-start(bf16[288,512]{1,0:T(8,128)(2,1)S(1)} %copy-done.53), channel_id=1, source_target_pairs={{0,2},{2,0},{1,3},{3,1},{4,6},{6,4},{5,7},{7,5},{8,10},{10,8},{9,1... | collective-permute-start | bytes 884744 | tf_op jit(solution)/shard_map/ppermute | solution.py:278
  176.2 26.9 %collective-permute-start.31 = (bf16[288,768]{1,0:T(8,128)(2,1)S(1)}, bf16[288,768]{1,0:T(8,128)(2,1)S(1)}, u32[]{:S(2)}, u32[]{:S(2)}) collective-permute-start(bf16[288,768]{1,0:T(8,128)(2,1)S(1)} %get-tuple-element.87.right_own), channel_id=1, source_target_pairs={{0,2},{2,0},{1,3},{3,1},{4,6},{6,4},{5,7},{7,5},{8,10},{10,8},{9,1... | collective-permute-start | bytes 1327112 | tf_op jit(solution)/shard_map/ppermute | solution.py:278
  180.3 18.3 %collective-permute-start.27 = (bf16[288,768]{1,0:T(8,128)(2,1)S(1)}, bf16[288,768]{1,0:T(8,128)(2,1)S(1)}, u32[]{:S(2)}, u32[]{:S(2)}) collective-permute-start(bf16[288,768]{1,0:T(8,128)(2,1)S(1)} %get-tuple-element.88.right_own), channel_id=1, source_target_pairs={{0,2},{2,0},{1,3},{3,1},{4,6},{6,4},{5,7},{7,5},{8,10},{10,8},{9,1... | collective-permute-start | bytes 1327112 | tf_op jit(solution)/shard_map/ppermute | solution.py:278
  196.6 14.8 %collective-permute-start.38 = (bf16[128,512]{1,0:T(8,128)(2,1)S(1)}, bf16[128,512]{1,0:T(8,128)(2,1)S(1)}, u32[]{:S(2)}, u32[]{:S(2)}) collective-permute-start(bf16[128,512]{1,0:T(8,128)(2,1)S(1)} %fusion.15), channel_id=1, source_target_pairs={{0,4},{4,8},{8,12},{12,0},{1,5},{5,9},{9,13},{13,1},{2,6},{6,10},{... | collective-permute-start | bytes 393224 | tf_op jit(solution)/shard_map/ppermute | solution.py:354
  202.7 10.6 %collective-permute-start.28 = (bf16[128,768]{1,0:T(8,128)(2,1)}, bf16[128,768]{1,0:T(8,128)(2,1)S(1)}, u32[]{:S(2)}, u32[]{:S(2)}) collective-permute-start(bf16[128,768]{1,0:T(8,128)(2,1)} %get-tuple-element.60), channel_id=1, source_target_pairs={{0,4},{4,8},{8,12},{12,0},{1,5},{5,9},{9,13},{13,1},{2,6},{6,10},{... | collective-permute-start | bytes 589832 | tf_op jit(solution)/shard_map/ppermute | solution.py:354
  207.2 9.8 %collective-permute-start.32 = (bf16[128,768]{1,0:T(8,128)(2,1)}, bf16[128,768]{1,0:T(8,128)(2,1)S(1)}, u32[]{:S(2)}, u32[]{:S(2)}) collective-permute-start(bf16[128,768]{1,0:T(8,128)(2,1)} %get-tuple-element.62), channel_id=1, source_target_pairs={{0,4},{4,8},{8,12},{12,0},{1,5},{5,9},{9,13},{13,1},{2,6},{6,10},{... | collective-permute-start | bytes 589832 | tf_op jit(solution)/shard_map/ppermute | solution.py:354
  212.5 17.0 %collective-permute-start.39 = (bf16[128,512]{1,0:T(8,128)(2,1)S(1)}, bf16[128,512]{1,0:T(8,128)(2,1)S(1)}, u32[]{:S(2)}, u32[]{:S(2)}) collective-permute-start(bf16[128,512]{1,0:T(8,128)(2,1)S(1)} %fusion.14), channel_id=1, source_target_pairs={{0,4},{4,8},{8,12},{12,0},{1,5},{5,9},{9,13},{13,1},{2,6},{6,10},{... | collective-permute-start | bytes 393224 | tf_op jit(solution)/shard_map/ppermute | solution.py:354
  213.3 10.2 %collective-permute-start.29 = (bf16[128,768]{1,0:T(8,128)(2,1)S(1)}, bf16[128,768]{1,0:T(8,128)(2,1)S(1)}, u32[]{:S(2)}, u32[]{:S(2)}) collective-permute-start(bf16[128,768]{1,0:T(8,128)(2,1)S(1)} %fusion.11), channel_id=1, source_target_pairs={{0,4},{4,8},{8,12},{12,0},{1,5},{5,9},{9,13},{13,1},{2,6},{6,10},{... | collective-permute-start | bytes 589832 | tf_op jit(solution)/shard_map/ppermute | solution.py:354
  217.1 10.7 %collective-permute-start.33 = (bf16[128,768]{1,0:T(8,128)(2,1)S(1)}, bf16[128,768]{1,0:T(8,128)(2,1)S(1)}, u32[]{:S(2)}, u32[]{:S(2)}) collective-permute-start(bf16[128,768]{1,0:T(8,128)(2,1)S(1)} %fusion.9), channel_id=1, source_target_pairs={{0,4},{4,8},{8,12},{12,0},{1,5},{5,9},{9,13},{13,1},{2,6},{6,10},{... | collective-permute-start | bytes 589832 | tf_op jit(solution)/shard_map/ppermute | solution.py:354
  223.6 7.5 %collective-permute-start.30 = (bf16[128,768]{1,0:T(8,128)(2,1)S(1)}, bf16[128,768]{1,0:T(8,128)(2,1)S(1)}, u32[]{:S(2)}, u32[]{:S(2)}) collective-permute-start(bf16[128,768]{1,0:T(8,128)(2,1)S(1)} %fusion.10), channel_id=1, source_target_pairs={{0,4},{4,8},{8,12},{12,0},{1,5},{5,9},{9,13},{13,1},{2,6},{6,10},{... | collective-permute-start | bytes 589832 | tf_op jit(solution)/shard_map/ppermute | solution.py:354
  227.8 7.5 %collective-permute-start.34 = (bf16[128,768]{1,0:T(8,128)(2,1)S(1)}, bf16[128,768]{1,0:T(8,128)(2,1)S(1)}, u32[]{:S(2)}, u32[]{:S(2)}) collective-permute-start(bf16[128,768]{1,0:T(8,128)(2,1)S(1)} %fusion.8), channel_id=1, source_target_pairs={{0,4},{4,8},{8,12},{12,0},{1,5},{5,9},{9,13},{13,1},{2,6},{6,10},{... | collective-permute-start | bytes 589832 | tf_op jit(solution)/shard_map/ppermute | solution.py:354
  (70 other events, 497.8 us)
where the time goes:
time: 240 us; the launch traced here: 239 us
  waiting for transfers between devices  82 us (34%)
  starting transfers between devices  60.5 us (25%)
  Pallas kernels  54.6 us (23%)
  local copies, waits for them, and re-layouts  28.9 us (12%)
  other arithmetic  11.2 us (5%)
    pallas_call x12, Pallas kernels, call(): pl.pallas_call(body, out_shape=list(outs), in_specs=specs, out_specs=[vme...  54.6 us
    ppermute x28, waiting for transfers between devices, swap(): return lax.ppermute(array, axis, [(0, 1), (1, 0)])  37.1 us
    ppermute x18, waiting for transfers between devices, ring_sum(): arrived = lax.ppermute(total, 'loc', ring)  35.8 us
    ppermute x28, starting transfers between devices, swap(): return lax.ppermute(array, axis, [(0, 1), (1, 0)])  29.7 us
    ppermute x18, starting transfers between devices, ring_sum(): arrived = lax.ppermute(total, 'loc', ring)  19.4 us
    unnamed x130, local copies, waits for them, and re-layouts  11.5 us
    squeeze x6, local copies, waits for them, and re-layouts, ring_sum(): return (arrived, rest[count - 2])  8.49 us
    ppermute x4, starting transfers between devices, gather_weights(): loc = lax.ppermute(across, 'loc', pairs)  6.41 us
  transfers between devices with their start and end apart: 54, of which 27 were waited for; matrix products, arithmetic and copies ran while one was open for 11% of the time, Pallas kernels for 13%

commit v1 on v0

--- a/solution.py
+++ b/solution.py
@@ -79,13 +79,19 @@
         out_ref[:, column + at : column + at + step] = total.astype(out_ref.dtype)
 
 
-def emit_columns(rows_ref, outs, place, date_count, loc_count):
-    block = rows_ref.shape[1] // (date_count * loc_count)
-    for number, out in enumerate(outs):
-        date = place if number == 0 else 1 - place
-        for loc in range(loc_count):
-            at = pl.multiple_of((loc * date_count + date) * block, block)
-            out[:, loc * block : (loc + 1) * block] = rows_ref[:, pl.ds(at, block)]
+def emit_own(rows_ref, out, at, date, loc_count):
+    block = rows_ref.shape[1] // (2 * loc_count)
+    for loc in range(loc_count):
+        first = pl.multiple_of((loc * 2 + date) * block, block)
+        out[:, at + loc * block : at + (loc + 1) * block] = rows_ref[:, pl.ds(first, block)]
+
+
+def emit_half(rows_ref, out, at, date, core, loc_count):
+    block = rows_ref.shape[1] // (2 * loc_count)
+    for number in range(loc_count // 2):
+        loc = core * (loc_count // 2) + number
+        first = pl.multiple_of((loc * 2 + date) * block, block)
+        out[:, at + number * block : at + (number + 1) * block] = rows_ref[:, pl.ds(first, block)]
 
 
 def attention(triple_ref, bias_ref, attend_ref, mixed_ref, blocks):
@@ -142,30 +148,45 @@
         hidden_ref[at, :] = (normed * gain_ref[...]).astype(BF)
 
 
-def spatial_forward_kernel(plan, place, offsets, gain, bias, *refs):
+def spatial_forward_kernel(plan, where, offsets, gain, bias, cotangent, *refs):
     sources, refs = refs[: plan.origins], refs[plan.origins :]
     arrays, refs = refs[: plan.arrays], refs[plan.arrays :]
     partials, refs = refs[: plan.origins], refs[plan.origins :]
-    columns, refs = refs[: plan.columns], refs[plan.columns :]
+    grads, refs = refs[: plan.grads], refs[plan.grads :]
     triple, attend, mixed, start, hidden, whole = refs
     for source, at, to, size in plan.moves:
         start[to : to + size, :] = sources[source][at : at + size, :]
     normalize_into(start, gain, hidden, plan.blocks)
-    plan.emit(hidden, columns, place[0])
+    width = mixed.shape[1]
     for kind in range(3):
-        rows_times(hidden, views(plan.table, arrays, offsets, kind), triple, kind * mixed.shape[1])
+        rows_times(hidden, views(plan.table, arrays, offsets, kind), triple, kind * width)
     attention(triple, bias, attend, mixed, plan.blocks)
     for part, features in views(plan.table, arrays, offsets, 3):
         whole[:, features] = dot(mixed[...], part[...], NT).astype(BF)
     for source, at, to, size in plan.moves:
         partials[source][at : at + size, :] = whole[to : to + size, :]
-
-
-def temporal_kernel(plan, place, offsets, gain, bias, date_rows, cotangent, *refs):
+    if plan.paired:
+        own_hidden, own_cotangent, sent = grads
+        half = hidden.shape[1] // 4
+        here, core = where[0], where[1]
+        emit_own(hidden, own_hidden, 0, here, plan.locs)
+        emit_own(cotangent, own_cotangent, 0, here, plan.locs)
+        emit_half(hidden, sent, 0, 1 - here, core, plan.locs)
+        emit_half(cotangent, sent, half, 1 - here, core, plan.locs)
+        sent[:, 2 * half :] = mixed[...]
+    else:
+        grads[0][...] = hidden[...]
+
+
+def between_kernel(start, here, there, kept, out, passed):
+    total = here[...].astype(F32) + there[...].astype(F32)
+    out[...] = (start[...].astype(F32) + total).astype(BF)
+
+
+def temporal_kernel(plan, where, offsets, gain, bias, date_rows, cotangent, *refs):
     sources, refs = refs[: plan.sources], refs[plan.sources :]
     arrays, refs = refs[: plan.arrays], refs[plan.arrays :]
-    hidden_columns, refs = refs[: plan.columns], refs[plan.columns :]
-    upstream_columns, refs = refs[: plan.columns], refs[plan.columns :]
+    grads, refs = refs[: plan.grads], refs[plan.grads :]
     joined, mixed, partial, back_triple, back_part, hidden, triple, attend, back_mixed = refs
     rows = date_rows.shape[0]
     for source, at, to, size in plan.moves:
@@ -177,8 +198,6 @@
         dated = out.astype(F32) + date_rows[to % rows : to % rows + size, :].astype(F32)
         joined[to : to + size, :] = dated.astype(BF)
     normalize_into(joined, gain, hidden, plan.blocks)
-    plan.emit(hidden, hidden_columns, place[0])
-    plan.emit(cotangent, upstream_columns, place[0])
     width = mixed.shape[1]
     for kind in range(3):
         rows_times(hidden, views(plan.table, arrays, offsets, kind), triple, kind * width)
@@ -187,6 +206,14 @@
     attention(triple, bias, attend, mixed, plan.blocks)
     for part, features in outlet:
         partial[:, features] = dot(mixed[...], part[...], NT).astype(BF)
+    if plan.paired:
+        own_hidden, sent = grads
+        half = hidden.shape[1] // 4
+        emit_own(hidden, own_hidden, 0, where[0], plan.locs)
+        emit_half(hidden, sent, 0, 1 - where[0], where[1], plan.locs)
+        sent[:, half:] = mixed[...]
+    else:
+        grads[0][...] = hidden[...]
     attention_back(triple, attend, back_mixed, back_triple, plan.blocks)
     intakes = [views(plan.table, arrays, offsets, kind) for kind in range(3)]
     for entries in zip(*intakes):
@@ -197,7 +224,7 @@
         back_part[:, features] = total.astype(BF)
 
 
-def norm_back_kernel(moves, step, gain, here, there, joined, cotangent, *outs):
+def norm_back_kernel(moves, step, gain, here, there, joined, cotangent, kept, *outs):
     for at in range(0, joined.shape[0], step):
         span_here = slice(at, at + step)
         normed, inv_scale = statistics(joined[span_here, :])
@@ -214,61 +241,99 @@
                 outs[target][to : to + size, :] = back[first - at : first - at + size]
 
 
-def spatial_backward_kernel(plan, place, offsets, triple, attend, *refs):
+def spatial_backward_kernel(plan, where, offsets, triple, attend, *refs):
     sources, refs = refs[: plan.origins], refs[plan.origins :]
     arrays, refs = refs[: plan.arrays], refs[plan.arrays :]
-    columns, refs = refs[: plan.columns], refs[plan.columns :]
-    back_triple, upstream, back_mixed = refs
+    grads, refs = refs[: plan.grads], refs[plan.grads :]
+    back_triples, (upstream, back_mixed, back_triple) = refs[:-3], refs[-3:]
     for source, at, to, size in plan.moves:
         upstream[to : to + size, :] = sources[source][at : at + size, :]
-    plan.emit(upstream, columns, place[0])
+    if plan.paired:
+        emit_own(upstream, grads[0], 0, where[0], plan.locs)
+        emit_half(upstream, grads[1], 0, 1 - where[0], where[1], plan.locs)
+    else:
+        grads[0][...] = upstream[...]
     rows_times(upstream, views(plan.table, arrays, offsets, 3), back_mixed, 0)
     attention_back(triple, attend, back_mixed, back_triple, plan.blocks)
-
-
-def grad_kernel(loc_count, loc, left_own, left_other, right_own, right_other, first, rest):
-    block = first.shape[0]
-    for step in range(loc_count):
-        at = lax.rem(loc[0] + (2 * loc_count - 1 - step), loc_count) * block
-        columns = pl.ds(pl.multiple_of(at, block), block)
-        total = dot(left_own[:, columns], right_own[...], TN)
-        total = total + dot(left_other[:, columns], right_other[...], TN)
-        if step == 0:
-            first[...] = total.astype(BF)
-        else:
-            rest[step - 1] = total
+    at = 0
+    for out in back_triples:
+        out[...] = back_triple[:, at : at + out.shape[1]]
+        at += out.shape[1]
+
+
+def grad_kernel(ats, width, where, left, half_here, half_there, right, right_other, sent, far, near, other):
+    half_at, there_at, right_at, other_at = ats
+    lanes = other.shape[1] // 2
+    core, loc = where[1], where[2]
+    at = pl.multiple_of(core * lanes, lanes)
+    other[:, pl.ds(at, lanes)] = half_here[:, half_at : half_at + lanes]
+    at = pl.multiple_of((1 - core) * lanes, lanes)
+    other[:, pl.ds(at, lanes)] = half_there[:, there_at : there_at + lanes]
+    block = near.shape[0]
+    parity = lax.rem(loc, 2)
+    beside = loc + 1 - 2 * parity
+    for number, place in enumerate((lax.rem(beside + 2, 4), beside, lax.rem(loc + 2, 4), loc)):
+        columns = pl.ds(pl.multiple_of(place * block, block), block)
+        for first in range(0, width, 256):
+            lane = slice(first, first + 256)
+            total = dot(left[:, columns], right[:, right_at + first : right_at + first + 256], TN)
+            total = total + dot(
+                other[:, columns], right_other[:, other_at + first : other_at + first + 256], TN
+            )
+            if number < 2:
+                sent[number * block : (number + 1) * block, lane] = total.astype(BF)
+            elif number == 2:
+                far[:, lane] = total
+            else:
+                near[:, lane] = total
 
 
 def finish_kernel(*refs):
     out = refs[-1]
+    block = out.shape[0]
     column = 0
-    for arrived, rest in zip(refs[0:-1:2], refs[1:-1:2]):
-        for at in range(0, rest.shape[1], 256):
-            total = arrived[:, at : at + 256].astype(F32) + rest[:, at : at + 256]
-            kind, lane = (column + at) // out.shape[2], (column + at) % out.shape[2]
-            out[:, kind, lane : lane + 256] = total
-        column += rest.shape[1]
+    for near, beside, far in zip(refs[0:-1:3], refs[1:-1:3], refs[2:-1:3]):
+        for at in range(0, near.shape[1], 256):
+            lane = slice(at, at + 256)
+            total = near[:, lane] + beside[block:, lane].astype(F32) + far[:, lane].astype(F32)
+            kind, first = (column + at) // out.shape[2], (column + at) % out.shape[2]
+            out[:, kind, first : first + 256] = total
+        column += near.shape[1]
+
+
+def slice_kernel(number, weights, out):
+    for kind in range(out.shape[0]):
+        out[kind] = weights[:, kind, :]
 
 
 class Plan:
-    def __init__(self, blocks, moves, origins, weights, emit, columns, sources=0):
+    def __init__(self, blocks, moves, origins, weights, paired, locs, grads, sources=0):
         self.blocks, self.moves, self.origins = blocks, moves, origins
         self.arrays, self.table = len(weights.arrays), weights.table
-        self.emit, self.columns, self.sources = emit, columns, sources
-
-
-def call(body, outs, args, scratch=(), flops=0):
+        self.paired, self.locs, self.grads, self.sources = paired, locs, grads, sources
+
+
+def call(body, outs, args, scratch=(), flops=0, kept=None):
     smem = pl.BlockSpec(memory_space=pltpu.SMEM)
     vmem = pl.BlockSpec(memory_space=pltpu.VMEM)
     specs = [smem if arg.dtype == jnp.int32 else vmem for arg in args]
+    out_specs = [vmem] * len(outs)
+    aliases = {}
+    outs = list(outs)
     moved = sum(arg.size * arg.dtype.itemsize for arg in args)
     moved = moved + sum(out.size * out.dtype.itemsize for out in outs)
+    if kept is not None:
+        specs[kept] = pl.BlockSpec(memory_space=pl.ANY)
+        out_specs.append(pl.BlockSpec(memory_space=pl.ANY))
+        outs.append(jax.ShapeDtypeStruct(args[kept].shape, args[kept].dtype))
+        aliases = {kept: len(outs) - 1}
     return pl.pallas_call(
         body,
-        out_shape=list(outs),
+        out_shape=outs,
         in_specs=specs,
-        out_specs=[vmem] * len(outs),
+        out_specs=out_specs,
         scratch_shapes=list(scratch),
+        input_output_aliases=aliases,
         compiler_params=pltpu.CompilerParams(vmem_limit_bytes=VMEM_LIMIT),
         cost_estimate=pl.CostEstimate(flops=flops, bytes_accessed=moved, transcendentals=0),
     )(*args)
@@ -278,42 +343,54 @@
     return lax.ppermute(array, axis, [(0, 1), (1, 0)])
 
 
-def gather_weights(weights, sizes):
-    rows = weights.shape[0]
-    own = weights.transpose(1, 0, 2)
-    if sizes["date"] != 2 or sizes["groups"] != 2 or sizes["loc"] % 2 or rows % 512:
-        whole = lax.all_gather(own, "date", axis=1, tiled=True)
-        table = {kind: [(0, kind, 0)] for kind in range(4)}
-        return Weights([whole], table, jnp.zeros((1,), jnp.int32))
+PAIRS = [(0, 1), (1, 0), (2, 3), (3, 2)]
+APART = [(0, 2), (1, 3), (2, 0), (3, 1)]
+
+
+def quarter_of(weights, number):
+    rows, kinds, width = weights.shape
+    return pl.pallas_call(
+        slice_kernel,
+        out_shape=jax.ShapeDtypeStruct((kinds, rows // 4, width), weights.dtype),
+        grid_spec=pltpu.PrefetchScalarGridSpec(
+            num_scalar_prefetch=1,
+            grid=(1,),
+            in_specs=[pl.BlockSpec((rows // 4, kinds, width), lambda at, number: (number[0], 0, 0))],
+            out_specs=pl.BlockSpec((kinds, rows // 4, width), lambda at, number: (0, 0, 0)),
+        ),
+    )(number.astype(jnp.int32)[None], weights)
+
+
+def gather_weights(spatial, temporal, paired):
+    if not paired:
+        found = []
+        for weights in (spatial, temporal):
+            whole = lax.all_gather(weights.transpose(1, 0, 2), "date", axis=1, tiled=True)
+            table = {kind: [(0, kind, 0)] for kind in range(4)}
+            found.append(Weights([whole], table, jnp.zeros((1,), jnp.int32)))
+        return found
+    rows = spatial.shape[0]
     side, here = lax.axis_index("groups"), lax.axis_index("date")
     even = lax.axis_index("loc") % 2
-    quarter = rows // 4
-    pairs = [(at, at ^ 1) for at in range(sizes["loc"])]
-
-    def place(group, loc):
-        return (1 - here) * rows + (group * 2 + loc) * quarter
-
-    offsets = [here * rows, place(side, even), place(1 - side, even), place(side, 1 - even)]
-    offsets = jnp.stack(offsets + [place(1 - side, 1 - even)]).astype(jnp.int32)
-    sent = lax.dynamic_slice_in_dim(weights, (side * 2 + even) * quarter, quarter, 0)
-    sent = sent.transpose(1, 0, 2)
-    arrays, table = [own], {}
-    for kinds in ((0, 1), (2, 3)):
-        across = swap(sent[kinds[0] : kinds[1] + 1], "date")
-        group = swap(across, "groups")
-        loc = lax.ppermute(across, "loc", pairs)
-        far = (swap(loc[0:1], "groups"), lax.ppermute(group[1:2], "loc", pairs))
-        first = len(arrays)
-        arrays += [across, group, loc, *far]
-        for number, kind in enumerate(kinds):
-            table[kind] = [
-                (0, kind, 0),
-                (first, number, 1),
-                (first + 1, number, 2),
-                (first + 2, number, 3),
-                (first + 3 + number, 0, 4),
-            ]
-    return Weights(arrays, table, offsets)
+    numbers = [side * 2 + even, (1 - side) * 2 + even, side * 2 + 1 - even, (1 - side) * 2 + 1 - even]
+    offsets = [here * rows] + [(1 - here) * rows + number * (rows // 4) for number in numbers]
+    offsets = jnp.stack(offsets).astype(jnp.int32)
+    own = quarter_of(spatial, numbers[0])
+    first = swap(own, "date")
+    last = swap(quarter_of(spatial, numbers[3]), "date")
+    arrays = [spatial.transpose(1, 0, 2), first, swap(first, "groups")]
+    arrays += [lax.ppermute(first, "loc", PAIRS), last]
+    table = {kind: [(number, kind, number) for number in range(5)] for kind in range(4)}
+    spatial = Weights(arrays, table, offsets)
+    first = swap(quarter_of(temporal, numbers[0]), "date")
+    group, loc = swap(first, "groups"), lax.ppermute(first, "loc", PAIRS)
+    far = (swap(loc[0:2], "groups"), lax.ppermute(group[2:4], "loc", PAIRS))
+    arrays = [temporal.transpose(1, 0, 2), first, group, loc, *far]
+    table = {
+        kind: [(number, kind, number) for number in range(4)] + [(4 + kind // 2, kind % 2, 4)]
+        for kind in range(4)
+    }
+    return [spatial, Weights(arrays, table, offsets)]
 
 
 def add_over_heads(partial, sizes):
@@ -331,49 +408,30 @@
     return part.astype(F32)
 
 
-def ring_terms(left, right, other_left, other_right, sizes):
-    count = sizes["loc"]
-    loc = lax.axis_index("loc").astype(jnp.int32)[None]
-    block, width = left.shape[1] // count, right.shape[1]
-    return call(
-        functools.partial(grad_kernel, count),
+def summed(where, left, halves, right, other_right, width):
+    (half_here, half_at), (half_there, there_at) = halves
+    (right, right_at), (other_right, other_at) = right, other_right
+    rows, columns = left.shape
+    block = columns // 4
+    sent, far, near = call(
+        functools.partial(grad_kernel, (half_at, there_at, right_at, other_at), width),
         (
-            jax.ShapeDtypeStruct((block, width), BF),
-            jax.ShapeDtypeStruct((count - 1, block, width), F32),
+            jax.ShapeDtypeStruct((2 * block, width), BF),
+            jax.ShapeDtypeStruct((block, width), F32),
+            jax.ShapeDtypeStruct((block, width), F32),
         ),
-        (loc, left, other_left, right, other_right),
-        flops=4 * left.shape[0] * left.shape[1] * width,
-    )
-
-
-def ring_sum(terms, sizes):
-    count = sizes["loc"]
-    ring = [(at, (at + 1) % count) for at in range(count)]
-    total, rest = terms
-    for step in range(count - 1):
-        arrived = lax.ppermute(total, "loc", ring)
-        if step < count - 2:
-            total = (arrived.astype(F32) + rest[step]).astype(BF)
-    return arrived, rest[count - 2]
-
-
-def weight_grads(hidden, back_triple, upstream, mixed, sizes):
-    width = mixed.shape[1]
-    block = hidden[0].shape[1] // sizes["loc"]
-    half = back_triple.shape[1] // 2
-    other_hidden, other_upstream = swap(hidden[1], "date"), swap(upstream[1], "date")
-    outlet = ring_terms(upstream[0], mixed, other_upstream, swap(mixed, "date"), sizes)
-    outlet = ring_sum(outlet, sizes)
-    intakes = []
-    for at in (0, half):
-        right = back_triple[:, at : at + half]
-        terms = ring_terms(hidden[0], right, other_hidden, swap(right, "date"), sizes)
-        intakes += ring_sum(terms, sizes)
-    return call(
-        finish_kernel,
-        (jax.ShapeDtypeStruct((block, 4, width), F32),),
-        (*intakes, *outlet),
-    )[0]
+        (where, left, half_here, half_there, right, other_right),
+        scratch=(pltpu.VMEM((rows, columns), BF),),
+        flops=4 * rows * columns * width,
+    )
+    beside = lax.ppermute(sent, "loc", PAIRS)
+    far = (far + beside[:block].astype(F32)).astype(BF)
+    return near, beside, lax.ppermute(far, "loc", APART)
+
+
+def finish(terms, width):
+    block = terms[0].shape[0]
+    return call(finish_kernel, (jax.ShapeDtypeStruct((block, 4, width), F32),), terms)[0]
 
 
 def per_device(
@@ -391,15 +449,15 @@
     temporal_weights,
     cotangent,
 ):
-    spatial = gather_weights(spatial_weights, sizes)
-    temporal = gather_weights(temporal_weights, sizes)
     _, patches, dates_here, model = optical.shape
     patches_here, dates = cotangent.shape[1:3]
     width = spatial_weights.shape[2]
     rows = patches * dates_here
     here = lax.axis_index("date")
     first = here * dates_here
-    paired = sizes["date"] == 2 and dates_here % 2 == 0 and patches_here % 8 == 0
+    paired = sizes["groups"] == 2 and sizes["loc"] == 4 and sizes["date"] == 2 and sizes["mp"] == 2
+    paired = paired and dates_here % 2 == 0 and patches_here % 8 == 0 and model % 1024 == 0
+    spatial, temporal = gather_weights(spatial_weights, temporal_weights, paired)
 
     if paired:
         pairs, eights = dates_here // 2, patches_here // 8
@@ -480,14 +538,9 @@
         return (blocks * (width // lanes), lanes // HEAD_DIM * (rows // blocks), rows // blocks)
 
     layer_flops = 2 * rows * model * width * 4
-    place = here.astype(jnp.int32)[None]
+    where = jnp.stack([here, lax.axis_index("mp"), lax.axis_index("loc")]).astype(jnp.int32)
     if paired:
         half = rows // 2
-
-        def emit(rows_ref, outs, at):
-            emit_columns(rows_ref, outs, at, 2, sizes["loc"])
-
-        column_shapes = (shape(rows, model // 2), shape(rows, model // 2))
         blocked = start.reshape(pairs, 2, half_rows, model)
         origins = (blocked[:, 0].reshape(half, model), blocked[:, 1].reshape(half, model))
         spatial_moves = [
@@ -502,32 +555,36 @@
             for eight in range(eights)
         ]
         half_shapes = (shape(half, model), shape(half, model))
+        own, quarter = shape(rows, model // 2), model // 4
+        forward_grads = (own, own, shape(rows, 2 * quarter + width))
+        temporal_grads = (own, shape(rows, quarter + width))
+        backward_grads = (own, shape(rows, quarter))
+        back_shapes = (shape(rows, 3 * width // 2), shape(rows, 3 * width // 2))
     else:
-
-        def emit(rows_ref, outs, at):
-            outs[0][...] = rows_ref[...]
-
-        column_shapes = (shape(rows, model),)
         origins = (start,)
         spatial_moves = [(0, at * spatial_size, at * spatial_size, spatial_size) for at in range(spatial_blocks)]
         temporal_moves = [(0, at * temporal_size, at * temporal_size, temporal_size) for at in range(temporal_blocks)]
         half_shapes = (shape(rows, model),)
-    columns = len(column_shapes)
+        forward_grads = temporal_grads = backward_grads = (shape(rows, model),)
+        back_shapes = (shape(rows, 3 * width),)
     origins, spatial_bias, temporal_bias, date_rows, cotangent_rows = lax.optimization_barrier(
         (origins, spatial_bias, temporal_bias, date_rows, cotangent_rows)
     )
 
-    plan = Plan(spatial_blocks, spatial_moves, len(origins), spatial, emit, columns)
+    def plan_of(blocks, moves, weights, grads, sources=0):
+        return Plan(blocks, moves, len(origins), weights, paired, sizes["loc"], len(grads), sources)
+
+    plan = plan_of(spatial_blocks, spatial_moves, spatial, forward_grads)
     outs = call(
         functools.partial(spatial_forward_kernel, plan),
         (
             *half_shapes,
-            *column_shapes,
+            *forward_grads,
             shape(rows, 3 * width),
             shape(*attend_dims(spatial_blocks), dtype=F32),
             shape(rows, width),
         ),
-        (place, spatial.offsets, spatial_gain, spatial_bias, *origins, *spatial.arrays),
+        (where, spatial.offsets, spatial_gain, spatial_bias, cotangent_rows, *origins, *spatial.arrays),
         scratch=(
             pltpu.VMEM((rows, model), BF),
             pltpu.VMEM((rows, model), BF),
@@ -536,10 +593,16 @@
         flops=layer_flops,
     )
     partials, outs = outs[: len(origins)], outs[len(origins) :]
-    hidden, (triple, attend, mixed) = outs[:columns], outs[columns:]
+    forward, (triple, attend, mixed) = outs[: len(forward_grads)], outs[len(forward_grads) :]
     if paired:
-        there = (origins[1].astype(F32) + add_over_heads(partials[1], sizes)).astype(BF)
+        there, early = call(
+            between_kernel,
+            (shape(half, model),),
+            (origins[1], partials[1], swap(partials[1], "mp"), forward[2]),
+            kept=3,
+        )
         sources = (origins[0], partials[0], swap(partials[0], "mp"), swap(there, "date"))
+        early_other = swap(early, "date")
     else:
         spatial_out = (start.astype(F32) + add_over_heads(partials[0], sizes)).astype(BF)
         moved = lax.all_to_all(
@@ -550,14 +613,11 @@
             tiled=True,
         )
         sources = (temporal_rows(moved),)
-    plan = Plan(
-        temporal_blocks, temporal_moves, len(origins), temporal, emit, columns, len(sources)
-    )
+    plan = plan_of(temporal_blocks, temporal_moves, temporal, temporal_grads, len(sources))
     outs = call(
         functools.partial(temporal_kernel, plan),
         (
-            *column_shapes,
-            *column_shapes,
+            *temporal_grads,
             shape(rows, model),
             shape(rows, width),
             shape(rows, model),
@@ -565,7 +625,7 @@
             shape(rows, model),
         ),
         (
-            place,
+            where,
             temporal.offsets,
             temporal_gain,
             temporal_bias,
@@ -582,17 +642,18 @@
         ),
         flops=2 * layer_flops,
     )
-    temporal_hidden, temporal_upstream = outs[:columns], outs[columns : 2 * columns]
-    joined, temporal_mixed, temporal_partial, temporal_triple, back_part = outs[2 * columns :]
+    middle, outs = outs[: len(temporal_grads)], outs[len(temporal_grads) :]
+    joined, temporal_mixed, temporal_partial, temporal_triple, back_part = outs
 
     if sizes["mp"] == 2:
         others = swap(back_part, "mp")
     else:
         others = (lax.psum(back_part.astype(F32), "mp") - back_part.astype(F32)).astype(BF)
-    backs = call(
+    *backs, temporal_triple = call(
         functools.partial(norm_back_kernel, temporal_moves, temporal_size),
         half_shapes,
-        (temporal_gain, back_part, others, joined, cotangent_rows),
+        (temporal_gain, back_part, others, joined, cotangent_rows, temporal_triple),
+        kept=5,
     )
     if paired:
         back_origins = (backs[0], swap(backs[1], "date"))
@@ -602,27 +663,70 @@
         )
         back_origins = (back.reshape(rows, model),)
     outlet = spatial.only((3,))
-    plan = Plan(spatial_blocks, spatial_moves, len(origins), outlet, emit, columns)
+    plan = plan_of(spatial_blocks, spatial_moves, outlet, backward_grads)
     outs = call(
         functools.partial(spatial_backward_kernel, plan),
-        (*column_shapes, shape(rows, 3 * width)),
-        (place, outlet.offsets, triple, attend, *back_origins, *outlet.arrays),
-        scratch=(pltpu.VMEM((rows, model), BF), pltpu.VMEM((rows, width), BF)),
+        (*backward_grads, *back_shapes),
+        (where, outlet.offsets, triple, attend, *back_origins, *outlet.arrays),
+        scratch=(
+            pltpu.VMEM((rows, model), BF),
+            pltpu.VMEM((rows, width), BF),
+            pltpu.VMEM((rows, 3 * width), BF),
+        ),
         flops=layer_flops,
     )
-    upstream, back_triple = outs[:columns], outs[columns]
+    backward, back_triples = outs[: len(backward_grads)], outs[len(backward_grads) :]
     encoded = (joined.astype(F32) + add_over_heads(temporal_partial, sizes)).astype(BF)
     encoded = temporal_whole(encoded).transpose(1, 0, 2)[None]
-    if paired:
-        temporal_grads = weight_grads(
-            temporal_hidden, temporal_triple, temporal_upstream, temporal_mixed, sizes
+    if not paired:
+        return (
+            encoded,
+            whole_grads(forward[0], back_triples[0], backward[0], mixed),
+            whole_grads(middle[0], temporal_triple, cotangent_rows, temporal_mixed),
         )
-        spatial_grads = weight_grads(hidden, back_triple, upstream, mixed, sizes)
-    else:
-        temporal_grads = whole_grads(
-            temporal_hidden[0], temporal_triple, temporal_upstream[0], temporal_mixed
+    early_there = swap(early_other[:, : 2 * quarter], "mp")
+    middle_other = swap(middle[1], "date")
+    middle_there = swap(middle_other[:, :quarter], "mp")
+    triple_other = swap(temporal_triple, "date")
+    temporal_outlet = summed(
+        where,
+        forward[1],
+        ((early_other, quarter), (early_there, quarter)),
+        (temporal_mixed, 0),
+        (middle_other, quarter),
+        width,
+    )
+    temporal_intake = summed(
+        where,
+        middle[0],
+        ((middle_other, 0), (middle_there, 0)),
+        (temporal_triple, 0),
+        (triple_other, 0),
+        3 * width,
+    )
+    backward_other = swap(backward[1], "date")
+    backward_there = swap(backward_other, "mp")
+    back_others = [swap(array, "date") for array in back_triples]
+    spatial_outlet = summed(
+        where,
+        backward[0],
+        ((backward_other, 0), (backward_there, 0)),
+        (mixed, 0),
+        (early_other, 2 * quarter),
+        width,
+    )
+    terms = []
+    for right, other in zip(back_triples, back_others):
+        terms += summed(
+            where,
+            forward[0],
+            ((early_other, 0), (early_there, 0)),
+            (right, 0),
+            (other, 0),
+            right.shape[1],
         )
-        spatial_grads = whole_grads(hidden[0], back_triple, upstream[0], mixed)
+    temporal_grads = finish((*temporal_intake, *temporal_outlet), width)
+    spatial_grads = finish((*terms, *spatial_outlet), width)
     return (encoded, spatial_grads, temporal_grads)
 
 

time: 240 us -> 229 us (0.954)
  starting transfers between devices: 60.5 us -> 35.3 us
  waiting for transfers between devices: 82 us -> 105 us
  local copies, waits for them, and re-layouts: 28.9 us -> 18.3 us
  Pallas kernels: 54.6 us -> 64.4 us
  other arithmetic: 11.2 us -> 4.67 us
    ppermute x28 -> x21, waiting for transfers between devices: 37.1 us -> 51.2 us  [swap(): return lax.ppermute(array, axis, [(0, 1), (1, 0)])]
    ppermute x26 -> x13, starting transfers between devices: 30.8 us -> 17.2 us  [the longest x5 6.19 us: summed(): return (near, beside, lax.ppermute(far, 'loc', APART))]
    ppermute x28 -> x21, starting transfers between devices: 29.7 us -> 18.1 us  [swap(): return lax.ppermute(array, axis, [(0, 1), (1, 0)])]
    pallas_call x12 -> x15, Pallas kernels: 54.6 us -> 64.4 us  [the longest x12 55.8 us: call(): pl.pallas_call(body, out_shape=outs, in_specs=specs, out_specs=out_specs,...]
    ppermute x26 -> x13, waiting for transfers between devices: 44.9 us -> 53.6 us  [the longest x5 28.9 us: summed(): beside = lax.ppermute(sent, 'loc', PAIRS)]
    squeeze x6 -> x0, local copies, waits for them, and re-layouts: 8.49 us -> none  [ring_sum(): return (arrived, rest[count - 2])]
    convert_element_type x14 -> x6, other arithmetic: 5.61 us -> 0.27 us  [the longest x5 0.19 us: summed(): far = (far + beside[:block].astype(F32)).astype(BF)]
    slice x12 -> x4, local copies, waits for them, and re-layouts: 2.56 us -> 0.07 us  [the longest x2 0.04 us: gather_weights(): far = (swap(loc[0:2], 'groups'), lax.ppermute(group[2:4], 'loc', PAIRS))]
  transfers between devices with their start and end apart: 54 -> 34, of which waited for: 27 -> 13; matrix products, arithmetic and copies ran while one was open for 11% -> 6% of each run, Pallas kernels for 13% -> 20%
where the time goes in v1:
time: 229 us
  waiting for transfers between devices  105 us (46%)
  Pallas kernels  64.4 us (28%)
  starting transfers between devices  35.3 us (15%)
  local copies, waits for them, and re-layouts  18.3 us (8%)
  other arithmetic  4.67 us (2%)
    pallas_call x12, Pallas kernels, call(): pl.pallas_call(body, out_shape=outs, in_specs=specs, out_specs=out_specs,...  55.8 us
    ppermute x21, waiting for transfers between devices, swap(): return lax.ppermute(array, axis, [(0, 1), (1, 0)])  51.2 us
    ppermute x5, waiting for transfers between devices, summed(): beside = lax.ppermute(sent, 'loc', PAIRS)  28.9 us
    ppermute x5, waiting for transfers between devices, summed(): return (near, beside, lax.ppermute(far, 'loc', APART))  23.3 us
    ppermute x21, starting transfers between devices, swap(): return lax.ppermute(array, axis, [(0, 1), (1, 0)])  18.1 us
    unnamed x102, local copies, waits for them, and re-layouts  12.7 us
    pallas_call x3, Pallas kernels, quarter_of(): pl.pallas_call(slice_kernel, out_shape=jax.ShapeDtypeStruct((kinds, rows...  8.58 us
    ppermute x5, starting transfers between devices, summed(): return (near, beside, lax.ppermute(far, 'loc', APART))  6.19 us
  transfers between devices with their start and end apart: 34, of which 13 were waited for; matrix products, arithmetic and copies ran while one was open for 6% of the time, Pallas kernels for 20%

profile of v1, /device:TPU:0, one launch (start us, length us, event | category | flops | bytes accessed | tf_op | source)
XLA Modules:
  0.0 228.7 jit_solution(1846816269681470976)
XLA Ops:
  0.7 2.9 %shard_map.139 = bf16[4,128,512]{2,1,0:T(8,128)(2,1)} custom-call(s32[1]{0:T(128)} %bitcast.36.number, bf16[512,4,512]{2,1,0:T(4,128)(2,1)} %weights.4), custom_call_target="tpu_custom_call" | custom-call | tf_op jit(solution)/shard_map/pallas_call | solution.py:352
  3.5 2.9 %collective-permute-start = (bf16[4,128,512]{2,1,0:T(8,128)(2,1)}, bf16[4,128,512]{2,1,0:T(8,128)(2,1)}, u32[]{:S(2)}, u32[]{:S(2)}) collective-permute-start(bf16[4,128,512]{2,1,0:T(8,128)(2,1)} %shard_map.139), channel_id=1, source_target_pairs={{0,2},{2,0},{1,3},{3,1},{4,6},{6,4},{5,7},{7,5},{8,10},{10,8},{9,1... | collective-permute-start | bytes 1572872 | tf_op jit(solution)/shard_map/ppermute | solution.py:343
  6.5 2.8 %shard_map.143 = bf16[4,128,512]{2,1,0:T(8,128)(2,1)} custom-call(s32[1]{0:T(128)} %bitcast.36.number, bf16[512,4,512]{2,1,0:T(4,128)(2,1)} %weights.5), custom_call_target="tpu_custom_call" | custom-call | tf_op jit(solution)/shard_map/pallas_call | solution.py:352
  9.3 2.9 %shard_map.140 = bf16[4,128,512]{2,1,0:T(8,128)(2,1)} custom-call(s32[1]{0:T(128)} %bitcast.37.number, bf16[512,4,512]{2,1,0:T(4,128)(2,1)} %weights.4), custom_call_target="tpu_custom_call" | custom-call | tf_op jit(solution)/shard_map/pallas_call | solution.py:352
  12.2 2.0 collective-permute-start.3
  17.2 1.3 reverse_select_fusion.1
  19.3 1.7 copy.32
  21.1 1.6 slice.92
  22.8 1.6 collective-permute-start.2
  24.3 1.5 collective-permute-start.1
  28.1 2.7 %collective-permute-done.7.refs_5_ = bf16[4,128,512]{2,1,0:T(8,128)(2,1)} collective-permute-done((bf16[4,128,512]{2,1,0:T(8,128)(2,1)}, bf16[4,128,512]{2,1,0:T(8,128)(2,1)}, u32[]{:S(2)}, u32[]{:S(2)}) %collective-permute-start.7) | collective-permute-done | bytes 524320 | tf_op jit(solution)/shard_map/ppermute | solution.py:343
  30.8 2.1 collective-permute-start.9
  32.9 1.5 collective-permute-start.8
  35.0 6.1 %collective-permute-done.3.refs_6_ = bf16[4,128,512]{2,1,0:T(8,128)(2,1)} collective-permute-done((bf16[4,128,512]{2,1,0:T(8,128)(2,1)}, bf16[4,128,512]{2,1,0:T(8,128)(2,1)}, u32[]{:S(2)}, u32[]{:S(2)}) %collective-permute-start.3) | collective-permute-done | bytes 524320 | tf_op jit(solution)/shard_map/ppermute | solution.py:343
  42.2 8.0 %shard_map.141 = (bf16[144,1024]{1,0:T(8,128)(2,1)}, bf16[144,1024]{1,0:T(8,128)(2,1)}, bf16[288,512]{1,0:T(8,128)(2,1)}, bf16[288,512]{1,0:T(8,128)(2,1)}, bf16...) custom-call(s32[3]{0:T(128)} %pad_add_fusion.where, ...), custom_call_target="tpu_custom_call" | custom-call | flops 1207959552 | bytes 9248800 | tf_op jit(solution)/shard_map/pallas_call | solution.py:330
  50.7 1.3 collective-permute-done.5.there
  52.7 2.1 shard_map.142
  54.9 1.7 collective-permute-start.6
  56.6 1.6 collective-permute-start.10
  58.2 1.6 collective-permute-start.11
  59.9 1.7 copy.31
  61.6 3.1 %collective-permute-done.10.refs_8_ = bf16[2,128,512]{2,1,0:T(8,128)(2,1)S(1)} collective-permute-done((bf16[2,128,512]{2,1,0:T(8,128)(2,1)S(1)}, bf16[2,128,512]{2,1,0:T(8,128)(2,1)S(1)}, u32[]{:S(2)}, u32[]{:S(2)}) %collective-permute-start.10) | collective-permute-done | bytes 262176 | tf_op jit(solution)/shard_map/ppermute | solution.py:343
  64.8 1.3 collective-permute-done.11.refs_9_
  67.0 12.0 %shard_map.144 = (bf16[288,512]{1,0:T(8,128)(2,1)}, bf16[288,768]{1,0:T(8,128)(2,1)}, bf16[288,1024]{1,0:T(8,128)(2,1)}, bf16[288,512]{1,0:T(8,128)(2,1)}, bf16[...) custom-call(s32[3]{0:T(128)} %pad_add_fusion.where, s32[5]{0:T(128)} %stack.39.offsets, ...), custom_call_target="tpu_custom_call" | custom-call | flops 2415919104 | bytes 9887776 | tf_op jit(solution)/shard_map/pallas_call | solution.py:330
  79.7 1.6 collective-permute-done.15.there
  82.1 3.4 %shard_map.145 = (bf16[144,1024]{1,0:T(8,128)(2,1)}, bf16[144,1024]{1,0:T(8,128)(2,1)}, bf16[288,1536]{1,0:T(8,128)(2,1)}) custom-call(f32[1,1024]{1,0:T(1,128)} %bitcast.96, bf16[288,1024]{1,0:T(8,128)(2,1)} %get-tuple-element.64.here, bf16[288,1024]{1,0:T(8,128)(2,1)} %copy-done.17, ...), custom_call_target="tpu_custom_call", output_to_operand_aliasing={{2}: (5, {})} | custom-call | bytes 3837952 | tf_op jit(solution)/shard_map/pallas_call | solution.py:330
  86.0 1.5 collective-permute-start.29
  88.0 7.2 %collective-permute-done.13.half_here.right_other = bf16[288,1024]{1,0:T(8,128)(2,1)S(1)} collective-permute-done((bf16[288,1024]{1,0:T(8,128)(2,1)S(1)}, bf16[288,1024]{1,0:T(8,128)(2,1)S(1)}, u32[]{:S(2)}, u32[]{:S(2)}) %collective-permute-start.13) | collective-permute-done | bytes 589856 | tf_op jit(solution)/shard_map/ppermute | solution.py:343
  95.4 6.2 %collective-permute-done.16.refs_1_ = bf16[144,1024]{1,0:T(8,128)(2,1)S(1)} collective-permute-done((bf16[144,1024]{1,0:T(8,128)(2,1)}, bf16[144,1024]{1,0:T(8,128)(2,1)S(1)}, u32[]{:S(2)}, u32[]{:S(2)}) %collective-permute-start.16) | collective-permute-done | bytes 294944 | tf_op jit(solution)/shard_map/ppermute | solution.py:343
  102.3 7.0 %shard_map.146 = (bf16[288,512]{1,0:T(8,128)(2,1)}, bf16[288,256]{1,0:T(8,128)(2,1)}, bf16[288,768]{1,0:T(8,128)(2,1)}, bf16[288,768]{1,0:T(8,128)(2,1)}) custom-call(s32[3]{0:T(128)} %pad_add_fusion.where, s32[5]{0:T(128)} %stack.39.offsets, bf16[288,1536]{1,0:T(8,128)(2,1)} %get-tuple-element.62.triple, f32[6,384,96]{2,1,0:T(8,128)} %get-tuple-element.63.attend, ...), custom_call_target="tpu_custom_call" | custom-call | flops 1207959552 | bytes 7880736 | tf_op jit(solution)/shard_map/pallas_call | solution.py:330
  109.9 22.8 %collective-permute-done.23.half_here = bf16[288,256]{1,0:T(8,128)(2,1)S(1)} collective-permute-done((bf16[288,256]{1,0:T(8,128)(2,1)}, bf16[288,256]{1,0:T(8,128)(2,1)S(1)}, u32[]{:S(2)}, u32[]{:S(2)}) %collective-permute-start.23) | collective-permute-done | bytes 147488 | tf_op jit(solution)/shard_map/ppermute | solution.py:343
  134.1 3.0 %shard_map.152 = (bf16[256,512]{1,0:T(8,128)(2,1)}, f32[128,512]{1,0:T(8,128)}, f32[128,512]{1,0:T(8,128)}) custom-call(s32[3]{0:T(128)} %pad_add_fusion.where, bf16[288,512]{1,0:T(8,128)(2,1)} %get-tuple-element.88.left, bf16[288,1024]{1,0:T(8,128)(2,1)} %copy-done.2, bf16[288,512]{1,0:T(8,128)(2,1)} %copy-done.4, ...), custom_call_target="tpu_custom_call" | custom-call | flops 301989888 | bytes 2703372 | tf_op jit(solution)/shard_map/pallas_call | solution.py:330
  137.1 1.6 collective-permute-start.32
  138.6 1.6 collective-permute-start.17
  140.5 2.9 %shard_map.149 = (bf16[256,512]{1,0:T(8,128)(2,1)}, f32[128,512]{1,0:T(8,128)}, f32[128,512]{1,0:T(8,128)}) custom-call(s32[3]{0:T(128)} %pad_add_fusion.where, bf16[288,512]{1,0:T(8,128)(2,1)} %get-tuple-element.76.left, bf16[288,256]{1,0:T(8,128)(2,1)} %copy-done.33, bf16[288,256]{1,0:T(8,128)(2,1)} %copy-done.34, ...), custom_call_target="tpu_custom_call" | custom-call | flops 301989888 | bytes 2261004 | tf_op jit(solution)/shard_map/pallas_call | solution.py:330
  144.8 4.8 %shard_map.151 = (bf16[256,1536]{1,0:T(8,128)(2,1)}, f32[128,1536]{1,0:T(8,128)}, f32[128,1536]{1,0:T(8,128)}) custom-call(s32[3]{0:T(128)} %pad_add_fusion.where, bf16[288,512]{1,0:T(8,128)(2,1)} %get-tuple-element.82.left, bf16[288,768]{1,0:T(8,128)(2,1)} %copy-done.12, bf16[288,256]{1,0:T(8,128)(2,1)} %copy-done.48, ...), custom_call_target="tpu_custom_call" | custom-call | flops 905969664 | bytes 5013516 | tf_op jit(solution)/shard_map/pallas_call | solution.py:330
  149.6 1.6 collective-permute-start.30
  152.0 3.4 %shard_map.148 = (bf16[256,768]{1,0:T(8,128)(2,1)}, f32[128,768]{1,0:T(8,128)}, f32[128,768]{1,0:T(8,128)}) custom-call(s32[3]{0:T(128)} %pad_add_fusion.where, bf16[288,512]{1,0:T(8,128)(2,1)} %get-tuple-element.60.left, bf16[288,1024]{1,0:T(8,128)(2,1)} %copy-done.2, bf16[288,512]{1,0:T(8,128)(2,1)} %copy-done.4, ...), custom_call_target="tpu_custom_call" | custom-call | flops 452984832 | bytes 3244044 | tf_op jit(solution)/shard_map/pallas_call | solution.py:330
  155.8 2.6 %collective-permute-start.33 = (bf16[128,512]{1,0:T(8,128)(2,1)S(1)}, bf16[128,512]{1,0:T(8,128)(2,1)S(1)}, u32[]{:S(2)}, u32[]{:S(2)}) collective-permute-start(bf16[128,512]{1,0:T(8,128)(2,1)S(1)} %add_convert_fusion.4), channel_id=1, source_target_pairs={{0,8},{4,12},{8,0},{12,4},{1,9},{5,13},{9,1},{13,5},{2,10},{6,14},... | collective-permute-start | bytes 393224 | tf_op jit(solution)/shard_map/ppermute | solution.py:429
  159.2 3.3 %shard_map.147 = (bf16[256,768]{1,0:T(8,128)(2,1)}, f32[128,768]{1,0:T(8,128)}, f32[128,768]{1,0:T(8,128)}) custom-call(s32[3]{0:T(128)} %pad_add_fusion.where, bf16[288,512]{1,0:T(8,128)(2,1)} %get-tuple-element.60.left, bf16[288,1024]{1,0:T(8,128)(2,1)} %copy-done.2, bf16[288,512]{1,0:T(8,128)(2,1)} %copy-done.4, ...), custom_call_target="tpu_custom_call" | custom-call | flops 452984832 | bytes 3244044 | tf_op jit(solution)/shard_map/pallas_call | solution.py:330
  162.6 1.6 collective-permute-start.18
  164.6 19.7 %collective-permute-done.21.refs_4_ = bf16[256,768]{1,0:T(8,128)(2,1)S(1)} collective-permute-done((bf16[256,768]{1,0:T(8,128)(2,1)}, bf16[256,768]{1,0:T(8,128)(2,1)S(1)}, u32[]{:S(2)}, u32[]{:S(2)}) %collective-permute-start.21) | collective-permute-done | bytes 393248 | tf_op jit(solution)/shard_map/ppermute | solution.py:427
  184.4 1.8 collective-permute-start.22
  187.5 9.2 %collective-permute-done.18.refs_1_ = bf16[256,768]{1,0:T(8,128)(2,1)S(1)} collective-permute-done((bf16[256,768]{1,0:T(8,128)(2,1)}, bf16[256,768]{1,0:T(8,128)(2,1)S(1)}, u32[]{:S(2)}, u32[]{:S(2)}) %collective-permute-start.18) | collective-permute-done | bytes 393248 | tf_op jit(solution)/shard_map/ppermute | solution.py:427
  197.9 14.8 %collective-permute-done.22.refs_5_ = bf16[128,768]{1,0:T(8,128)(2,1)S(1)} collective-permute-done((bf16[128,768]{1,0:T(8,128)(2,1)S(1)}, bf16[128,768]{1,0:T(8,128)(2,1)S(1)}, u32[]{:S(2)}, u32[]{:S(2)}) %collective-permute-start.22) | collective-permute-done | bytes 196640 | tf_op jit(solution)/shard_map/ppermute | solution.py:429
  212.7 8.5 %collective-permute-done.19.refs_2_ = bf16[128,768]{1,0:T(8,128)(2,1)S(1)} collective-permute-done((bf16[128,768]{1,0:T(8,128)(2,1)S(1)}, bf16[128,768]{1,0:T(8,128)(2,1)S(1)}, u32[]{:S(2)}, u32[]{:S(2)}) %collective-permute-start.19) | collective-permute-done | bytes 196640 | tf_op jit(solution)/shard_map/ppermute | solution.py:429
  221.9 3.0 %shard_map.150 = f32[128,4,512]{2,1,0:T(4,128)} custom-call(f32[128,768]{1,0:T(8,128)} %get-tuple-element.69.refs_0_, bf16[256,768]{1,0:T(8,128)(2,1)} %copy-done.10, bf16[128,768]{1,0:T(8,128)(2,1)} %copy-done.32, f32[128,768]{1,0:T(8,128)} %get-tuple-element.73.refs_3_, bf16[256,768]{1,0:T(8,128)(2,1)} %copy-done.9, bf16[128,768]{1,0:T(8,128)(2,1)} %copy-done.31, ...), custom_call_target="tpu_custom_call" | custom-call | bytes 3670016 | tf_op jit(solution)/shard_map/pallas_call | solution.py:330
  225.7 3.0 %shard_map.153 = f32[128,4,512]{2,1,0:T(4,128)} custom-call(f32[128,1536]{1,0:T(8,128)} %get-tuple-element.85.refs_0_, bf16[256,1536]{1,0:T(8,128)(2,1)} %copy-done.8, bf16[128,1536]{1,0:T(8,128)(2,1)} %copy-done.24, f32[128,512]{1,0:T(8,128)} %get-tuple-element.90.refs_3_, bf16[256,512]{1,0:T(8,128)(2,1)} %copy-done.13, bf16[128,512]{1,0:T(8,128)(2,1)} %copy-done.35), custom_call_target="tpu_custom_call" | custom-call | bytes 3670016 | tf_op jit(solution)/shard_map/pallas_call | solution.py:330
  (189 shorter events, 23.0 us)
Async XLA Ops:
  0.6 14.4 %copy-start = (bf16[196,1024]{1,0:T(8,128)(2,1)S(1)}, bf16[196,1024]{1,0:T(8,128)(2,1)}, u32[]{:S(2)}) copy-start(bf16[196,1024]{1,0:T(8,128)(2,1)} %param.17) | copy-start | bytes 1204228
  3.5 19.2 %collective-permute-start = (bf16[4,128,512]{2,1,0:T(8,128)(2,1)}, bf16[4,128,512]{2,1,0:T(8,128)(2,1)}, u32[]{:S(2)}, u32[]{:S(2)}) collective-permute-start(bf16[4,128,512]{2,1,0:T(8,128)(2,1)} %shard_map.139), channel_id=1, source_target_pairs={{0,2},{2,0},{1,3},{3,1},{4,6},{6,4},{5,7},{7,5},{8,10},{10,8},{9,1... | collective-permute-start | bytes 1572872 | tf_op jit(solution)/shard_map/ppermute | solution.py:343
  9.3 21.5 %collective-permute-start.7 = (bf16[4,128,512]{2,1,0:T(8,128)(2,1)}, bf16[4,128,512]{2,1,0:T(8,128)(2,1)}, u32[]{:S(2)}, u32[]{:S(2)}) collective-permute-start(bf16[4,128,512]{2,1,0:T(8,128)(2,1)} %shard_map.143), channel_id=1, source_target_pairs={{0,2},{2,0},{1,3},{3,1},{4,6},{6,4},{5,7},{7,5},{8,10},{10,8},{9,1... | collective-permute-start | bytes 1572872 | tf_op jit(solution)/shard_map/ppermute | solution.py:343
  12.2 29.0 %collective-permute-start.3 = (bf16[4,128,512]{2,1,0:T(8,128)(2,1)}, bf16[4,128,512]{2,1,0:T(8,128)(2,1)}, u32[]{:S(2)}, u32[]{:S(2)}) collective-permute-start(bf16[4,128,512]{2,1,0:T(8,128)(2,1)} %shard_map.140), channel_id=1, source_target_pairs={{0,2},{2,0},{1,3},{3,1},{4,6},{6,4},{5,7},{7,5},{8,10},{10,8},{9,1... | collective-permute-start | bytes 1572872 | tf_op jit(solution)/shard_map/ppermute | solution.py:343
  22.8 18.4 %collective-permute-start.2 = (bf16[4,128,512]{2,1,0:T(8,128)(2,1)}, bf16[4,128,512]{2,1,0:T(8,128)(2,1)S(1)}, u32[]{:S(2)}, u32[]{:S(2)}) collective-permute-start(bf16[4,128,512]{2,1,0:T(8,128)(2,1)} %collective-permute-done.refs_3_), channel_id=1, source_target_pairs={{0,4},{4,0},{8,12},{12,8},{1,5},{5,1},{9,13},{13,9},{2,6},{6,2},{1... | collective-permute-start | bytes 1572872 | tf_op jit(solution)/shard_map/ppermute | solution.py:382
  24.3 16.9 %collective-permute-start.1 = (bf16[4,128,512]{2,1,0:T(8,128)(2,1)}, bf16[4,128,512]{2,1,0:T(8,128)(2,1)S(1)}, u32[]{:S(2)}, u32[]{:S(2)}) collective-permute-start(bf16[4,128,512]{2,1,0:T(8,128)(2,1)} %collective-permute-done.refs_3_), channel_id=1, source_target_pairs={{0,16},{16,0},{1,17},{17,1},{2,18},{18,2},{3,19},{19,3},{4,20},{20... | collective-permute-start | bytes 1572872 | tf_op jit(solution)/shard_map/ppermute | solution.py:343
  30.8 25.8 %collective-permute-start.9 = (bf16[4,128,512]{2,1,0:T(8,128)(2,1)}, bf16[4,128,512]{2,1,0:T(8,128)(2,1)S(1)}, u32[]{:S(2)}, u32[]{:S(2)}) collective-permute-start(bf16[4,128,512]{2,1,0:T(8,128)(2,1)} %collective-permute-done.7.refs_5_), channel_id=1, source_target_pairs={{0,4},{4,0},{8,12},{12,8},{1,5},{5,1},{9,13},{13,9},{2,6},{6,2},{1... | collective-permute-start | bytes 1572872 | tf_op jit(solution)/shard_map/ppermute | solution.py:386
  32.9 25.3 %collective-permute-start.8 = (bf16[4,128,512]{2,1,0:T(8,128)(2,1)}, bf16[4,128,512]{2,1,0:T(8,128)(2,1)S(1)}, u32[]{:S(2)}, u32[]{:S(2)}) collective-permute-start(bf16[4,128,512]{2,1,0:T(8,128)(2,1)} %collective-permute-done.7.refs_5_), channel_id=1, source_target_pairs={{0,16},{16,0},{1,17},{17,1},{2,18},{18,2},{3,19},{19,3},{4,20},{20... | collective-permute-start | bytes 1572872 | tf_op jit(solution)/shard_map/ppermute | solution.py:343
  50.2 1.9 collective-permute-start.5
  50.2 15.9 %collective-permute-start.4 = (bf16[144,1024]{1,0:T(8,128)(2,1)}, bf16[144,1024]{1,0:T(8,128)(2,1)S(1)}, u32[]{:S(2)}, u32[]{:S(2)}) collective-permute-start(bf16[144,1024]{1,0:T(8,128)(2,1)} %get-tuple-element.54.refs_1_), channel_id=1, source_target_pairs={{0,1},{1,0},{2,3},{3,2},{4,5},{5,4},{6,7},{7,6},{8,9},{9,8},{10,11... | collective-permute-start | bytes 884744 | tf_op jit(solution)/shard_map/ppermute | solution.py:343
  54.9 11.3 %collective-permute-start.6 = (bf16[144,1024]{1,0:T(8,128)(2,1)}, bf16[144,1024]{1,0:T(8,128)(2,1)S(1)}, u32[]{:S(2)}, u32[]{:S(2)}) collective-permute-start(bf16[144,1024]{1,0:T(8,128)(2,1)} %get-tuple-element.57), channel_id=1, source_target_pairs={{0,2},{2,0},{1,3},{3,1},{4,6},{6,4},{5,7},{7,5},{8,10},{10,8},{9,1... | collective-permute-start | bytes 884744 | tf_op jit(solution)/shard_map/ppermute | solution.py:343
  56.6 8.1 %collective-permute-start.10 = (bf16[2,128,512]{2,1,0:T(8,128)(2,1)S(1)}, bf16[2,128,512]{2,1,0:T(8,128)(2,1)S(1)}, u32[]{:S(2)}, u32[]{:S(2)}) collective-permute-start(bf16[2,128,512]{2,1,0:T(8,128)(2,1)S(1)} %slice.93), channel_id=1, source_target_pairs={{0,16},{16,0},{1,17},{17,1},{2,18},{18,2},{3,19},{19,3},{4,20},{20... | collective-permute-start | bytes 786440 | tf_op jit(solution)/shard_map/ppermute | solution.py:343
  58.2 7.9 %collective-permute-start.11 = (bf16[2,128,512]{2,1,0:T(8,128)(2,1)S(1)}, bf16[2,128,512]{2,1,0:T(8,128)(2,1)S(1)}, u32[]{:S(2)}, u32[]{:S(2)}) collective-permute-start(bf16[2,128,512]{2,1,0:T(8,128)(2,1)S(1)} %slice.94), channel_id=1, source_target_pairs={{0,4},{4,0},{8,12},{12,8},{1,5},{5,1},{9,13},{13,9},{2,6},{6,2},{1... | collective-permute-start | bytes 786440 | tf_op jit(solution)/shard_map/ppermute | solution.py:387
  67.0 12.0 %copy-start.20 = (bf16[288,1024]{1,0:T(8,128)(2,1)S(1)}, bf16[288,1024]{1,0:T(8,128)(2,1)}, u32[]{:S(2)}) copy-start(bf16[288,1024]{1,0:T(8,128)(2,1)} %get-tuple-element.61) | copy-start | bytes 1769476
  79.1 2.2 collective-permute-start.15
  79.1 16.2 %collective-permute-start.13 = (bf16[288,1024]{1,0:T(8,128)(2,1)S(1)}, bf16[288,1024]{1,0:T(8,128)(2,1)S(1)}, u32[]{:S(2)}, u32[]{:S(2)}) collective-permute-start(bf16[288,1024]{1,0:T(8,128)(2,1)S(1)} %copy-done.20), channel_id=1, source_target_pairs={{0,2},{2,0},{1,3},{3,1},{4,6},{6,4},{5,7},{7,5},{8,10},{10,8},{9,1... | collective-permute-start | bytes 1769480 | tf_op jit(solution)/shard_map/ppermute | solution.py:343
  85.5 16.1 %collective-permute-start.16 = (bf16[144,1024]{1,0:T(8,128)(2,1)}, bf16[144,1024]{1,0:T(8,128)(2,1)S(1)}, u32[]{:S(2)}, u32[]{:S(2)}) collective-permute-start(bf16[144,1024]{1,0:T(8,128)(2,1)} %get-tuple-element.67), channel_id=1, source_target_pairs={{0,2},{2,0},{1,3},{3,1},{4,6},{6,4},{5,7},{7,5},{8,10},{10,8},{9,1... | collective-permute-start | bytes 884744 | tf_op jit(solution)/shard_map/ppermute | solution.py:343
  86.0 51.1 %collective-permute-start.12 = (bf16[288,1024]{1,0:T(8,128)(2,1)S(1)}, bf16[288,1024]{1,0:T(8,128)(2,1)S(1)}, u32[]{:S(2)}, u32[]{:S(2)}) collective-permute-start(bf16[288,1024]{1,0:T(8,128)(2,1)S(1)} %copy-done.19), channel_id=1, source_target_pairs={{0,1},{1,0},{2,3},{3,2},{4,5},{5,4},{6,7},{7,6},{8,9},{9,8},{10,11... | collective-permute-start | bytes 1769480 | tf_op jit(solution)/shard_map/ppermute | solution.py:343
  86.0 57.9 %collective-permute-start.29 = (bf16[288,1536]{1,0:T(8,128)(2,1)}, bf16[288,1536]{1,0:T(8,128)(2,1)S(1)}, u32[]{:S(2)}, u32[]{:S(2)}) collective-permute-start(bf16[288,1536]{1,0:T(8,128)(2,1)} %get-tuple-element.84.right), channel_id=1, source_target_pairs={{0,2},{2,0},{1,3},{3,1},{4,6},{6,4},{5,7},{7,5},{8,10},{10,8},{9,1... | collective-permute-start | bytes 2654216 | tf_op jit(solution)/shard_map/ppermute | solution.py:343
  87.5 45.2 %collective-permute-start.27 = (bf16[288,768]{1,0:T(8,128)(2,1)S(1)}, bf16[288,768]{1,0:T(8,128)(2,1)S(1)}, u32[]{:S(2)}, u32[]{:S(2)}) collective-permute-start(bf16[288,768]{1,0:T(8,128)(2,1)S(1)} %copy-done.43), channel_id=1, source_target_pairs={{0,2},{2,0},{1,3},{3,1},{4,6},{6,4},{5,7},{7,5},{8,10},{10,8},{9,1... | collective-permute-start | bytes 1327112 | tf_op jit(solution)/shard_map/ppermute | solution.py:343
  95.3 14.0 %copy-start.2 = (bf16[288,1024]{1,0:T(8,128)(2,1)}, bf16[288,1024]{1,0:T(8,128)(2,1)S(1)}, u32[]{:S(2)}) copy-start(bf16[288,1024]{1,0:T(8,128)(2,1)S(1)} %collective-permute-done.13.half_here.right_other) | copy-start | bytes 1769476
  95.3 38.1 %collective-permute-start.14 = (bf16[288,512]{1,0:T(8,128)(2,1)S(1)}, bf16[288,512]{1,0:T(8,128)(2,1)S(1)}, u32[]{:S(2)}, u32[]{:S(2)}) collective-permute-start(bf16[288,512]{1,0:T(8,128)(2,1)S(1)} %slice.95), channel_id=1, source_target_pairs={{0,1},{1,0},{2,3},{3,2},{4,5},{5,4},{6,7},{7,6},{8,9},{9,8},{10,11... | collective-permute-start | bytes 884744 | tf_op jit(solution)/shard_map/ppermute | solution.py:343
  109.3 29.4 %copy-start.21 = (bf16[288,768]{1,0:T(8,128)(2,1)S(1)}, bf16[288,768]{1,0:T(8,128)(2,1)}, u32[]{:S(2)}) copy-start(bf16[288,768]{1,0:T(8,128)(2,1)} %get-tuple-element.68.right) | copy-start | bytes 1327108
  109.3 30.9 %copy-start.5 = (bf16[288,1024]{1,0:T(8,128)(2,1)S(1)}, bf16[288,1024]{1,0:T(8,128)(2,1)}, u32[]{:S(2)}) copy-start(bf16[288,1024]{1,0:T(8,128)(2,1)} %get-tuple-element.58.joined) | copy-start | bytes 1769476
  109.3 23.4 %collective-permute-start.23 = (bf16[288,256]{1,0:T(8,128)(2,1)}, bf16[288,256]{1,0:T(8,128)(2,1)S(1)}, u32[]{:S(2)}, u32[]{:S(2)}) collective-permute-start(bf16[288,256]{1,0:T(8,128)(2,1)} %get-tuple-element.77), channel_id=1, source_target_pairs={{0,2},{2,0},{1,3},{3,1},{4,6},{6,4},{5,7},{7,5},{8,10},{10,8},{9,1... | collective-permute-start | bytes 442376 | tf_op jit(solution)/shard_map/ppermute | solution.py:343
  132.7 7.8 %copy-start.33 = (bf16[288,256]{1,0:T(8,128)(2,1)}, bf16[288,256]{1,0:T(8,128)(2,1)S(1)}, u32[]{:S(2)}) copy-start(bf16[288,256]{1,0:T(8,128)(2,1)S(1)} %collective-permute-done.23.half_here) | copy-start | bytes 442372
  132.7 5.9 %collective-permute-start.24 = (bf16[288,256]{1,0:T(8,128)(2,1)S(1)}, bf16[288,256]{1,0:T(8,128)(2,1)S(1)}, u32[]{:S(2)}, u32[]{:S(2)}) collective-permute-start(bf16[288,256]{1,0:T(8,128)(2,1)S(1)} %collective-permute-done.23.half_here), channel_id=1, source_target_pairs={{0,1},{1,0},{2,3},{3,2},{4,5},{5,4},{6,7},{7,6},{8,9},{9,8},{10,11... | collective-permute-start | bytes 442376 | tf_op jit(solution)/shard_map/ppermute | solution.py:343
  132.8 18.4 %collective-permute-start.20 = (bf16[288,768]{1,0:T(8,128)(2,1)}, bf16[288,768]{1,0:T(8,128)(2,1)S(1)}, u32[]{:S(2)}, u32[]{:S(2)}) collective-permute-start(bf16[288,768]{1,0:T(8,128)(2,1)} %get-tuple-element.72.right), channel_id=1, source_target_pairs={{0,2},{2,0},{1,3},{3,1},{4,6},{6,4},{5,7},{7,5},{8,10},{10,8},{9,1... | collective-permute-start | bytes 1327112 | tf_op jit(solution)/shard_map/ppermute | solution.py:343
  133.4 10.0 %collective-permute-start.28 = (bf16[288,256]{1,0:T(8,128)(2,1)S(1)}, bf16[288,256]{1,0:T(8,128)(2,1)S(1)}, u32[]{:S(2)}, u32[]{:S(2)}) collective-permute-start(bf16[288,256]{1,0:T(8,128)(2,1)S(1)} %slice.99), channel_id=1, source_target_pairs={{0,1},{1,0},{2,3},{3,2},{4,5},{5,4},{6,7},{7,6},{8,9},{9,8},{10,11... | collective-permute-start | bytes 442376 | tf_op jit(solution)/shard_map/ppermute | solution.py:343
  137.1 18.7 %collective-permute-start.32 = (bf16[256,512]{1,0:T(8,128)(2,1)}, bf16[256,512]{1,0:T(8,128)(2,1)S(1)}, u32[]{:S(2)}, u32[]{:S(2)}) collective-permute-start(bf16[256,512]{1,0:T(8,128)(2,1)} %get-tuple-element.91), channel_id=1, source_target_pairs={{0,4},{4,0},{8,12},{12,8},{1,5},{5,1},{9,13},{13,9},{2,6},{6,2},{1... | collective-permute-start | bytes 786440 | tf_op jit(solution)/shard_map/ppermute | solution.py:427
  138.6 19.8 %collective-permute-start.17 = (bf16[288,768]{1,0:T(8,128)(2,1)S(1)}, bf16[288,768]{1,0:T(8,128)(2,1)S(1)}, u32[]{:S(2)}, u32[]{:S(2)}) collective-permute-start(bf16[288,768]{1,0:T(8,128)(2,1)S(1)} %copy-done.21), channel_id=1, source_target_pairs={{0,2},{2,0},{1,3},{3,1},{4,6},{6,4},{5,7},{7,5},{8,10},{10,8},{9,1... | collective-permute-start | bytes 1327112 | tf_op jit(solution)/shard_map/ppermute | solution.py:343
  143.4 20.7 %collective-permute-start.25 = (bf16[256,512]{1,0:T(8,128)(2,1)}, bf16[256,512]{1,0:T(8,128)(2,1)S(1)}, u32[]{:S(2)}, u32[]{:S(2)}) collective-permute-start(bf16[256,512]{1,0:T(8,128)(2,1)} %get-tuple-element.80), channel_id=1, source_target_pairs={{0,4},{4,0},{8,12},{12,8},{1,5},{5,1},{9,13},{13,9},{2,6},{6,2},{1... | collective-permute-start | bytes 786440 | tf_op jit(solution)/shard_map/ppermute | solution.py:427
  149.6 36.6 %collective-permute-start.30 = (bf16[256,1536]{1,0:T(8,128)(2,1)}, bf16[256,1536]{1,0:T(8,128)(2,1)S(1)}, u32[]{:S(2)}, u32[]{:S(2)}) collective-permute-start(bf16[256,1536]{1,0:T(8,128)(2,1)} %get-tuple-element.86), channel_id=1, source_target_pairs={{0,4},{4,0},{8,12},{12,8},{1,5},{5,1},{9,13},{13,9},{2,6},{6,2},{1... | collective-permute-start | bytes 2359304 | tf_op jit(solution)/shard_map/ppermute | solution.py:427
  155.3 29.0 %collective-permute-start.21 = (bf16[256,768]{1,0:T(8,128)(2,1)}, bf16[256,768]{1,0:T(8,128)(2,1)S(1)}, u32[]{:S(2)}, u32[]{:S(2)}) collective-permute-start(bf16[256,768]{1,0:T(8,128)(2,1)} %get-tuple-element.74), channel_id=1, source_target_pairs={{0,4},{4,0},{8,12},{12,8},{1,5},{5,1},{9,13},{13,9},{2,6},{6,2},{1... | collective-permute-start | bytes 1179656 | tf_op jit(solution)/shard_map/ppermute | solution.py:427
  155.8 8.4 %copy-start.29 = (f32[128,512]{1,0:T(8,128)S(1)}, f32[128,512]{1,0:T(8,128)}, u32[]{:S(2)}) copy-start(f32[128,512]{1,0:T(8,128)} %get-tuple-element.81) | copy-start | bytes 786436
  155.8 28.5 %copy-start.25 = (f32[128,768]{1,0:T(8,128)S(1)}, f32[128,768]{1,0:T(8,128)}, u32[]{:S(2)}) copy-start(f32[128,768]{1,0:T(8,128)} %get-tuple-element.75) | copy-start | bytes 1179652
  155.8 30.4 %copy-start.11 = (f32[128,1536]{1,0:T(8,128)S(1)}, f32[128,1536]{1,0:T(8,128)}, u32[]{:S(2)}) copy-start(f32[128,1536]{1,0:T(8,128)} %get-tuple-element.87) | copy-start | bytes 2359300
  155.8 69.1 %collective-permute-start.33 = (bf16[128,512]{1,0:T(8,128)(2,1)S(1)}, bf16[128,512]{1,0:T(8,128)(2,1)S(1)}, u32[]{:S(2)}, u32[]{:S(2)}) collective-permute-start(bf16[128,512]{1,0:T(8,128)(2,1)S(1)} %add_convert_fusion.4), channel_id=1, source_target_pairs={{0,8},{4,12},{8,0},{12,4},{1,9},{5,13},{9,1},{13,5},{2,10},{6,14},... | collective-permute-start | bytes 393224 | tf_op jit(solution)/shard_map/ppermute | solution.py:429
  162.6 34.2 %collective-permute-start.18 = (bf16[256,768]{1,0:T(8,128)(2,1)}, bf16[256,768]{1,0:T(8,128)(2,1)S(1)}, u32[]{:S(2)}, u32[]{:S(2)}) collective-permute-start(bf16[256,768]{1,0:T(8,128)(2,1)} %get-tuple-element.70), channel_id=1, source_target_pairs={{0,4},{4,0},{8,12},{12,8},{1,5},{5,1},{9,13},{13,9},{2,6},{6,2},{1... | collective-permute-start | bytes 1179656 | tf_op jit(solution)/shard_map/ppermute | solution.py:427
  164.2 22.2 %copy-start.14 = (bf16[256,512]{1,0:T(8,128)(2,1)}, bf16[256,512]{1,0:T(8,128)(2,1)S(1)}, u32[]{:S(2)}) copy-start(bf16[256,512]{1,0:T(8,128)(2,1)S(1)} %collective-permute-done.25.refs_7_) | copy-start | bytes 786436
  164.2 33.7 %collective-permute-start.26 = (bf16[128,512]{1,0:T(8,128)(2,1)S(1)}, bf16[128,512]{1,0:T(8,128)(2,1)S(1)}, u32[]{:S(2)}, u32[]{:S(2)}) collective-permute-start(bf16[128,512]{1,0:T(8,128)(2,1)S(1)} %add_convert_fusion.5), channel_id=1, source_target_pairs={{0,8},{4,12},{8,0},{12,4},{1,9},{5,13},{9,1},{13,5},{2,10},{6,14},... | collective-permute-start | bytes 393224 | tf_op jit(solution)/shard_map/ppermute | solution.py:429
  184.3 12.4 %copy-start.26 = (f32[128,768]{1,0:T(8,128)S(1)}, f32[128,768]{1,0:T(8,128)}, u32[]{:S(2)}) copy-start(f32[128,768]{1,0:T(8,128)} %get-tuple-element.71) | copy-start | bytes 1179652
  184.4 28.3 %collective-permute-start.22 = (bf16[128,768]{1,0:T(8,128)(2,1)S(1)}, bf16[128,768]{1,0:T(8,128)(2,1)S(1)}, u32[]{:S(2)}, u32[]{:S(2)}) collective-permute-start(bf16[128,768]{1,0:T(8,128)(2,1)S(1)} %add_convert_fusion.2), channel_id=1, source_target_pairs={{0,8},{4,12},{8,0},{12,4},{1,9},{5,13},{9,1},{13,5},{2,10},{6,14},... | collective-permute-start | bytes 589832 | tf_op jit(solution)/shard_map/ppermute | solution.py:429
  186.2 10.6 %copy-start.8 = (bf16[256,1536]{1,0:T(8,128)(2,1)}, bf16[256,1536]{1,0:T(8,128)(2,1)S(1)}, u32[]{:S(2)}) copy-start(bf16[256,1536]{1,0:T(8,128)(2,1)S(1)} %collective-permute-done.30.refs_1_) | copy-start | bytes 2359300
  186.3 38.6 %collective-permute-start.31 = (bf16[128,1536]{1,0:T(8,128)(2,1)S(1)}, bf16[128,1536]{1,0:T(8,128)(2,1)S(1)}, u32[]{:S(2)}, u32[]{:S(2)}) collective-permute-start(bf16[128,1536]{1,0:T(8,128)(2,1)S(1)} %add_convert_fusion.1), channel_id=1, source_target_pairs={{0,8},{4,12},{8,0},{12,4},{1,9},{5,13},{9,1},{13,5},{2,10},{6,14},... | collective-permute-start | bytes 1179656 | tf_op jit(solution)/shard_map/ppermute | solution.py:429
  196.8 24.4 %collective-permute-start.19 = (bf16[128,768]{1,0:T(8,128)(2,1)S(1)}, bf16[128,768]{1,0:T(8,128)(2,1)S(1)}, u32[]{:S(2)}, u32[]{:S(2)}) collective-permute-start(bf16[128,768]{1,0:T(8,128)(2,1)S(1)} %add_convert_fusion.3), channel_id=1, source_target_pairs={{0,8},{4,12},{8,0},{12,4},{1,9},{5,13},{9,1},{13,5},{2,10},{6,14},... | collective-permute-start | bytes 589832 | tf_op jit(solution)/shard_map/ppermute | solution.py:429
  197.9 23.4 %copy-start.36 = (bf16[128,512]{1,0:T(8,128)(2,1)}, bf16[128,512]{1,0:T(8,128)(2,1)S(1)}, u32[]{:S(2)}) copy-start(bf16[128,512]{1,0:T(8,128)(2,1)S(1)} %collective-permute-done.26.refs_8_) | copy-start | bytes 393220
  212.7 8.6 %copy-start.31 = (bf16[128,768]{1,0:T(8,128)(2,1)}, bf16[128,768]{1,0:T(8,128)(2,1)S(1)}, u32[]{:S(2)}) copy-start(bf16[128,768]{1,0:T(8,128)(2,1)S(1)} %collective-permute-done.22.refs_5_) | copy-start | bytes 589828
  (36 other events, 84.1 us)

commit v2 on v1

--- a/solution.py
+++ b/solution.py
@@ -187,7 +187,8 @@
     sources, refs = refs[: plan.sources], refs[plan.sources :]
     arrays, refs = refs[: plan.arrays], refs[plan.arrays :]
     grads, refs = refs[: plan.grads], refs[plan.grads :]
-    joined, mixed, partial, back_triple, back_part, hidden, triple, attend, back_mixed = refs
+    joined, mixed, partial, back_part = refs[:4]
+    back_triples, (hidden, triple, attend, back_mixed, back_triple) = refs[4:-5], refs[-5:]
     rows = date_rows.shape[0]
     for source, at, to, size in plan.moves:
         if source == 0 and plan.sources > 1:
@@ -222,6 +223,14 @@
             term = dot(back_triple[:, kind * width : (kind + 1) * width], part[...], NT)
             total = term if total is None else total + term
         back_part[:, features] = total.astype(BF)
+    split_columns(back_triple, back_triples)
+
+
+def split_columns(whole, outs):
+    at = 0
+    for out in outs:
+        out[...] = whole[:, at : at + out.shape[1]]
+        at += out.shape[1]
 
 
 def norm_back_kernel(moves, step, gain, here, there, joined, cotangent, kept, *outs):
@@ -241,51 +250,55 @@
                 outs[target][to : to + size, :] = back[first - at : first - at + size]
 
 
-def spatial_backward_kernel(plan, where, offsets, triple, attend, *refs):
+def spatial_backward_kernel(plan, where, offsets, triple, attend, kept, *refs):
     sources, refs = refs[: plan.origins], refs[plan.origins :]
     arrays, refs = refs[: plan.arrays], refs[plan.arrays :]
     grads, refs = refs[: plan.grads], refs[plan.grads :]
-    back_triples, (upstream, back_mixed, back_triple) = refs[:-3], refs[-3:]
+    back_triples, (upstream, back_mixed, back_triple) = refs[:-4], refs[-3:]
     for source, at, to, size in plan.moves:
         upstream[to : to + size, :] = sources[source][at : at + size, :]
     if plan.paired:
         emit_own(upstream, grads[0], 0, where[0], plan.locs)
-        emit_half(upstream, grads[1], 0, 1 - where[0], where[1], plan.locs)
+        emit_own(upstream, grads[1], 0, 1 - where[0], plan.locs)
     else:
         grads[0][...] = upstream[...]
     rows_times(upstream, views(plan.table, arrays, offsets, 3), back_mixed, 0)
     attention_back(triple, attend, back_mixed, back_triple, plan.blocks)
-    at = 0
-    for out in back_triples:
-        out[...] = back_triple[:, at : at + out.shape[1]]
-        at += out.shape[1]
-
-
-def grad_kernel(ats, width, where, left, half_here, half_there, right, right_other, sent, far, near, other):
-    half_at, there_at, right_at, other_at = ats
-    lanes = other.shape[1] // 2
+    split_columns(back_triple, back_triples)
+    if plan.paired:
+        half = upstream.shape[1] // 2
+        grads[1][:, half:] = back_triple[:, : grads[1].shape[1] - half]
+
+
+def grad_kernel(products, count, where, *refs):
+    sent, far, near, other = refs[-4:]
     core, loc = where[1], where[2]
-    at = pl.multiple_of(core * lanes, lanes)
-    other[:, pl.ds(at, lanes)] = half_here[:, half_at : half_at + lanes]
-    at = pl.multiple_of((1 - core) * lanes, lanes)
-    other[:, pl.ds(at, lanes)] = half_there[:, there_at : there_at + lanes]
     block = near.shape[0]
-    parity = lax.rem(loc, 2)
-    beside = loc + 1 - 2 * parity
-    for number, place in enumerate((lax.rem(beside + 2, 4), beside, lax.rem(loc + 2, 4), loc)):
-        columns = pl.ds(pl.multiple_of(place * block, block), block)
-        for first in range(0, width, 256):
-            lane = slice(first, first + 256)
-            total = dot(left[:, columns], right[:, right_at + first : right_at + first + 256], TN)
-            total = total + dot(
-                other[:, columns], right_other[:, other_at + first : other_at + first + 256], TN
-            )
-            if number < 2:
-                sent[number * block : (number + 1) * block, lane] = total.astype(BF)
-            elif number == 2:
-                far[:, lane] = total
-            else:
-                near[:, lane] = total
+    beside = loc + 1 - 2 * lax.rem(loc, 2)
+    places = (lax.rem(beside + 2, 4), beside, lax.rem(loc + 2, 4), loc)
+    column = 0
+    for left, others, (right, right_at), (right_other, other_at), width in products:
+        left, right, right_other = refs[left], refs[right], refs[right_other]
+        lanes = other.shape[1] // len(others)
+        for number, (source, at) in enumerate(others):
+            to = 0
+            if len(others) > 1:
+                to = pl.multiple_of((core if number == 0 else 1 - core) * lanes, lanes)
+            other[:, pl.ds(to, lanes)] = refs[source][:, at : at + lanes]
+        for number, place in enumerate(places):
+            columns = pl.ds(pl.multiple_of(place * block, block), block)
+            for first in range(0, width, 256):
+                lane = slice(column + first, column + first + 256)
+                here = right[:, right_at + first : right_at + first + 256]
+                there = right_other[:, other_at + first : other_at + first + 256]
+                total = dot(left[:, columns], here, TN) + dot(other[:, columns], there, TN)
+                if number < 2:
+                    sent[number * block : (number + 1) * block, lane] = total.astype(BF)
+                elif number == 2:
+                    far[:, lane] = total
+                else:
+                    near[:, lane] = total
+        column += width
 
 
 def finish_kernel(*refs):
@@ -296,14 +309,22 @@
         for at in range(0, near.shape[1], 256):
             lane = slice(at, at + 256)
             total = near[:, lane] + beside[block:, lane].astype(F32) + far[:, lane].astype(F32)
-            kind, first = (column + at) // out.shape[2], (column + at) % out.shape[2]
+            kind, first = (3 * out.shape[2] + column + at) // out.shape[2] % 4, (column + at) % out.shape[2]
             out[:, kind, first : first + 256] = total
         column += near.shape[1]
 
 
-def slice_kernel(number, weights, out):
-    for kind in range(out.shape[0]):
-        out[kind] = weights[:, kind, :]
+def finish_last_kernel(kept, *refs):
+    finish_kernel(*refs[:-1])
+
+
+def fence_kernel(*refs):
+    pass
+
+
+def grad_after_kernel(products, count, where, *refs):
+    args, rest = refs[:count], refs[count + 1 :]
+    grad_kernel(products, count, where, *args, *rest[:3], *rest[4:])
 
 
 class Plan:
@@ -339,6 +360,17 @@
     )(*args)
 
 
+def fence(*arrays):
+    anywhere = [pl.BlockSpec(memory_space=pl.ANY)] * len(arrays)
+    return pl.pallas_call(
+        fence_kernel,
+        out_shape=[jax.ShapeDtypeStruct(array.shape, array.dtype) for array in arrays],
+        in_specs=anywhere,
+        out_specs=anywhere,
+        input_output_aliases={number: number for number in range(len(arrays))},
+    )(*arrays)
+
+
 def swap(array, axis):
     return lax.ppermute(array, axis, [(0, 1), (1, 0)])
 
@@ -348,17 +380,12 @@
 
 
 def quarter_of(weights, number):
-    rows, kinds, width = weights.shape
-    return pl.pallas_call(
-        slice_kernel,
-        out_shape=jax.ShapeDtypeStruct((kinds, rows // 4, width), weights.dtype),
-        grid_spec=pltpu.PrefetchScalarGridSpec(
-            num_scalar_prefetch=1,
-            grid=(1,),
-            in_specs=[pl.BlockSpec((rows // 4, kinds, width), lambda at, number: (number[0], 0, 0))],
-            out_specs=pl.BlockSpec((kinds, rows // 4, width), lambda at, number: (0, 0, 0)),
-        ),
-    )(number.astype(jnp.int32)[None], weights)
+    rows = weights.shape[0]
+    return lax.dynamic_slice_in_dim(weights, number * (rows // 4), rows // 4, 0)
+
+
+def by_kind(weights):
+    return weights.transpose(1, 0, 2)
 
 
 def gather_weights(spatial, temporal, paired):
@@ -375,22 +402,18 @@
     numbers = [side * 2 + even, (1 - side) * 2 + even, side * 2 + 1 - even, (1 - side) * 2 + 1 - even]
     offsets = [here * rows] + [(1 - here) * rows + number * (rows // 4) for number in numbers]
     offsets = jnp.stack(offsets).astype(jnp.int32)
-    own = quarter_of(spatial, numbers[0])
-    first = swap(own, "date")
+    first = swap(quarter_of(spatial, numbers[0]), "date")
     last = swap(quarter_of(spatial, numbers[3]), "date")
-    arrays = [spatial.transpose(1, 0, 2), first, swap(first, "groups")]
-    arrays += [lax.ppermute(first, "loc", PAIRS), last]
+    temporal_sent, first = fence(quarter_of(temporal, numbers[0]), first)
+    arrays = [spatial, first, swap(first, "groups"), lax.ppermute(first, "loc", PAIRS), last]
     table = {kind: [(number, kind, number) for number in range(5)] for kind in range(4)}
-    spatial = Weights(arrays, table, offsets)
-    first = swap(quarter_of(temporal, numbers[0]), "date")
+    spatial_parts = Weights([by_kind(array) for array in arrays], table, offsets)
+    first = swap(temporal_sent, "date")
     group, loc = swap(first, "groups"), lax.ppermute(first, "loc", PAIRS)
-    far = (swap(loc[0:2], "groups"), lax.ppermute(group[2:4], "loc", PAIRS))
-    arrays = [temporal.transpose(1, 0, 2), first, group, loc, *far]
-    table = {
-        kind: [(number, kind, number) for number in range(4)] + [(4 + kind // 2, kind % 2, 4)]
-        for kind in range(4)
-    }
-    return [spatial, Weights(arrays, table, offsets)]
+    middle = rows // 8
+    far = (swap(loc[:middle], "groups"), lax.ppermute(group[middle:], "loc", PAIRS))
+    arrays = [temporal, first, group, loc, jnp.concatenate(far, axis=0)]
+    return [spatial_parts, Weights([by_kind(array) for array in arrays], table, offsets)]
 
 
 def add_over_heads(partial, sizes):
@@ -408,30 +431,37 @@
     return part.astype(F32)
 
 
-def summed(where, left, halves, right, other_right, width):
-    (half_here, half_at), (half_there, there_at) = halves
-    (right, right_at), (other_right, other_at) = right, other_right
-    rows, columns = left.shape
-    block = columns // 4
-    sent, far, near = call(
-        functools.partial(grad_kernel, (half_at, there_at, right_at, other_at), width),
+def summed(where, args, products, kept=None):
+    rows, columns = args[products[0][0]].shape
+    block, width = columns // 4, sum(product[-1] for product in products)
+    passed = () if kept is None else (kept,)
+    outs = call(
+        functools.partial(grad_kernel if kept is None else grad_after_kernel, products, len(args)),
         (
             jax.ShapeDtypeStruct((2 * block, width), BF),
             jax.ShapeDtypeStruct((block, width), F32),
             jax.ShapeDtypeStruct((block, width), F32),
         ),
-        (where, left, half_here, half_there, right, other_right),
+        (where, *args, *passed),
         scratch=(pltpu.VMEM((rows, columns), BF),),
         flops=4 * rows * columns * width,
-    )
+        kept=None if kept is None else 1 + len(args),
+    )
+    return outs
+
+
+def summed_over_loc(outs):
+    sent, far, near = outs[:3]
     beside = lax.ppermute(sent, "loc", PAIRS)
-    far = (far + beside[:block].astype(F32)).astype(BF)
+    far = (far + beside[: far.shape[0]].astype(F32)).astype(BF)
     return near, beside, lax.ppermute(far, "loc", APART)
 
 
-def finish(terms, width):
-    block = terms[0].shape[0]
-    return call(finish_kernel, (jax.ShapeDtypeStruct((block, 4, width), F32),), terms)[0]
+def finish(terms, width, kept=None):
+    out = jax.ShapeDtypeStruct((terms[0].shape[0], 4, width), F32)
+    if kept is None:
+        return call(finish_kernel, (out,), terms)
+    return call(finish_last_kernel, (out,), (kept, *terms), kept=0)
 
 
 def per_device(
@@ -558,8 +588,8 @@
         own, quarter = shape(rows, model // 2), model // 4
         forward_grads = (own, own, shape(rows, 2 * quarter + width))
         temporal_grads = (own, shape(rows, quarter + width))
-        backward_grads = (own, shape(rows, quarter))
         back_shapes = (shape(rows, 3 * width // 2), shape(rows, 3 * width // 2))
+        backward_grads = (own, shape(rows, model // 2 + 3 * width // 2))
     else:
         origins = (start,)
         spatial_moves = [(0, at * spatial_size, at * spatial_size, spatial_size) for at in range(spatial_blocks)]
@@ -602,6 +632,7 @@
             kept=3,
         )
         sources = (origins[0], partials[0], swap(partials[0], "mp"), swap(there, "date"))
+        early, temporal.arrays[-1] = fence(early, temporal.arrays[-1])
         early_other = swap(early, "date")
     else:
         spatial_out = (start.astype(F32) + add_over_heads(partials[0], sizes)).astype(BF)
@@ -621,8 +652,8 @@
             shape(rows, model),
             shape(rows, width),
             shape(rows, model),
-            shape(rows, 3 * width),
             shape(rows, model),
+            *back_shapes,
         ),
         (
             where,
@@ -639,41 +670,56 @@
             pltpu.VMEM((rows, 3 * width), BF),
             pltpu.VMEM(attend_dims(temporal_blocks), F32),
             pltpu.VMEM((rows, width), BF),
+            pltpu.VMEM((rows, 3 * width), BF),
         ),
         flops=2 * layer_flops,
     )
     middle, outs = outs[: len(temporal_grads)], outs[len(temporal_grads) :]
-    joined, temporal_mixed, temporal_partial, temporal_triple, back_part = outs
+    (joined, temporal_mixed, temporal_partial, back_part), temporal_triples = outs[:4], outs[4:]
+    if paired:
+        back_part, early_other = fence(back_part, early_other)
 
     if sizes["mp"] == 2:
         others = swap(back_part, "mp")
     else:
         others = (lax.psum(back_part.astype(F32), "mp") - back_part.astype(F32)).astype(BF)
-    *backs, temporal_triple = call(
+    *backs, temporal_last = call(
         functools.partial(norm_back_kernel, temporal_moves, temporal_size),
         half_shapes,
-        (temporal_gain, back_part, others, joined, cotangent_rows, temporal_triple),
+        (temporal_gain, back_part, others, joined, cotangent_rows, temporal_triples[-1]),
         kept=5,
     )
+    temporal_triples = (*temporal_triples[:-1], temporal_last)
     if paired:
         back_origins = (backs[0], swap(backs[1], "date"))
+        early_there = swap(early_other[:, : 2 * quarter], "mp")
+        middle_other = swap(middle[1], "date")
+        sums = summed(
+            where,
+            (forward[1], early_other, early_there, temporal_mixed, middle_other),
+            ((0, ((1, quarter), (2, quarter)), (3, 0), (4, quarter), width),),
+        )
+        temporal_sums = [(sums[0], sums[1])]
+        kept = sums[2]
     else:
         back = lax.all_to_all(
             temporal_whole(backs[0]), "date", split_axis=0, concat_axis=1, tiled=True
         )
         back_origins = (back.reshape(rows, model),)
+        kept = temporal_last
     outlet = spatial.only((3,))
     plan = plan_of(spatial_blocks, spatial_moves, outlet, backward_grads)
-    outs = call(
+    *outs, kept = call(
         functools.partial(spatial_backward_kernel, plan),
         (*backward_grads, *back_shapes),
-        (where, outlet.offsets, triple, attend, *back_origins, *outlet.arrays),
+        (where, outlet.offsets, triple, attend, kept, *back_origins, *outlet.arrays),
         scratch=(
             pltpu.VMEM((rows, model), BF),
             pltpu.VMEM((rows, width), BF),
             pltpu.VMEM((rows, 3 * width), BF),
         ),
         flops=layer_flops,
+        kept=4,
     )
     backward, back_triples = outs[: len(backward_grads)], outs[len(backward_grads) :]
     encoded = (joined.astype(F32) + add_over_heads(temporal_partial, sizes)).astype(BF)
@@ -682,51 +728,54 @@
         return (
             encoded,
             whole_grads(forward[0], back_triples[0], backward[0], mixed),
-            whole_grads(middle[0], temporal_triple, cotangent_rows, temporal_mixed),
+            whole_grads(middle[0], kept, cotangent_rows, temporal_mixed),
         )
-    early_there = swap(early_other[:, : 2 * quarter], "mp")
-    middle_other = swap(middle[1], "date")
+    temporal_terms = [*summed_over_loc((*temporal_sums[0], kept))]
     middle_there = swap(middle_other[:, :quarter], "mp")
-    triple_other = swap(temporal_triple, "date")
-    temporal_outlet = summed(
+    kept = backward[0]
+    for number, right in enumerate(temporal_triples):
+        *sums, kept = summed(
+            where,
+            (middle[0], middle_other, middle_there, right, swap(right, "date")),
+            ((0, ((1, 0), (2, 0)), (3, 0), (4, 0), right.shape[1]),),
+            kept=kept,
+        )
+        if number == 0:
+            upstream_own, kept = kept, sums[2]
+            first_sums = sums
+        else:
+            temporal_terms += summed_over_loc((*first_sums[:2], kept))
+            temporal_terms += summed_over_loc(sums)
+            kept = None
+    half = model // 2
+    backward_other = swap(backward[1], "date")
+    *sums, kept = summed(
         where,
-        forward[1],
-        ((early_other, quarter), (early_there, quarter)),
-        (temporal_mixed, 0),
-        (middle_other, quarter),
-        width,
-    )
-    temporal_intake = summed(
+        (
+            upstream_own,
+            backward_other,
+            mixed,
+            early_other,
+            forward[0],
+            early_there,
+            back_triples[0],
+        ),
+        (
+            (0, ((1, 0),), (2, 0), (3, 2 * quarter), width),
+            (4, ((3, 0), (5, 0)), (6, 0), (1, half), back_triples[0].shape[1]),
+        ),
+        kept=temporal_terms[6],
+    )
+    temporal_terms[6] = kept
+    spatial_terms = [*summed_over_loc(sums)]
+    sums = summed(
         where,
-        middle[0],
-        ((middle_other, 0), (middle_there, 0)),
-        (temporal_triple, 0),
-        (triple_other, 0),
-        3 * width,
-    )
-    backward_other = swap(backward[1], "date")
-    backward_there = swap(backward_other, "mp")
-    back_others = [swap(array, "date") for array in back_triples]
-    spatial_outlet = summed(
-        where,
-        backward[0],
-        ((backward_other, 0), (backward_there, 0)),
-        (mixed, 0),
-        (early_other, 2 * quarter),
-        width,
-    )
-    terms = []
-    for right, other in zip(back_triples, back_others):
-        terms += summed(
-            where,
-            forward[0],
-            ((early_other, 0), (early_there, 0)),
-            (right, 0),
-            (other, 0),
-            right.shape[1],
-        )
-    temporal_grads = finish((*temporal_intake, *temporal_outlet), width)
-    spatial_grads = finish((*terms, *spatial_outlet), width)
+        (forward[0], early_other, early_there, back_triples[1], swap(back_triples[1], "date")),
+        ((0, ((1, 0), (2, 0)), (3, 0), (4, 0), back_triples[1].shape[1]),),
+    )
+    spatial_terms += summed_over_loc(sums)
+    (temporal_grads,) = finish(temporal_terms, width)
+    spatial_grads, temporal_grads = finish(spatial_terms, width, kept=temporal_grads)
     return (encoded, spatial_grads, temporal_grads)
 
 

time: 229 us -> 230 us (level)
  local copies, waits for them, and re-layouts: 18.3 us -> 31.1 us
  Pallas kernels: 64.4 us -> 55.8 us
  starting transfers between devices: 35.3 us -> 31.8 us
    ppermute x12, waiting for transfers between devices: 53.6 us -> 40.9 us  [the longest x5 28.5 us: summed_over_loc(): beside = lax.ppermute(sent, 'loc', PAIRS)]
    ppermute x21 -> x20, waiting for transfers between devices: 51.2 us -> 62.4 us  [swap(): return lax.ppermute(array, axis, [(0, 1), (1, 0)])]
    pallas_call x3, Pallas kernels: 8.58 us -> 0.01 us  [fence(): pl.pallas_call(fence_kernel, out_shape=[jax.ShapeDtypeStruct(array.shape,...]
    dynamic_slice x0 -> x3, local copies, waits for them, and re-layouts: none -> 4.92 us  [quarter_of(): return lax.dynamic_slice_in_dim(weights, number * (rows // 4), rows // 4, 0)]
    ppermute x12, starting transfers between devices: 15.1 us -> 11.7 us  [the longest x5 5.48 us: summed_over_loc(): return (near, beside, lax.ppermute(far, 'loc', APART))]
    unnamed x102 -> x100, local copies, waits for them, and re-layouts: 12.7 us -> 15.3 us
    ppermute x21 -> x20, starting transfers between devices: 18.1 us -> 18.3 us  [swap(): return lax.ppermute(array, axis, [(0, 1), (1, 0)])]
  transfers between devices with their start and end apart: 34 -> 33, of which waited for: 13 -> 13; matrix products, arithmetic and copies ran while one was open for 6% -> 10% of each run, Pallas kernels for 20% -> 23%
where the time goes in v2:
time: 230 us
  waiting for transfers between devices  103 us (45%)
  Pallas kernels  55.8 us (24%)
  starting transfers between devices  31.8 us (14%)
  local copies, waits for them, and re-layouts  31.1 us (14%)
  other arithmetic  6.38 us (3%)
    ppermute x20, waiting for transfers between devices, swap(): return lax.ppermute(array, axis, [(0, 1), (1, 0)])  62.4 us
    pallas_call x12, Pallas kernels, call(): pl.pallas_call(body, out_shape=outs, in_specs=specs, out_specs=out_specs,...  55.8 us
    ppermute x5, waiting for transfers between devices, summed_over_loc(): beside = lax.ppermute(sent, 'loc', PAIRS)  28.5 us
    ppermute x20, starting transfers between devices, swap(): return lax.ppermute(array, axis, [(0, 1), (1, 0)])  18.3 us
    unnamed x100, local copies, waits for them, and re-layouts  15.3 us
    ppermute x5, waiting for transfers between devices, summed_over_loc(): return (near, beside, lax.ppermute(far, 'loc', APART))  11.1 us
    ppermute x5, starting transfers between devices, summed_over_loc(): return (near, beside, lax.ppermute(far, 'loc', APART))  5.48 us
    dynamic_slice x3, local copies, waits for them, and re-layouts, quarter_of(): return lax.dynamic_slice_in_dim(weights, number * (rows // 4), rows // 4, 0)  4.92 us
  transfers between devices with their start and end apart: 33, of which 13 were waited for; matrix products, arithmetic and copies ran while one was open for 10% of the time, Pallas kernels for 23%

profile of v2, /device:TPU:0, one launch (start us, length us, event | category | flops | bytes accessed | tf_op | source)
XLA Modules:
  0.0 229.6 jit_solution(436324653651241584)
XLA Ops:
  0.7 2.1 constant_dynamic-slice_fusion.1
  2.7 2.9 %collective-permute-start = (bf16[128,4,512]{2,1,0:T(4,128)(2,1)}, bf16[128,4,512]{2,1,0:T(4,128)(2,1)S(1)}, u32[]{:S(2)}, u32[]{:S(2)}) collective-permute-start(bf16[128,4,512]{2,1,0:T(4,128)(2,1)} %constant_dynamic-slice_fusion.1), channel_id=1, source_target_pairs={{0,2},{2,0},{1,3},{3,1},{4,6},{6,4},{5,7},{7,5},{8,10},{10,8},{9,1... | collective-permute-start | bytes 1572872 | tf_op jit(solution)/shard_map/ppermute | solution.py:375
  5.7 2.0 copy.56
  9.5 2.0 constant_dynamic-slice_fusion.2.refs_0_
  12.4 1.2 copy.41
  14.4 1.4 fusion.2
  15.8 2.9 %collective-permute-done.refs_1_ = bf16[128,4,512]{2,1,0:T(4,128)(2,1)S(1)} collective-permute-done((bf16[128,4,512]{2,1,0:T(4,128)(2,1)}, bf16[128,4,512]{2,1,0:T(4,128)(2,1)S(1)}, u32[]{:S(2)}, u32[]{:S(2)}) %collective-permute-start) | collective-permute-done | bytes 524320 | tf_op jit(solution)/shard_map/ppermute | solution.py:375
  19.4 1.1 copy.48
  20.6 2.1 collective-permute-start.7
  22.9 1.1 reverse_select_fusion.1
  24.1 1.6 collective-permute-start.2
  25.8 1.5 collective-permute-start.1
  27.3 13.1 %collective-permute-done.7 = bf16[128,4,512]{2,0,1:T(8,128)(2,1)} collective-permute-done((bf16[128,4,512]{2,0,1:T(8,128)(2,1)S(1)}, bf16[128,4,512]{2,0,1:T(8,128)(2,1)}, u32[]{:S(2)}, u32[]{:S(2)}) %collective-permute-start.7) | collective-permute-done | bytes 524320 | tf_op jit(solution)/shard_map/ppermute | solution.py:375
  40.4 1.8 collective-permute-start.9
  42.2 1.5 collective-permute-start.8
  48.3 8.0 %shard_map.140 = (bf16[144,1024]{1,0:T(8,128)(2,1)}, bf16[144,1024]{1,0:T(8,128)(2,1)}, bf16[288,512]{1,0:T(8,128)(2,1)}, bf16[288,512]{1,0:T(8,128)(2,1)}, bf16...) custom-call(s32[3]{0:T(128)} %pad_add_fusion.where, ...), custom_call_target="tpu_custom_call" | custom-call | flops 1207959552 | bytes 9248800 | tf_op jit(solution)/shard_map/pallas_call | solution.py:351
  59.9 2.0 shard_map.141
  61.9 4.2 %collective-permute-done.10 = bf16[64,4,512]{2,0,1:T(8,128)(2,1)S(1)} collective-permute-done((bf16[64,4,512]{2,0,1:T(8,128)(2,1)S(1)}, bf16[64,4,512]{2,0,1:T(8,128)(2,1)S(1)}, u32[]{:S(2)}, u32[]{:S(2)}) %collective-permute-start.10) | collective-permute-done | bytes 262176 | tf_op jit(solution)/shard_map/ppermute | solution.py:375
  66.1 1.3 collective-permute-done.11
  68.2 1.5 collective-permute-start.13
  70.3 1.7 copy.55
  72.0 17.4 %collective-permute-done.6.refs_3_ = bf16[144,1024]{1,0:T(8,128)(2,1)S(1)} collective-permute-done((bf16[144,1024]{1,0:T(8,128)(2,1)}, bf16[144,1024]{1,0:T(8,128)(2,1)S(1)}, u32[]{:S(2)}, u32[]{:S(2)}) %collective-permute-start.6) | collective-permute-done | bytes 294944 | tf_op jit(solution)/shard_map/ppermute | solution.py:375
  90.1 12.0 %shard_map.143 = (bf16[288,512]{1,0:T(8,128)(2,1)}, bf16[288,768]{1,0:T(8,128)(2,1)}, bf16[288,1024]{1,0:T(8,128)(2,1)}, bf16[288,512]{1,0:T(8,128)(2,1)}, bf16[...) custom-call(s32[3]{0:T(128)} %pad_add_fusion.where, ...), custom_call_target="tpu_custom_call" | custom-call | flops 2415919104 | bytes 9887776 | tf_op jit(solution)/shard_map/pallas_call | solution.py:351
  103.3 1.5 collective-permute-start.15
  104.8 1.0 slice.77
  106.7 3.4 %shard_map.146 = (bf16[144,1024]{1,0:T(8,128)(2,1)}, bf16[144,1024]{1,0:T(8,128)(2,1)}, bf16[288,768]{1,0:T(8,128)(2,1)}) custom-call(f32[1,1024]{1,0:T(1,128)} %bitcast.109, bf16[288,1024]{1,0:T(8,128)(2,1)} %get-tuple-element.86.here, bf16[288,1024]{1,0:T(8,128)(2,1)} %copy-done.23, ...), custom_call_target="tpu_custom_call", output_to_operand_aliasing={{2}: (5, {})} | custom-call | bytes 3395584 | tf_op jit(solution)/shard_map/pallas_call | solution.py:351
  110.9 1.5 collective-permute-start.22
  112.3 4.0 %collective-permute-done.15.refs_4_.refs_1_ = bf16[288,768]{1,0:T(8,128)(2,1)S(1)} collective-permute-done((bf16[288,768]{1,0:T(8,128)(2,1)S(1)}, bf16[288,768]{1,0:T(8,128)(2,1)S(1)}, u32[]{:S(2)}, u32[]{:S(2)}) %collective-permute-start.15) | collective-permute-done | bytes 442400 | tf_op jit(solution)/shard_map/ppermute | solution.py:375
  117.2 3.0 %shard_map.145 = (bf16[256,512]{1,0:T(8,128)(2,1)}, f32[128,512]{1,0:T(8,128)}, f32[128,512]{1,0:T(8,128)}) custom-call(s32[3]{0:T(128)} %pad_add_fusion.where, bf16[288,512]{1,0:T(8,128)(2,1)} %get-tuple-element.79.refs_0_, bf16[288,1024]{1,0:T(8,128)(2,1)} %get-tuple-element.82.refs_1_.refs_3_, bf16[288,512]{1,0:T(8,128)(2,1)} %copy-done.6, ...), custom_call_target="tpu_custom_call" | custom-call | flops 301989888 | bytes 2703372 | tf_op jit(solution)/shard_map/pallas_call | solution.py:351
  120.2 2.5 %collective-permute-done.17.refs_1_ = bf16[144,1024]{1,0:T(8,128)(2,1)S(1)} collective-permute-done((bf16[144,1024]{1,0:T(8,128)(2,1)}, bf16[144,1024]{1,0:T(8,128)(2,1)S(1)}, u32[]{:S(2)}, u32[]{:S(2)}) %collective-permute-start.17) | collective-permute-done | bytes 294944 | tf_op jit(solution)/shard_map/ppermute | solution.py:375
  123.4 7.2 %shard_map.147 = (bf16[288,512]{1,0:T(8,128)(2,1)}, bf16[288,1280]{1,0:T(8,128)(2,1)}, bf16[288,768]{1,0:T(8,128)(2,1)}, bf16[288,768]{1,0:T(8,128)(2,1)}, f32[128,512]{1,0:T(8,128)}) custom-call(s32[3]{0:T(128)} %pad_add_fusion.where, s32[5]{0:T(128)} %stack.39.offsets, ...), custom_call_target="tpu_custom_call", output_to_operand_aliasing={{4}: (4, {})} | custom-call | flops 1207959552 | bytes 8732704 | tf_op jit(solution)/shard_map/pallas_call | solution.py:351
  130.6 1.5 collective-permute-start.25
  135.1 3.2 %shard_map.148 = (bf16[256,768]{1,0:T(8,128)(2,1)}, f32[128,768]{1,0:T(8,128)}, f32[128,768]{1,0:T(8,128)}, bf16[288,512]{1,0:T(8,128)(2,1)}) custom-call(s32[3]{0:T(128)} %pad_add_fusion.where, bf16[288,512]{1,0:T(8,128)(2,1)} %get-tuple-element.93.refs_0_, bf16[288,768]{1,0:T(8,128)(2,1)} %copy-done.3, ...), custom_call_target="tpu_custom_call", output_to_operand_aliasing={{3}: (6, {})} | custom-call | flops 452984832 | bytes 3244044 | tf_op jit(solution)/shard_map/pallas_call | solution.py:351
  138.3 1.4 collective-permute-start.23
  140.0 1.6 collective-permute-start.30
  141.5 18.1 %collective-permute-done.21.refs_4_ = bf16[288,768]{1,0:T(8,128)(2,1)S(1)} collective-permute-done((bf16[288,768]{1,0:T(8,128)(2,1)S(1)}, bf16[288,768]{1,0:T(8,128)(2,1)S(1)}, u32[]{:S(2)}, u32[]{:S(2)}) %collective-permute-start.21) | collective-permute-done | bytes 442400 | tf_op jit(solution)/shard_map/ppermute | solution.py:375
  160.4 3.3 %shard_map.149 = (bf16[256,768]{1,0:T(8,128)(2,1)}, f32[128,768]{1,0:T(8,128)}, f32[128,768]{1,0:T(8,128)}, f32[128,768]{1,0:T(8,128)}) custom-call(s32[3]{0:T(128)} %pad_add_fusion.where, bf16[288,512]{1,0:T(8,128)(2,1)} %get-tuple-element.93.refs_0_, bf16[288,768]{1,0:T(8,128)(2,1)} %copy-done.3, ...), custom_call_target="tpu_custom_call", output_to_operand_aliasing={{3}: (6, {})} | custom-call | flops 452984832 | bytes 3342348 | tf_op jit(solution)/shard_map/pallas_call | solution.py:351
  165.0 4.4 %shard_map.150 = (bf16[256,1280]{1,0:T(8,128)(2,1)}, f32[128,1280]{1,0:T(8,128)}, f32[128,1280]{1,0:T(8,128)}, f32[128,768]{1,0:T(8,128)}) custom-call(s32[3]{0:T(128)} %pad_add_fusion.where, bf16[288,512]{1,0:T(8,128)(2,1)} %get-tuple-element.101.refs_0_, bf16[288,1280]{1,0:T(8,128)(2,1)} %copy-done.17, ...), custom_call_target="tpu_custom_call", output_to_operand_aliasing={{3}: (8, {})} | custom-call | flops 754974720 | bytes 5308428 | tf_op jit(solution)/shard_map/pallas_call | solution.py:351
  169.4 1.6 collective-permute-start.28
  171.1 2.6 %collective-permute-start.19 = (bf16[128,512]{1,0:T(8,128)(2,1)S(1)}, bf16[128,512]{1,0:T(8,128)(2,1)S(1)}, u32[]{:S(2)}, u32[]{:S(2)}) collective-permute-start(bf16[128,512]{1,0:T(8,128)(2,1)S(1)} %add_convert_fusion.5), channel_id=1, source_target_pairs={{0,8},{4,12},{8,0},{12,4},{1,9},{5,13},{9,1},{13,5},{2,10},{6,14},... | collective-permute-start | bytes 393224 | tf_op jit(solution)/shard_map/ppermute | solution.py:457
  175.0 3.4 %shard_map.152 = (bf16[256,768]{1,0:T(8,128)(2,1)}, f32[128,768]{1,0:T(8,128)}, f32[128,768]{1,0:T(8,128)}) custom-call(s32[3]{0:T(128)} %pad_add_fusion.where, bf16[288,512]{1,0:T(8,128)(2,1)} %get-tuple-element.104.refs_4_.refs_0_, bf16[288,1024]{1,0:T(8,128)(2,1)} %get-tuple-element.82.refs_1_.refs_3_, bf16[288,512]{1,0:T(8,128)(2,1)} %copy-done.6, ...), custom_call_target="tpu_custom_call" | custom-call | flops 452984832 | bytes 3244044 | tf_op jit(solution)/shard_map/pallas_call | solution.py:351
  178.8 6.2 %collective-permute-done.26.refs_7_ = bf16[256,768]{1,0:T(8,128)(2,1)S(1)} collective-permute-done((bf16[256,768]{1,0:T(8,128)(2,1)}, bf16[256,768]{1,0:T(8,128)(2,1)S(1)}, u32[]{:S(2)}, u32[]{:S(2)}) %collective-permute-start.26) | collective-permute-done | bytes 393248 | tf_op jit(solution)/shard_map/ppermute | solution.py:455
  185.3 18.8 %collective-permute-done.28.refs_1_ = bf16[256,1280]{1,0:T(8,128)(2,1)S(1)} collective-permute-done((bf16[256,1280]{1,0:T(8,128)(2,1)}, bf16[256,1280]{1,0:T(8,128)(2,1)S(1)}, u32[]{:S(2)}, u32[]{:S(2)}) %collective-permute-start.28) | collective-permute-done | bytes 655392 | tf_op jit(solution)/shard_map/ppermute | solution.py:455
  204.9 3.5 %collective-permute-done.31.refs_4_ = bf16[256,768]{1,0:T(8,128)(2,1)S(1)} collective-permute-done((bf16[256,768]{1,0:T(8,128)(2,1)}, bf16[256,768]{1,0:T(8,128)(2,1)S(1)}, u32[]{:S(2)}, u32[]{:S(2)}) %collective-permute-start.31) | collective-permute-done | bytes 393248 | tf_op jit(solution)/shard_map/ppermute | solution.py:455
  208.4 1.4 collective-permute-start.32
  211.7 3.0 %shard_map.151.kept = f32[128,4,512]{2,1,0:T(4,128)} custom-call(f32[128,512]{1,0:T(8,128)} %get-tuple-element.90.refs_0_, bf16[256,512]{1,0:T(8,128)(2,1)} %copy-done.19, bf16[128,512]{1,0:T(8,128)(2,1)} %copy-done.39, f32[128,768]{1,0:T(8,128)} %get-tuple-element.98.refs_3_, bf16[256,768]{1,0:T(8,128)(2,1)} %copy-done.14, bf16[128,768]{1,0:T(8,128)(2,1)} %copy-done.36, ...), custom_call_target="tpu_custom_call" | custom-call | bytes 3670016 | tf_op jit(solution)/shard_map/pallas_call | solution.py:351
  214.7 11.1 %collective-permute-done.32.refs_5_ = bf16[128,768]{1,0:T(8,128)(2,1)S(1)} collective-permute-done((bf16[128,768]{1,0:T(8,128)(2,1)S(1)}, bf16[128,768]{1,0:T(8,128)(2,1)S(1)}, u32[]{:S(2)}, u32[]{:S(2)}) %collective-permute-start.32) | collective-permute-done | bytes 196640 | tf_op jit(solution)/shard_map/ppermute | solution.py:457
  226.6 3.0 %shard_map.153 = (f32[128,4,512]{2,1,0:T(4,128)}, f32[128,4,512]{2,1,0:T(4,128)}) custom-call(f32[128,4,512]{2,1,0:T(4,128)} %shard_map.151.kept, f32[128,1280]{1,0:T(8,128)} %get-tuple-element.110.refs_0_, bf16[256,1280]{1,0:T(8,128)(2,1)} %copy-done.13, bf16[128,1280]{1,0:T(8,128)(2,1)} %copy-done.32, ...), custom_call_target="tpu_custom_call", output_to_operand_aliasing={{1}: (0, {})} | custom-call | bytes 4718592 | tf_op jit(solution)/shard_map/pallas_call | solution.py:351
  (191 shorter events, 29.8 us)
Async XLA Ops:
  0.6 13.0 %copy-start = (bf16[196,1024]{1,0:T(8,128)(2,1)S(1)}, bf16[196,1024]{1,0:T(8,128)(2,1)}, u32[]{:S(2)}) copy-start(bf16[196,1024]{1,0:T(8,128)(2,1)} %param.17) | copy-start | bytes 1204228
  2.7 15.9 %collective-permute-start = (bf16[128,4,512]{2,1,0:T(4,128)(2,1)}, bf16[128,4,512]{2,1,0:T(4,128)(2,1)S(1)}, u32[]{:S(2)}, u32[]{:S(2)}) collective-permute-start(bf16[128,4,512]{2,1,0:T(4,128)(2,1)} %constant_dynamic-slice_fusion.1), channel_id=1, source_target_pairs={{0,2},{2,0},{1,3},{3,1},{4,6},{6,4},{5,7},{7,5},{8,10},{10,8},{9,1... | collective-permute-start | bytes 1572872 | tf_op jit(solution)/shard_map/ppermute | solution.py:375
  8.6 38.7 %collective-permute-start.3 = (bf16[128,4,512]{2,0,1:T(8,128)(2,1)}, bf16[128,4,512]{2,0,1:T(8,128)(2,1)}, u32[]{:S(2)}, u32[]{:S(2)}) collective-permute-start(bf16[128,4,512]{2,0,1:T(8,128)(2,1)} %constant_dynamic-slice_fusion), channel_id=1, source_target_pairs={{0,2},{2,0},{1,3},{3,1},{4,6},{6,4},{5,7},{7,5},{8,10},{10,8},{9,1... | collective-permute-start | bytes 1572872 | tf_op jit(solution)/shard_map/ppermute | solution.py:375
  20.6 19.8 %collective-permute-start.7 = (bf16[128,4,512]{2,0,1:T(8,128)(2,1)S(1)}, bf16[128,4,512]{2,0,1:T(8,128)(2,1)}, u32[]{:S(2)}, u32[]{:S(2)}) collective-permute-start(bf16[128,4,512]{2,0,1:T(8,128)(2,1)S(1)} %copy.48), channel_id=1, source_target_pairs={{0,2},{2,0},{1,3},{3,1},{4,6},{6,4},{5,7},{7,5},{8,10},{10,8},{9,1... | collective-permute-start | bytes 1572872 | tf_op jit(solution)/shard_map/ppermute | solution.py:375
  24.1 21.9 %copy-start.4 = (bf16[128,4,512]{2,0,1:T(8,128)(2,1)}, bf16[128,4,512]{2,0,1:T(8,128)(2,1)S(1)}, u32[]{:S(2)}) copy-start(bf16[128,4,512]{2,0,1:T(8,128)(2,1)S(1)} %copy.57) | copy-start | bytes 1572868
  24.1 23.2 %collective-permute-start.2 = (bf16[128,4,512]{2,0,1:T(8,128)(2,1)S(1)}, bf16[128,4,512]{2,0,1:T(8,128)(2,1)S(1)}, u32[]{:S(2)}, u32[]{:S(2)}) collective-permute-start(bf16[128,4,512]{2,0,1:T(8,128)(2,1)S(1)} %copy.57), channel_id=1, source_target_pairs={{0,4},{4,0},{8,12},{12,8},{1,5},{5,1},{9,13},{13,9},{2,6},{6,2},{1... | collective-permute-start | bytes 1572872 | tf_op jit(solution)/shard_map/ppermute | solution.py:408
  25.8 21.5 %collective-permute-start.1 = (bf16[128,4,512]{2,0,1:T(8,128)(2,1)S(1)}, bf16[128,4,512]{2,0,1:T(8,128)(2,1)S(1)}, u32[]{:S(2)}, u32[]{:S(2)}) collective-permute-start(bf16[128,4,512]{2,0,1:T(8,128)(2,1)S(1)} %copy.57), channel_id=1, source_target_pairs={{0,16},{16,0},{1,17},{17,1},{2,18},{18,2},{3,19},{19,3},{4,20},{20... | collective-permute-start | bytes 1572872 | tf_op jit(solution)/shard_map/ppermute | solution.py:375
  40.4 16.0 %collective-permute-start.9 = (bf16[128,4,512]{2,0,1:T(8,128)(2,1)}, bf16[128,4,512]{2,0,1:T(8,128)(2,1)}, u32[]{:S(2)}, u32[]{:S(2)}) collective-permute-start(bf16[128,4,512]{2,0,1:T(8,128)(2,1)} %collective-permute-done.7), channel_id=1, source_target_pairs={{0,4},{4,0},{8,12},{12,8},{1,5},{5,1},{9,13},{13,9},{2,6},{6,2},{1... | collective-permute-start | bytes 1572872 | tf_op jit(solution)/shard_map/ppermute | solution.py:412
  42.2 15.7 %collective-permute-start.8 = (bf16[128,4,512]{2,0,1:T(8,128)(2,1)}, bf16[128,4,512]{2,0,1:T(8,128)(2,1)}, u32[]{:S(2)}, u32[]{:S(2)}) collective-permute-start(bf16[128,4,512]{2,0,1:T(8,128)(2,1)} %collective-permute-done.7), channel_id=1, source_target_pairs={{0,16},{16,0},{1,17},{17,1},{2,18},{18,2},{3,19},{19,3},{4,20},{20... | collective-permute-start | bytes 1572872 | tf_op jit(solution)/shard_map/ppermute | solution.py:375
  56.3 2.9 %collective-permute-start.5 = (bf16[144,1024]{1,0:T(8,128)(2,1)}, bf16[144,1024]{1,0:T(8,128)(2,1)S(1)}, u32[]{:S(2)}, u32[]{:S(2)}) collective-permute-start(bf16[144,1024]{1,0:T(8,128)(2,1)} %get-tuple-element.69.here), channel_id=1, source_target_pairs={{0,1},{1,0},{2,3},{3,2},{4,5},{5,4},{6,7},{7,6},{8,9},{9,8},{10,11... | collective-permute-start | bytes 884744 | tf_op jit(solution)/shard_map/ppermute | solution.py:375
  57.4 8.8 %collective-permute-start.10 = (bf16[64,4,512]{2,0,1:T(8,128)(2,1)S(1)}, bf16[64,4,512]{2,0,1:T(8,128)(2,1)S(1)}, u32[]{:S(2)}, u32[]{:S(2)}) collective-permute-start(bf16[64,4,512]{2,0,1:T(8,128)(2,1)S(1)} %slice.93), channel_id=1, source_target_pairs={{0,16},{16,0},{1,17},{17,1},{2,18},{18,2},{3,19},{19,3},{4,20},{20... | collective-permute-start | bytes 786440 | tf_op jit(solution)/shard_map/ppermute | solution.py:375
  58.9 8.5 %collective-permute-start.11 = (bf16[64,4,512]{2,0,1:T(8,128)(2,1)S(1)}, bf16[64,4,512]{2,0,1:T(8,128)(2,1)S(1)}, u32[]{:S(2)}, u32[]{:S(2)}) collective-permute-start(bf16[64,4,512]{2,0,1:T(8,128)(2,1)S(1)} %slice.94), channel_id=1, source_target_pairs={{0,4},{4,0},{8,12},{12,8},{1,5},{5,1},{9,13},{13,9},{2,6},{6,2},{1... | collective-permute-start | bytes 786440 | tf_op jit(solution)/shard_map/ppermute | solution.py:414
  59.9 9.9 %copy-start.44 = (bf16[144,1024]{1,0:T(8,128)(2,1)S(1)}, bf16[144,1024]{1,0:T(8,128)(2,1)}, u32[]{:S(2)}) copy-start(bf16[144,1024]{1,0:T(8,128)(2,1)} %get-tuple-element.68.refs_1_) | copy-start | bytes 884740
  61.9 8.4 %copy-start.5 = (bf16[512,4,512]{2,1,0:T(4,128)(2,1)S(1)}, bf16[512,4,512]{2,1,0:T(4,128)(2,1)}, u32[]{:S(2)}) copy-start(bf16[512,4,512]{2,1,0:T(4,128)(2,1)} %param.22) | copy-start | bytes 6291460
  68.2 33.9 %collective-permute-start.13 = (bf16[288,1024]{1,0:T(8,128)(2,1)}, bf16[288,1024]{1,0:T(8,128)(2,1)S(1)}, u32[]{:S(2)}, u32[]{:S(2)}) collective-permute-start(bf16[288,1024]{1,0:T(8,128)(2,1)} %get-tuple-element.81), channel_id=1, source_target_pairs={{0,2},{2,0},{1,3},{3,1},{4,6},{6,4},{5,7},{7,5},{8,10},{10,8},{9,1... | collective-permute-start | bytes 1769480 | tf_op jit(solution)/shard_map/ppermute | solution.py:375
  69.7 2.3 collective-permute-start.4
  69.7 19.6 %collective-permute-start.6 = (bf16[144,1024]{1,0:T(8,128)(2,1)}, bf16[144,1024]{1,0:T(8,128)(2,1)S(1)}, u32[]{:S(2)}, u32[]{:S(2)}) collective-permute-start(bf16[144,1024]{1,0:T(8,128)(2,1)} %get-tuple-element.71), channel_id=1, source_target_pairs={{0,2},{2,0},{1,3},{3,1},{4,6},{6,4},{5,7},{7,5},{8,10},{10,8},{9,1... | collective-permute-start | bytes 884744 | tf_op jit(solution)/shard_map/ppermute | solution.py:375
  72.0 17.4 %copy-start.45 = (bf16[144,1024]{1,0:T(8,128)(2,1)}, bf16[144,1024]{1,0:T(8,128)(2,1)S(1)}, u32[]{:S(2)}) copy-start(bf16[144,1024]{1,0:T(8,128)(2,1)S(1)} %collective-permute-done.4.refs_2_) | copy-start | bytes 884740
  103.0 2.9 %collective-permute-start.16 = (bf16[288,1024]{1,0:T(8,128)(2,1)}, bf16[288,1024]{1,0:T(8,128)(2,1)S(1)}, u32[]{:S(2)}, u32[]{:S(2)}) collective-permute-start(bf16[288,1024]{1,0:T(8,128)(2,1)} %get-tuple-element.86.here), channel_id=1, source_target_pairs={{0,1},{1,0},{2,3},{3,2},{4,5},{5,4},{6,7},{7,6},{8,9},{9,8},{10,11... | collective-permute-start | bytes 1769480 | tf_op jit(solution)/shard_map/ppermute | solution.py:375
  103.3 13.0 %collective-permute-start.15 = (bf16[288,768]{1,0:T(8,128)(2,1)S(1)}, bf16[288,768]{1,0:T(8,128)(2,1)S(1)}, u32[]{:S(2)}, u32[]{:S(2)}) collective-permute-start(bf16[288,768]{1,0:T(8,128)(2,1)S(1)} %copy-done.43), channel_id=1, source_target_pairs={{0,2},{2,0},{1,3},{3,1},{4,6},{6,4},{5,7},{7,5},{8,10},{10,8},{9,1... | collective-permute-start | bytes 1327112 | tf_op jit(solution)/shard_map/ppermute | solution.py:375
  105.8 10.6 %collective-permute-start.14 = (bf16[288,512]{1,0:T(8,128)(2,1)S(1)}, bf16[288,512]{1,0:T(8,128)(2,1)S(1)}, u32[]{:S(2)}, u32[]{:S(2)}) collective-permute-start(bf16[288,512]{1,0:T(8,128)(2,1)S(1)} %slice.77), channel_id=1, source_target_pairs={{0,1},{1,0},{2,3},{3,2},{4,5},{5,4},{6,7},{7,6},{8,9},{9,8},{10,11... | collective-permute-start | bytes 884744 | tf_op jit(solution)/shard_map/ppermute | solution.py:375
  110.1 12.6 %collective-permute-start.17 = (bf16[144,1024]{1,0:T(8,128)(2,1)}, bf16[144,1024]{1,0:T(8,128)(2,1)S(1)}, u32[]{:S(2)}, u32[]{:S(2)}) collective-permute-start(bf16[144,1024]{1,0:T(8,128)(2,1)} %get-tuple-element.89), channel_id=1, source_target_pairs={{0,2},{2,0},{1,3},{3,1},{4,6},{6,4},{5,7},{7,5},{8,10},{10,8},{9,1... | collective-permute-start | bytes 884744 | tf_op jit(solution)/shard_map/ppermute | solution.py:375
  110.8 28.8 %collective-permute-start.12 = (bf16[288,1024]{1,0:T(8,128)(2,1)S(1)}, bf16[288,1024]{1,0:T(8,128)(2,1)S(1)}, u32[]{:S(2)}, u32[]{:S(2)}) collective-permute-start(bf16[288,1024]{1,0:T(8,128)(2,1)S(1)} %copy-done.22), channel_id=1, source_target_pairs={{0,1},{1,0},{2,3},{3,2},{4,5},{5,4},{6,7},{7,6},{8,9},{9,8},{10,11... | collective-permute-start | bytes 1769480 | tf_op jit(solution)/shard_map/ppermute | solution.py:375
  110.9 22.8 %collective-permute-start.22 = (bf16[288,768]{1,0:T(8,128)(2,1)S(1)}, bf16[288,768]{1,0:T(8,128)(2,1)S(1)}, u32[]{:S(2)}, u32[]{:S(2)}) collective-permute-start(bf16[288,768]{1,0:T(8,128)(2,1)S(1)} %copy-done.25), channel_id=1, source_target_pairs={{0,2},{2,0},{1,3},{3,1},{4,6},{6,4},{5,7},{7,5},{8,10},{10,8},{9,1... | collective-permute-start | bytes 1327112 | tf_op jit(solution)/shard_map/ppermute | solution.py:375
  123.4 9.7 %copy-start.12 = (bf16[288,768]{1,0:T(8,128)(2,1)S(1)}, bf16[288,768]{1,0:T(8,128)(2,1)}, u32[]{:S(2)}) copy-start(bf16[288,768]{1,0:T(8,128)(2,1)} %get-tuple-element.94.refs_3_) | copy-start | bytes 1327108
  123.4 10.3 %copy-start.47 = (bf16[256,512]{1,0:T(8,128)(2,1)S(1)}, bf16[256,512]{1,0:T(8,128)(2,1)}, u32[]{:S(2)}) copy-start(bf16[256,512]{1,0:T(8,128)(2,1)} %get-tuple-element.91) | copy-start | bytes 786436
  130.6 9.1 %copy-start.7 = (bf16[288,1024]{1,0:T(8,128)(2,1)S(1)}, bf16[288,1024]{1,0:T(8,128)(2,1)}, u32[]{:S(2)}) copy-start(bf16[288,1024]{1,0:T(8,128)(2,1)} %get-tuple-element.75.joined) | copy-start | bytes 1769476
  130.6 33.6 %collective-permute-start.25 = (bf16[288,1280]{1,0:T(8,128)(2,1)}, bf16[288,1280]{1,0:T(8,128)(2,1)S(1)}, u32[]{:S(2)}, u32[]{:S(2)}) collective-permute-start(bf16[288,1280]{1,0:T(8,128)(2,1)} %get-tuple-element.102), channel_id=1, source_target_pairs={{0,2},{2,0},{1,3},{3,1},{4,6},{6,4},{5,7},{7,5},{8,10},{10,8},{9,1... | collective-permute-start | bytes 2211848 | tf_op jit(solution)/shard_map/ppermute | solution.py:375
  133.0 1.4 collective-permute-start.20
  133.1 26.6 %collective-permute-start.21 = (bf16[288,768]{1,0:T(8,128)(2,1)S(1)}, bf16[288,768]{1,0:T(8,128)(2,1)S(1)}, u32[]{:S(2)}, u32[]{:S(2)}) collective-permute-start(bf16[288,768]{1,0:T(8,128)(2,1)S(1)} %copy-done.12), channel_id=1, source_target_pairs={{0,2},{2,0},{1,3},{3,1},{4,6},{6,4},{5,7},{7,5},{8,10},{10,8},{9,1... | collective-permute-start | bytes 1327112 | tf_op jit(solution)/shard_map/ppermute | solution.py:375
  133.7 37.4 %collective-permute-start.18 = (bf16[256,512]{1,0:T(8,128)(2,1)S(1)}, bf16[256,512]{1,0:T(8,128)(2,1)S(1)}, u32[]{:S(2)}, u32[]{:S(2)}) collective-permute-start(bf16[256,512]{1,0:T(8,128)(2,1)S(1)} %copy-done.47), channel_id=1, source_target_pairs={{0,4},{4,0},{8,12},{12,8},{1,5},{5,1},{9,13},{13,9},{2,6},{6,2},{1... | collective-permute-start | bytes 786440 | tf_op jit(solution)/shard_map/ppermute | solution.py:455
  138.3 35.4 %collective-permute-start.23 = (bf16[256,768]{1,0:T(8,128)(2,1)}, bf16[256,768]{1,0:T(8,128)(2,1)S(1)}, u32[]{:S(2)}, u32[]{:S(2)}) collective-permute-start(bf16[256,768]{1,0:T(8,128)(2,1)} %get-tuple-element.99), channel_id=1, source_target_pairs={{0,4},{4,0},{8,12},{12,8},{1,5},{5,1},{9,13},{13,9},{2,6},{6,2},{1... | collective-permute-start | bytes 1179656 | tf_op jit(solution)/shard_map/ppermute | solution.py:455
  140.0 34.2 %collective-permute-start.30 = (bf16[288,768]{1,0:T(8,128)(2,1)S(1)}, bf16[288,768]{1,0:T(8,128)(2,1)S(1)}, u32[]{:S(2)}, u32[]{:S(2)}) collective-permute-start(bf16[288,768]{1,0:T(8,128)(2,1)S(1)} %copy-done.24), channel_id=1, source_target_pairs={{0,2},{2,0},{1,3},{3,1},{4,6},{6,4},{5,7},{7,5},{8,10},{10,8},{9,1... | collective-permute-start | bytes 1327112 | tf_op jit(solution)/shard_map/ppermute | solution.py:375
  163.7 21.3 %collective-permute-start.26 = (bf16[256,768]{1,0:T(8,128)(2,1)}, bf16[256,768]{1,0:T(8,128)(2,1)S(1)}, u32[]{:S(2)}, u32[]{:S(2)}) collective-permute-start(bf16[256,768]{1,0:T(8,128)(2,1)} %get-tuple-element.108), channel_id=1, source_target_pairs={{0,4},{4,0},{8,12},{12,8},{1,5},{5,1},{9,13},{13,9},{2,6},{6,2},{1... | collective-permute-start | bytes 1179656 | tf_op jit(solution)/shard_map/ppermute | solution.py:455
  165.0 6.0 %copy-start.35 = (f32[128,512]{1,0:T(8,128)S(1)}, f32[128,512]{1,0:T(8,128)}, u32[]{:S(2)}) copy-start(f32[128,512]{1,0:T(8,128)} %get-tuple-element.92) | copy-start | bytes 786436
  165.0 8.7 %copy-start.30 = (f32[128,768]{1,0:T(8,128)S(1)}, f32[128,768]{1,0:T(8,128)}, u32[]{:S(2)}) copy-start(f32[128,768]{1,0:T(8,128)} %get-tuple-element.100) | copy-start | bytes 1179652
  169.4 34.7 %collective-permute-start.28 = (bf16[256,1280]{1,0:T(8,128)(2,1)}, bf16[256,1280]{1,0:T(8,128)(2,1)S(1)}, u32[]{:S(2)}, u32[]{:S(2)}) collective-permute-start(bf16[256,1280]{1,0:T(8,128)(2,1)} %get-tuple-element.111), channel_id=1, source_target_pairs={{0,4},{4,0},{8,12},{12,8},{1,5},{5,1},{9,13},{13,9},{2,6},{6,2},{1... | collective-permute-start | bytes 1966088 | tf_op jit(solution)/shard_map/ppermute | solution.py:455
  171.0 7.3 %copy-start.19 = (bf16[256,512]{1,0:T(8,128)(2,1)}, bf16[256,512]{1,0:T(8,128)(2,1)S(1)}, u32[]{:S(2)}) copy-start(bf16[256,512]{1,0:T(8,128)(2,1)S(1)} %collective-permute-done.18.refs_1_) | copy-start | bytes 786436
  171.1 39.8 %collective-permute-start.19 = (bf16[128,512]{1,0:T(8,128)(2,1)S(1)}, bf16[128,512]{1,0:T(8,128)(2,1)S(1)}, u32[]{:S(2)}, u32[]{:S(2)}) collective-permute-start(bf16[128,512]{1,0:T(8,128)(2,1)S(1)} %add_convert_fusion.5), channel_id=1, source_target_pairs={{0,8},{4,12},{8,0},{12,4},{1,9},{5,13},{9,1},{13,5},{2,10},{6,14},... | collective-permute-start | bytes 393224 | tf_op jit(solution)/shard_map/ppermute | solution.py:457
  173.8 11.3 %copy-start.29 = (f32[128,768]{1,0:T(8,128)S(1)}, f32[128,768]{1,0:T(8,128)}, u32[]{:S(2)}) copy-start(f32[128,768]{1,0:T(8,128)} %get-tuple-element.109) | copy-start | bytes 1179652
  173.8 30.4 %copy-start.18 = (f32[128,1280]{1,0:T(8,128)S(1)}, f32[128,1280]{1,0:T(8,128)}, u32[]{:S(2)}) copy-start(f32[128,1280]{1,0:T(8,128)} %get-tuple-element.112) | copy-start | bytes 1966084
  173.8 37.1 %collective-permute-start.24 = (bf16[128,768]{1,0:T(8,128)(2,1)S(1)}, bf16[128,768]{1,0:T(8,128)(2,1)S(1)}, u32[]{:S(2)}, u32[]{:S(2)}) collective-permute-start(bf16[128,768]{1,0:T(8,128)(2,1)S(1)} %add_convert_fusion.4), channel_id=1, source_target_pairs={{0,8},{4,12},{8,0},{12,4},{1,9},{5,13},{9,1},{13,5},{2,10},{6,14},... | collective-permute-start | bytes 589832 | tf_op jit(solution)/shard_map/ppermute | solution.py:457
  178.3 30.1 %copy-start.31 = (f32[128,768]{1,0:T(8,128)S(1)}, f32[128,768]{1,0:T(8,128)}, u32[]{:S(2)}) copy-start(f32[128,768]{1,0:T(8,128)} %get-tuple-element.116) | copy-start | bytes 1179652
  178.3 30.1 %collective-permute-start.31 = (bf16[256,768]{1,0:T(8,128)(2,1)}, bf16[256,768]{1,0:T(8,128)(2,1)S(1)}, u32[]{:S(2)}, u32[]{:S(2)}) collective-permute-start(bf16[256,768]{1,0:T(8,128)(2,1)} %get-tuple-element.115), channel_id=1, source_target_pairs={{0,4},{4,0},{8,12},{12,8},{1,5},{5,1},{9,13},{13,9},{2,6},{6,2},{1... | collective-permute-start | bytes 1179656 | tf_op jit(solution)/shard_map/ppermute | solution.py:455
  185.0 23.4 %copy-start.15 = (bf16[256,768]{1,0:T(8,128)(2,1)}, bf16[256,768]{1,0:T(8,128)(2,1)S(1)}, u32[]{:S(2)}) copy-start(bf16[256,768]{1,0:T(8,128)(2,1)S(1)} %collective-permute-done.26.refs_7_) | copy-start | bytes 1179652
  185.1 25.9 %collective-permute-start.27 = (bf16[128,768]{1,0:T(8,128)(2,1)S(1)}, bf16[128,768]{1,0:T(8,128)(2,1)S(1)}, u32[]{:S(2)}, u32[]{:S(2)}) collective-permute-start(bf16[128,768]{1,0:T(8,128)(2,1)S(1)} %add_convert_fusion.3), channel_id=1, source_target_pairs={{0,8},{4,12},{8,0},{12,4},{1,9},{5,13},{9,1},{13,5},{2,10},{6,14},... | collective-permute-start | bytes 589832 | tf_op jit(solution)/shard_map/ppermute | solution.py:457
  204.2 21.7 %collective-permute-start.29 = (bf16[128,1280]{1,0:T(8,128)(2,1)S(1)}, bf16[128,1280]{1,0:T(8,128)(2,1)S(1)}, u32[]{:S(2)}, u32[]{:S(2)}) collective-permute-start(bf16[128,1280]{1,0:T(8,128)(2,1)S(1)} %add_convert_fusion.1), channel_id=1, source_target_pairs={{0,8},{4,12},{8,0},{12,4},{1,9},{5,13},{9,1},{13,5},{2,10},{6,14},... | collective-permute-start | bytes 983048 | tf_op jit(solution)/shard_map/ppermute | solution.py:457
  208.4 17.4 %collective-permute-start.32 = (bf16[128,768]{1,0:T(8,128)(2,1)S(1)}, bf16[128,768]{1,0:T(8,128)(2,1)S(1)}, u32[]{:S(2)}, u32[]{:S(2)}) collective-permute-start(bf16[128,768]{1,0:T(8,128)(2,1)S(1)} %add_convert_fusion.2), channel_id=1, source_target_pairs={{0,8},{4,12},{8,0},{12,4},{1,9},{5,13},{9,1},{13,5},{2,10},{6,14},... | collective-permute-start | bytes 589832 | tf_op jit(solution)/shard_map/ppermute | solution.py:457
  (34 other events, 60.2 us)

commit v3 on v2

--- a/solution.py
+++ b/solution.py
@@ -322,9 +322,9 @@
     pass
 
 
-def grad_after_kernel(products, count, where, *refs):
-    args, rest = refs[:count], refs[count + 1 :]
-    grad_kernel(products, count, where, *args, *rest[:3], *rest[4:])
+def grad_after_kernel(products, count, passed, where, *refs):
+    args, rest = refs[:count], refs[count + passed :]
+    grad_kernel(products, count, where, *args, *rest[:3], rest[-1])
 
 
 class Plan:
@@ -334,7 +334,7 @@
         self.paired, self.locs, self.grads, self.sources = paired, locs, grads, sources
 
 
-def call(body, outs, args, scratch=(), flops=0, kept=None):
+def call(body, outs, args, scratch=(), flops=0, kept=()):
     smem = pl.BlockSpec(memory_space=pltpu.SMEM)
     vmem = pl.BlockSpec(memory_space=pltpu.VMEM)
     specs = [smem if arg.dtype == jnp.int32 else vmem for arg in args]
@@ -343,11 +343,11 @@
     outs = list(outs)
     moved = sum(arg.size * arg.dtype.itemsize for arg in args)
     moved = moved + sum(out.size * out.dtype.itemsize for out in outs)
-    if kept is not None:
-        specs[kept] = pl.BlockSpec(memory_space=pl.ANY)
+    for number in kept:
+        specs[number] = pl.BlockSpec(memory_space=pl.ANY)
         out_specs.append(pl.BlockSpec(memory_space=pl.ANY))
-        outs.append(jax.ShapeDtypeStruct(args[kept].shape, args[kept].dtype))
-        aliases = {kept: len(outs) - 1}
+        outs.append(jax.ShapeDtypeStruct(args[number].shape, args[number].dtype))
+        aliases[number] = len(outs) - 1
     return pl.pallas_call(
         body,
         out_shape=outs,
@@ -388,32 +388,36 @@
     return weights.transpose(1, 0, 2)
 
 
-def gather_weights(spatial, temporal, paired):
-    if not paired:
-        found = []
-        for weights in (spatial, temporal):
-            whole = lax.all_gather(weights.transpose(1, 0, 2), "date", axis=1, tiled=True)
-            table = {kind: [(0, kind, 0)] for kind in range(4)}
-            found.append(Weights([whole], table, jnp.zeros((1,), jnp.int32)))
-        return found
-    rows = spatial.shape[0]
+def whole_weights(weights):
+    whole = lax.all_gather(weights.transpose(1, 0, 2), "date", axis=1, tiled=True)
+    return Weights([whole], {kind: [(0, kind, 0)] for kind in range(4)}, jnp.zeros((1,), jnp.int32))
+
+
+def quarters(rows):
     side, here = lax.axis_index("groups"), lax.axis_index("date")
     even = lax.axis_index("loc") % 2
     numbers = [side * 2 + even, (1 - side) * 2 + even, side * 2 + 1 - even, (1 - side) * 2 + 1 - even]
     offsets = [here * rows] + [(1 - here) * rows + number * (rows // 4) for number in numbers]
-    offsets = jnp.stack(offsets).astype(jnp.int32)
-    first = swap(quarter_of(spatial, numbers[0]), "date")
-    last = swap(quarter_of(spatial, numbers[3]), "date")
-    temporal_sent, first = fence(quarter_of(temporal, numbers[0]), first)
-    arrays = [spatial, first, swap(first, "groups"), lax.ppermute(first, "loc", PAIRS), last]
+    return numbers, jnp.stack(offsets).astype(jnp.int32)
+
+
+def weights_of(arrays, offsets):
     table = {kind: [(number, kind, number) for number in range(5)] for kind in range(4)}
-    spatial_parts = Weights([by_kind(array) for array in arrays], table, offsets)
-    first = swap(temporal_sent, "date")
+    return Weights([by_kind(array) for array in arrays], table, offsets)
+
+
+def gather_first(weights, last, numbers, offsets):
+    first = swap(quarter_of(weights, numbers[0]), "date")
+    last = swap(last, "date")
+    arrays = [weights, first, swap(first, "groups"), lax.ppermute(first, "loc", PAIRS), last]
+    return weights_of(arrays, offsets)
+
+
+def gather_second(weights, first, offsets):
     group, loc = swap(first, "groups"), lax.ppermute(first, "loc", PAIRS)
-    middle = rows // 8
+    middle = first.shape[0] // 2
     far = (swap(loc[:middle], "groups"), lax.ppermute(group[middle:], "loc", PAIRS))
-    arrays = [temporal, first, group, loc, jnp.concatenate(far, axis=0)]
-    return [spatial_parts, Weights([by_kind(array) for array in arrays], table, offsets)]
+    return weights_of([weights, first, group, loc, jnp.concatenate(far, axis=0)], offsets)
 
 
 def add_over_heads(partial, sizes):
@@ -431,23 +435,21 @@
     return part.astype(F32)
 
 
-def summed(where, args, products, kept=None):
+def summed(where, args, products, kept=()):
     rows, columns = args[products[0][0]].shape
     block, width = columns // 4, sum(product[-1] for product in products)
-    passed = () if kept is None else (kept,)
-    outs = call(
-        functools.partial(grad_kernel if kept is None else grad_after_kernel, products, len(args)),
+    return call(
+        functools.partial(grad_after_kernel, products, len(args), len(kept)),
         (
             jax.ShapeDtypeStruct((2 * block, width), BF),
             jax.ShapeDtypeStruct((block, width), F32),
             jax.ShapeDtypeStruct((block, width), F32),
         ),
-        (where, *args, *passed),
+        (where, *args, *kept),
         scratch=(pltpu.VMEM((rows, columns), BF),),
         flops=4 * rows * columns * width,
-        kept=None if kept is None else 1 + len(args),
-    )
-    return outs
+        kept=tuple(range(1 + len(args), 1 + len(args) + len(kept))),
+    )
 
 
 def summed_over_loc(outs):
@@ -461,7 +463,7 @@
     out = jax.ShapeDtypeStruct((terms[0].shape[0], 4, width), F32)
     if kept is None:
         return call(finish_kernel, (out,), terms)
-    return call(finish_last_kernel, (out,), (kept, *terms), kept=0)
+    return call(finish_last_kernel, (out,), (kept, *terms), kept=(0,))
 
 
 def per_device(
@@ -487,7 +489,11 @@
     first = here * dates_here
     paired = sizes["groups"] == 2 and sizes["loc"] == 4 and sizes["date"] == 2 and sizes["mp"] == 2
     paired = paired and dates_here % 2 == 0 and patches_here % 8 == 0 and model % 1024 == 0
-    spatial, temporal = gather_weights(spatial_weights, temporal_weights, paired)
+    if paired:
+        numbers, offsets = quarters(spatial_weights.shape[0])
+        last_sent = quarter_of(spatial_weights, numbers[3])
+    else:
+        spatial, temporal = whole_weights(spatial_weights), whole_weights(temporal_weights)
 
     if paired:
         pairs, eights = dates_here // 2, patches_here // 8
@@ -601,6 +607,13 @@
         (origins, spatial_bias, temporal_bias, date_rows, cotangent_rows)
     )
 
+    if paired:
+        sent = quarter_of(temporal_weights, numbers[0])
+        last_sent, sent, far_origin = fence(last_sent, sent, origins[1])
+        origins = (origins[0], far_origin)
+        spatial = gather_first(spatial_weights, last_sent, numbers, offsets)
+        temporal_first = swap(sent, "date")
+
     def plan_of(blocks, moves, weights, grads, sources=0):
         return Plan(blocks, moves, len(origins), weights, paired, sizes["loc"], len(grads), sources)
 
@@ -625,14 +638,17 @@
     partials, outs = outs[: len(origins)], outs[len(origins) :]
     forward, (triple, attend, mixed) = outs[: len(forward_grads)], outs[len(forward_grads) :]
     if paired:
+        temporal_first, kept = fence(temporal_first, partials[1])
+        partials = (partials[0], kept)
+        temporal = gather_second(temporal_weights, temporal_first, offsets)
         there, early = call(
             between_kernel,
             (shape(half, model),),
             (origins[1], partials[1], swap(partials[1], "mp"), forward[2]),
-            kept=3,
+            kept=(3,),
         )
-        sources = (origins[0], partials[0], swap(partials[0], "mp"), swap(there, "date"))
-        early, temporal.arrays[-1] = fence(early, temporal.arrays[-1])
+        early, there = fence(early, swap(there, "date"))
+        sources = (origins[0], partials[0], swap(partials[0], "mp"), there)
         early_other = swap(early, "date")
     else:
         spatial_out = (start.astype(F32) + add_over_heads(partials[0], sizes)).astype(BF)
@@ -687,7 +703,7 @@
         functools.partial(norm_back_kernel, temporal_moves, temporal_size),
         half_shapes,
         (temporal_gain, back_part, others, joined, cotangent_rows, temporal_triples[-1]),
-        kept=5,
+        kept=(5,),
     )
     temporal_triples = (*temporal_triples[:-1], temporal_last)
     if paired:
@@ -719,7 +735,7 @@
             pltpu.VMEM((rows, 3 * width), BF),
         ),
         flops=layer_flops,
-        kept=4,
+        kept=(4,),
     )
     backward, back_triples = outs[: len(backward_grads)], outs[len(backward_grads) :]
     encoded = (joined.astype(F32) + add_over_heads(temporal_partial, sizes)).astype(BF)
@@ -732,21 +748,17 @@
         )
     temporal_terms = [*summed_over_loc((*temporal_sums[0], kept))]
     middle_there = swap(middle_other[:, :quarter], "mp")
-    kept = backward[0]
-    for number, right in enumerate(temporal_triples):
-        *sums, kept = summed(
-            where,
-            (middle[0], middle_other, middle_there, right, swap(right, "date")),
-            ((0, ((1, 0), (2, 0)), (3, 0), (4, 0), right.shape[1]),),
-            kept=kept,
-        )
-        if number == 0:
-            upstream_own, kept = kept, sums[2]
-            first_sums = sums
-        else:
-            temporal_terms += summed_over_loc((*first_sums[:2], kept))
-            temporal_terms += summed_over_loc(sums)
-            kept = None
+    others = [swap(array, "date") for array in temporal_triples]
+    *sums, upstream_own, temporal_terms[1] = summed(
+        where,
+        (middle[0], middle_other, middle_there, *temporal_triples, *others),
+        tuple(
+            (0, ((1, 0), (2, 0)), (3 + number, 0), (5 + number, 0), temporal_triples[number].shape[1])
+            for number in range(2)
+        ),
+        kept=(backward[0], temporal_terms[1]),
+    )
+    temporal_terms += summed_over_loc(sums)
     half = model // 2
     backward_other = swap(backward[1], "date")
     *sums, kept = summed(
@@ -764,9 +776,9 @@
             (0, ((1, 0),), (2, 0), (3, 2 * quarter), width),
             (4, ((3, 0), (5, 0)), (6, 0), (1, half), back_triples[0].shape[1]),
         ),
-        kept=temporal_terms[6],
-    )
-    temporal_terms[6] = kept
+        kept=(temporal_terms[3],),
+    )
+    temporal_terms[3] = kept
     spatial_terms = [*summed_over_loc(sums)]
     sums = summed(
         where,

time: 230 us -> 233 us (1.013)
  waiting for transfers between devices: 103 us -> 86 us
  local copies, waits for them, and re-layouts: 31.1 us -> 44.7 us
  other arithmetic: 6.38 us -> 17.9 us
  starting transfers between devices: 31.8 us -> 28.4 us
    ppermute x20, waiting for transfers between devices: 62.4 us -> 37.6 us  [swap(): return lax.ppermute(array, axis, [(0, 1), (1, 0)])]
    ppermute x3, waiting for transfers between devices: 1.28 us -> 10 us  [the longest x1 8.01 us: gather_second(): group, loc = (swap(first, 'groups'), lax.ppermute(first, 'loc', PAIRS))]
    ppermute x5 -> x4, waiting for transfers between devices: 28.5 us -> 25.9 us  [summed_over_loc(): beside = lax.ppermute(sent, 'loc', PAIRS)]
    ppermute x20, starting transfers between devices: 18.3 us -> 15.8 us  [swap(): return lax.ppermute(array, axis, [(0, 1), (1, 0)])]
    ppermute x5 -> x4, starting transfers between devices: 5.48 us -> 3.16 us  [summed_over_loc(): return (near, beside, lax.ppermute(far, 'loc', APART))]
    pallas_call x12 -> x11, Pallas kernels: 55.8 us -> 54 us  [call(): pl.pallas_call(body, out_shape=outs, in_specs=specs, out_specs=out_specs,...]
    ppermute x5 -> x4, waiting for transfers between devices: 11.1 us -> 12.5 us  [summed_over_loc(): return (near, beside, lax.ppermute(far, 'loc', APART))]
    unnamed x100 -> x92, local copies, waits for them, and re-layouts: 15.3 us -> 15 us
  transfers between devices with their start and end apart: 33 -> 31, of which waited for: 13 -> 13; matrix products, arithmetic and copies ran while one was open for 10% -> 21% of each run, Pallas kernels for 23% -> 22%
where the time goes in v3:
time: 233 us; the launch traced here: 232 us
  waiting for transfers between devices  86 us (37%)
  Pallas kernels  54 us (23%)
  local copies, waits for them, and re-layouts  44.7 us (19%)
  starting transfers between devices  28.4 us (12%)
  other arithmetic  17.9 us (8%)
    pallas_call x11, Pallas kernels, call(): pl.pallas_call(body, out_shape=outs, in_specs=specs, out_specs=out_specs,...  54 us
    ppermute x20, waiting for transfers between devices, swap(): return lax.ppermute(array, axis, [(0, 1), (1, 0)])  37.6 us
    ppermute x4, waiting for transfers between devices, summed_over_loc(): beside = lax.ppermute(sent, 'loc', PAIRS)  25.9 us
    ppermute x20, starting transfers between devices, swap(): return lax.ppermute(array, axis, [(0, 1), (1, 0)])  15.8 us
    unnamed x92, local copies, waits for them, and re-layouts  15 us
    ppermute x4, waiting for transfers between devices, summed_over_loc(): return (near, beside, lax.ppermute(far, 'loc', APART))  12.5 us
    ppermute x1, waiting for transfers between devices, gather_second(): group, loc = (swap(first, 'groups'), lax.ppermute(first, 'loc', PAIRS))  8.01 us
  transfers between devices with their start and end apart: 31, of which 13 were waited for; matrix products, arithmetic and copies ran while one was open for 21% of the time, Pallas kernels for 22%

profile of v3, /device:TPU:0, one launch (start us, length us, event | category | flops | bytes accessed | tf_op | source)
XLA Modules:
  0.0 232.1 jit_solution(4993924556945619583)
XLA Ops:
  0.7 2.0 copy.59
  2.8 3.0 %collective-permute-start = (bf16[128,4,512]{2,0,1:T(8,128)(2,1)S(1)}, bf16[128,4,512]{2,0,1:T(8,128)(2,1)S(1)}, u32[]{:S(2)}, u32[]{:S(2)}) collective-permute-start(bf16[128,4,512]{2,0,1:T(8,128)(2,1)S(1)} %constant_dynamic-slice_fusion), channel_id=1, source_target_pairs={{0,2},{2,0},{1,3},{3,1},{4,6},{6,4},{5,7},{7,5},{8,10},{10,8},{9,1... | collective-permute-start | bytes 1572872 | tf_op jit(solution)/shard_map/ppermute | solution.py:375
  10.6 1.3 fusion.6
  12.4 1.3 mul.134
  15.0 1.4 sub.49
  19.1 1.4 eq.83
  21.7 1.4 eq.82
  28.3 1.4 broadcast_in_dim.54
  29.7 1.4 gather_fusion
  32.1 1.6 fusion.2
  34.6 1.3 reverse_select_fusion.1
  37.4 1.6 slice.88
  40.0 2.0 constant_dynamic-slice_fusion.2.refs_0_
  43.0 1.9 copy.47
  44.9 2.1 collective-permute-start.2
  47.0 1.5 collective-permute-start.1
  48.6 1.5 collective-permute-start.5
  51.2 8.8 %collective-permute-done.3 = bf16[128,4,512]{2,0,1:T(8,128)(2,1)} collective-permute-done((bf16[128,4,512]{2,0,1:T(8,128)(2,1)}, bf16[128,4,512]{2,0,1:T(8,128)(2,1)}, u32[]{:S(2)}, u32[]{:S(2)}) %collective-permute-start.3) | collective-permute-done | bytes 524320 | tf_op jit(solution)/shard_map/ppermute | solution.py:375
  60.1 8.0 %shard_map.140 = (bf16[144,1024]{1,0:T(8,128)(2,1)}, bf16[144,1024]{1,0:T(8,128)(2,1)}, bf16[288,512]{1,0:T(8,128)(2,1)}, bf16[288,512]{1,0:T(8,128)(2,1)}, bf16...) custom-call(s32[3]{0:T(128)} %pad_add_fusion.where, ...), custom_call_target="tpu_custom_call" | custom-call | flops 1207959552 | bytes 9248800 | tf_op jit(solution)/shard_map/pallas_call | solution.py:351
  68.1 1.6 collective-permute-done.5.refs_0_
  71.7 1.6 collective-permute-start.9
  73.3 1.5 collective-permute-start.8
  75.5 2.0 shard_map.142
  78.1 8.0 %collective-permute-done.9 = bf16[128,4,512]{2,0,1:T(8,128)(2,1)S(1)} collective-permute-done((bf16[128,4,512]{2,0,1:T(8,128)(2,1)S(1)}, bf16[128,4,512]{2,0,1:T(8,128)(2,1)S(1)}, u32[]{:S(2)}, u32[]{:S(2)}) %collective-permute-start.9) | collective-permute-done | bytes 524320 | tf_op jit(solution)/shard_map/ppermute | solution.py:417
  86.9 1.5 collective-permute-start.10
  89.2 1.6 collective-permute-start.11
  92.1 1.8 copy.58
  95.1 2.0 collective-permute-done.11
  97.2 1.9 maximum_bitcast_fusion.refs_8_
  99.7 12.0 %shard_map.144 = (bf16[288,512]{1,0:T(8,128)(2,1)}, bf16[288,768]{1,0:T(8,128)(2,1)}, bf16[288,1024]{1,0:T(8,128)(2,1)}, bf16[288,512]{1,0:T(8,128)(2,1)}, bf16[...) custom-call(s32[3]{0:T(128)} %pad_add_fusion.where, ...), custom_call_target="tpu_custom_call" | custom-call | flops 2415919104 | bytes 9887776 | tf_op jit(solution)/shard_map/pallas_call | solution.py:351
  115.6 3.3 %shard_map.147 = (bf16[144,1024]{1,0:T(8,128)(2,1)}, bf16[144,1024]{1,0:T(8,128)(2,1)}, bf16[288,768]{1,0:T(8,128)(2,1)}) custom-call(f32[1,1024]{1,0:T(1,128)} %bitcast.107, bf16[288,1024]{1,0:T(8,128)(2,1)} %get-tuple-element.89.here, bf16[288,1024]{1,0:T(8,128)(2,1)} %copy-done.18, ...), custom_call_target="tpu_custom_call", output_to_operand_aliasing={{2}: (5, {})} | custom-call | bytes 3395584 | tf_op jit(solution)/shard_map/pallas_call | solution.py:351
  120.2 5.8 %collective-permute-done.15.refs_4_.refs_1_ = bf16[288,768]{1,0:T(8,128)(2,1)S(1)} collective-permute-done((bf16[288,768]{1,0:T(8,128)(2,1)S(1)}, bf16[288,768]{1,0:T(8,128)(2,1)S(1)}, u32[]{:S(2)}, u32[]{:S(2)}) %collective-permute-start.15) | collective-permute-done | bytes 442400 | tf_op jit(solution)/shard_map/ppermute | solution.py:375
  126.8 3.0 %shard_map.146 = (bf16[256,512]{1,0:T(8,128)(2,1)}, f32[128,512]{1,0:T(8,128)}, f32[128,512]{1,0:T(8,128)}) custom-call(s32[3]{0:T(128)} %pad_add_fusion.where, bf16[288,512]{1,0:T(8,128)(2,1)} %get-tuple-element.82.refs_0_, bf16[288,1024]{1,0:T(8,128)(2,1)} %get-tuple-element.85.refs_1_.refs_3_, bf16[288,512]{1,0:T(8,128)(2,1)} %copy-done.4, ...), custom_call_target="tpu_custom_call" | custom-call | flops 301989888 | bytes 2703372 | tf_op jit(solution)/shard_map/pallas_call | solution.py:351
  129.8 1.6 collective-permute-start.21
  132.0 1.5 collective-permute-start.20
  134.2 7.2 %shard_map.148 = (bf16[288,512]{1,0:T(8,128)(2,1)}, bf16[288,1280]{1,0:T(8,128)(2,1)}, bf16[288,768]{1,0:T(8,128)(2,1)}, bf16[288,768]{1,0:T(8,128)(2,1)}, f32[128,512]{1,0:T(8,128)}) custom-call(s32[3]{0:T(128)} %pad_add_fusion.where, s32[5]{0:T(128)} %stack.39.offsets, ...), custom_call_target="tpu_custom_call", output_to_operand_aliasing={{4}: (4, {})} | custom-call | flops 1207959552 | bytes 8732704 | tf_op jit(solution)/shard_map/pallas_call | solution.py:351
  144.5 9.5 %collective-permute-done.20.refs_6_ = bf16[288,768]{1,0:T(8,128)(2,1)S(1)} collective-permute-done((bf16[288,768]{1,0:T(8,128)(2,1)S(1)}, bf16[288,768]{1,0:T(8,128)(2,1)S(1)}, u32[]{:S(2)}, u32[]{:S(2)}) %collective-permute-start.20) | collective-permute-done | bytes 442400 | tf_op jit(solution)/shard_map/ppermute | solution.py:375
  154.8 4.7 %shard_map.149 = (bf16[256,1536]{1,0:T(8,128)(2,1)}, f32[128,1536]{1,0:T(8,128)}, f32[128,1536]{1,0:T(8,128)}, bf16[288,512]{1,0:T(8,128)(2,1)}, bf16[256,512]{1,0:T(8,128)(2,1)}) custom-call(s32[3]{0:T(128)} %pad_add_fusion.where, bf16[288,512]{1,0:T(8,128)(2,1)} %get-tuple-element.94.refs_0_, ...), custom_call_target="tpu_custom_call", output_to_operand_aliasing={{3}: (8, {}), {4}: (9, {})} | custom-call | flops 905969664 | bytes 5570572 | tf_op jit(solution)/shard_map/pallas_call | solution.py:351
  160.5 9.3 %collective-permute-done.23.refs_1_ = bf16[288,1280]{1,0:T(8,128)(2,1)S(1)} collective-permute-done((bf16[288,1280]{1,0:T(8,128)(2,1)}, bf16[288,1280]{1,0:T(8,128)(2,1)S(1)}, u32[]{:S(2)}, u32[]{:S(2)}) %collective-permute-start.23) | collective-permute-done | bytes 737312 | tf_op jit(solution)/shard_map/ppermute | solution.py:375
  170.7 4.4 %shard_map.150 = (bf16[256,1280]{1,0:T(8,128)(2,1)}, f32[128,1280]{1,0:T(8,128)}, f32[128,1280]{1,0:T(8,128)}, f32[128,1536]{1,0:T(8,128)}) custom-call(s32[3]{0:T(128)} %pad_add_fusion.where, bf16[288,512]{1,0:T(8,128)(2,1)} %get-tuple-element.101.refs_0_, bf16[288,1280]{1,0:T(8,128)(2,1)} %copy-done.13, ...), custom_call_target="tpu_custom_call", output_to_operand_aliasing={{3}: (8, {})} | custom-call | flops 754974720 | bytes 5701644 | tf_op jit(solution)/shard_map/pallas_call | solution.py:351
  175.8 2.6 %collective-permute-start.22 = (bf16[128,512]{1,0:T(8,128)(2,1)S(1)}, bf16[128,512]{1,0:T(8,128)(2,1)S(1)}, u32[]{:S(2)}, u32[]{:S(2)}) collective-permute-start(bf16[128,512]{1,0:T(8,128)(2,1)S(1)} %add_convert_fusion.4), channel_id=1, source_target_pairs={{0,8},{4,12},{8,0},{12,4},{1,9},{5,13},{9,1},{13,5},{2,10},{6,14},... | collective-permute-start | bytes 393224 | tf_op jit(solution)/shard_map/ppermute | solution.py:459
  179.2 3.4 %shard_map.152 = (bf16[256,768]{1,0:T(8,128)(2,1)}, f32[128,768]{1,0:T(8,128)}, f32[128,768]{1,0:T(8,128)}) custom-call(s32[3]{0:T(128)} %pad_add_fusion.where, bf16[288,512]{1,0:T(8,128)(2,1)} %get-tuple-element.104.refs_4_.refs_0_, bf16[288,1024]{1,0:T(8,128)(2,1)} %get-tuple-element.85.refs_1_.refs_3_, bf16[288,512]{1,0:T(8,128)(2,1)} %copy-done.4, ...), custom_call_target="tpu_custom_call" | custom-call | flops 452984832 | bytes 3244044 | tf_op jit(solution)/shard_map/pallas_call | solution.py:351
  182.6 1.6 collective-permute-start.29
  184.7 21.6 %collective-permute-done.26.refs_1_ = bf16[256,1280]{1,0:T(8,128)(2,1)S(1)} collective-permute-done((bf16[256,1280]{1,0:T(8,128)(2,1)}, bf16[256,1280]{1,0:T(8,128)(2,1)S(1)}, u32[]{:S(2)}, u32[]{:S(2)}) %collective-permute-start.26) | collective-permute-done | bytes 655392 | tf_op jit(solution)/shard_map/ppermute | solution.py:457
  206.4 4.3 %collective-permute-done.29.refs_4_ = bf16[256,768]{1,0:T(8,128)(2,1)S(1)} collective-permute-done((bf16[256,768]{1,0:T(8,128)(2,1)}, bf16[256,768]{1,0:T(8,128)(2,1)S(1)}, u32[]{:S(2)}, u32[]{:S(2)}) %collective-permute-start.29) | collective-permute-done | bytes 393248 | tf_op jit(solution)/shard_map/ppermute | solution.py:457
  212.7 3.0 %shard_map.151.kept = f32[128,4,512]{2,1,0:T(4,128)} custom-call(f32[128,512]{1,0:T(8,128)} %get-tuple-element.93.refs_0_, bf16[256,512]{1,0:T(8,128)(2,1)} %get-tuple-element.99.refs_1_, bf16[128,512]{1,0:T(8,128)(2,1)} %copy-done.31, f32[128,1536]{1,0:T(8,128)} %get-tuple-element.107.refs_3_, bf16[256,1536]{1,0:T(8,128)(2,1)} %copy-done.8, ...), custom_call_target="tpu_custom_call" | custom-call | bytes 3670016 | tf_op jit(solution)/shard_map/pallas_call | solution.py:351
  215.7 12.5 %collective-permute-done.30.refs_5_ = bf16[128,768]{1,0:T(8,128)(2,1)S(1)} collective-permute-done((bf16[128,768]{1,0:T(8,128)(2,1)S(1)}, bf16[128,768]{1,0:T(8,128)(2,1)S(1)}, u32[]{:S(2)}, u32[]{:S(2)}) %collective-permute-start.30) | collective-permute-done | bytes 196640 | tf_op jit(solution)/shard_map/ppermute | solution.py:459
  229.0 3.0 %shard_map.153 = (f32[128,4,512]{2,1,0:T(4,128)}, f32[128,4,512]{2,1,0:T(4,128)}) custom-call(f32[128,4,512]{2,1,0:T(4,128)} %shard_map.151.kept, f32[128,1280]{1,0:T(8,128)} %get-tuple-element.110.refs_0_, bf16[256,1280]{1,0:T(8,128)(2,1)} %copy-done.9, bf16[128,1280]{1,0:T(8,128)(2,1)} %copy-done.25, ...), custom_call_target="tpu_custom_call", output_to_operand_aliasing={{1}: (0, {})} | custom-call | bytes 4718592 | tf_op jit(solution)/shard_map/pallas_call | solution.py:351
  (178 shorter events, 48.3 us)
Async XLA Ops:
  0.6 29.1 %copy-start = (bf16[196,1024]{1,0:T(8,128)(2,1)S(1)}, bf16[196,1024]{1,0:T(8,128)(2,1)}, u32[]{:S(2)}) copy-start(bf16[196,1024]{1,0:T(8,128)(2,1)} %param.17) | copy-start | bytes 1204228
  2.7 29.4 %copy-start.1 = (bf16[512,4,512]{2,0,1:T(8,128)(2,1)}, bf16[512,4,512]{2,0,1:T(8,128)(2,1)S(1)}, u32[]{:S(2)}) copy-start(bf16[512,4,512]{2,0,1:T(8,128)(2,1)S(1)} %copy.59) | copy-start | bytes 6291460
  2.8 42.2 %collective-permute-start = (bf16[128,4,512]{2,0,1:T(8,128)(2,1)S(1)}, bf16[128,4,512]{2,0,1:T(8,128)(2,1)S(1)}, u32[]{:S(2)}, u32[]{:S(2)}) collective-permute-start(bf16[128,4,512]{2,0,1:T(8,128)(2,1)S(1)} %constant_dynamic-slice_fusion), channel_id=1, source_target_pairs={{0,2},{2,0},{1,3},{3,1},{4,6},{6,4},{5,7},{7,5},{8,10},{10,8},{9,1... | collective-permute-start | bytes 1572872 | tf_op jit(solution)/shard_map/ppermute | solution.py:375
  44.9 15.2 %collective-permute-start.3 = (bf16[128,4,512]{2,0,1:T(8,128)(2,1)}, bf16[128,4,512]{2,0,1:T(8,128)(2,1)}, u32[]{:S(2)}, u32[]{:S(2)}) collective-permute-start(bf16[128,4,512]{2,0,1:T(8,128)(2,1)} %copy.47), channel_id=1, source_target_pairs={{0,2},{2,0},{1,3},{3,1},{4,6},{6,4},{5,7},{7,5},{8,10},{10,8},{9,1... | collective-permute-start | bytes 1572872 | tf_op jit(solution)/shard_map/ppermute | solution.py:375
  44.9 15.1 %copy-start.7 = (bf16[128,4,512]{2,0,1:T(8,128)(2,1)}, bf16[128,4,512]{2,0,1:T(8,128)(2,1)S(1)}, u32[]{:S(2)}) copy-start(bf16[128,4,512]{2,0,1:T(8,128)(2,1)S(1)} %collective-permute-done) | copy-start | bytes 1572868
  44.9 15.1 %collective-permute-start.2 = (bf16[128,4,512]{2,0,1:T(8,128)(2,1)S(1)}, bf16[128,4,512]{2,0,1:T(8,128)(2,1)}, u32[]{:S(2)}, u32[]{:S(2)}) collective-permute-start(bf16[128,4,512]{2,0,1:T(8,128)(2,1)S(1)} %collective-permute-done), channel_id=1, source_target_pairs={{0,4},{4,0},{8,12},{12,8},{1,5},{5,1},{9,13},{13,9},{2,6},{6,2},{1... | collective-permute-start | bytes 1572872 | tf_op jit(solution)/shard_map/ppermute | solution.py:412
  47.0 13.0 %collective-permute-start.1 = (bf16[128,4,512]{2,0,1:T(8,128)(2,1)S(1)}, bf16[128,4,512]{2,0,1:T(8,128)(2,1)}, u32[]{:S(2)}, u32[]{:S(2)}) collective-permute-start(bf16[128,4,512]{2,0,1:T(8,128)(2,1)S(1)} %collective-permute-done), channel_id=1, source_target_pairs={{0,16},{16,0},{1,17},{17,1},{2,18},{18,2},{3,19},{19,3},{4,20},{20... | collective-permute-start | bytes 1572872 | tf_op jit(solution)/shard_map/ppermute | solution.py:375
  48.6 21.2 %collective-permute-start.5 = (bf16[128,4,512]{2,1,0:T(4,128)(2,1)}, bf16[128,4,512]{2,1,0:T(4,128)(2,1)S(1)}, u32[]{:S(2)}, u32[]{:S(2)}) collective-permute-start(bf16[128,4,512]{2,1,0:T(4,128)(2,1)} %get-tuple-element.70), channel_id=1, source_target_pairs={{0,2},{2,0},{1,3},{3,1},{4,6},{6,4},{5,7},{7,5},{8,10},{10,8},{9,1... | collective-permute-start | bytes 1572872 | tf_op jit(solution)/shard_map/ppermute | solution.py:375
  70.5 4.3 %collective-permute-start.6 = (bf16[144,1024]{1,0:T(8,128)(2,1)}, bf16[144,1024]{1,0:T(8,128)(2,1)S(1)}, u32[]{:S(2)}, u32[]{:S(2)}) collective-permute-start(bf16[144,1024]{1,0:T(8,128)(2,1)} %get-tuple-element.72.here), channel_id=1, source_target_pairs={{0,1},{1,0},{2,3},{3,2},{4,5},{5,4},{6,7},{7,6},{8,9},{9,8},{10,11... | collective-permute-start | bytes 884744 | tf_op jit(solution)/shard_map/ppermute | solution.py:375
  71.7 17.5 %copy-start.19 = (bf16[128,4,512]{2,0,1:T(8,128)(2,1)}, bf16[128,4,512]{2,0,1:T(8,128)(2,1)S(1)}, u32[]{:S(2)}) copy-start(bf16[128,4,512]{2,0,1:T(8,128)(2,1)S(1)} %copy.60) | copy-start | bytes 1572868
  71.7 14.4 %collective-permute-start.9 = (bf16[128,4,512]{2,0,1:T(8,128)(2,1)S(1)}, bf16[128,4,512]{2,0,1:T(8,128)(2,1)S(1)}, u32[]{:S(2)}, u32[]{:S(2)}) collective-permute-start(bf16[128,4,512]{2,0,1:T(8,128)(2,1)S(1)} %copy.60), channel_id=1, source_target_pairs={{0,4},{4,0},{8,12},{12,8},{1,5},{5,1},{9,13},{13,9},{2,6},{6,2},{1... | collective-permute-start | bytes 1572872 | tf_op jit(solution)/shard_map/ppermute | solution.py:417
  73.3 15.1 %collective-permute-start.8 = (bf16[128,4,512]{2,0,1:T(8,128)(2,1)S(1)}, bf16[128,4,512]{2,0,1:T(8,128)(2,1)S(1)}, u32[]{:S(2)}, u32[]{:S(2)}) collective-permute-start(bf16[128,4,512]{2,0,1:T(8,128)(2,1)S(1)} %copy.60), channel_id=1, source_target_pairs={{0,16},{16,0},{1,17},{17,1},{2,18},{18,2},{3,19},{19,3},{4,20},{20... | collective-permute-start | bytes 1572872 | tf_op jit(solution)/shard_map/ppermute | solution.py:375
  77.5 13.3 %collective-permute-start.7 = (bf16[144,1024]{1,0:T(8,128)(2,1)}, bf16[144,1024]{1,0:T(8,128)(2,1)S(1)}, u32[]{:S(2)}, u32[]{:S(2)}) collective-permute-start(bf16[144,1024]{1,0:T(8,128)(2,1)} %get-tuple-element.75), channel_id=1, source_target_pairs={{0,2},{2,0},{1,3},{3,1},{4,6},{6,4},{5,7},{7,5},{8,10},{10,8},{9,1... | collective-permute-start | bytes 884744 | tf_op jit(solution)/shard_map/ppermute | solution.py:375
  86.9 8.3 %collective-permute-start.10 = (bf16[64,4,512]{2,0,1:T(8,128)(2,1)}, bf16[64,4,512]{2,0,1:T(8,128)(2,1)}, u32[]{:S(2)}, u32[]{:S(2)}) collective-permute-start(bf16[64,4,512]{2,0,1:T(8,128)(2,1)} %slice.89), channel_id=1, source_target_pairs={{0,16},{16,0},{1,17},{17,1},{2,18},{18,2},{3,19},{19,3},{4,20},{20... | collective-permute-start | bytes 786440 | tf_op jit(solution)/shard_map/ppermute | solution.py:375
  89.2 8.0 %collective-permute-start.11 = (bf16[64,4,512]{2,0,1:T(8,128)(2,1)}, bf16[64,4,512]{2,0,1:T(8,128)(2,1)}, u32[]{:S(2)}, u32[]{:S(2)}) collective-permute-start(bf16[64,4,512]{2,0,1:T(8,128)(2,1)} %slice.90), channel_id=1, source_target_pairs={{0,4},{4,0},{8,12},{12,8},{1,5},{5,1},{9,13},{13,9},{2,6},{6,2},{1... | collective-permute-start | bytes 786440 | tf_op jit(solution)/shard_map/ppermute | solution.py:419
  91.5 20.2 %collective-permute-start.13 = (bf16[288,1024]{1,0:T(8,128)(2,1)}, bf16[288,1024]{1,0:T(8,128)(2,1)S(1)}, u32[]{:S(2)}, u32[]{:S(2)}) collective-permute-start(bf16[288,1024]{1,0:T(8,128)(2,1)} %get-tuple-element.84), channel_id=1, source_target_pairs={{0,2},{2,0},{1,3},{3,1},{4,6},{6,4},{5,7},{7,5},{8,10},{10,8},{9,1... | collective-permute-start | bytes 1769480 | tf_op jit(solution)/shard_map/ppermute | solution.py:375
  92.1 6.9 %collective-permute-start.4 = (bf16[144,1024]{1,0:T(8,128)(2,1)}, bf16[144,1024]{1,0:T(8,128)(2,1)S(1)}, u32[]{:S(2)}, u32[]{:S(2)}) collective-permute-start(bf16[144,1024]{1,0:T(8,128)(2,1)} %get-tuple-element.69.refs_1_), channel_id=1, source_target_pairs={{0,1},{1,0},{2,3},{3,2},{4,5},{5,4},{6,7},{7,6},{8,9},{9,8},{10,11... | collective-permute-start | bytes 884744 | tf_op jit(solution)/shard_map/ppermute | solution.py:375
  112.6 2.2 collective-permute-start.16
  113.0 13.0 %collective-permute-start.15 = (bf16[288,768]{1,0:T(8,128)(2,1)S(1)}, bf16[288,768]{1,0:T(8,128)(2,1)S(1)}, u32[]{:S(2)}, u32[]{:S(2)}) collective-permute-start(bf16[288,768]{1,0:T(8,128)(2,1)S(1)} %copy-done.42), channel_id=1, source_target_pairs={{0,2},{2,0},{1,3},{3,1},{4,6},{6,4},{5,7},{7,5},{8,10},{10,8},{9,1... | collective-permute-start | bytes 1327112 | tf_op jit(solution)/shard_map/ppermute | solution.py:375
  114.5 11.5 %collective-permute-start.14 = (bf16[288,512]{1,0:T(8,128)(2,1)S(1)}, bf16[288,512]{1,0:T(8,128)(2,1)S(1)}, u32[]{:S(2)}, u32[]{:S(2)}) collective-permute-start(bf16[288,512]{1,0:T(8,128)(2,1)S(1)} %slice.74), channel_id=1, source_target_pairs={{0,1},{1,0},{2,3},{3,2},{4,5},{5,4},{6,7},{7,6},{8,9},{9,8},{10,11... | collective-permute-start | bytes 884744 | tf_op jit(solution)/shard_map/ppermute | solution.py:375
  118.9 12.5 %copy-start.39 = (bf16[288,768]{1,0:T(8,128)(2,1)S(1)}, bf16[288,768]{1,0:T(8,128)(2,1)}, u32[]{:S(2)}) copy-start(bf16[288,768]{1,0:T(8,128)(2,1)} %get-tuple-element.95.refs_3_) | copy-start | bytes 1327108
  118.9 13.1 %copy-start.22 = (bf16[288,768]{1,0:T(8,128)(2,1)S(1)}, bf16[288,768]{1,0:T(8,128)(2,1)}, u32[]{:S(2)}) copy-start(bf16[288,768]{1,0:T(8,128)(2,1)} %get-tuple-element.96.refs_4_) | copy-start | bytes 1327108
  118.9 14.6 %collective-permute-start.17 = (bf16[144,1024]{1,0:T(8,128)(2,1)}, bf16[144,1024]{1,0:T(8,128)(2,1)S(1)}, u32[]{:S(2)}, u32[]{:S(2)}) collective-permute-start(bf16[144,1024]{1,0:T(8,128)(2,1)} %get-tuple-element.92), channel_id=1, source_target_pairs={{0,2},{2,0},{1,3},{3,1},{4,6},{6,4},{5,7},{7,5},{8,10},{10,8},{9,1... | collective-permute-start | bytes 884744 | tf_op jit(solution)/shard_map/ppermute | solution.py:375
  129.8 13.0 %collective-permute-start.21 = (bf16[256,512]{1,0:T(8,128)(2,1)}, bf16[256,512]{1,0:T(8,128)(2,1)S(1)}, u32[]{:S(2)}, u32[]{:S(2)}) collective-permute-start(bf16[256,512]{1,0:T(8,128)(2,1)} %get-tuple-element.98), channel_id=1, source_target_pairs={{0,4},{4,0},{8,12},{12,8},{1,5},{5,1},{9,13},{13,9},{2,6},{6,2},{1... | collective-permute-start | bytes 786440 | tf_op jit(solution)/shard_map/ppermute | solution.py:457
  131.4 13.1 %collective-permute-start.19 = (bf16[288,768]{1,0:T(8,128)(2,1)S(1)}, bf16[288,768]{1,0:T(8,128)(2,1)S(1)}, u32[]{:S(2)}, u32[]{:S(2)}) collective-permute-start(bf16[288,768]{1,0:T(8,128)(2,1)S(1)} %copy-done.39), channel_id=1, source_target_pairs={{0,2},{2,0},{1,3},{3,1},{4,6},{6,4},{5,7},{7,5},{8,10},{10,8},{9,1... | collective-permute-start | bytes 1327112 | tf_op jit(solution)/shard_map/ppermute | solution.py:375
  132.0 22.0 %collective-permute-start.20 = (bf16[288,768]{1,0:T(8,128)(2,1)S(1)}, bf16[288,768]{1,0:T(8,128)(2,1)S(1)}, u32[]{:S(2)}, u32[]{:S(2)}) collective-permute-start(bf16[288,768]{1,0:T(8,128)(2,1)S(1)} %copy-done.22), channel_id=1, source_target_pairs={{0,2},{2,0},{1,3},{3,1},{4,6},{6,4},{5,7},{7,5},{8,10},{10,8},{9,1... | collective-permute-start | bytes 1327112 | tf_op jit(solution)/shard_map/ppermute | solution.py:375
  134.2 7.8 %copy-start.17 = (bf16[288,1024]{1,0:T(8,128)(2,1)S(1)}, bf16[288,1024]{1,0:T(8,128)(2,1)}, u32[]{:S(2)}) copy-start(bf16[288,1024]{1,0:T(8,128)(2,1)} %get-tuple-element.79) | copy-start | bytes 1769476
  134.2 9.3 %copy-start.29 = (f32[128,512]{1,0:T(8,128)S(1)}, f32[128,512]{1,0:T(8,128)}, u32[]{:S(2)}) copy-start(f32[128,512]{1,0:T(8,128)} %get-tuple-element.100) | copy-start | bytes 786436
  141.4 28.4 %collective-permute-start.23 = (bf16[288,1280]{1,0:T(8,128)(2,1)}, bf16[288,1280]{1,0:T(8,128)(2,1)S(1)}, u32[]{:S(2)}, u32[]{:S(2)}) collective-permute-start(bf16[288,1280]{1,0:T(8,128)(2,1)} %get-tuple-element.102), channel_id=1, source_target_pairs={{0,2},{2,0},{1,3},{3,1},{4,6},{6,4},{5,7},{7,5},{8,10},{10,8},{9,1... | collective-permute-start | bytes 2211848 | tf_op jit(solution)/shard_map/ppermute | solution.py:375
  141.9 33.6 %collective-permute-start.12 = (bf16[288,1024]{1,0:T(8,128)(2,1)S(1)}, bf16[288,1024]{1,0:T(8,128)(2,1)S(1)}, u32[]{:S(2)}, u32[]{:S(2)}) collective-permute-start(bf16[288,1024]{1,0:T(8,128)(2,1)S(1)} %copy-done.17), channel_id=1, source_target_pairs={{0,1},{1,0},{2,3},{3,2},{4,5},{5,4},{6,7},{7,6},{8,9},{9,8},{10,11... | collective-permute-start | bytes 1769480 | tf_op jit(solution)/shard_map/ppermute | solution.py:375
  142.9 11.1 %copy-start.15 = (bf16[256,512]{1,0:T(8,128)(2,1)}, bf16[256,512]{1,0:T(8,128)(2,1)S(1)}, u32[]{:S(2)}) copy-start(bf16[256,512]{1,0:T(8,128)(2,1)S(1)} %collective-permute-done.21.refs_8_) | copy-start | bytes 786436
  142.9 1.6 collective-permute-start.18
  144.5 9.5 %copy-start.40 = (bf16[288,768]{1,0:T(8,128)(2,1)}, bf16[288,768]{1,0:T(8,128)(2,1)S(1)}, u32[]{:S(2)}) copy-start(bf16[288,768]{1,0:T(8,128)(2,1)S(1)} %collective-permute-done.19.refs_5_) | copy-start | bytes 1327108
  144.5 9.5 %copy-start.44 = (bf16[288,256]{1,0:T(8,128)(2,1)}, bf16[288,256]{1,0:T(8,128)(2,1)S(1)}, u32[]{:S(2)}) copy-start(bf16[288,256]{1,0:T(8,128)(2,1)S(1)} %collective-permute-done.18.refs_2_) | copy-start | bytes 442372
  154.8 5.1 %copy-start.20 = (bf16[288,768]{1,0:T(8,128)(2,1)S(1)}, bf16[288,768]{1,0:T(8,128)(2,1)}, u32[]{:S(2)}) copy-start(bf16[288,768]{1,0:T(8,128)(2,1)} %get-tuple-element.113.refs_3_) | copy-start | bytes 1327108
  159.4 24.8 %collective-permute-start.24 = (bf16[256,1536]{1,0:T(8,128)(2,1)}, bf16[256,1536]{1,0:T(8,128)(2,1)S(1)}, u32[]{:S(2)}, u32[]{:S(2)}) collective-permute-start(bf16[256,1536]{1,0:T(8,128)(2,1)} %get-tuple-element.108), channel_id=1, source_target_pairs={{0,4},{4,0},{8,12},{12,8},{1,5},{5,1},{9,13},{13,9},{2,6},{6,2},{1... | collective-permute-start | bytes 2359304 | tf_op jit(solution)/shard_map/ppermute | solution.py:457
  159.9 18.6 %collective-permute-start.28 = (bf16[288,768]{1,0:T(8,128)(2,1)S(1)}, bf16[288,768]{1,0:T(8,128)(2,1)S(1)}, u32[]{:S(2)}, u32[]{:S(2)}) collective-permute-start(bf16[288,768]{1,0:T(8,128)(2,1)S(1)} %copy-done.20), channel_id=1, source_target_pairs={{0,2},{2,0},{1,3},{3,1},{4,6},{6,4},{5,7},{7,5},{8,10},{10,8},{9,1... | collective-permute-start | bytes 1327112 | tf_op jit(solution)/shard_map/ppermute | solution.py:375
  170.7 4.9 %copy-start.5 = (bf16[288,1024]{1,0:T(8,128)(2,1)S(1)}, bf16[288,1024]{1,0:T(8,128)(2,1)}, u32[]{:S(2)}) copy-start(bf16[288,1024]{1,0:T(8,128)(2,1)} %get-tuple-element.78.joined) | copy-start | bytes 1769476
  175.1 31.2 %collective-permute-start.26 = (bf16[256,1280]{1,0:T(8,128)(2,1)}, bf16[256,1280]{1,0:T(8,128)(2,1)S(1)}, u32[]{:S(2)}, u32[]{:S(2)}) collective-permute-start(bf16[256,1280]{1,0:T(8,128)(2,1)} %get-tuple-element.111), channel_id=1, source_target_pairs={{0,4},{4,0},{8,12},{12,8},{1,5},{5,1},{9,13},{13,9},{2,6},{6,2},{1... | collective-permute-start | bytes 1966088 | tf_op jit(solution)/shard_map/ppermute | solution.py:457
  175.8 8.4 %copy-start.11 = (f32[128,1536]{1,0:T(8,128)S(1)}, f32[128,1536]{1,0:T(8,128)}, u32[]{:S(2)}) copy-start(f32[128,1536]{1,0:T(8,128)} %get-tuple-element.109) | copy-start | bytes 2359300
  175.8 36.0 %collective-permute-start.22 = (bf16[128,512]{1,0:T(8,128)(2,1)S(1)}, bf16[128,512]{1,0:T(8,128)(2,1)S(1)}, u32[]{:S(2)}, u32[]{:S(2)}) collective-permute-start(bf16[128,512]{1,0:T(8,128)(2,1)S(1)} %add_convert_fusion.4), channel_id=1, source_target_pairs={{0,8},{4,12},{8,0},{12,4},{1,9},{5,13},{9,1},{13,5},{2,10},{6,14},... | collective-permute-start | bytes 393224 | tf_op jit(solution)/shard_map/ppermute | solution.py:459
  182.6 23.6 %copy-start.14 = (f32[128,1280]{1,0:T(8,128)S(1)}, f32[128,1280]{1,0:T(8,128)}, u32[]{:S(2)}) copy-start(f32[128,1280]{1,0:T(8,128)} %get-tuple-element.112) | copy-start | bytes 1966084
  182.6 28.1 %collective-permute-start.29 = (bf16[256,768]{1,0:T(8,128)(2,1)}, bf16[256,768]{1,0:T(8,128)(2,1)S(1)}, u32[]{:S(2)}, u32[]{:S(2)}) collective-permute-start(bf16[256,768]{1,0:T(8,128)(2,1)} %get-tuple-element.115), channel_id=1, source_target_pairs={{0,4},{4,0},{8,12},{12,8},{1,5},{5,1},{9,13},{13,9},{2,6},{6,2},{1... | collective-permute-start | bytes 1179656 | tf_op jit(solution)/shard_map/ppermute | solution.py:457
  184.2 22.1 %copy-start.8 = (bf16[256,1536]{1,0:T(8,128)(2,1)}, bf16[256,1536]{1,0:T(8,128)(2,1)S(1)}, u32[]{:S(2)}) copy-start(bf16[256,1536]{1,0:T(8,128)(2,1)S(1)} %collective-permute-done.24.refs_4_) | copy-start | bytes 2359300
  184.2 26.5 %copy-start.24 = (f32[128,768]{1,0:T(8,128)S(1)}, f32[128,768]{1,0:T(8,128)}, u32[]{:S(2)}) copy-start(f32[128,768]{1,0:T(8,128)} %get-tuple-element.116) | copy-start | bytes 1179652
  184.3 27.6 %collective-permute-start.25 = (bf16[128,1536]{1,0:T(8,128)(2,1)S(1)}, bf16[128,1536]{1,0:T(8,128)(2,1)S(1)}, u32[]{:S(2)}, u32[]{:S(2)}) collective-permute-start(bf16[128,1536]{1,0:T(8,128)(2,1)S(1)} %add_convert_fusion.1), channel_id=1, source_target_pairs={{0,8},{4,12},{8,0},{12,4},{1,9},{5,13},{9,1},{13,5},{2,10},{6,14},... | collective-permute-start | bytes 1179656 | tf_op jit(solution)/shard_map/ppermute | solution.py:459
  206.3 21.9 %collective-permute-start.27 = (bf16[128,1280]{1,0:T(8,128)(2,1)S(1)}, bf16[128,1280]{1,0:T(8,128)(2,1)S(1)}, u32[]{:S(2)}, u32[]{:S(2)}) collective-permute-start(bf16[128,1280]{1,0:T(8,128)(2,1)S(1)} %add_convert_fusion.2), channel_id=1, source_target_pairs={{0,8},{4,12},{8,0},{12,4},{1,9},{5,13},{9,1},{13,5},{2,10},{6,14},... | collective-permute-start | bytes 983048 | tf_op jit(solution)/shard_map/ppermute | solution.py:459
  210.8 17.4 %collective-permute-start.30 = (bf16[128,768]{1,0:T(8,128)(2,1)S(1)}, bf16[128,768]{1,0:T(8,128)(2,1)S(1)}, u32[]{:S(2)}, u32[]{:S(2)}) collective-permute-start(bf16[128,768]{1,0:T(8,128)(2,1)S(1)} %add_convert_fusion.3), channel_id=1, source_target_pairs={{0,8},{4,12},{8,0},{12,4},{1,9},{5,13},{9,1},{13,5},{2,10},{6,14},... | collective-permute-start | bytes 589832 | tf_op jit(solution)/shard_map/ppermute | solution.py:459
  (28 other events, 38.1 us)

commit v4 on v3

--- a/solution.py
+++ b/solution.py
@@ -48,8 +48,8 @@
 
 
 class Weights:
-    def __init__(self, arrays, table, offsets):
-        self.arrays, self.table, self.offsets = list(arrays), table, offsets
+    def __init__(self, arrays, table):
+        self.arrays, self.table = list(arrays), table
 
     def only(self, kinds):
         used = sorted({entry[0] for kind in kinds for entry in self.table[kind]})
@@ -57,14 +57,27 @@
             kind: [(used.index(array), at, place) for array, at, place in self.table[kind]]
             for kind in kinds
         }
-        return Weights([self.arrays[number] for number in used], table, self.offsets)
-
-
-def views(table, refs, offsets, kind):
+        return Weights([self.arrays[number] for number in used], table)
+
+
+def first_row(number, rows, where):
+    if number == 0:
+        return where[0] * rows
+    side, even = where[3], lax.rem(where[2], 2)
+    side = side if number in (1, 3) else 1 - side
+    even = even if number in (1, 2) else 1 - even
+    return (1 - where[0]) * rows + (side * 2 + even) * (rows // 4)
+
+
+def views(plan, refs, where, kind):
     found = []
-    for array, at, place in table[kind]:
+    for array, at, place in plan.table[kind]:
         part = refs[array].at[at]
-        found.append((part, pl.ds(pl.multiple_of(offsets[place], 128), part.shape[0])))
+        if plan.paired:
+            first = pl.multiple_of(first_row(place, refs[plan.table[kind][0][0]].shape[1], where), 128)
+            found.append((part, pl.ds(first, part.shape[0])))
+        else:
+            found.append((part, slice(None)))
     return found
 
 
@@ -94,12 +107,29 @@
         out[:, at + number * block : at + (number + 1) * block] = rows_ref[:, pl.ds(first, block)]
 
 
-def attention(triple_ref, bias_ref, attend_ref, mixed_ref, blocks):
+def groups_of(size, spans, modulus, axis):
+    shape = (size, 1) if axis == 0 else (1, size)
+    return lax.rem(lax.broadcasted_iota(jnp.int32, shape, axis) // spans, modulus)
+
+
+def spatial_bias(plan, size):
+    query, key = (groups_of(size, *plan.date_of, axis) for axis in range(2))
+    return jnp.where(query == key, 0.0, CROSS).astype(F32)
+
+
+def temporal_bias(plan, size, survive):
+    query, key = (groups_of(size, *plan.patch_of, axis) for axis in range(2))
+    query_date, key_date = (groups_of(size, *plan.date_of, axis) for axis in range(2))
+    allowed = (survive[...] == 1.0) | (query_date == key_date)
+    return jnp.where(query == key, jnp.where(allowed, 0.0, -1000000000.0), CROSS).astype(F32)
+
+
+def attention(triple_ref, bias, attend_ref, mixed_ref, blocks):
     width = triple_ref.shape[1] // 3
     heads = Heads(width)
     rows = triple_ref.shape[0] // blocks
     groups = width // heads.lanes
-    bias = jnp.concatenate([bias_ref[...]] * heads.count, axis=0)
+    bias = jnp.concatenate([bias] * heads.count, axis=0)
     for block in range(blocks):
         at = slice(block * rows, (block + 1) * rows)
         for group in range(groups):
@@ -148,7 +178,7 @@
         hidden_ref[at, :] = (normed * gain_ref[...]).astype(BF)
 
 
-def spatial_forward_kernel(plan, where, offsets, gain, bias, cotangent, *refs):
+def spatial_forward_kernel(plan, where, gain, cotangent, *refs):
     sources, refs = refs[: plan.origins], refs[plan.origins :]
     arrays, refs = refs[: plan.arrays], refs[plan.arrays :]
     partials, refs = refs[: plan.origins], refs[plan.origins :]
@@ -159,9 +189,10 @@
     normalize_into(start, gain, hidden, plan.blocks)
     width = mixed.shape[1]
     for kind in range(3):
-        rows_times(hidden, views(plan.table, arrays, offsets, kind), triple, kind * width)
+        rows_times(hidden, views(plan, arrays, where, kind), triple, kind * width)
+    bias = spatial_bias(plan, start.shape[0] // plan.blocks)
     attention(triple, bias, attend, mixed, plan.blocks)
-    for part, features in views(plan.table, arrays, offsets, 3):
+    for part, features in views(plan, arrays, where, 3):
         whole[:, features] = dot(mixed[...], part[...], NT).astype(BF)
     for source, at, to, size in plan.moves:
         partials[source][at : at + size, :] = whole[to : to + size, :]
@@ -183,27 +214,33 @@
     out[...] = (start[...].astype(F32) + total).astype(BF)
 
 
-def temporal_kernel(plan, where, offsets, gain, bias, date_rows, cotangent, *refs):
+def temporal_kernel(plan, where, gain, survive, date_rows, cotangent, *refs):
     sources, refs = refs[: plan.sources], refs[plan.sources :]
     arrays, refs = refs[: plan.arrays], refs[plan.arrays :]
     grads, refs = refs[: plan.grads], refs[plan.grads :]
     joined, mixed, partial, back_part = refs[:4]
     back_triples, (hidden, triple, attend, back_mixed, back_triple) = refs[4:-5], refs[-5:]
-    rows = date_rows.shape[0]
+    rows = joined.shape[0] // plan.blocks
+    patches = rows // date_rows.shape[0]
     for source, at, to, size in plan.moves:
         if source == 0 and plan.sources > 1:
             total = sources[1][at : at + size, :].astype(F32) + sources[2][at : at + size, :].astype(F32)
             out = (sources[0][at : at + size, :].astype(F32) + total).astype(BF)
         else:
             out = sources[-1][at : at + size, :]
-        dated = out.astype(F32) + date_rows[to % rows : to % rows + size, :].astype(F32)
-        joined[to : to + size, :] = dated.astype(BF)
+        out = out.astype(F32)
+        dated = [
+            out[at : at + patches] + date_rows[(to % rows + at) // patches : (to % rows + at) // patches + 1, :]
+            for at in range(0, size, patches)
+        ]
+        joined[to : to + size, :] = jnp.concatenate(dated, axis=0).astype(BF)
     normalize_into(joined, gain, hidden, plan.blocks)
     width = mixed.shape[1]
     for kind in range(3):
-        rows_times(hidden, views(plan.table, arrays, offsets, kind), triple, kind * width)
-    outlet = views(plan.table, arrays, offsets, 3)
+        rows_times(hidden, views(plan, arrays, where, kind), triple, kind * width)
+    outlet = views(plan, arrays, where, 3)
     rows_times(cotangent, outlet, back_mixed, 0)
+    bias = temporal_bias(plan, joined.shape[0] // plan.blocks, survive)
     attention(triple, bias, attend, mixed, plan.blocks)
     for part, features in outlet:
         partial[:, features] = dot(mixed[...], part[...], NT).astype(BF)
@@ -212,11 +249,10 @@
         half = hidden.shape[1] // 4
         emit_own(hidden, own_hidden, 0, where[0], plan.locs)
         emit_half(hidden, sent, 0, 1 - where[0], where[1], plan.locs)
-        sent[:, half:] = mixed[...]
     else:
         grads[0][...] = hidden[...]
     attention_back(triple, attend, back_mixed, back_triple, plan.blocks)
-    intakes = [views(plan.table, arrays, offsets, kind) for kind in range(3)]
+    intakes = [views(plan, arrays, where, kind) for kind in range(3)]
     for entries in zip(*intakes):
         total = None
         for kind, (part, features) in enumerate(entries):
@@ -224,6 +260,8 @@
             total = term if total is None else total + term
         back_part[:, features] = total.astype(BF)
     split_columns(back_triple, back_triples)
+    if plan.paired:
+        sent[:, half:] = back_triple[:, : sent.shape[1] - half]
 
 
 def split_columns(whole, outs):
@@ -233,7 +271,7 @@
         at += out.shape[1]
 
 
-def norm_back_kernel(moves, step, gain, here, there, joined, cotangent, kept, *outs):
+def norm_back_kernel(moves, step, gain, here, there, joined, cotangent, *outs):
     for at in range(0, joined.shape[0], step):
         span_here = slice(at, at + step)
         normed, inv_scale = statistics(joined[span_here, :])
@@ -250,7 +288,7 @@
                 outs[target][to : to + size, :] = back[first - at : first - at + size]
 
 
-def spatial_backward_kernel(plan, where, offsets, triple, attend, kept, *refs):
+def spatial_backward_kernel(plan, where, triple, attend, kept, *refs):
     sources, refs = refs[: plan.origins], refs[plan.origins :]
     arrays, refs = refs[: plan.arrays], refs[plan.arrays :]
     grads, refs = refs[: plan.grads], refs[plan.grads :]
@@ -262,7 +300,7 @@
         emit_own(upstream, grads[1], 0, 1 - where[0], plan.locs)
     else:
         grads[0][...] = upstream[...]
-    rows_times(upstream, views(plan.table, arrays, offsets, 3), back_mixed, 0)
+    rows_times(upstream, views(plan, arrays, where, 3), back_mixed, 0)
     attention_back(triple, attend, back_mixed, back_triple, plan.blocks)
     split_columns(back_triple, back_triples)
     if plan.paired:
@@ -327,8 +365,46 @@
     grad_kernel(products, count, where, *args, *rest[:3], rest[-1])
 
 
+def rows_kernel(cloud, drop, keep, where, optical, radar, table, date_table, cotangent, *refs):
+    own, other, upstream, dates_out, wide_table, places = refs
+    here = where[0]
+    dates, patches, _ = optical.shape
+    pairs, half = dates // 2, patches // 2
+    wide_table[...] = table[...].astype(F32)
+    for patch in range(patches):
+        places[patch : patch + 1, :] = wide_table[pl.ds(keep[0, patch], 1), :]
+    for pair in range(pairs):
+        found = []
+        for number in range(2):
+            date = pair * 2 + number
+            at = here * dates + date
+            seen = (1 - cloud[0, at]).astype(F32)
+            kept = (1 - drop[0, at]).astype(F32)
+            found.append(optical[date].astype(F32) * seen + radar[date].astype(F32) * kept + places[...])
+        halves = [(rows[:half], rows[half:]) for rows in found]
+        for out, swapped in ((own, 0), (other, 1)):
+            picked = [jnp.where(here == swapped, first, second) for first, second in halves]
+            for eight in range(0, half, 8):
+                rows = jnp.concatenate([rows[eight : eight + 8] for rows in picked], axis=0)
+                at = pair * half * 2 + eight * 2
+                out[at : at + 16, :] = rows.astype(BF)
+    block = 4 * pairs * 8
+    for side in range(2):
+        owner = here if side == 0 else 1 - here
+        for pair in range(pairs):
+            found = [cotangent[owner * dates + pair * 2 + number].astype(F32) for number in range(2)]
+            for eight in range(half // 8):
+                rows = jnp.concatenate([rows[eight * 8 : eight * 8 + 8] for rows in found], axis=0)
+                at = eight * block + side * pairs * 16 + pair * 16
+                upstream[at : at + 16, :] = rows.astype(BF)
+    whole = date_table[...].astype(F32)
+    flipped = jnp.concatenate([whole[dates:], whole[:dates]], axis=0)
+    dates_out[...] = jnp.where(here == 0, whole, flipped)
+
+
 class Plan:
-    def __init__(self, blocks, moves, origins, weights, paired, locs, grads, sources=0):
+    def __init__(self, blocks, moves, origins, weights, paired, locs, grads, sources=0, date_of=None, patch_of=None):
+        self.date_of, self.patch_of = date_of, patch_of
         self.blocks, self.moves, self.origins = blocks, moves, origins
         self.arrays, self.table = len(weights.arrays), weights.table
         self.paired, self.locs, self.grads, self.sources = paired, locs, grads, sources
@@ -390,34 +466,18 @@
 
 def whole_weights(weights):
     whole = lax.all_gather(weights.transpose(1, 0, 2), "date", axis=1, tiled=True)
-    return Weights([whole], {kind: [(0, kind, 0)] for kind in range(4)}, jnp.zeros((1,), jnp.int32))
-
-
-def quarters(rows):
-    side, here = lax.axis_index("groups"), lax.axis_index("date")
-    even = lax.axis_index("loc") % 2
-    numbers = [side * 2 + even, (1 - side) * 2 + even, side * 2 + 1 - even, (1 - side) * 2 + 1 - even]
-    offsets = [here * rows] + [(1 - here) * rows + number * (rows // 4) for number in numbers]
-    return numbers, jnp.stack(offsets).astype(jnp.int32)
-
-
-def weights_of(arrays, offsets):
+    return Weights([whole], {kind: [(0, kind, 0)] for kind in range(4)})
+
+
+def quarters():
+    side, even = lax.axis_index("groups"), lax.axis_index("loc") % 2
+    return side * 2 + even, (1 - side) * 2 + 1 - even
+
+
+def gather_weights(weights, first, last):
+    arrays = [weights, first, swap(first, "groups"), lax.ppermute(first, "loc", PAIRS), swap(last, "date")]
     table = {kind: [(number, kind, number) for number in range(5)] for kind in range(4)}
-    return Weights([by_kind(array) for array in arrays], table, offsets)
-
-
-def gather_first(weights, last, numbers, offsets):
-    first = swap(quarter_of(weights, numbers[0]), "date")
-    last = swap(last, "date")
-    arrays = [weights, first, swap(first, "groups"), lax.ppermute(first, "loc", PAIRS), last]
-    return weights_of(arrays, offsets)
-
-
-def gather_second(weights, first, offsets):
-    group, loc = swap(first, "groups"), lax.ppermute(first, "loc", PAIRS)
-    middle = first.shape[0] // 2
-    far = (swap(loc[:middle], "groups"), lax.ppermute(group[middle:], "loc", PAIRS))
-    return weights_of([weights, first, group, loc, jnp.concatenate(far, axis=0)], offsets)
+    return Weights([by_kind(array) for array in arrays], table)
 
 
 def add_over_heads(partial, sizes):
@@ -490,8 +550,8 @@
     paired = sizes["groups"] == 2 and sizes["loc"] == 4 and sizes["date"] == 2 and sizes["mp"] == 2
     paired = paired and dates_here % 2 == 0 and patches_here % 8 == 0 and model % 1024 == 0
     if paired:
-        numbers, offsets = quarters(spatial_weights.shape[0])
-        last_sent = quarter_of(spatial_weights, numbers[3])
+        first_quarter, last_quarter = quarters()
+        first_sent = quarter_of(spatial_weights, first_quarter)
     else:
         spatial, temporal = whole_weights(spatial_weights), whole_weights(temporal_weights)
 
@@ -500,27 +560,14 @@
         spatial_blocks, temporal_blocks = pairs, eights
         half_rows = eights * 16
 
-        def own_first(array, axis):
-            return jnp.where(here == 0, array, jnp.flip(array, axis))
-
-        def spatial_rows(array):
-            array = array.reshape(pairs, 2, 2, eights, 8, -1)
-            return own_first(array, 2).transpose(0, 2, 3, 1, 4, 5).reshape(rows, -1)
-
-        def temporal_rows(array):
-            array = array.reshape(2, pairs, 2, eights, 8, -1)
-            return own_first(array, 0).transpose(3, 0, 1, 2, 4, 5).reshape(rows, -1)
-
         def temporal_whole(array):
             array = array.reshape(eights, 2, pairs, 2, 8, -1).transpose(1, 2, 3, 0, 4, 5)
-            return own_first(array, 0).reshape(dates, patches_here, -1)
-
+            return jnp.where(here == 0, array, jnp.flip(array, 0)).reshape(dates, patches_here, -1)
+
+        spatial_date, temporal_date, temporal_patch = (8, 2), (8, rows), (1, 8)
     else:
         spatial_blocks = 1 if rows <= 192 else dates_here
         temporal_blocks = patches_here // 8 if patches_here % 8 == 0 else 1
-
-        def spatial_rows(array):
-            return array.reshape(rows, -1)
 
         def temporal_rows(array):
             array = array.reshape(dates, temporal_blocks, patches_here // temporal_blocks, -1)
@@ -530,38 +577,30 @@
             array = array.reshape(temporal_blocks, dates, patches_here // temporal_blocks, -1)
             return array.transpose(1, 0, 2, 3).reshape(dates, patches_here, -1)
 
-    cloud_here = lax.dynamic_slice_in_dim(cloud, first, dates_here, 1)[0]
-    drop_here = lax.dynamic_slice_in_dim(radar_drop, first, dates_here, 1)[0]
-    optical_keep = (1 - cloud_here).astype(F32)[:, None, None]
-    radar_keep = (1 - drop_here).astype(F32)[:, None, None]
-    places = jnp.take(place_table, keep_index[0], axis=0).astype(F32)[None]
-    start = (
-        optical[0].transpose(1, 0, 2).astype(F32) * optical_keep
-        + radar[0].transpose(1, 0, 2).astype(F32) * radar_keep
-        + places
-    ).astype(BF)
-    start = spatial_rows(start)
-
-    dates_at = jnp.arange(dates, dtype=jnp.int32)
-    patches_at = jnp.arange(patches_here, dtype=jnp.int32)
-    ones_here = jnp.ones((dates, patches_here, 1), jnp.int32)
-    temporal_size = rows // temporal_blocks
-    date_at = temporal_rows(ones_here * dates_at[:, None, None])[:temporal_size, 0]
-    patch_at = temporal_rows(ones_here * patches_at[None, :, None])[:temporal_size, 0]
-    spatial_size = rows // spatial_blocks
-    spatial_date = jnp.ones((dates_here, patches, 1), jnp.int32) * dates_at[:dates_here, None, None]
-    spatial_date = spatial_rows(spatial_date)[:spatial_size, 0]
-    spatial_bias = jnp.where(spatial_date[:, None] == spatial_date[None, :], 0.0, CROSS).astype(F32)
-    survive = 1 - cloud[0] * radar_drop[0]
-    same_date = date_at[:, None] == date_at[None, :]
-    survive_at = temporal_rows(ones_here * survive[:, None, None])[:temporal_size, 0]
-    allowed = (survive_at[None, :] == 1) | same_date
-    temporal_bias = jnp.where(
-        patch_at[:, None] == patch_at[None, :], jnp.where(allowed, 0.0, -1000000000.0), CROSS
-    ).astype(F32)
-    date_rows = jnp.broadcast_to(date_table[:, None], (dates, patches_here, model))
-    date_rows = temporal_rows(date_rows)[:temporal_size]
-    cotangent_rows = temporal_rows(cotangent[0].transpose(1, 0, 2))
+        in_block = patches_here // temporal_blocks
+        spatial_date, temporal_date, temporal_patch = (patches, rows), (in_block, rows), (1, in_block)
+    spatial_size, temporal_size = rows // spatial_blocks, rows // temporal_blocks
+
+    survive = (1 - cloud[0] * radar_drop[0]).astype(F32)
+    side = lax.axis_index("groups") if paired else here
+    where = jnp.stack([here, lax.axis_index("mp"), lax.axis_index("loc"), side]).astype(jnp.int32)
+    optical_rows, radar_rows = optical[0].transpose(1, 0, 2), radar[0].transpose(1, 0, 2)
+    cotangent_rows = cotangent[0].transpose(1, 0, 2)
+    if paired:
+        survive = jnp.where(here == 0, survive, jnp.roll(survive, dates_here))
+    else:
+        cloud_here = lax.dynamic_slice_in_dim(cloud, first, dates_here, 1)[0]
+        drop_here = lax.dynamic_slice_in_dim(radar_drop, first, dates_here, 1)[0]
+        places = jnp.take(place_table, keep_index[0], axis=0).astype(F32)[None]
+        start = (
+            optical_rows.astype(F32) * (1 - cloud_here).astype(F32)[:, None, None]
+            + radar_rows.astype(F32) * (1 - drop_here).astype(F32)[:, None, None]
+            + places
+        ).astype(BF)
+        start = start.reshape(rows, model)
+        cotangent_rows = temporal_rows(cotangent_rows)
+        date_rows = date_table.astype(F32)
+    survive = jnp.repeat(survive, temporal_size // dates)[None]
 
     spatial_gain = spatial_gain[None]
     temporal_gain = temporal_gain[None]
@@ -574,11 +613,36 @@
         return (blocks * (width // lanes), lanes // HEAD_DIM * (rows // blocks), rows // blocks)
 
     layer_flops = 2 * rows * model * width * 4
-    where = jnp.stack([here, lax.axis_index("mp"), lax.axis_index("loc")]).astype(jnp.int32)
     if paired:
         half = rows // 2
-        blocked = start.reshape(pairs, 2, half_rows, model)
-        origins = (blocked[:, 0].reshape(half, model), blocked[:, 1].reshape(half, model))
+        own_start, other_start, cotangent_rows, date_rows = call(
+            rows_kernel,
+            (
+                shape(half, model),
+                shape(half, model),
+                shape(rows, model),
+                shape(dates, model, dtype=F32),
+            ),
+            (
+                cloud,
+                radar_drop,
+                keep_index,
+                where,
+                optical_rows,
+                radar_rows,
+                place_table,
+                date_table,
+                cotangent_rows,
+            ),
+            scratch=(pltpu.VMEM(place_table.shape, F32), pltpu.VMEM((patches, model), F32)),
+        )
+        last_sent = quarter_of(spatial_weights, last_quarter)
+        last_sent, own_start = fence(last_sent, own_start)
+        origins = (own_start, other_start)
+        spatial = gather_weights(spatial_weights, swap(first_sent, "date"), last_sent)
+        sent = [quarter_of(temporal_weights, number) for number in (first_quarter, last_quarter)]
+        *sent, cotangent_rows = fence(*sent, cotangent_rows)
+        temporal_first = swap(sent[0], "date")
         spatial_moves = [
             (side, pair * half_rows, (pair * 2 + side) * half_rows, half_rows)
             for side in range(2)
@@ -593,7 +657,7 @@
         half_shapes = (shape(half, model), shape(half, model))
         own, quarter = shape(rows, model // 2), model // 4
         forward_grads = (own, own, shape(rows, 2 * quarter + width))
-        temporal_grads = (own, shape(rows, quarter + width))
+        temporal_grads = (own, shape(rows, quarter + 3 * width // 2))
         back_shapes = (shape(rows, 3 * width // 2), shape(rows, 3 * width // 2))
         backward_grads = (own, shape(rows, model // 2 + 3 * width // 2))
     else:
@@ -603,19 +667,11 @@
         half_shapes = (shape(rows, model),)
         forward_grads = temporal_grads = backward_grads = (shape(rows, model),)
         back_shapes = (shape(rows, 3 * width),)
-    origins, spatial_bias, temporal_bias, date_rows, cotangent_rows = lax.optimization_barrier(
-        (origins, spatial_bias, temporal_bias, date_rows, cotangent_rows)
-    )
-
-    if paired:
-        sent = quarter_of(temporal_weights, numbers[0])
-        last_sent, sent, far_origin = fence(last_sent, sent, origins[1])
-        origins = (origins[0], far_origin)
-        spatial = gather_first(spatial_weights, last_sent, numbers, offsets)
-        temporal_first = swap(sent, "date")
-
-    def plan_of(blocks, moves, weights, grads, sources=0):
-        return Plan(blocks, moves, len(origins), weights, paired, sizes["loc"], len(grads), sources)
+
+    def plan_of(blocks, moves, weights, grads, sources=0, date_of=spatial_date, patch_of=None):
+        return Plan(
+            blocks, moves, len(origins), weights, paired, sizes["loc"], len(grads), sources, date_of, patch_of
+        )
 
     plan = plan_of(spatial_blocks, spatial_moves, spatial, forward_grads)
     outs = call(
@@ -627,7 +683,7 @@
             shape(*attend_dims(spatial_blocks), dtype=F32),
             shape(rows, width),
         ),
-        (where, spatial.offsets, spatial_gain, spatial_bias, cotangent_rows, *origins, *spatial.arrays),
+        (where, spatial_gain, cotangent_rows, *origins, *spatial.arrays),
         scratch=(
             pltpu.VMEM((rows, model), BF),
             pltpu.VMEM((rows, model), BF),
@@ -640,7 +696,7 @@
     if paired:
         temporal_first, kept = fence(temporal_first, partials[1])
         partials = (partials[0], kept)
-        temporal = gather_second(temporal_weights, temporal_first, offsets)
+        temporal = gather_weights(temporal_weights, temporal_first, sent[1])
         there, early = call(
             between_kernel,
             (shape(half, model),),
@@ -660,7 +716,15 @@
             tiled=True,
         )
         sources = (temporal_rows(moved),)
-    plan = plan_of(temporal_blocks, temporal_moves, temporal, temporal_grads, len(sources))
+    plan = plan_of(
+        temporal_blocks,
+        temporal_moves,
+        temporal,
+        temporal_grads,
+        len(sources),
+        temporal_date,
+        temporal_patch,
+    )
     outs = call(
         functools.partial(temporal_kernel, plan),
         (
@@ -673,9 +737,8 @@
         ),
         (
             where,
-            temporal.offsets,
             temporal_gain,
-            temporal_bias,
+            survive,
             date_rows,
             cotangent_rows,
             *sources,
@@ -699,43 +762,45 @@
         others = swap(back_part, "mp")
     else:
         others = (lax.psum(back_part.astype(F32), "mp") - back_part.astype(F32)).astype(BF)
-    *backs, temporal_last = call(
+    backs = call(
         functools.partial(norm_back_kernel, temporal_moves, temporal_size),
         half_shapes,
-        (temporal_gain, back_part, others, joined, cotangent_rows, temporal_triples[-1]),
-        kept=(5,),
-    )
-    temporal_triples = (*temporal_triples[:-1], temporal_last)
+        (temporal_gain, back_part, others, joined, cotangent_rows),
+    )
     if paired:
-        back_origins = (backs[0], swap(backs[1], "date"))
+        mixed_sent, back_sent = fence(temporal_mixed, swap(backs[1], "date"))
         early_there = swap(early_other[:, : 2 * quarter], "mp")
         middle_other = swap(middle[1], "date")
-        sums = summed(
+        middle_there = swap(middle_other[:, :quarter], "mp")
+        last_half = swap(temporal_triples[1], "date")
+        part = temporal_triples[0].shape[1]
+        others = ((1, 0), (2, 0))
+        *intake, kept, back_sent = summed(
             where,
-            (forward[1], early_other, early_there, temporal_mixed, middle_other),
-            ((0, ((1, quarter), (2, quarter)), (3, 0), (4, quarter), width),),
+            (middle[0], middle_other, middle_there, *temporal_triples, last_half),
+            ((0, others, (3, 0), (1, quarter), part), (0, others, (4, 0), (5, 0), part)),
+            kept=(back_sent,),
         )
-        temporal_sums = [(sums[0], sums[1])]
-        kept = sums[2]
+        back_origins = (backs[0], back_sent)
     else:
         back = lax.all_to_all(
             temporal_whole(backs[0]), "date", split_axis=0, concat_axis=1, tiled=True
         )
         back_origins = (back.reshape(rows, model),)
-        kept = temporal_last
+        kept = temporal_triples[0]
     outlet = spatial.only((3,))
     plan = plan_of(spatial_blocks, spatial_moves, outlet, backward_grads)
     *outs, kept = call(
         functools.partial(spatial_backward_kernel, plan),
         (*backward_grads, *back_shapes),
-        (where, outlet.offsets, triple, attend, kept, *back_origins, *outlet.arrays),
+        (where, triple, attend, kept, *back_origins, *outlet.arrays),
         scratch=(
             pltpu.VMEM((rows, model), BF),
             pltpu.VMEM((rows, width), BF),
             pltpu.VMEM((rows, 3 * width), BF),
         ),
         flops=layer_flops,
-        kept=(4,),
+        kept=(3,),
     )
     backward, back_triples = outs[: len(backward_grads)], outs[len(backward_grads) :]
     encoded = (joined.astype(F32) + add_over_heads(temporal_partial, sizes)).astype(BF)
@@ -746,19 +811,14 @@
             whole_grads(forward[0], back_triples[0], backward[0], mixed),
             whole_grads(middle[0], kept, cotangent_rows, temporal_mixed),
         )
-    temporal_terms = [*summed_over_loc((*temporal_sums[0], kept))]
-    middle_there = swap(middle_other[:, :quarter], "mp")
-    others = [swap(array, "date") for array in temporal_triples]
-    *sums, upstream_own, temporal_terms[1] = summed(
+    intake = summed_over_loc((*intake, kept))
+    *outlet, upstream_own = summed(
         where,
-        (middle[0], middle_other, middle_there, *temporal_triples, *others),
-        tuple(
-            (0, ((1, 0), (2, 0)), (3 + number, 0), (5 + number, 0), temporal_triples[number].shape[1])
-            for number in range(2)
-        ),
-        kept=(backward[0], temporal_terms[1]),
-    )
-    temporal_terms += summed_over_loc(sums)
+        (forward[1], early_other, early_there, mixed_sent, swap(mixed_sent, "date")),
+        ((0, ((1, quarter), (2, quarter)), (3, 0), (4, 0), width),),
+        kept=(backward[0],),
+    )
+    temporal_terms = [*summed_over_loc(outlet), *intake]
     half = model // 2
     backward_other = swap(backward[1], "date")
     *sums, kept = summed(
@@ -776,9 +836,9 @@
             (0, ((1, 0),), (2, 0), (3, 2 * quarter), width),
             (4, ((3, 0), (5, 0)), (6, 0), (1, half), back_triples[0].shape[1]),
         ),
-        kept=(temporal_terms[3],),
-    )
-    temporal_terms[3] = kept
+        kept=(temporal_terms[4],),
+    )
+    temporal_terms[4] = kept
     spatial_terms = [*summed_over_loc(sums)]
     sums = summed(
         where,

time: 233 us -> 226 us (0.970)
  waiting for transfers between devices: 86 us -> 114 us
  local copies, waits for them, and re-layouts: 44.7 us -> 22.4 us
  other arithmetic: 17.9 us -> 1.3 us
  Pallas kernels: 54 us -> 56.9 us
    ppermute x20, waiting for transfers between devices: 37.6 us -> 58 us  [swap(): return lax.ppermute(array, axis, [(0, 1), (1, 0)])]
    ppermute x4, waiting for transfers between devices: 12.5 us -> 25.4 us  [summed_over_loc(): return (near, beside, lax.ppermute(far, 'loc', APART))]
    ppermute x3 -> x2, waiting for transfers between devices: 10 us -> 1.05 us  [gather_weights(): lax.ppermute(first, 'loc', PAIRS)]
    slice x7 -> x1, local copies, waits for them, and re-layouts: 5.88 us -> 0.07 us  [per_device(): survive = jnp.where(here == 0, survive, jnp.roll(survive, dates_here))]
    eq x4 -> x0, local copies, waits for them, and re-layouts: 5.33 us -> none  [the longest x1 1.37 us: per_device(): allowed = (survive_at[None, :] == 1) | same_date]
    mul x5 -> x0, local copies, waits for them, and re-layouts: 4.23 us -> none  [the longest x2 2.05 us: per_device(): jnp.ones((dates_here, patches, 1), jnp.int32)]
    select_n x5 -> x2, other arithmetic: 4.03 us -> 0.21 us  [the longest x1 0.13 us: temporal_whole(): jnp.where(here == 0, array, jnp.flip(array, 0))]
    ppermute x4, waiting for transfers between devices: 25.9 us -> 29.6 us  [summed_over_loc(): beside = lax.ppermute(sent, 'loc', PAIRS)]
  transfers between devices with their start and end apart: 31 -> 30, of which waited for: 13 -> 18; matrix products, arithmetic and copies ran while one was open for 21% -> 5% of each run, Pallas kernels for 22% -> 21%
where the time goes in v4:
time: 226 us; the launch traced here: 225 us
  waiting for transfers between devices  114 us (50%)
  Pallas kernels  56.9 us (25%)
  starting transfers between devices  29.4 us (13%)
  local copies, waits for them, and re-layouts  22.4 us (10%)
    ppermute x20, waiting for transfers between devices, swap(): return lax.ppermute(array, axis, [(0, 1), (1, 0)])  58 us
    pallas_call x12, Pallas kernels, call(): pl.pallas_call(body, out_shape=outs, in_specs=specs, out_specs=out_specs,...  56.9 us
    ppermute x4, waiting for transfers between devices, summed_over_loc(): beside = lax.ppermute(sent, 'loc', PAIRS)  29.6 us
    ppermute x4, waiting for transfers between devices, summed_over_loc(): return (near, beside, lax.ppermute(far, 'loc', APART))  25.4 us
    ppermute x20, starting transfers between devices, swap(): return lax.ppermute(array, axis, [(0, 1), (1, 0)])  18.7 us
    unnamed x84, local copies, waits for them, and re-layouts  14 us
    dynamic_slice x3, local copies, waits for them, and re-layouts, quarter_of(): return lax.dynamic_slice_in_dim(weights, number * (rows // 4), rows // 4, 0)  4.65 us
  transfers between devices with their start and end apart: 30, of which 18 were waited for; matrix products, arithmetic and copies ran while one was open for 5% of the time, Pallas kernels for 21%

profile of v4, /device:TPU:0, one launch (start us, length us, event | category | flops | bytes accessed | tf_op | source)
XLA Modules:
  0.0 225.1 jit_solution(10128718393574703361)
XLA Ops:
  0.6 2.0 copy.58
  2.7 3.0 %collective-permute-start = (bf16[128,4,512]{2,0,1:T(8,128)(2,1)S(1)}, bf16[128,4,512]{2,0,1:T(8,128)(2,1)S(1)}, u32[]{:S(2)}, u32[]{:S(2)}) collective-permute-start(bf16[128,4,512]{2,0,1:T(8,128)(2,1)S(1)} %constant_dynamic-slice_fusion), channel_id=1, source_target_pairs={{0,2},{2,0},{1,3},{3,1},{4,6},{6,4},{5,7},{7,5},{8,10},{10,8},{9,1... | collective-permute-start | bytes 1572872 | tf_op jit(solution)/shard_map/ppermute | solution.py:451
  6.3 3.1 %shard_map.139 = (bf16[144,1024]{1,0:T(8,128)(2,1)}, bf16[144,1024]{1,0:T(8,128)(2,1)}, bf16[288,1024]{1,0:T(8,128)(2,1)}, f32[12,1024]{1,0:T(8,128)}) custom-call(s32[1,12]{1,0:T(1,128)} %cloud.1, s32[1,12]{1,0:T(1,128)} %drop.1, s32[1,48]{1,0:T(1,128)} %keep.1, s32[4]{0:T(128)} %pad_add_fusion.where, bf16[6,48,1024]{2,1,0:T(8,128)(2,1)} %bitcast.55, ...), custom_call_target="tpu_custom_call" | custom-call | bytes 3424560 | tf_op jit(solution)/shard_map/pallas_call | solution.py:427
  9.4 2.0 constant_dynamic-slice_fusion.1.refs_0_
  11.4 1.1 copy.45
  12.8 5.6 %collective-permute-done = bf16[128,4,512]{2,0,1:T(8,128)(2,1)S(1)} collective-permute-done((bf16[128,4,512]{2,0,1:T(8,128)(2,1)S(1)}, bf16[128,4,512]{2,0,1:T(8,128)(2,1)S(1)}, u32[]{:S(2)}, u32[]{:S(2)}) %collective-permute-start) | collective-permute-done | bytes 524320 | tf_op jit(solution)/shard_map/ppermute | solution.py:451
  18.5 2.1 collective-permute-start.2
  20.6 1.5 collective-permute-start.1
  22.1 2.6 %constant_dynamic-slice_fusion.2 = (bf16[128,4,512]{2,1,0:T(4,128)(2,1)}, bf16[128,4,512]{2,1,0:T(4,128)(2,1)}) fusion(bf16[512,4,512]{2,1,0:T(4,128)(2,1)} %param.22, s32[]{:T(128)S(6)} %select_n.36, s32[]{:T(128)S(6)} %select_n.35), kind=kLoop, calls=%fused_computation.9 | loop fusion | bytes 2097160 | tf_op jit(solution)/shard_map/dynamic_slice | solution.py:460
  24.7 1.5 collective-permute-start.5
  26.2 3.5 %collective-permute-done.3 = bf16[128,4,512]{2,0,1:T(8,128)(2,1)S(1)} collective-permute-done((bf16[128,4,512]{2,0,1:T(8,128)(2,1)S(1)}, bf16[128,4,512]{2,0,1:T(8,128)(2,1)S(1)}, u32[]{:S(2)}, u32[]{:S(2)}) %collective-permute-start.3) | collective-permute-done | bytes 524320 | tf_op jit(solution)/shard_map/ppermute | solution.py:451
  30.8 1.2 collective-permute-done.1
  32.8 8.0 %shard_map.142 = (bf16[144,1024]{1,0:T(8,128)(2,1)}, bf16[144,1024]{1,0:T(8,128)(2,1)}, bf16[288,512]{1,0:T(8,128)(2,1)}, bf16[288,512]{1,0:T(8,128)(2,1)}, bf16...) custom-call(s32[4]{0:T(128)} %pad_add_fusion.where, ...), custom_call_target="tpu_custom_call" | custom-call | flops 1207959552 | bytes 9211920 | tf_op jit(solution)/shard_map/pallas_call | solution.py:427
  41.6 1.8 collective-permute-done.6.there
  44.1 2.1 shard_map.144
  46.2 1.5 collective-permute-start.7
  49.3 1.2 collective-permute-start.9
  50.5 1.5 collective-permute-start.8
  52.1 4.2 %collective-permute-done.7.refs_1_ = bf16[144,1024]{1,0:T(8,128)(2,1)S(1)} collective-permute-done((bf16[144,1024]{1,0:T(8,128)(2,1)}, bf16[144,1024]{1,0:T(8,128)(2,1)S(1)}, u32[]{:S(2)}, u32[]{:S(2)}) %collective-permute-start.7) | collective-permute-done | bytes 294944 | tf_op jit(solution)/shard_map/ppermute | solution.py:451
  57.0 1.5 collective-permute-start.12
  58.6 1.7 copy.57
  61.2 6.5 %collective-permute-done.10 = bf16[128,4,512]{2,0,1:T(8,128)(2,1)} collective-permute-done((bf16[128,4,512]{2,0,1:T(8,128)(2,1)}, bf16[128,4,512]{2,0,1:T(8,128)(2,1)}, u32[]{:S(2)}, u32[]{:S(2)}) %collective-permute-start.10) | collective-permute-done | bytes 524320 | tf_op jit(solution)/shard_map/ppermute | solution.py:451
  67.7 12.0 %shard_map.146 = (bf16[288,512]{1,0:T(8,128)(2,1)}, bf16[288,1024]{1,0:T(8,128)(2,1)}, bf16[288,1024]{1,0:T(8,128)(2,1)}, bf16[288,512]{1,0:T(8,128)(2,1)}, bf16...) custom-call(s32[4]{0:T(128)} %pad_add_fusion.where, ...), custom_call_target="tpu_custom_call" | custom-call | flops 2415919104 | bytes 9851280 | tf_op jit(solution)/shard_map/pallas_call | solution.py:427
  80.5 1.5 collective-permute-start.17
  83.5 3.4 %shard_map.148 = (bf16[144,1024]{1,0:T(8,128)(2,1)}, bf16[144,1024]{1,0:T(8,128)(2,1)}) custom-call(f32[1,1024]{1,0:T(1,128)} %bitcast.62, bf16[288,1024]{1,0:T(8,128)(2,1)} %get-tuple-element.86.here, bf16[288,1024]{1,0:T(8,128)(2,1)} %copy-done.23, bf16[288,1024]{1,0:T(8,128)(2,1)} %get-tuple-element.79.joined, bf16[288,1024]{1,0:T(8,128)(2,1)} %get-tuple-element.64.cotangent), custom_call_target="tpu_custom_call" | custom-call | bytes 2953216 | tf_op jit(solution)/shard_map/pallas_call | solution.py:427
  86.9 1.5 collective-permute-start.15
  88.4 8.5 %collective-permute-done.17.refs_1_ = bf16[288,1024]{1,0:T(8,128)(2,1)S(1)} collective-permute-done((bf16[288,1024]{1,0:T(8,128)(2,1)}, bf16[288,1024]{1,0:T(8,128)(2,1)S(1)}, u32[]{:S(2)}, u32[]{:S(2)}) %collective-permute-start.17) | collective-permute-done | bytes 589856 | tf_op jit(solution)/shard_map/ppermute | solution.py:451
  96.9 15.3 %collective-permute-done.15.refs_1_ = bf16[144,1024]{1,0:T(8,128)(2,1)S(1)} collective-permute-done((bf16[144,1024]{1,0:T(8,128)(2,1)}, bf16[144,1024]{1,0:T(8,128)(2,1)S(1)}, u32[]{:S(2)}, u32[]{:S(2)}) %collective-permute-start.15) | collective-permute-done | bytes 294944 | tf_op jit(solution)/shard_map/ppermute | solution.py:451
  113.8 4.5 %shard_map.150 = (bf16[256,1536]{1,0:T(8,128)(2,1)}, f32[128,1536]{1,0:T(8,128)}, f32[128,1536]{1,0:T(8,128)}, bf16[144,1024]{1,0:T(8,128)(2,1)}) custom-call(s32[4]{0:T(128)} %pad_add_fusion.where, bf16[288,512]{1,0:T(8,128)(2,1)} %get-tuple-element.91.refs_0_, bf16[288,1024]{1,0:T(8,128)(2,1)} %copy-done.35, ...), custom_call_target="tpu_custom_call", output_to_operand_aliasing={{3}: (7, {})} | custom-call | flops 905969664 | bytes 5013520 | tf_op jit(solution)/shard_map/pallas_call | solution.py:427
  118.4 1.2 collective-permute-start.23
  119.7 1.5 collective-permute-start.16
  121.2 7.2 %shard_map.151 = (bf16[288,512]{1,0:T(8,128)(2,1)}, bf16[288,1280]{1,0:T(8,128)(2,1)}, bf16[288,768]{1,0:T(8,128)(2,1)}, bf16[288,768]{1,0:T(8,128)(2,1)}, f32[128,1536]{1,0:T(8,128)}) custom-call(s32[4]{0:T(128)} %pad_add_fusion.where, bf16[288,1536]{1,0:T(8,128)(2,1)} %get-tuple-element.89.triple, ...), custom_call_target="tpu_custom_call", output_to_operand_aliasing={{4}: (3, {})} | custom-call | flops 1207959552 | bytes 9256976 | tf_op jit(solution)/shard_map/pallas_call | solution.py:427
  129.0 1.6 collective-permute-start.27
  131.2 2.9 %shard_map.152 = (bf16[256,512]{1,0:T(8,128)(2,1)}, f32[128,512]{1,0:T(8,128)}, f32[128,512]{1,0:T(8,128)}, bf16[288,512]{1,0:T(8,128)(2,1)}) custom-call(s32[4]{0:T(128)} %pad_add_fusion.where, bf16[288,512]{1,0:T(8,128)(2,1)} %get-tuple-element.81.refs_0_, bf16[288,1024]{1,0:T(8,128)(2,1)} %get-tuple-element.84.refs_1_.refs_3_, ...), custom_call_target="tpu_custom_call", output_to_operand_aliasing={{3}: (6, {})} | custom-call | flops 301989888 | bytes 2850832 | tf_op jit(solution)/shard_map/pallas_call | solution.py:427
  134.2 3.6 %collective-permute-done.23.refs_7_ = bf16[256,1536]{1,0:T(8,128)(2,1)S(1)} collective-permute-done((bf16[256,1536]{1,0:T(8,128)(2,1)}, bf16[256,1536]{1,0:T(8,128)(2,1)S(1)}, u32[]{:S(2)}, u32[]{:S(2)}) %collective-permute-start.23) | collective-permute-done | bytes 786464 | tf_op jit(solution)/shard_map/ppermute | solution.py:517
  137.9 10.1 %collective-permute-done.22.refs_1_ = bf16[288,1280]{1,0:T(8,128)(2,1)S(1)} collective-permute-done((bf16[288,1280]{1,0:T(8,128)(2,1)}, bf16[288,1280]{1,0:T(8,128)(2,1)S(1)}, u32[]{:S(2)}, u32[]{:S(2)}) %collective-permute-start.22) | collective-permute-done | bytes 737312 | tf_op jit(solution)/shard_map/ppermute | solution.py:451
  148.8 4.3 %shard_map.153 = (bf16[256,1280]{1,0:T(8,128)(2,1)}, f32[128,1280]{1,0:T(8,128)}, f32[128,1280]{1,0:T(8,128)}, bf16[256,1536]{1,0:T(8,128)(2,1)}) custom-call(s32[4]{0:T(128)} %pad_add_fusion.where, bf16[288,512]{1,0:T(8,128)(2,1)} %get-tuple-element.104.refs_0_, bf16[288,1280]{1,0:T(8,128)(2,1)} %copy-done.19, ...), custom_call_target="tpu_custom_call", output_to_operand_aliasing={{3}: (8, {})} | custom-call | flops 754974720 | bytes 5701648 | tf_op jit(solution)/shard_map/pallas_call | solution.py:427
  154.0 1.2 collective-permute-start.20
  155.5 1.2 collective-permute-done.27.refs_4_
  157.4 3.4 %shard_map.155 = (bf16[256,768]{1,0:T(8,128)(2,1)}, f32[128,768]{1,0:T(8,128)}, f32[128,768]{1,0:T(8,128)}) custom-call(s32[4]{0:T(128)} %pad_add_fusion.where, bf16[288,512]{1,0:T(8,128)(2,1)} %get-tuple-element.107.refs_4_.refs_0_, bf16[288,1024]{1,0:T(8,128)(2,1)} %get-tuple-element.84.refs_1_.refs_3_, bf16[288,512]{1,0:T(8,128)(2,1)} %copy-done.6, ...), custom_call_target="tpu_custom_call" | custom-call | flops 452984832 | bytes 3244048 | tf_op jit(solution)/shard_map/pallas_call | solution.py:427
  161.6 21.1 %collective-permute-done.20.refs_1_ = bf16[256,512]{1,0:T(8,128)(2,1)S(1)} collective-permute-done((bf16[256,512]{1,0:T(8,128)(2,1)S(1)}, bf16[256,512]{1,0:T(8,128)(2,1)S(1)}, u32[]{:S(2)}, u32[]{:S(2)}) %collective-permute-start.20) | collective-permute-done | bytes 262176 | tf_op jit(solution)/shard_map/ppermute | solution.py:517
  183.0 2.8 %collective-permute-start.24 = (bf16[128,1536]{1,0:T(8,128)(2,1)S(1)}, bf16[128,1536]{1,0:T(8,128)(2,1)S(1)}, u32[]{:S(2)}, u32[]{:S(2)}) collective-permute-start(bf16[128,1536]{1,0:T(8,128)(2,1)S(1)} %add_convert_fusion.1), channel_id=1, source_target_pairs={{0,8},{4,12},{8,0},{12,4},{1,9},{5,13},{9,1},{13,5},{2,10},{6,14},... | collective-permute-start | bytes 1179656 | tf_op jit(solution)/shard_map/ppermute | solution.py:519
  186.0 4.9 %collective-permute-done.28.refs_4_ = bf16[256,768]{1,0:T(8,128)(2,1)S(1)} collective-permute-done((bf16[256,768]{1,0:T(8,128)(2,1)}, bf16[256,768]{1,0:T(8,128)(2,1)S(1)}, u32[]{:S(2)}, u32[]{:S(2)}) %collective-permute-start.28) | collective-permute-done | bytes 393248 | tf_op jit(solution)/shard_map/ppermute | solution.py:517
  192.1 17.9 %collective-permute-done.21.refs_2_ = bf16[128,512]{1,0:T(8,128)(2,1)S(1)} collective-permute-done((bf16[128,512]{1,0:T(8,128)(2,1)S(1)}, bf16[128,512]{1,0:T(8,128)(2,1)S(1)}, u32[]{:S(2)}, u32[]{:S(2)}) %collective-permute-start.21) | collective-permute-done | bytes 131104 | tf_op jit(solution)/shard_map/ppermute | solution.py:519
  210.0 5.6 %collective-permute-done.24.refs_5_ = bf16[128,1536]{1,0:T(8,128)(2,1)S(1)} collective-permute-done((bf16[128,1536]{1,0:T(8,128)(2,1)S(1)}, bf16[128,1536]{1,0:T(8,128)(2,1)S(1)}, u32[]{:S(2)}, u32[]{:S(2)}) %collective-permute-start.24) | collective-permute-done | bytes 393248 | tf_op jit(solution)/shard_map/ppermute | solution.py:519
  216.4 3.0 %shard_map.154.kept = f32[128,4,512]{2,1,0:T(4,128)} custom-call(f32[128,512]{1,0:T(8,128)} %get-tuple-element.100.refs_0_, bf16[256,512]{1,0:T(8,128)(2,1)} %copy-done.21, bf16[128,512]{1,0:T(8,128)(2,1)} %copy-done.34, f32[128,1536]{1,0:T(8,128)} %get-tuple-element.103.refs_3_, bf16[256,1536]{1,0:T(8,128)(2,1)} %get-tuple-element.110.refs_4_, ...), custom_call_target="tpu_custom_call" | custom-call | bytes 3670016 | tf_op jit(solution)/shard_map/pallas_call | solution.py:427
  219.4 1.8 collective-permute-done.29.refs_5_
  222.0 3.0 %shard_map.156 = (f32[128,4,512]{2,1,0:T(4,128)}, f32[128,4,512]{2,1,0:T(4,128)}) custom-call(f32[128,4,512]{2,1,0:T(4,128)} %shard_map.154.kept, f32[128,1280]{1,0:T(8,128)} %get-tuple-element.112.refs_0_, bf16[256,1280]{1,0:T(8,128)(2,1)} %copy-done.14, bf16[128,1280]{1,0:T(8,128)(2,1)} %copy-done.28, ...), custom_call_target="tpu_custom_call", output_to_operand_aliasing={{1}: (0, {})} | custom-call | bytes 4718592 | tf_op jit(solution)/shard_map/pallas_call | solution.py:427
  (135 shorter events, 19.9 us)
Async XLA Ops:
  2.7 8.8 %copy-start = (bf16[512,4,512]{2,0,1:T(8,128)(2,1)}, bf16[512,4,512]{2,0,1:T(8,128)(2,1)S(1)}, u32[]{:S(2)}) copy-start(bf16[512,4,512]{2,0,1:T(8,128)(2,1)S(1)} %copy.58) | copy-start | bytes 6291460
  2.7 15.8 %collective-permute-start = (bf16[128,4,512]{2,0,1:T(8,128)(2,1)S(1)}, bf16[128,4,512]{2,0,1:T(8,128)(2,1)S(1)}, u32[]{:S(2)}, u32[]{:S(2)}) collective-permute-start(bf16[128,4,512]{2,0,1:T(8,128)(2,1)S(1)} %constant_dynamic-slice_fusion), channel_id=1, source_target_pairs={{0,2},{2,0},{1,3},{3,1},{4,6},{6,4},{5,7},{7,5},{8,10},{10,8},{9,1... | collective-permute-start | bytes 1572872 | tf_op jit(solution)/shard_map/ppermute | solution.py:451
  12.6 17.1 %collective-permute-start.3 = (bf16[128,4,512]{2,0,1:T(8,128)(2,1)S(1)}, bf16[128,4,512]{2,0,1:T(8,128)(2,1)S(1)}, u32[]{:S(2)}, u32[]{:S(2)}) collective-permute-start(bf16[128,4,512]{2,0,1:T(8,128)(2,1)S(1)} %copy.45), channel_id=1, source_target_pairs={{0,2},{2,0},{1,3},{3,1},{4,6},{6,4},{5,7},{7,5},{8,10},{10,8},{9,1... | collective-permute-start | bytes 1572872 | tf_op jit(solution)/shard_map/ppermute | solution.py:451
  18.5 13.5 %copy-start.10 = (bf16[128,4,512]{2,0,1:T(8,128)(2,1)}, bf16[128,4,512]{2,0,1:T(8,128)(2,1)S(1)}, u32[]{:S(2)}) copy-start(bf16[128,4,512]{2,0,1:T(8,128)(2,1)S(1)} %collective-permute-done) | copy-start | bytes 1572868
  18.5 12.3 %collective-permute-start.2 = (bf16[128,4,512]{2,0,1:T(8,128)(2,1)S(1)}, bf16[128,4,512]{2,0,1:T(8,128)(2,1)S(1)}, u32[]{:S(2)}, u32[]{:S(2)}) collective-permute-start(bf16[128,4,512]{2,0,1:T(8,128)(2,1)S(1)} %collective-permute-done), channel_id=1, source_target_pairs={{0,4},{4,0},{8,12},{12,8},{1,5},{5,1},{9,13},{13,9},{2,6},{6,2},{1... | collective-permute-start | bytes 1572872 | tf_op jit(solution)/shard_map/ppermute | solution.py:478
  20.6 11.4 %collective-permute-start.1 = (bf16[128,4,512]{2,0,1:T(8,128)(2,1)S(1)}, bf16[128,4,512]{2,0,1:T(8,128)(2,1)S(1)}, u32[]{:S(2)}, u32[]{:S(2)}) collective-permute-start(bf16[128,4,512]{2,0,1:T(8,128)(2,1)S(1)} %collective-permute-done), channel_id=1, source_target_pairs={{0,16},{16,0},{1,17},{17,1},{2,18},{18,2},{3,19},{19,3},{4,20},{20... | collective-permute-start | bytes 1572872 | tf_op jit(solution)/shard_map/ppermute | solution.py:451
  24.7 16.1 %collective-permute-start.5 = (bf16[128,4,512]{2,1,0:T(4,128)(2,1)}, bf16[128,4,512]{2,1,0:T(4,128)(2,1)S(1)}, u32[]{:S(2)}, u32[]{:S(2)}) collective-permute-start(bf16[128,4,512]{2,1,0:T(4,128)(2,1)} %get-tuple-element.70), channel_id=1, source_target_pairs={{0,2},{2,0},{1,3},{3,1},{4,6},{6,4},{5,7},{7,5},{8,10},{10,8},{9,1... | collective-permute-start | bytes 1572872 | tf_op jit(solution)/shard_map/ppermute | solution.py:451
  41.6 10.4 %copy-start.36 = (s32[1,12]{1,0:T(1,128)S(1)}, s32[1,12]{1,0:T(1,128)}, u32[]{:S(2)}) copy-start(s32[1,12]{1,0:T(1,128)} %cloud.1) | copy-start | bytes 148
  41.6 10.4 %copy-start.37 = (s32[1,12]{1,0:T(1,128)S(1)}, s32[1,12]{1,0:T(1,128)}, u32[]{:S(2)}) copy-start(s32[1,12]{1,0:T(1,128)} %drop.1) | copy-start | bytes 148
  41.6 1.8 collective-permute-start.6
  44.1 14.5 %copy-start.5 = (bf16[512,4,512]{2,1,0:T(4,128)(2,1)S(1)}, bf16[512,4,512]{2,1,0:T(4,128)(2,1)}, u32[]{:S(2)}) copy-start(bf16[512,4,512]{2,1,0:T(4,128)(2,1)} %param.22) | copy-start | bytes 6291460
  46.2 10.1 %collective-permute-start.7 = (bf16[144,1024]{1,0:T(8,128)(2,1)}, bf16[144,1024]{1,0:T(8,128)(2,1)S(1)}, u32[]{:S(2)}, u32[]{:S(2)}) collective-permute-start(bf16[144,1024]{1,0:T(8,128)(2,1)} %get-tuple-element.75), channel_id=1, source_target_pairs={{0,2},{2,0},{1,3},{3,1},{4,6},{6,4},{5,7},{7,5},{8,10},{10,8},{9,1... | collective-permute-start | bytes 884744 | tf_op jit(solution)/shard_map/ppermute | solution.py:451
  48.6 19.0 %collective-permute-start.10 = (bf16[128,4,512]{2,0,1:T(8,128)(2,1)}, bf16[128,4,512]{2,0,1:T(8,128)(2,1)}, u32[]{:S(2)}, u32[]{:S(2)}) collective-permute-start(bf16[128,4,512]{2,0,1:T(8,128)(2,1)} %copy.50), channel_id=1, source_target_pairs={{0,2},{2,0},{1,3},{3,1},{4,6},{6,4},{5,7},{7,5},{8,10},{10,8},{9,1... | collective-permute-start | bytes 1572872 | tf_op jit(solution)/shard_map/ppermute | solution.py:451
  49.3 11.1 %copy-start.24 = (bf16[128,4,512]{2,0,1:T(8,128)(2,1)}, bf16[128,4,512]{2,0,1:T(8,128)(2,1)S(1)}, u32[]{:S(2)}) copy-start(bf16[128,4,512]{2,0,1:T(8,128)(2,1)S(1)} %copy.59) | copy-start | bytes 1572868
  49.3 18.4 %collective-permute-start.9 = (bf16[128,4,512]{2,0,1:T(8,128)(2,1)S(1)}, bf16[128,4,512]{2,0,1:T(8,128)(2,1)}, u32[]{:S(2)}, u32[]{:S(2)}) collective-permute-start(bf16[128,4,512]{2,0,1:T(8,128)(2,1)S(1)} %copy.59), channel_id=1, source_target_pairs={{0,4},{4,0},{8,12},{12,8},{1,5},{5,1},{9,13},{13,9},{2,6},{6,2},{1... | collective-permute-start | bytes 1572872 | tf_op jit(solution)/shard_map/ppermute | solution.py:478
  50.5 17.2 %collective-permute-start.8 = (bf16[128,4,512]{2,0,1:T(8,128)(2,1)S(1)}, bf16[128,4,512]{2,0,1:T(8,128)(2,1)}, u32[]{:S(2)}, u32[]{:S(2)}) collective-permute-start(bf16[128,4,512]{2,0,1:T(8,128)(2,1)S(1)} %copy.59), channel_id=1, source_target_pairs={{0,16},{16,0},{1,17},{17,1},{2,18},{18,2},{3,19},{19,3},{4,20},{20... | collective-permute-start | bytes 1572872 | tf_op jit(solution)/shard_map/ppermute | solution.py:451
  52.0 15.6 %collective-permute-start.4 = (bf16[144,1024]{1,0:T(8,128)(2,1)}, bf16[144,1024]{1,0:T(8,128)(2,1)}, u32[]{:S(2)}, u32[]{:S(2)}) collective-permute-start(bf16[144,1024]{1,0:T(8,128)(2,1)} %get-tuple-element.69.refs_1_), channel_id=1, source_target_pairs={{0,1},{1,0},{2,3},{3,2},{4,5},{5,4},{6,7},{7,6},{8,9},{9,8},{10,11... | collective-permute-start | bytes 884744 | tf_op jit(solution)/shard_map/ppermute | solution.py:451
  57.0 22.6 %collective-permute-start.12 = (bf16[288,1024]{1,0:T(8,128)(2,1)}, bf16[288,1024]{1,0:T(8,128)(2,1)S(1)}, u32[]{:S(2)}, u32[]{:S(2)}) collective-permute-start(bf16[288,1024]{1,0:T(8,128)(2,1)} %get-tuple-element.83), channel_id=1, source_target_pairs={{0,2},{2,0},{1,3},{3,1},{4,6},{6,4},{5,7},{7,5},{8,10},{10,8},{9,1... | collective-permute-start | bytes 1769480 | tf_op jit(solution)/shard_map/ppermute | solution.py:451
  80.5 2.2 collective-permute-start.14
  80.5 16.3 %collective-permute-start.17 = (bf16[288,1024]{1,0:T(8,128)(2,1)}, bf16[288,1024]{1,0:T(8,128)(2,1)S(1)}, u32[]{:S(2)}, u32[]{:S(2)}) collective-permute-start(bf16[288,1024]{1,0:T(8,128)(2,1)} %get-tuple-element.92), channel_id=1, source_target_pairs={{0,2},{2,0},{1,3},{3,1},{4,6},{6,4},{5,7},{7,5},{8,10},{10,8},{9,1... | collective-permute-start | bytes 1769480 | tf_op jit(solution)/shard_map/ppermute | solution.py:451
  82.0 31.0 %collective-permute-start.19 = (bf16[288,768]{1,0:T(8,128)(2,1)}, bf16[288,768]{1,0:T(8,128)(2,1)S(1)}, u32[]{:S(2)}, u32[]{:S(2)}) collective-permute-start(bf16[288,768]{1,0:T(8,128)(2,1)} %get-tuple-element.94.refs_4_), channel_id=1, source_target_pairs={{0,2},{2,0},{1,3},{3,1},{4,6},{6,4},{5,7},{7,5},{8,10},{10,8},{9,1... | collective-permute-start | bytes 1327112 | tf_op jit(solution)/shard_map/ppermute | solution.py:451
  86.9 32.6 %copy-start.2 = (bf16[288,1024]{1,0:T(8,128)(2,1)S(1)}, bf16[288,1024]{1,0:T(8,128)(2,1)}, u32[]{:S(2)}) copy-start(bf16[288,1024]{1,0:T(8,128)(2,1)} %get-tuple-element.84.refs_1_.refs_3_) | copy-start | bytes 1769476
  86.9 25.3 %collective-permute-start.15 = (bf16[144,1024]{1,0:T(8,128)(2,1)}, bf16[144,1024]{1,0:T(8,128)(2,1)S(1)}, u32[]{:S(2)}, u32[]{:S(2)}) collective-permute-start(bf16[144,1024]{1,0:T(8,128)(2,1)} %get-tuple-element.87), channel_id=1, source_target_pairs={{0,2},{2,0},{1,3},{3,1},{4,6},{6,4},{5,7},{7,5},{8,10},{10,8},{9,1... | collective-permute-start | bytes 884744 | tf_op jit(solution)/shard_map/ppermute | solution.py:451
  96.8 16.2 %copy-start.35 = (bf16[288,1024]{1,0:T(8,128)(2,1)}, bf16[288,1024]{1,0:T(8,128)(2,1)S(1)}, u32[]{:S(2)}) copy-start(bf16[288,1024]{1,0:T(8,128)(2,1)S(1)} %collective-permute-done.17.refs_1_) | copy-start | bytes 1769476
  96.9 16.1 %collective-permute-start.18 = (bf16[288,256]{1,0:T(8,128)(2,1)S(1)}, bf16[288,256]{1,0:T(8,128)(2,1)S(1)}, u32[]{:S(2)}, u32[]{:S(2)}) collective-permute-start(bf16[288,256]{1,0:T(8,128)(2,1)S(1)} %slice.42), channel_id=1, source_target_pairs={{0,1},{1,0},{2,3},{3,2},{4,5},{5,4},{6,7},{7,6},{8,9},{9,8},{10,11... | collective-permute-start | bytes 442376 | tf_op jit(solution)/shard_map/ppermute | solution.py:451
  118.4 19.4 %collective-permute-start.23 = (bf16[256,1536]{1,0:T(8,128)(2,1)}, bf16[256,1536]{1,0:T(8,128)(2,1)S(1)}, u32[]{:S(2)}, u32[]{:S(2)}) collective-permute-start(bf16[256,1536]{1,0:T(8,128)(2,1)} %get-tuple-element.109), channel_id=1, source_target_pairs={{0,4},{4,0},{8,12},{12,8},{1,5},{5,1},{9,13},{13,9},{2,6},{6,2},{1... | collective-permute-start | bytes 2359304 | tf_op jit(solution)/shard_map/ppermute | solution.py:517
  119.6 9.4 %collective-permute-start.13 = (bf16[288,512]{1,0:T(8,128)(2,1)S(1)}, bf16[288,512]{1,0:T(8,128)(2,1)S(1)}, u32[]{:S(2)}, u32[]{:S(2)}) collective-permute-start(bf16[288,512]{1,0:T(8,128)(2,1)S(1)} %slice.36), channel_id=1, source_target_pairs={{0,1},{1,0},{2,3},{3,2},{4,5},{5,4},{6,7},{7,6},{8,9},{9,8},{10,11... | collective-permute-start | bytes 884744 | tf_op jit(solution)/shard_map/ppermute | solution.py:451
  119.7 10.9 %collective-permute-start.16 = (bf16[288,512]{1,0:T(8,128)(2,1)S(1)}, bf16[288,512]{1,0:T(8,128)(2,1)S(1)}, u32[]{:S(2)}, u32[]{:S(2)}) collective-permute-start(bf16[288,512]{1,0:T(8,128)(2,1)S(1)} %copy-done.15), channel_id=1, source_target_pairs={{0,2},{2,0},{1,3},{3,1},{4,6},{6,4},{5,7},{7,5},{8,10},{10,8},{9,1... | collective-permute-start | bytes 884744 | tf_op jit(solution)/shard_map/ppermute | solution.py:451
  121.2 7.7 %copy-start.22 = (bf16[288,1024]{1,0:T(8,128)(2,1)S(1)}, bf16[288,1024]{1,0:T(8,128)(2,1)}, u32[]{:S(2)}) copy-start(bf16[288,1024]{1,0:T(8,128)(2,1)} %get-tuple-element.80) | copy-start | bytes 1769476
  128.4 9.4 %copy-start.18 = (f32[128,1536]{1,0:T(8,128)S(1)}, f32[128,1536]{1,0:T(8,128)}, u32[]{:S(2)}) copy-start(f32[128,1536]{1,0:T(8,128)} %get-tuple-element.111) | copy-start | bytes 2359300
  128.4 19.5 %collective-permute-start.22 = (bf16[288,1280]{1,0:T(8,128)(2,1)}, bf16[288,1280]{1,0:T(8,128)(2,1)S(1)}, u32[]{:S(2)}, u32[]{:S(2)}) collective-permute-start(bf16[288,1280]{1,0:T(8,128)(2,1)} %get-tuple-element.105), channel_id=1, source_target_pairs={{0,2},{2,0},{1,3},{3,1},{4,6},{6,4},{5,7},{7,5},{8,10},{10,8},{9,1... | collective-permute-start | bytes 2211848 | tf_op jit(solution)/shard_map/ppermute | solution.py:451
  128.9 26.2 %collective-permute-start.11 = (bf16[288,1024]{1,0:T(8,128)(2,1)S(1)}, bf16[288,1024]{1,0:T(8,128)(2,1)S(1)}, u32[]{:S(2)}, u32[]{:S(2)}) collective-permute-start(bf16[288,1024]{1,0:T(8,128)(2,1)S(1)} %copy-done.22), channel_id=1, source_target_pairs={{0,1},{1,0},{2,3},{3,2},{4,5},{5,4},{6,7},{7,6},{8,9},{9,8},{10,11... | collective-permute-start | bytes 1769480 | tf_op jit(solution)/shard_map/ppermute | solution.py:451
  129.0 27.7 %collective-permute-start.27 = (bf16[288,768]{1,0:T(8,128)(2,1)}, bf16[288,768]{1,0:T(8,128)(2,1)S(1)}, u32[]{:S(2)}, u32[]{:S(2)}) collective-permute-start(bf16[288,768]{1,0:T(8,128)(2,1)} %get-tuple-element.115.refs_3_), channel_id=1, source_target_pairs={{0,2},{2,0},{1,3},{3,1},{4,6},{6,4},{5,7},{7,5},{8,10},{10,8},{9,1... | collective-permute-start | bytes 1327112 | tf_op jit(solution)/shard_map/ppermute | solution.py:451
  137.8 10.2 %copy-start.3 = (bf16[256,1536]{1,0:T(8,128)(2,1)}, bf16[256,1536]{1,0:T(8,128)(2,1)S(1)}, u32[]{:S(2)}) copy-start(bf16[256,1536]{1,0:T(8,128)(2,1)S(1)} %collective-permute-done.23.refs_7_) | copy-start | bytes 2359300
  137.8 16.2 %copy-start.39 = (bf16[256,512]{1,0:T(8,128)(2,1)S(1)}, bf16[256,512]{1,0:T(8,128)(2,1)}, u32[]{:S(2)}) copy-start(bf16[256,512]{1,0:T(8,128)(2,1)} %get-tuple-element.101) | copy-start | bytes 786436
  137.9 17.3 %copy-start.7 = (bf16[288,1024]{1,0:T(8,128)(2,1)S(1)}, bf16[288,1024]{1,0:T(8,128)(2,1)}, u32[]{:S(2)}) copy-start(bf16[288,1024]{1,0:T(8,128)(2,1)} %get-tuple-element.79.joined) | copy-start | bytes 1769476
  153.1 32.6 %collective-permute-start.25 = (bf16[256,1280]{1,0:T(8,128)(2,1)}, bf16[256,1280]{1,0:T(8,128)(2,1)S(1)}, u32[]{:S(2)}, u32[]{:S(2)}) collective-permute-start(bf16[256,1280]{1,0:T(8,128)(2,1)} %get-tuple-element.113), channel_id=1, source_target_pairs={{0,4},{4,0},{8,12},{12,8},{1,5},{5,1},{9,13},{13,9},{2,6},{6,2},{1... | collective-permute-start | bytes 1966088 | tf_op jit(solution)/shard_map/ppermute | solution.py:517
  154.0 28.8 %copy-start.32 = (f32[128,512]{1,0:T(8,128)S(1)}, f32[128,512]{1,0:T(8,128)}, u32[]{:S(2)}) copy-start(f32[128,512]{1,0:T(8,128)} %get-tuple-element.102) | copy-start | bytes 786436
  154.0 31.8 %copy-start.20 = (f32[128,1280]{1,0:T(8,128)S(1)}, f32[128,1280]{1,0:T(8,128)}, u32[]{:S(2)}) copy-start(f32[128,1280]{1,0:T(8,128)} %get-tuple-element.114) | copy-start | bytes 1966084
  154.0 28.7 %collective-permute-start.20 = (bf16[256,512]{1,0:T(8,128)(2,1)S(1)}, bf16[256,512]{1,0:T(8,128)(2,1)S(1)}, u32[]{:S(2)}, u32[]{:S(2)}) collective-permute-start(bf16[256,512]{1,0:T(8,128)(2,1)S(1)} %copy-done.39), channel_id=1, source_target_pairs={{0,4},{4,0},{8,12},{12,8},{1,5},{5,1},{9,13},{13,9},{2,6},{6,2},{1... | collective-permute-start | bytes 786440 | tf_op jit(solution)/shard_map/ppermute | solution.py:517
  160.8 30.2 %copy-start.27 = (f32[128,768]{1,0:T(8,128)S(1)}, f32[128,768]{1,0:T(8,128)}, u32[]{:S(2)}) copy-start(f32[128,768]{1,0:T(8,128)} %get-tuple-element.118) | copy-start | bytes 1179652
  160.8 30.2 %collective-permute-start.28 = (bf16[256,768]{1,0:T(8,128)(2,1)}, bf16[256,768]{1,0:T(8,128)(2,1)S(1)}, u32[]{:S(2)}, u32[]{:S(2)}) collective-permute-start(bf16[256,768]{1,0:T(8,128)(2,1)} %get-tuple-element.117), channel_id=1, source_target_pairs={{0,4},{4,0},{8,12},{12,8},{1,5},{5,1},{9,13},{13,9},{2,6},{6,2},{1... | collective-permute-start | bytes 1179656 | tf_op jit(solution)/shard_map/ppermute | solution.py:517
  182.7 9.3 %copy-start.21 = (bf16[256,512]{1,0:T(8,128)(2,1)}, bf16[256,512]{1,0:T(8,128)(2,1)S(1)}, u32[]{:S(2)}) copy-start(bf16[256,512]{1,0:T(8,128)(2,1)S(1)} %collective-permute-done.20.refs_1_) | copy-start | bytes 786436
  182.8 27.2 %collective-permute-start.21 = (bf16[128,512]{1,0:T(8,128)(2,1)S(1)}, bf16[128,512]{1,0:T(8,128)(2,1)S(1)}, u32[]{:S(2)}, u32[]{:S(2)}) collective-permute-start(bf16[128,512]{1,0:T(8,128)(2,1)S(1)} %add_convert_fusion.4), channel_id=1, source_target_pairs={{0,8},{4,12},{8,0},{12,4},{1,9},{5,13},{9,1},{13,5},{2,10},{6,14},... | collective-permute-start | bytes 393224 | tf_op jit(solution)/shard_map/ppermute | solution.py:519
  183.0 32.6 %collective-permute-start.24 = (bf16[128,1536]{1,0:T(8,128)(2,1)S(1)}, bf16[128,1536]{1,0:T(8,128)(2,1)S(1)}, u32[]{:S(2)}, u32[]{:S(2)}) collective-permute-start(bf16[128,1536]{1,0:T(8,128)(2,1)S(1)} %add_convert_fusion.1), channel_id=1, source_target_pairs={{0,8},{4,12},{8,0},{12,4},{1,9},{5,13},{9,1},{13,5},{2,10},{6,14},... | collective-permute-start | bytes 1179656 | tf_op jit(solution)/shard_map/ppermute | solution.py:519
  185.8 35.4 %collective-permute-start.26 = (bf16[128,1280]{1,0:T(8,128)(2,1)S(1)}, bf16[128,1280]{1,0:T(8,128)(2,1)S(1)}, u32[]{:S(2)}, u32[]{:S(2)}) collective-permute-start(bf16[128,1280]{1,0:T(8,128)(2,1)S(1)} %add_convert_fusion.2), channel_id=1, source_target_pairs={{0,8},{4,12},{8,0},{12,4},{1,9},{5,13},{9,1},{13,5},{2,10},{6,14},... | collective-permute-start | bytes 983048 | tf_op jit(solution)/shard_map/ppermute | solution.py:519
  190.9 28.5 %copy-start.17 = (bf16[256,768]{1,0:T(8,128)(2,1)}, bf16[256,768]{1,0:T(8,128)(2,1)S(1)}, u32[]{:S(2)}) copy-start(bf16[256,768]{1,0:T(8,128)(2,1)S(1)} %collective-permute-done.28.refs_4_) | copy-start | bytes 1179652
  191.0 30.2 %collective-permute-start.29 = (bf16[128,768]{1,0:T(8,128)(2,1)S(1)}, bf16[128,768]{1,0:T(8,128)(2,1)S(1)}, u32[]{:S(2)}, u32[]{:S(2)}) collective-permute-start(bf16[128,768]{1,0:T(8,128)(2,1)S(1)} %add_convert_fusion.3), channel_id=1, source_target_pairs={{0,8},{4,12},{8,0},{12,4},{1,9},{5,13},{9,1},{13,5},{2,10},{6,14},... | collective-permute-start | bytes 589832 | tf_op jit(solution)/shard_map/ppermute | solution.py:519
  (23 other events, 49.9 us)

commit v5 on v4

--- a/solution.py
+++ b/solution.py
@@ -245,7 +245,7 @@
     for part, features in outlet:
         partial[:, features] = dot(mixed[...], part[...], NT).astype(BF)
     if plan.paired:
-        own_hidden, sent = grads
+        own_hidden, sent, last = grads
         half = hidden.shape[1] // 4
         emit_own(hidden, own_hidden, 0, where[0], plan.locs)
         emit_half(hidden, sent, 0, 1 - where[0], where[1], plan.locs)
@@ -261,7 +261,10 @@
         back_part[:, features] = total.astype(BF)
     split_columns(back_triple, back_triples)
     if plan.paired:
-        sent[:, half:] = back_triple[:, : sent.shape[1] - half]
+        split = sent.shape[1] - half
+        sent[:, half:] = back_triple[:, :split]
+        last[:, :split] = back_triple[:, split:]
+        last[:, split:] = mixed[...]
 
 
 def split_columns(whole, outs):
@@ -271,7 +274,7 @@
         at += out.shape[1]
 
 
-def norm_back_kernel(moves, step, gain, here, there, joined, cotangent, *outs):
+def norm_back_kernel(moves, step, gain, here, there, joined, cotangent, kept, *outs):
     for at in range(0, joined.shape[0], step):
         span_here = slice(at, at + step)
         normed, inv_scale = statistics(joined[span_here, :])
@@ -339,7 +342,7 @@
         column += width
 
 
-def finish_kernel(*refs):
+def finish_kernel(kind_first, *refs):
     out = refs[-1]
     block = out.shape[0]
     column = 0
@@ -347,13 +350,13 @@
         for at in range(0, near.shape[1], 256):
             lane = slice(at, at + 256)
             total = near[:, lane] + beside[block:, lane].astype(F32) + far[:, lane].astype(F32)
-            kind, first = (3 * out.shape[2] + column + at) // out.shape[2] % 4, (column + at) % out.shape[2]
+            kind, first = (kind_first * out.shape[2] + column + at) // out.shape[2] % 4, (column + at) % out.shape[2]
             out[:, kind, first : first + 256] = total
         column += near.shape[1]
 
 
-def finish_last_kernel(kept, *refs):
-    finish_kernel(*refs[:-1])
+def finish_last_kernel(kind_first, kept, *refs):
+    finish_kernel(kind_first, *refs[:-1])
 
 
 def fence_kernel(*refs):
@@ -519,11 +522,11 @@
     return near, beside, lax.ppermute(far, "loc", APART)
 
 
-def finish(terms, width, kept=None):
+def finish(terms, width, kind_first, kept=None):
     out = jax.ShapeDtypeStruct((terms[0].shape[0], 4, width), F32)
     if kept is None:
-        return call(finish_kernel, (out,), terms)
-    return call(finish_last_kernel, (out,), (kept, *terms), kept=(0,))
+        return call(functools.partial(finish_kernel, kind_first), (out,), terms)
+    return call(functools.partial(finish_last_kernel, kind_first), (out,), (kept, *terms), kept=(0,))
 
 
 def per_device(
@@ -657,7 +660,11 @@
         half_shapes = (shape(half, model), shape(half, model))
         own, quarter = shape(rows, model // 2), model // 4
         forward_grads = (own, own, shape(rows, 2 * quarter + width))
-        temporal_grads = (own, shape(rows, quarter + 3 * width // 2))
+        temporal_grads = (
+            own,
+            shape(rows, quarter + 3 * width // 2),
+            shape(rows, 3 * width // 2 + width),
+        )
         back_shapes = (shape(rows, 3 * width // 2), shape(rows, 3 * width // 2))
         backward_grads = (own, shape(rows, model // 2 + 3 * width // 2))
     else:
@@ -733,7 +740,7 @@
             shape(rows, width),
             shape(rows, model),
             shape(rows, model),
-            *back_shapes,
+            *(() if paired else back_shapes),
         ),
         (
             where,
@@ -762,26 +769,25 @@
         others = swap(back_part, "mp")
     else:
         others = (lax.psum(back_part.astype(F32), "mp") - back_part.astype(F32)).astype(BF)
-    backs = call(
+    *backs, last_sent = call(
         functools.partial(norm_back_kernel, temporal_moves, temporal_size),
         half_shapes,
-        (temporal_gain, back_part, others, joined, cotangent_rows),
+        (temporal_gain, back_part, others, joined, cotangent_rows, middle[-1]),
+        kept=(5,),
     )
     if paired:
-        mixed_sent, back_sent = fence(temporal_mixed, swap(backs[1], "date"))
+        back_origins = (backs[0], swap(backs[1], "date"))
         early_there = swap(early_other[:, : 2 * quarter], "mp")
-        middle_other = swap(middle[1], "date")
+        middle_other, back_own = fence(swap(middle[1], "date"), backs[0])
+        back_origins = (back_own, back_origins[1])
         middle_there = swap(middle_other[:, :quarter], "mp")
-        last_half = swap(temporal_triples[1], "date")
-        part = temporal_triples[0].shape[1]
+        part = 3 * width // 2
         others = ((1, 0), (2, 0))
-        *intake, kept, back_sent = summed(
+        *intake, kept = summed(
             where,
-            (middle[0], middle_other, middle_there, *temporal_triples, last_half),
-            ((0, others, (3, 0), (1, quarter), part), (0, others, (4, 0), (5, 0), part)),
-            kept=(back_sent,),
+            (middle[0], middle_other, middle_there, middle[1]),
+            ((0, others, (3, quarter), (1, quarter), part),),
         )
-        back_origins = (backs[0], back_sent)
     else:
         back = lax.all_to_all(
             temporal_whole(backs[0]), "date", split_axis=0, concat_axis=1, tiled=True
@@ -811,17 +817,21 @@
             whole_grads(forward[0], back_triples[0], backward[0], mixed),
             whole_grads(middle[0], kept, cotangent_rows, temporal_mixed),
         )
-    intake = summed_over_loc((*intake, kept))
-    *outlet, upstream_own = summed(
+    intake = [*summed_over_loc((*intake, kept))]
+    last_other = swap(last_sent, "date")
+    *sums, upstream_own, intake[1] = summed(
         where,
-        (forward[1], early_other, early_there, mixed_sent, swap(mixed_sent, "date")),
-        ((0, ((1, quarter), (2, quarter)), (3, 0), (4, 0), width),),
-        kept=(backward[0],),
-    )
-    temporal_terms = [*summed_over_loc(outlet), *intake]
+        (middle[0], middle_other, middle_there, last_sent, last_other, forward[1], early_other, early_there),
+        (
+            (0, others, (3, 0), (4, 0), part),
+            (5, ((6, quarter), (7, quarter)), (3, part), (4, part), width),
+        ),
+        kept=(backward[0], intake[1]),
+    )
+    outlet = [*summed_over_loc(sums)]
     half = model // 2
     backward_other = swap(backward[1], "date")
-    *sums, kept = summed(
+    *sums, intake[2], outlet[0] = summed(
         where,
         (
             upstream_own,
@@ -836,18 +846,19 @@
             (0, ((1, 0),), (2, 0), (3, 2 * quarter), width),
             (4, ((3, 0), (5, 0)), (6, 0), (1, half), back_triples[0].shape[1]),
         ),
-        kept=(temporal_terms[4],),
-    )
-    temporal_terms[4] = kept
+        kept=(intake[2], outlet[0]),
+    )
     spatial_terms = [*summed_over_loc(sums)]
     sums = summed(
         where,
         (forward[0], early_other, early_there, back_triples[1], swap(back_triples[1], "date")),
         ((0, ((1, 0), (2, 0)), (3, 0), (4, 0), back_triples[1].shape[1]),),
-    )
+        kept=(spatial_terms[0],),
+    )
+    *sums, spatial_terms[0] = sums
     spatial_terms += summed_over_loc(sums)
-    (temporal_grads,) = finish(temporal_terms, width)
-    spatial_grads, temporal_grads = finish(spatial_terms, width, kept=temporal_grads)
+    (temporal_grads,) = finish((*intake, *outlet), width, 0)
+    spatial_grads, temporal_grads = finish(spatial_terms, width, 3, kept=temporal_grads)
     return (encoded, spatial_grads, temporal_grads)
 
 

time: 226 us -> 213 us (0.942)
  waiting for transfers between devices: 114 us -> 95.8 us
  starting transfers between devices: 29.4 us -> 32.4 us
  local copies, waits for them, and re-layouts: 22.4 us -> 25 us
    ppermute x20 -> x19, waiting for transfers between devices: 58 us -> 42.1 us  [swap(): return lax.ppermute(array, axis, [(0, 1), (1, 0)])]
    ppermute x4, waiting for transfers between devices: 29.6 us -> 24.5 us  [summed_over_loc(): beside = lax.ppermute(sent, 'loc', PAIRS)]
    ppermute x4, waiting for transfers between devices: 25.4 us -> 28.1 us  [summed_over_loc(): return (near, beside, lax.ppermute(far, 'loc', APART))]
    unnamed x84 -> x80, local copies, waits for them, and re-layouts: 14 us -> 14.7 us
    ppermute x20 -> x19, starting transfers between devices: 18.7 us -> 18.3 us  [swap(): return lax.ppermute(array, axis, [(0, 1), (1, 0)])]
  transfers between devices with their start and end apart: 30 -> 29, of which waited for: 18 -> 16; matrix products, arithmetic and copies ran while one was open for 5% -> 5% of each run, Pallas kernels for 21% -> 25%
where the time goes in v5:
time: 213 us
  waiting for transfers between devices  95.8 us (45%)
  Pallas kernels  57.3 us (27%)
  starting transfers between devices  32.4 us (15%)
  local copies, waits for them, and re-layouts  25 us (12%)
    pallas_call x12, Pallas kernels, call(): pl.pallas_call(body, out_shape=outs, in_specs=specs, out_specs=out_specs,...  57.3 us
    ppermute x19, waiting for transfers between devices, swap(): return lax.ppermute(array, axis, [(0, 1), (1, 0)])  42.1 us
    ppermute x4, waiting for transfers between devices, summed_over_loc(): return (near, beside, lax.ppermute(far, 'loc', APART))  28.1 us
    ppermute x4, waiting for transfers between devices, summed_over_loc(): beside = lax.ppermute(sent, 'loc', PAIRS)  24.5 us
    ppermute x19, starting transfers between devices, swap(): return lax.ppermute(array, axis, [(0, 1), (1, 0)])  18.3 us
    unnamed x80, local copies, waits for them, and re-layouts  14.7 us
    ppermute x4, starting transfers between devices, summed_over_loc(): beside = lax.ppermute(sent, 'loc', PAIRS)  6.27 us
    dynamic_slice x3, local copies, waits for them, and re-layouts, quarter_of(): return lax.dynamic_slice_in_dim(weights, number * (rows // 4), rows // 4, 0)  5.5 us
  transfers between devices with their start and end apart: 29, of which 16 were waited for; matrix products, arithmetic and copies ran while one was open for 5% of the time, Pallas kernels for 25%

profile of v5, /device:TPU:0, one launch (start us, length us, event | category | flops | bytes accessed | tf_op | source)
XLA Modules:
  0.0 212.7 jit_solution(10062481177476637138)
XLA Ops:
  0.6 2.0 copy.61
  3.6 2.9 %collective-permute-start = (bf16[128,4,512]{2,0,1:T(8,128)(2,1)}, bf16[128,4,512]{2,0,1:T(8,128)(2,1)S(1)}, u32[]{:S(2)}, u32[]{:S(2)}) collective-permute-start(bf16[128,4,512]{2,0,1:T(8,128)(2,1)} %constant_dynamic-slice_fusion), channel_id=1, source_target_pairs={{0,2},{2,0},{1,3},{3,1},{4,6},{6,4},{5,7},{7,5},{8,10},{10,8},{9,1... | collective-permute-start | bytes 1572872 | tf_op jit(solution)/shard_map/ppermute | solution.py:454
  7.2 3.1 %shard_map.139 = (bf16[144,1024]{1,0:T(8,128)(2,1)}, bf16[144,1024]{1,0:T(8,128)(2,1)}, bf16[288,1024]{1,0:T(8,128)(2,1)}, f32[12,1024]{1,0:T(8,128)}) custom-call(s32[1,12]{1,0:T(1,128)} %cloud.1, s32[1,12]{1,0:T(1,128)} %drop.1, s32[1,48]{1,0:T(1,128)} %keep.1, s32[4]{0:T(128)} %pad_add_fusion.where, bf16[6,48,1024]{2,1,0:T(8,128)(2,1)} %bitcast.55, ...), custom_call_target="tpu_custom_call" | custom-call | bytes 3424560 | tf_op jit(solution)/shard_map/pallas_call | solution.py:430
  10.3 2.0 constant_dynamic-slice_fusion.1.refs_0_
  12.3 1.1 copy.48
  13.5 6.0 %collective-permute-done = bf16[128,4,512]{2,0,1:T(8,128)(2,1)S(1)} collective-permute-done((bf16[128,4,512]{2,0,1:T(8,128)(2,1)}, bf16[128,4,512]{2,0,1:T(8,128)(2,1)S(1)}, u32[]{:S(2)}, u32[]{:S(2)}) %collective-permute-start) | collective-permute-done | bytes 524320 | tf_op jit(solution)/shard_map/ppermute | solution.py:454
  19.5 2.1 %collective-permute-start.2 = (bf16[128,4,512]{2,0,1:T(8,128)(2,1)S(1)}, bf16[128,4,512]{2,0,1:T(8,128)(2,1)S(1)}, u32[]{:S(2)}, u32[]{:S(2)}) collective-permute-start(bf16[128,4,512]{2,0,1:T(8,128)(2,1)S(1)} %collective-permute-done), channel_id=1, source_target_pairs={{0,4},{4,0},{8,12},{12,8},{1,5},{5,1},{9,13},{13,9},{2,6},{6,2},{1... | collective-permute-start | bytes 1572872 | tf_op jit(solution)/shard_map/ppermute | solution.py:481
  21.7 1.5 collective-permute-start.1
  23.2 2.5 %constant_dynamic-slice_fusion.2 = (bf16[128,4,512]{2,1,0:T(4,128)(2,1)}, bf16[128,4,512]{2,1,0:T(4,128)(2,1)}) fusion(bf16[512,4,512]{2,1,0:T(4,128)(2,1)} %param.22, s32[]{:T(128)S(6)} %select_n.36, s32[]{:T(128)S(6)} %select_n.35), kind=kLoop, calls=%fused_computation.9 | loop fusion | bytes 2097160 | tf_op jit(solution)/shard_map/dynamic_slice | solution.py:463
  25.7 1.5 collective-permute-start.5
  27.2 3.5 %collective-permute-done.3 = bf16[128,4,512]{2,0,1:T(8,128)(2,1)S(1)} collective-permute-done((bf16[128,4,512]{2,0,1:T(8,128)(2,1)S(1)}, bf16[128,4,512]{2,0,1:T(8,128)(2,1)S(1)}, u32[]{:S(2)}, u32[]{:S(2)}) %collective-permute-start.3) | collective-permute-done | bytes 524320 | tf_op jit(solution)/shard_map/ppermute | solution.py:454
  30.8 1.0 collective-permute-done.2
  31.8 1.2 collective-permute-done.1
  33.9 8.0 %shard_map.142 = (bf16[144,1024]{1,0:T(8,128)(2,1)}, bf16[144,1024]{1,0:T(8,128)(2,1)}, bf16[288,512]{1,0:T(8,128)(2,1)}, bf16[288,512]{1,0:T(8,128)(2,1)}, bf16...) custom-call(s32[4]{0:T(128)} %pad_add_fusion.where, ...), custom_call_target="tpu_custom_call" | custom-call | flops 1207959552 | bytes 9211920 | tf_op jit(solution)/shard_map/pallas_call | solution.py:430
  42.6 1.8 collective-permute-done.6.there
  45.1 2.1 shard_map.144
  47.2 1.5 collective-permute-start.7
  50.3 1.2 collective-permute-start.9
  51.5 1.5 collective-permute-start.8
  53.1 4.2 %collective-permute-done.7.refs_1_ = bf16[144,1024]{1,0:T(8,128)(2,1)S(1)} collective-permute-done((bf16[144,1024]{1,0:T(8,128)(2,1)}, bf16[144,1024]{1,0:T(8,128)(2,1)S(1)}, u32[]{:S(2)}, u32[]{:S(2)}) %collective-permute-start.7) | collective-permute-done | bytes 294944 | tf_op jit(solution)/shard_map/ppermute | solution.py:454
  58.0 1.5 collective-permute-start.13
  59.6 1.8 copy.60
  62.2 6.5 %collective-permute-done.10 = bf16[128,4,512]{2,0,1:T(8,128)(2,1)} collective-permute-done((bf16[128,4,512]{2,0,1:T(8,128)(2,1)}, bf16[128,4,512]{2,0,1:T(8,128)(2,1)}, u32[]{:S(2)}, u32[]{:S(2)}) %collective-permute-start.10) | collective-permute-done | bytes 524320 | tf_op jit(solution)/shard_map/ppermute | solution.py:454
  68.7 11.8 %shard_map.146 = (bf16[288,512]{1,0:T(8,128)(2,1)}, bf16[288,1024]{1,0:T(8,128)(2,1)}, bf16[288,1280]{1,0:T(8,128)(2,1)}, bf16[288,1024]{1,0:T(8,128)(2,1)}, bf1...) custom-call(s32[4]{0:T(128)} %pad_add_fusion.where, f32[1,1024]{1,0:T(1,128)} %bitcast.61, ...), custom_call_target="tpu_custom_call" | custom-call | flops 2415919104 | bytes 9703824 | tf_op jit(solution)/shard_map/pallas_call | solution.py:430
  81.3 1.5 collective-permute-start.12
  84.3 3.3 %shard_map.148 = (bf16[144,1024]{1,0:T(8,128)(2,1)}, bf16[144,1024]{1,0:T(8,128)(2,1)}, bf16[288,1280]{1,0:T(8,128)(2,1)}) custom-call(f32[1,1024]{1,0:T(1,128)} %bitcast.62, bf16[288,1024]{1,0:T(8,128)(2,1)} %get-tuple-element.88.here, bf16[288,1024]{1,0:T(8,128)(2,1)} %copy-done.24, ...), custom_call_target="tpu_custom_call", output_to_operand_aliasing={{2}: (5, {})} | custom-call | bytes 3690496 | tf_op jit(solution)/shard_map/pallas_call | solution.py:430
  87.6 9.6 %collective-permute-done.12.refs_0_ = bf16[288,1024]{1,0:T(8,128)(2,1)S(1)} collective-permute-done((bf16[288,1024]{1,0:T(8,128)(2,1)}, bf16[288,1024]{1,0:T(8,128)(2,1)S(1)}, u32[]{:S(2)}, u32[]{:S(2)}) %collective-permute-start.12) | collective-permute-done | bytes 589856 | tf_op jit(solution)/shard_map/ppermute | solution.py:454
  99.1 1.6 collective-permute-start.16
  101.8 3.3 %shard_map.150 = (bf16[256,768]{1,0:T(8,128)(2,1)}, f32[128,768]{1,0:T(8,128)}, f32[128,768]{1,0:T(8,128)}) custom-call(s32[4]{0:T(128)} %pad_add_fusion.where, bf16[288,512]{1,0:T(8,128)(2,1)} %get-tuple-element.84.refs_0_, bf16[288,1024]{1,0:T(8,128)(2,1)} %get-tuple-element.91.refs_1_, bf16[288,256]{1,0:T(8,128)(2,1)} %copy-done.36, ...), custom_call_target="tpu_custom_call" | custom-call | flops 452984832 | bytes 2801680 | tf_op jit(solution)/shard_map/pallas_call | solution.py:430
  105.1 1.2 collective-permute-start.19
  106.3 2.9 %collective-permute-done.16.refs_1_ = bf16[144,1024]{1,0:T(8,128)(2,1)S(1)} collective-permute-done((bf16[144,1024]{1,0:T(8,128)(2,1)}, bf16[144,1024]{1,0:T(8,128)(2,1)S(1)}, u32[]{:S(2)}, u32[]{:S(2)}) %collective-permute-start.16) | collective-permute-done | bytes 294944 | tf_op jit(solution)/shard_map/ppermute | solution.py:454
  109.9 7.3 %shard_map.151 = (bf16[288,512]{1,0:T(8,128)(2,1)}, bf16[288,1280]{1,0:T(8,128)(2,1)}, bf16[288,768]{1,0:T(8,128)(2,1)}, bf16[288,768]{1,0:T(8,128)(2,1)}, f32[128,768]{1,0:T(8,128)}) custom-call(s32[4]{0:T(128)} %pad_add_fusion.where, bf16[288,1536]{1,0:T(8,128)(2,1)} %get-tuple-element.82.triple, ...), custom_call_target="tpu_custom_call", output_to_operand_aliasing={{4}: (3, {})} | custom-call | flops 1207959552 | bytes 8863760 | tf_op jit(solution)/shard_map/pallas_call | solution.py:430
  117.2 1.5 collective-permute-start.20
  120.3 4.6 %collective-permute-done.17.refs_4_ = bf16[288,1280]{1,0:T(8,128)(2,1)S(1)} collective-permute-done((bf16[288,1280]{1,0:T(8,128)(2,1)}, bf16[288,1280]{1,0:T(8,128)(2,1)S(1)}, u32[]{:S(2)}, u32[]{:S(2)}) %collective-permute-start.17) | collective-permute-done | bytes 737312 | tf_op jit(solution)/shard_map/ppermute | solution.py:454
  125.8 4.7 %shard_map.152 = (bf16[256,1280]{1,0:T(8,128)(2,1)}, f32[128,1280]{1,0:T(8,128)}, f32[128,1280]{1,0:T(8,128)}, bf16[288,512]{1,0:T(8,128)(2,1)}, bf16[256,768]{1,0:T(8,128)(2,1)}) custom-call(s32[4]{0:T(128)} %pad_add_fusion.where, bf16[288,512]{1,0:T(8,128)(2,1)} %get-tuple-element.84.refs_0_, ...), custom_call_target="tpu_custom_call", output_to_operand_aliasing={{3}: (9, {}), {4}: (10, {})} | custom-call | flops 754974720 | bytes 6340624 | tf_op jit(solution)/shard_map/pallas_call | solution.py:430
  130.6 1.2 collective-permute-start.22
  131.8 2.6 %collective-permute-start.21 = (bf16[128,768]{1,0:T(8,128)(2,1)S(1)}, bf16[128,768]{1,0:T(8,128)(2,1)S(1)}, u32[]{:S(2)}, u32[]{:S(2)}) collective-permute-start(bf16[128,768]{1,0:T(8,128)(2,1)S(1)} %add_convert_fusion.4), channel_id=1, source_target_pairs={{0,8},{4,12},{8,0},{12,4},{1,9},{5,13},{9,1},{13,5},{2,10},{6,14},... | collective-permute-start | bytes 589832 | tf_op jit(solution)/shard_map/ppermute | solution.py:522
  134.3 1.5 collective-permute-start.24
  135.8 13.7 %collective-permute-done.21.refs_7_ = bf16[128,768]{1,0:T(8,128)(2,1)S(1)} collective-permute-done((bf16[128,768]{1,0:T(8,128)(2,1)S(1)}, bf16[128,768]{1,0:T(8,128)(2,1)S(1)}, u32[]{:S(2)}, u32[]{:S(2)}) %collective-permute-start.21) | collective-permute-done | bytes 196640 | tf_op jit(solution)/shard_map/ppermute | solution.py:522
  150.5 4.3 %shard_map.153 = (bf16[256,1280]{1,0:T(8,128)(2,1)}, f32[128,1280]{1,0:T(8,128)}, f32[128,1280]{1,0:T(8,128)}, bf16[128,768]{1,0:T(8,128)(2,1)}, f32[128,1280]{1,0:T(8,128)}) custom-call(s32[4]{0:T(128)} %pad_add_fusion.where, bf16[288,512]{1,0:T(8,128)(2,1)} %get-tuple-element.102.refs_0_, ...), custom_call_target="tpu_custom_call", output_to_operand_aliasing={{3}: (8, {}), {4}: (9, {})} | custom-call | flops 754974720 | bytes 5767184 | tf_op jit(solution)/shard_map/pallas_call | solution.py:430
  154.8 3.9 %collective-permute-start.25 = (bf16[256,1280]{1,0:T(8,128)(2,1)}, bf16[256,1280]{1,0:T(8,128)(2,1)S(1)}, u32[]{:S(2)}, u32[]{:S(2)}) collective-permute-start(bf16[256,1280]{1,0:T(8,128)(2,1)} %get-tuple-element.116), channel_id=1, source_target_pairs={{0,4},{4,0},{8,12},{12,8},{1,5},{5,1},{9,13},{13,9},{2,6},{6,2},{1... | collective-permute-start | bytes 1966088 | tf_op jit(solution)/shard_map/ppermute | solution.py:520
  159.8 3.4 %shard_map.155 = (bf16[256,768]{1,0:T(8,128)(2,1)}, f32[128,768]{1,0:T(8,128)}, f32[128,768]{1,0:T(8,128)}, f32[128,1280]{1,0:T(8,128)}) custom-call(s32[4]{0:T(128)} %pad_add_fusion.where, bf16[288,512]{1,0:T(8,128)(2,1)} %get-tuple-element.105.refs_4_.refs_0_, ...), custom_call_target="tpu_custom_call", output_to_operand_aliasing={{3}: (6, {})} | custom-call | flops 452984832 | bytes 3899408 | tf_op jit(solution)/shard_map/pallas_call | solution.py:430
  163.3 1.5 collective-permute-start.23
  164.8 18.0 %collective-permute-done.25.refs_1_ = bf16[256,1280]{1,0:T(8,128)(2,1)S(1)} collective-permute-done((bf16[256,1280]{1,0:T(8,128)(2,1)}, bf16[256,1280]{1,0:T(8,128)(2,1)S(1)}, u32[]{:S(2)}, u32[]{:S(2)}) %collective-permute-start.25) | collective-permute-done | bytes 655392 | tf_op jit(solution)/shard_map/ppermute | solution.py:520
  183.0 6.5 %collective-permute-done.27.refs_4_ = bf16[256,768]{1,0:T(8,128)(2,1)S(1)} collective-permute-done((bf16[256,768]{1,0:T(8,128)(2,1)}, bf16[256,768]{1,0:T(8,128)(2,1)S(1)}, u32[]{:S(2)}, u32[]{:S(2)}) %collective-permute-start.27) | collective-permute-done | bytes 393248 | tf_op jit(solution)/shard_map/ppermute | solution.py:520
  191.4 3.0 %shard_map.154.kept = f32[128,4,512]{2,1,0:T(4,128)} custom-call(f32[128,768]{1,0:T(8,128)} %get-tuple-element.95.refs_0_, bf16[256,768]{1,0:T(8,128)(2,1)} %get-tuple-element.101.refs_1_, bf16[128,768]{1,0:T(8,128)(2,1)} %get-tuple-element.109.refs_2_, f32[128,1280]{1,0:T(8,128)} %get-tuple-element.110.refs_3_, bf16[256,1280]{1,0:T(8,128)(2,1)} %copy-done.15, ...), custom_call_target="tpu_custom_call" | custom-call | bytes 3670016 | tf_op jit(solution)/shard_map/pallas_call | solution.py:430
  194.5 14.4 %collective-permute-done.28.refs_5_ = bf16[128,768]{1,0:T(8,128)(2,1)S(1)} collective-permute-done((bf16[128,768]{1,0:T(8,128)(2,1)S(1)}, bf16[128,768]{1,0:T(8,128)(2,1)S(1)}, u32[]{:S(2)}, u32[]{:S(2)}) %collective-permute-start.28) | collective-permute-done | bytes 196640 | tf_op jit(solution)/shard_map/ppermute | solution.py:522
  209.7 3.0 %shard_map.156 = (f32[128,4,512]{2,1,0:T(4,128)}, f32[128,4,512]{2,1,0:T(4,128)}) custom-call(f32[128,4,512]{2,1,0:T(4,128)} %shard_map.154.kept, f32[128,1280]{1,0:T(8,128)} %get-tuple-element.115.refs_0_, bf16[256,1280]{1,0:T(8,128)(2,1)} %copy-done.16, bf16[128,1280]{1,0:T(8,128)(2,1)} %copy-done.30, ...), custom_call_target="tpu_custom_call", output_to_operand_aliasing={{1}: (0, {})} | custom-call | bytes 4718592 | tf_op jit(solution)/shard_map/pallas_call | solution.py:430
  (129 shorter events, 20.8 us)
Async XLA Ops:
  2.7 9.7 %copy-start = (bf16[512,4,512]{2,0,1:T(8,128)(2,1)}, bf16[512,4,512]{2,0,1:T(8,128)(2,1)S(1)}, u32[]{:S(2)}) copy-start(bf16[512,4,512]{2,0,1:T(8,128)(2,1)S(1)} %copy.61) | copy-start | bytes 6291460
  3.6 15.9 %collective-permute-start = (bf16[128,4,512]{2,0,1:T(8,128)(2,1)}, bf16[128,4,512]{2,0,1:T(8,128)(2,1)S(1)}, u32[]{:S(2)}, u32[]{:S(2)}) collective-permute-start(bf16[128,4,512]{2,0,1:T(8,128)(2,1)} %constant_dynamic-slice_fusion), channel_id=1, source_target_pairs={{0,2},{2,0},{1,3},{3,1},{4,6},{6,4},{5,7},{7,5},{8,10},{10,8},{9,1... | collective-permute-start | bytes 1572872 | tf_op jit(solution)/shard_map/ppermute | solution.py:454
  13.5 17.3 %collective-permute-start.3 = (bf16[128,4,512]{2,0,1:T(8,128)(2,1)S(1)}, bf16[128,4,512]{2,0,1:T(8,128)(2,1)S(1)}, u32[]{:S(2)}, u32[]{:S(2)}) collective-permute-start(bf16[128,4,512]{2,0,1:T(8,128)(2,1)S(1)} %copy.48), channel_id=1, source_target_pairs={{0,2},{2,0},{1,3},{3,1},{4,6},{6,4},{5,7},{7,5},{8,10},{10,8},{9,1... | collective-permute-start | bytes 1572872 | tf_op jit(solution)/shard_map/ppermute | solution.py:454
  19.5 13.5 %copy-start.9 = (bf16[128,4,512]{2,0,1:T(8,128)(2,1)}, bf16[128,4,512]{2,0,1:T(8,128)(2,1)S(1)}, u32[]{:S(2)}) copy-start(bf16[128,4,512]{2,0,1:T(8,128)(2,1)S(1)} %collective-permute-done) | copy-start | bytes 1572868
  19.5 12.3 %collective-permute-start.2 = (bf16[128,4,512]{2,0,1:T(8,128)(2,1)S(1)}, bf16[128,4,512]{2,0,1:T(8,128)(2,1)S(1)}, u32[]{:S(2)}, u32[]{:S(2)}) collective-permute-start(bf16[128,4,512]{2,0,1:T(8,128)(2,1)S(1)} %collective-permute-done), channel_id=1, source_target_pairs={{0,4},{4,0},{8,12},{12,8},{1,5},{5,1},{9,13},{13,9},{2,6},{6,2},{1... | collective-permute-start | bytes 1572872 | tf_op jit(solution)/shard_map/ppermute | solution.py:481
  21.7 11.4 %collective-permute-start.1 = (bf16[128,4,512]{2,0,1:T(8,128)(2,1)S(1)}, bf16[128,4,512]{2,0,1:T(8,128)(2,1)S(1)}, u32[]{:S(2)}, u32[]{:S(2)}) collective-permute-start(bf16[128,4,512]{2,0,1:T(8,128)(2,1)S(1)} %collective-permute-done), channel_id=1, source_target_pairs={{0,16},{16,0},{1,17},{17,1},{2,18},{18,2},{3,19},{19,3},{4,20},{20... | collective-permute-start | bytes 1572872 | tf_op jit(solution)/shard_map/ppermute | solution.py:454
  25.7 16.1 %collective-permute-start.5 = (bf16[128,4,512]{2,1,0:T(4,128)(2,1)}, bf16[128,4,512]{2,1,0:T(4,128)(2,1)S(1)}, u32[]{:S(2)}, u32[]{:S(2)}) collective-permute-start(bf16[128,4,512]{2,1,0:T(4,128)(2,1)} %get-tuple-element.71), channel_id=1, source_target_pairs={{0,2},{2,0},{1,3},{3,1},{4,6},{6,4},{5,7},{7,5},{8,10},{10,8},{9,1... | collective-permute-start | bytes 1572872 | tf_op jit(solution)/shard_map/ppermute | solution.py:454
  41.8 6.9 %copy-start.3 = (bf16[128,4,512]{2,1,0:T(4,128)(2,1)S(1)}, bf16[128,4,512]{2,1,0:T(4,128)(2,1)}, u32[]{:S(2)}) copy-start(bf16[128,4,512]{2,1,0:T(4,128)(2,1)} %get-tuple-element.79) | copy-start | bytes 1572868
  42.6 10.4 %copy-start.37 = (s32[1,12]{1,0:T(1,128)S(1)}, s32[1,12]{1,0:T(1,128)}, u32[]{:S(2)}) copy-start(s32[1,12]{1,0:T(1,128)} %cloud.1) | copy-start | bytes 148
  42.6 10.4 %copy-start.38 = (s32[1,12]{1,0:T(1,128)S(1)}, s32[1,12]{1,0:T(1,128)}, u32[]{:S(2)}) copy-start(s32[1,12]{1,0:T(1,128)} %drop.1) | copy-start | bytes 148
  42.6 7.5 %copy-start.14 = (bf16[128,4,512]{2,1,0:T(4,128)(2,1)S(1)}, bf16[128,4,512]{2,1,0:T(4,128)(2,1)}, u32[]{:S(2)}) copy-start(bf16[128,4,512]{2,1,0:T(4,128)(2,1)} %get-tuple-element.78) | copy-start | bytes 1572868
  42.6 1.8 collective-permute-start.6
  45.1 14.4 %copy-start.4 = (bf16[512,4,512]{2,1,0:T(4,128)(2,1)S(1)}, bf16[512,4,512]{2,1,0:T(4,128)(2,1)}, u32[]{:S(2)}) copy-start(bf16[512,4,512]{2,1,0:T(4,128)(2,1)} %param.22) | copy-start | bytes 6291460
  47.2 10.1 %collective-permute-start.7 = (bf16[144,1024]{1,0:T(8,128)(2,1)}, bf16[144,1024]{1,0:T(8,128)(2,1)S(1)}, u32[]{:S(2)}, u32[]{:S(2)}) collective-permute-start(bf16[144,1024]{1,0:T(8,128)(2,1)} %get-tuple-element.76), channel_id=1, source_target_pairs={{0,2},{2,0},{1,3},{3,1},{4,6},{6,4},{5,7},{7,5},{8,10},{10,8},{9,1... | collective-permute-start | bytes 884744 | tf_op jit(solution)/shard_map/ppermute | solution.py:454
  49.6 19.0 %collective-permute-start.10 = (bf16[128,4,512]{2,0,1:T(8,128)(2,1)}, bf16[128,4,512]{2,0,1:T(8,128)(2,1)}, u32[]{:S(2)}, u32[]{:S(2)}) collective-permute-start(bf16[128,4,512]{2,0,1:T(8,128)(2,1)} %copy.53), channel_id=1, source_target_pairs={{0,2},{2,0},{1,3},{3,1},{4,6},{6,4},{5,7},{7,5},{8,10},{10,8},{9,1... | collective-permute-start | bytes 1572872 | tf_op jit(solution)/shard_map/ppermute | solution.py:454
  50.3 11.1 %copy-start.25 = (bf16[128,4,512]{2,0,1:T(8,128)(2,1)}, bf16[128,4,512]{2,0,1:T(8,128)(2,1)S(1)}, u32[]{:S(2)}) copy-start(bf16[128,4,512]{2,0,1:T(8,128)(2,1)S(1)} %copy.62) | copy-start | bytes 1572868
  50.3 18.4 %collective-permute-start.9 = (bf16[128,4,512]{2,0,1:T(8,128)(2,1)S(1)}, bf16[128,4,512]{2,0,1:T(8,128)(2,1)}, u32[]{:S(2)}, u32[]{:S(2)}) collective-permute-start(bf16[128,4,512]{2,0,1:T(8,128)(2,1)S(1)} %copy.62), channel_id=1, source_target_pairs={{0,4},{4,0},{8,12},{12,8},{1,5},{5,1},{9,13},{13,9},{2,6},{6,2},{1... | collective-permute-start | bytes 1572872 | tf_op jit(solution)/shard_map/ppermute | solution.py:481
  51.5 17.2 %collective-permute-start.8 = (bf16[128,4,512]{2,0,1:T(8,128)(2,1)S(1)}, bf16[128,4,512]{2,0,1:T(8,128)(2,1)}, u32[]{:S(2)}, u32[]{:S(2)}) collective-permute-start(bf16[128,4,512]{2,0,1:T(8,128)(2,1)S(1)} %copy.62), channel_id=1, source_target_pairs={{0,16},{16,0},{1,17},{17,1},{2,18},{18,2},{3,19},{19,3},{4,20},{20... | collective-permute-start | bytes 1572872 | tf_op jit(solution)/shard_map/ppermute | solution.py:454
  53.0 15.6 %collective-permute-start.4 = (bf16[144,1024]{1,0:T(8,128)(2,1)}, bf16[144,1024]{1,0:T(8,128)(2,1)}, u32[]{:S(2)}, u32[]{:S(2)}) collective-permute-start(bf16[144,1024]{1,0:T(8,128)(2,1)} %get-tuple-element.70.refs_1_), channel_id=1, source_target_pairs={{0,1},{1,0},{2,3},{3,2},{4,5},{5,4},{6,7},{7,6},{8,9},{9,8},{10,11... | collective-permute-start | bytes 884744 | tf_op jit(solution)/shard_map/ppermute | solution.py:454
  58.0 22.5 %collective-permute-start.13 = (bf16[288,1024]{1,0:T(8,128)(2,1)}, bf16[288,1024]{1,0:T(8,128)(2,1)S(1)}, u32[]{:S(2)}, u32[]{:S(2)}) collective-permute-start(bf16[288,1024]{1,0:T(8,128)(2,1)} %get-tuple-element.87), channel_id=1, source_target_pairs={{0,2},{2,0},{1,3},{3,1},{4,6},{6,4},{5,7},{7,5},{8,10},{10,8},{9,1... | collective-permute-start | bytes 1769480 | tf_op jit(solution)/shard_map/ppermute | solution.py:454
  81.3 2.2 %collective-permute-start.14 = (bf16[288,1024]{1,0:T(8,128)(2,1)}, bf16[288,1024]{1,0:T(8,128)(2,1)S(1)}, u32[]{:S(2)}, u32[]{:S(2)}) collective-permute-start(bf16[288,1024]{1,0:T(8,128)(2,1)} %get-tuple-element.88.here), channel_id=1, source_target_pairs={{0,1},{1,0},{2,3},{3,2},{4,5},{5,4},{6,7},{7,6},{8,9},{9,8},{10,11... | collective-permute-start | bytes 1769480 | tf_op jit(solution)/shard_map/ppermute | solution.py:454
  81.3 16.0 %collective-permute-start.12 = (bf16[288,1024]{1,0:T(8,128)(2,1)}, bf16[288,1024]{1,0:T(8,128)(2,1)S(1)}, u32[]{:S(2)}, u32[]{:S(2)}) collective-permute-start(bf16[288,1024]{1,0:T(8,128)(2,1)} %get-tuple-element.85.refs_3_), channel_id=1, source_target_pairs={{0,2},{2,0},{1,3},{3,1},{4,6},{6,4},{5,7},{7,5},{8,10},{10,8},{9,1... | collective-permute-start | bytes 1769480 | tf_op jit(solution)/shard_map/ppermute | solution.py:454
  99.0 2.2 %collective-permute-start.15 = (bf16[288,256]{1,0:T(8,128)(2,1)S(1)}, bf16[288,256]{1,0:T(8,128)(2,1)S(1)}, u32[]{:S(2)}, u32[]{:S(2)}) collective-permute-start(bf16[288,256]{1,0:T(8,128)(2,1)S(1)} %slice.36), channel_id=1, source_target_pairs={{0,1},{1,0},{2,3},{3,2},{4,5},{5,4},{6,7},{7,6},{8,9},{9,8},{10,11... | collective-permute-start | bytes 442376 | tf_op jit(solution)/shard_map/ppermute | solution.py:454
  99.1 10.1 %collective-permute-start.16 = (bf16[144,1024]{1,0:T(8,128)(2,1)}, bf16[144,1024]{1,0:T(8,128)(2,1)S(1)}, u32[]{:S(2)}, u32[]{:S(2)}) collective-permute-start(bf16[144,1024]{1,0:T(8,128)(2,1)} %get-tuple-element.94), channel_id=1, source_target_pairs={{0,2},{2,0},{1,3},{3,1},{4,6},{6,4},{5,7},{7,5},{8,10},{10,8},{9,1... | collective-permute-start | bytes 884744 | tf_op jit(solution)/shard_map/ppermute | solution.py:454
  100.7 24.3 %collective-permute-start.17 = (bf16[288,1280]{1,0:T(8,128)(2,1)}, bf16[288,1280]{1,0:T(8,128)(2,1)S(1)}, u32[]{:S(2)}, u32[]{:S(2)}) collective-permute-start(bf16[288,1280]{1,0:T(8,128)(2,1)} %get-tuple-element.96.refs_3_), channel_id=1, source_target_pairs={{0,2},{2,0},{1,3},{3,1},{4,6},{6,4},{5,7},{7,5},{8,10},{10,8},{9,1... | collective-permute-start | bytes 2211848 | tf_op jit(solution)/shard_map/ppermute | solution.py:454
  105.1 14.2 %collective-permute-start.19 = (bf16[256,768]{1,0:T(8,128)(2,1)}, bf16[256,768]{1,0:T(8,128)(2,1)S(1)}, u32[]{:S(2)}, u32[]{:S(2)}) collective-permute-start(bf16[256,768]{1,0:T(8,128)(2,1)} %get-tuple-element.100), channel_id=1, source_target_pairs={{0,4},{4,0},{8,12},{12,8},{1,5},{5,1},{9,13},{13,9},{2,6},{6,2},{1... | collective-permute-start | bytes 1179656 | tf_op jit(solution)/shard_map/ppermute | solution.py:520
  109.9 8.8 %copy-start.2 = (bf16[288,1024]{1,0:T(8,128)(2,1)S(1)}, bf16[288,1024]{1,0:T(8,128)(2,1)}, u32[]{:S(2)}) copy-start(bf16[288,1024]{1,0:T(8,128)(2,1)} %get-tuple-element.98.refs_6_.refs_3_.refs_1_) | copy-start | bytes 1769476
  109.9 8.9 %copy-start.23 = (bf16[288,1024]{1,0:T(8,128)(2,1)S(1)}, bf16[288,1024]{1,0:T(8,128)(2,1)}, u32[]{:S(2)}) copy-start(bf16[288,1024]{1,0:T(8,128)(2,1)} %get-tuple-element.81) | copy-start | bytes 1769476
  109.9 9.4 %copy-start.28 = (f32[128,768]{1,0:T(8,128)S(1)}, f32[128,768]{1,0:T(8,128)}, u32[]{:S(2)}) copy-start(f32[128,768]{1,0:T(8,128)} %get-tuple-element.107) | copy-start | bytes 1179652
  117.2 32.4 %collective-permute-start.20 = (bf16[288,1280]{1,0:T(8,128)(2,1)}, bf16[288,1280]{1,0:T(8,128)(2,1)S(1)}, u32[]{:S(2)}, u32[]{:S(2)}) collective-permute-start(bf16[288,1280]{1,0:T(8,128)(2,1)} %get-tuple-element.103), channel_id=1, source_target_pairs={{0,2},{2,0},{1,3},{3,1},{4,6},{6,4},{5,7},{7,5},{8,10},{10,8},{9,1... | collective-permute-start | bytes 2211848 | tf_op jit(solution)/shard_map/ppermute | solution.py:454
  118.7 1.6 collective-permute-start.18
  118.8 39.9 %collective-permute-start.11 = (bf16[288,1024]{1,0:T(8,128)(2,1)S(1)}, bf16[288,1024]{1,0:T(8,128)(2,1)S(1)}, u32[]{:S(2)}, u32[]{:S(2)}) collective-permute-start(bf16[288,1024]{1,0:T(8,128)(2,1)S(1)} %copy-done.23), channel_id=1, source_target_pairs={{0,1},{1,0},{2,3},{3,2},{4,5},{5,4},{6,7},{7,6},{8,9},{9,8},{10,11... | collective-permute-start | bytes 1769480 | tf_op jit(solution)/shard_map/ppermute | solution.py:454
  119.3 5.7 %copy-start.7 = (bf16[256,768]{1,0:T(8,128)(2,1)}, bf16[256,768]{1,0:T(8,128)(2,1)S(1)}, u32[]{:S(2)}) copy-start(bf16[256,768]{1,0:T(8,128)(2,1)S(1)} %collective-permute-done.19.refs_9_) | copy-start | bytes 1179652
  125.8 8.5 %copy-start.26 = (bf16[288,768]{1,0:T(8,128)(2,1)S(1)}, bf16[288,768]{1,0:T(8,128)(2,1)}, u32[]{:S(2)}) copy-start(bf16[288,768]{1,0:T(8,128)(2,1)} %get-tuple-element.113.refs_3_) | copy-start | bytes 1327108
  130.6 28.1 %copy-start.8 = (bf16[288,1024]{1,0:T(8,128)(2,1)S(1)}, bf16[288,1024]{1,0:T(8,128)(2,1)}, u32[]{:S(2)}) copy-start(bf16[288,1024]{1,0:T(8,128)(2,1)} %get-tuple-element.80.joined) | copy-start | bytes 1769476
  130.6 32.6 %collective-permute-start.22 = (bf16[256,1280]{1,0:T(8,128)(2,1)}, bf16[256,1280]{1,0:T(8,128)(2,1)S(1)}, u32[]{:S(2)}, u32[]{:S(2)}) collective-permute-start(bf16[256,1280]{1,0:T(8,128)(2,1)} %get-tuple-element.111), channel_id=1, source_target_pairs={{0,4},{4,0},{8,12},{12,8},{1,5},{5,1},{9,13},{13,9},{2,6},{6,2},{1... | collective-permute-start | bytes 1966088 | tf_op jit(solution)/shard_map/ppermute | solution.py:520
  131.8 17.8 %collective-permute-start.21 = (bf16[128,768]{1,0:T(8,128)(2,1)S(1)}, bf16[128,768]{1,0:T(8,128)(2,1)S(1)}, u32[]{:S(2)}, u32[]{:S(2)}) collective-permute-start(bf16[128,768]{1,0:T(8,128)(2,1)S(1)} %add_convert_fusion.4), channel_id=1, source_target_pairs={{0,8},{4,12},{8,0},{12,4},{1,9},{5,13},{9,1},{13,5},{2,10},{6,14},... | collective-permute-start | bytes 589832 | tf_op jit(solution)/shard_map/ppermute | solution.py:522
  134.3 24.7 %collective-permute-start.24 = (bf16[288,768]{1,0:T(8,128)(2,1)S(1)}, bf16[288,768]{1,0:T(8,128)(2,1)S(1)}, u32[]{:S(2)}, u32[]{:S(2)}) collective-permute-start(bf16[288,768]{1,0:T(8,128)(2,1)S(1)} %copy-done.26), channel_id=1, source_target_pairs={{0,2},{2,0},{1,3},{3,1},{4,6},{6,4},{5,7},{7,5},{8,10},{10,8},{9,1... | collective-permute-start | bytes 1327112 | tf_op jit(solution)/shard_map/ppermute | solution.py:454
  154.8 8.4 %copy-start.21 = (f32[128,1280]{1,0:T(8,128)S(1)}, f32[128,1280]{1,0:T(8,128)}, u32[]{:S(2)}) copy-start(f32[128,1280]{1,0:T(8,128)} %get-tuple-element.112) | copy-start | bytes 1966084
  154.8 28.0 %collective-permute-start.25 = (bf16[256,1280]{1,0:T(8,128)(2,1)}, bf16[256,1280]{1,0:T(8,128)(2,1)S(1)}, u32[]{:S(2)}, u32[]{:S(2)}) collective-permute-start(bf16[256,1280]{1,0:T(8,128)(2,1)} %get-tuple-element.116), channel_id=1, source_target_pairs={{0,4},{4,0},{8,12},{12,8},{1,5},{5,1},{9,13},{13,9},{2,6},{6,2},{1... | collective-permute-start | bytes 1966088 | tf_op jit(solution)/shard_map/ppermute | solution.py:520
  159.0 23.8 %copy-start.22 = (f32[128,1280]{1,0:T(8,128)S(1)}, f32[128,1280]{1,0:T(8,128)}, u32[]{:S(2)}) copy-start(f32[128,1280]{1,0:T(8,128)} %get-tuple-element.117) | copy-start | bytes 1966084
  163.2 26.2 %copy-start.29 = (f32[128,768]{1,0:T(8,128)S(1)}, f32[128,768]{1,0:T(8,128)}, u32[]{:S(2)}) copy-start(f32[128,768]{1,0:T(8,128)} %get-tuple-element.120) | copy-start | bytes 1179652
  163.2 26.2 %collective-permute-start.27 = (bf16[256,768]{1,0:T(8,128)(2,1)}, bf16[256,768]{1,0:T(8,128)(2,1)S(1)}, u32[]{:S(2)}, u32[]{:S(2)}) collective-permute-start(bf16[256,768]{1,0:T(8,128)(2,1)} %get-tuple-element.119), channel_id=1, source_target_pairs={{0,4},{4,0},{8,12},{12,8},{1,5},{5,1},{9,13},{13,9},{2,6},{6,2},{1... | collective-permute-start | bytes 1179656 | tf_op jit(solution)/shard_map/ppermute | solution.py:520
  163.2 26.6 %copy-start.15 = (bf16[256,1280]{1,0:T(8,128)(2,1)}, bf16[256,1280]{1,0:T(8,128)(2,1)S(1)}, u32[]{:S(2)}) copy-start(bf16[256,1280]{1,0:T(8,128)(2,1)S(1)} %collective-permute-done.22.refs_4_) | copy-start | bytes 1966084
  163.3 27.4 %collective-permute-start.23 = (bf16[128,1280]{1,0:T(8,128)(2,1)S(1)}, bf16[128,1280]{1,0:T(8,128)(2,1)S(1)}, u32[]{:S(2)}, u32[]{:S(2)}) collective-permute-start(bf16[128,1280]{1,0:T(8,128)(2,1)S(1)} %add_convert_fusion.2), channel_id=1, source_target_pairs={{0,8},{4,12},{8,0},{12,4},{1,9},{5,13},{9,1},{13,5},{2,10},{6,14},... | collective-permute-start | bytes 983048 | tf_op jit(solution)/shard_map/ppermute | solution.py:522
  182.8 7.9 %copy-start.16 = (bf16[256,1280]{1,0:T(8,128)(2,1)}, bf16[256,1280]{1,0:T(8,128)(2,1)S(1)}, u32[]{:S(2)}) copy-start(bf16[256,1280]{1,0:T(8,128)(2,1)S(1)} %collective-permute-done.25.refs_1_) | copy-start | bytes 1966084
  182.9 26.0 %collective-permute-start.26 = (bf16[128,1280]{1,0:T(8,128)(2,1)S(1)}, bf16[128,1280]{1,0:T(8,128)(2,1)S(1)}, u32[]{:S(2)}, u32[]{:S(2)}) collective-permute-start(bf16[128,1280]{1,0:T(8,128)(2,1)S(1)} %add_convert_fusion.1), channel_id=1, source_target_pairs={{0,8},{4,12},{8,0},{12,4},{1,9},{5,13},{9,1},{13,5},{2,10},{6,14},... | collective-permute-start | bytes 983048 | tf_op jit(solution)/shard_map/ppermute | solution.py:522
  189.5 19.4 %collective-permute-start.28 = (bf16[128,768]{1,0:T(8,128)(2,1)S(1)}, bf16[128,768]{1,0:T(8,128)(2,1)S(1)}, u32[]{:S(2)}, u32[]{:S(2)}) collective-permute-start(bf16[128,768]{1,0:T(8,128)(2,1)S(1)} %add_convert_fusion.3), channel_id=1, source_target_pairs={{0,8},{4,12},{8,0},{12,4},{1,9},{5,13},{9,1},{13,5},{2,10},{6,14},... | collective-permute-start | bytes 589832 | tf_op jit(solution)/shard_map/ppermute | solution.py:522
  (20 other events, 25.5 us)

commit v6 on v5

--- a/solution.py
+++ b/solution.py
@@ -246,9 +246,9 @@
         partial[:, features] = dot(mixed[...], part[...], NT).astype(BF)
     if plan.paired:
         own_hidden, sent, last = grads
-        half = hidden.shape[1] // 4
+        half = hidden.shape[1] // 2
         emit_own(hidden, own_hidden, 0, where[0], plan.locs)
-        emit_half(hidden, sent, 0, 1 - where[0], where[1], plan.locs)
+        emit_own(hidden, sent, 0, 1 - where[0], plan.locs)
     else:
         grads[0][...] = hidden[...]
     attention_back(triple, attend, back_mixed, back_triple, plan.blocks)
@@ -460,7 +460,7 @@
 
 def quarter_of(weights, number):
     rows = weights.shape[0]
-    return lax.dynamic_slice_in_dim(weights, number * (rows // 4), rows // 4, 0)
+    return by_kind(lax.dynamic_slice_in_dim(weights, number * (rows // 4), rows // 4, 0))
 
 
 def by_kind(weights):
@@ -478,9 +478,8 @@
 
 
 def gather_weights(weights, first, last):
-    arrays = [weights, first, swap(first, "groups"), lax.ppermute(first, "loc", PAIRS), swap(last, "date")]
-    table = {kind: [(number, kind, number) for number in range(5)] for kind in range(4)}
-    return Weights([by_kind(array) for array in arrays], table)
+    arrays = [by_kind(weights), first, swap(first, "groups"), lax.ppermute(first, "loc", PAIRS), last]
+    return Weights(arrays, {kind: [(number, kind, number) for number in range(5)] for kind in range(4)})
 
 
 def add_over_heads(partial, sizes):
@@ -642,7 +641,7 @@
         last_sent = quarter_of(spatial_weights, last_quarter)
         last_sent, own_start = fence(last_sent, own_start)
         origins = (own_start, other_start)
-        spatial = gather_weights(spatial_weights, swap(first_sent, "date"), last_sent)
+        spatial = gather_weights(spatial_weights, swap(first_sent, "date"), swap(last_sent, "date"))
         sent = [quarter_of(temporal_weights, number) for number in (first_quarter, last_quarter)]
         *sent, cotangent_rows = fence(*sent, cotangent_rows)
         temporal_first = swap(sent[0], "date")
@@ -662,7 +661,7 @@
         forward_grads = (own, own, shape(rows, 2 * quarter + width))
         temporal_grads = (
             own,
-            shape(rows, quarter + 3 * width // 2),
+            shape(rows, model // 2 + 3 * width // 2),
             shape(rows, 3 * width // 2 + width),
         )
         back_shapes = (shape(rows, 3 * width // 2), shape(rows, 3 * width // 2))
@@ -703,14 +702,14 @@
     if paired:
         temporal_first, kept = fence(temporal_first, partials[1])
         partials = (partials[0], kept)
-        temporal = gather_weights(temporal_weights, temporal_first, sent[1])
         there, early = call(
             between_kernel,
             (shape(half, model),),
             (origins[1], partials[1], swap(partials[1], "mp"), forward[2]),
             kept=(3,),
         )
-        early, there = fence(early, swap(there, "date"))
+        temporal = gather_weights(temporal_weights, temporal_first, swap(sent[1], "date"))
+        early, there, *temporal.arrays[2:] = fence(early, swap(there, "date"), *temporal.arrays[2:])
         sources = (origins[0], partials[0], swap(partials[0], "mp"), there)
         early_other = swap(early, "date")
     else:
@@ -778,15 +777,12 @@
     if paired:
         back_origins = (backs[0], swap(backs[1], "date"))
         early_there = swap(early_other[:, : 2 * quarter], "mp")
-        middle_other, back_own = fence(swap(middle[1], "date"), backs[0])
-        back_origins = (back_own, back_origins[1])
-        middle_there = swap(middle_other[:, :quarter], "mp")
-        part = 3 * width // 2
-        others = ((1, 0), (2, 0))
+        middle_other = swap(middle[1], "date")
+        part, columns = 3 * width // 2, model // 2
         *intake, kept = summed(
             where,
-            (middle[0], middle_other, middle_there, middle[1]),
-            ((0, others, (3, quarter), (1, quarter), part),),
+            (middle[0], middle_other, middle[1]),
+            ((0, ((1, 0),), (2, columns), (1, columns), part),),
         )
     else:
         back = lax.all_to_all(
@@ -821,17 +817,17 @@
     last_other = swap(last_sent, "date")
     *sums, upstream_own, intake[1] = summed(
         where,
-        (middle[0], middle_other, middle_there, last_sent, last_other, forward[1], early_other, early_there),
+        (middle[0], middle_other, last_sent, last_other, forward[1], early_other, early_there),
         (
-            (0, others, (3, 0), (4, 0), part),
-            (5, ((6, quarter), (7, quarter)), (3, part), (4, part), width),
+            (0, ((1, 0),), (2, 0), (3, 0), part),
+            (4, ((5, quarter), (6, quarter)), (2, part), (3, part), width),
         ),
         kept=(backward[0], intake[1]),
     )
     outlet = [*summed_over_loc(sums)]
     half = model // 2
     backward_other = swap(backward[1], "date")
-    *sums, intake[2], outlet[0] = summed(
+    *sums, outlet[0] = summed(
         where,
         (
             upstream_own,
@@ -846,7 +842,7 @@
             (0, ((1, 0),), (2, 0), (3, 2 * quarter), width),
             (4, ((3, 0), (5, 0)), (6, 0), (1, half), back_triples[0].shape[1]),
         ),
-        kept=(intake[2], outlet[0]),
+        kept=(outlet[0],),
     )
     spatial_terms = [*summed_over_loc(sums)]
     sums = summed(

time: 213 us -> 201 us (0.944)
  local copies, waits for them, and re-layouts: 25 us -> 18.4 us
  starting transfers between devices: 32.4 us -> 29.4 us
  waiting for transfers between devices: 95.8 us -> 93.3 us
    ppermute x4, waiting for transfers between devices: 28.1 us -> 12.7 us  [summed_over_loc(): return (near, beside, lax.ppermute(far, 'loc', APART))]
    ppermute x19 -> x18, waiting for transfers between devices: 42.1 us -> 53 us  [swap(): return lax.ppermute(array, axis, [(0, 1), (1, 0)])]
    dynamic_slice x3 -> x0, local copies, waits for them, and re-layouts: 5.5 us -> none  [quarter_of(): return lax.dynamic_slice_in_dim(weights, number * (rows // 4), rows // 4, 0)]
    ppermute x19 -> x18, starting transfers between devices: 18.3 us -> 15.3 us  [swap(): return lax.ppermute(array, axis, [(0, 1), (1, 0)])]
    transpose x0 -> x2, local copies, waits for them, and re-layouts: none -> 2.33 us  [by_kind(): return weights.transpose(1, 0, 2)]
    unnamed x80 -> x78, local copies, waits for them, and re-layouts: 14.7 us -> 14.4 us
  transfers between devices with their start and end apart: 29 -> 28, of which waited for: 16 -> 17; matrix products, arithmetic and copies ran while one was open for 5% -> 3% of each run, Pallas kernels for 25% -> 27%
where the time goes in v6:
time: 201 us
  waiting for transfers between devices  93.3 us (46%)
  Pallas kernels  57.2 us (28%)
  starting transfers between devices  29.4 us (15%)
  local copies, waits for them, and re-layouts  18.4 us (9%)
    pallas_call x12, Pallas kernels, call(): pl.pallas_call(body, out_shape=outs, in_specs=specs, out_specs=out_specs,...  57.2 us
    ppermute x18, waiting for transfers between devices, swap(): return lax.ppermute(array, axis, [(0, 1), (1, 0)])  53 us
    ppermute x4, waiting for transfers between devices, summed_over_loc(): beside = lax.ppermute(sent, 'loc', PAIRS)  25.4 us
    ppermute x18, starting transfers between devices, swap(): return lax.ppermute(array, axis, [(0, 1), (1, 0)])  15.3 us
    unnamed x78, local copies, waits for them, and re-layouts  14.4 us
    ppermute x4, waiting for transfers between devices, summed_over_loc(): return (near, beside, lax.ppermute(far, 'loc', APART))  12.7 us
    ppermute x4, starting transfers between devices, summed_over_loc(): beside = lax.ppermute(sent, 'loc', PAIRS)  5.21 us
    ppermute x4, starting transfers between devices, summed_over_loc(): return (near, beside, lax.ppermute(far, 'loc', APART))  5.11 us
  transfers between devices with their start and end apart: 28, of which 17 were waited for; matrix products, arithmetic and copies ran while one was open for 3% of the time, Pallas kernels for 27%

profile of v6, /device:TPU:0, one launch (start us, length us, event | category | flops | bytes accessed | tf_op | source)
XLA Modules:
  0.0 200.5 jit_solution(15755740712224880336)
XLA Ops:
  0.7 2.0 copy.55
  2.7 1.2 dynamic-slice_bitcast_fusion
  3.9 2.9 %collective-permute-start = (bf16[4,128,512]{2,1,0:T(8,128)(2,1)}, bf16[4,128,512]{2,1,0:T(8,128)(2,1)S(1)}, u32[]{:S(2)}, u32[]{:S(2)}) collective-permute-start(bf16[4,128,512]{2,1,0:T(8,128)(2,1)} %get-tuple-element.125), channel_id=1, source_target_pairs={{0,2},{2,0},{1,3},{3,1},{4,6},{6,4},{5,7},{7,5},{8,10},{10,8},{9,1... | collective-permute-start | bytes 1572872 | tf_op jit(solution)/shard_map/ppermute | solution.py:454
  7.4 3.1 %shard_map.139 = (bf16[144,1024]{1,0:T(8,128)(2,1)}, bf16[144,1024]{1,0:T(8,128)(2,1)}, bf16[288,1024]{1,0:T(8,128)(2,1)}, f32[12,1024]{1,0:T(8,128)}) custom-call(s32[1,12]{1,0:T(1,128)} %cloud.1, s32[1,12]{1,0:T(1,128)} %drop.1, s32[1,48]{1,0:T(1,128)} %keep.1, s32[4]{0:T(128)} %pad_add_fusion.where, bf16[6,48,1024]{2,1,0:T(8,128)(2,1)} %bitcast.47, ...), custom_call_target="tpu_custom_call" | custom-call | bytes 3424560 | tf_op jit(solution)/shard_map/pallas_call | solution.py:430
  10.6 2.0 copy.56
  12.6 7.2 %collective-permute-done.refs_3_ = bf16[4,128,512]{2,1,0:T(8,128)(2,1)S(1)} collective-permute-done((bf16[4,128,512]{2,1,0:T(8,128)(2,1)}, bf16[4,128,512]{2,1,0:T(8,128)(2,1)S(1)}, u32[]{:S(2)}, u32[]{:S(2)}) %collective-permute-start) | collective-permute-done | bytes 524320 | tf_op jit(solution)/shard_map/ppermute | solution.py:454
  19.8 2.1 %collective-permute-start.2 = (bf16[4,128,512]{2,1,0:T(8,128)(2,1)S(1)}, bf16[4,128,512]{2,1,0:T(8,128)(2,1)}, u32[]{:S(2)}, u32[]{:S(2)}) collective-permute-start(bf16[4,128,512]{2,1,0:T(8,128)(2,1)S(1)} %collective-permute-done.refs_3_), channel_id=1, source_target_pairs={{0,4},{4,0},{8,12},{12,8},{1,5},{5,1},{9,13},{13,9},{2,6},{6,2},{1... | collective-permute-start | bytes 1572872 | tf_op jit(solution)/shard_map/ppermute | solution.py:481
  22.0 1.5 collective-permute-start.1
  23.5 1.1 dynamic-slice_bitcast_fusion.2
  24.6 1.5 collective-permute-start.5
  26.1 5.0 %collective-permute-done.3.refs_6_ = bf16[4,128,512]{2,1,0:T(8,128)(2,1)S(1)} collective-permute-done((bf16[4,128,512]{2,1,0:T(8,128)(2,1)}, bf16[4,128,512]{2,1,0:T(8,128)(2,1)S(1)}, u32[]{:S(2)}, u32[]{:S(2)}) %collective-permute-start.3) | collective-permute-done | bytes 524320 | tf_op jit(solution)/shard_map/ppermute | solution.py:454
  31.0 1.2 collective-permute-done.2.refs_5_
  32.2 1.2 collective-permute-done.1.refs_4_
  33.4 8.0 %shard_map.142 = (bf16[144,1024]{1,0:T(8,128)(2,1)}, bf16[144,1024]{1,0:T(8,128)(2,1)}, bf16[288,512]{1,0:T(8,128)(2,1)}, bf16[288,512]{1,0:T(8,128)(2,1)}, bf16...) custom-call(s32[4]{0:T(128)} %pad_add_fusion.where, ...), custom_call_target="tpu_custom_call" | custom-call | flops 1207959552 | bytes 9211920 | tf_op jit(solution)/shard_map/pallas_call | solution.py:430
  42.3 1.7 collective-permute-start.10
  44.0 1.6 collective-permute-start.9
  45.6 1.5 collective-permute-start.8
  47.8 2.0 shard_map.144
  50.4 6.8 %collective-permute-done.10.refs_4_ = bf16[4,128,512]{2,1,0:T(8,128)(2,1)S(1)} collective-permute-done((bf16[4,128,512]{2,1,0:T(8,128)(2,1)}, bf16[4,128,512]{2,1,0:T(8,128)(2,1)S(1)}, u32[]{:S(2)}, u32[]{:S(2)}) %collective-permute-start.10) | collective-permute-done | bytes 524320 | tf_op jit(solution)/shard_map/ppermute | solution.py:454
  57.2 1.1 collective-permute-done.9.refs_3_
  58.3 1.3 collective-permute-done.8.refs_2_
  59.6 3.6 %collective-permute-done.7.refs_1_ = bf16[144,1024]{1,0:T(8,128)(2,1)S(1)} collective-permute-done((bf16[144,1024]{1,0:T(8,128)(2,1)}, bf16[144,1024]{1,0:T(8,128)(2,1)S(1)}, u32[]{:S(2)}, u32[]{:S(2)}) %collective-permute-start.7) | collective-permute-done | bytes 294944 | tf_op jit(solution)/shard_map/ppermute | solution.py:454
  63.8 1.7 collective-permute-start.13
  67.2 12.0 %shard_map.146 = (bf16[288,512]{1,0:T(8,128)(2,1)}, bf16[288,1280]{1,0:T(8,128)(2,1)}, bf16[288,1280]{1,0:T(8,128)(2,1)}, bf16[288,1024]{1,0:T(8,128)(2,1)}, bf1...) custom-call(s32[4]{0:T(128)} %pad_add_fusion.where, f32[1,1024]{1,0:T(1,128)} %bitcast.52, ...), custom_call_target="tpu_custom_call" | custom-call | flops 2415919104 | bytes 9851280 | tf_op jit(solution)/shard_map/pallas_call | solution.py:430
  80.3 2.2 %collective-permute-done.14.there = bf16[288,1024]{1,0:T(8,128)(2,1)S(1)} collective-permute-done((bf16[288,1024]{1,0:T(8,128)(2,1)}, bf16[288,1024]{1,0:T(8,128)(2,1)S(1)}, u32[]{:S(2)}, u32[]{:S(2)}) %collective-permute-start.14) | collective-permute-done | bytes 589856 | tf_op jit(solution)/shard_map/ppermute | solution.py:454
  83.4 3.3 %shard_map.149 = (bf16[144,1024]{1,0:T(8,128)(2,1)}, bf16[144,1024]{1,0:T(8,128)(2,1)}, bf16[288,1280]{1,0:T(8,128)(2,1)}) custom-call(f32[1,1024]{1,0:T(1,128)} %bitcast.53, bf16[288,1024]{1,0:T(8,128)(2,1)} %get-tuple-element.92.here, bf16[288,1024]{1,0:T(8,128)(2,1)} %copy-done.18, ...), custom_call_target="tpu_custom_call", output_to_operand_aliasing={{2}: (5, {})} | custom-call | bytes 3690496 | tf_op jit(solution)/shard_map/pallas_call | solution.py:430
  86.6 1.7 collective-permute-start.15
  88.7 10.2 %collective-permute-done.12.refs_1_ = bf16[288,1280]{1,0:T(8,128)(2,1)S(1)} collective-permute-done((bf16[288,1280]{1,0:T(8,128)(2,1)}, bf16[288,1280]{1,0:T(8,128)(2,1)S(1)}, u32[]{:S(2)}, u32[]{:S(2)}) %collective-permute-start.12) | collective-permute-done | bytes 737312 | tf_op jit(solution)/shard_map/ppermute | solution.py:454
  98.8 0.9 copy-done.4
  99.7 3.3 %shard_map.147 = (bf16[256,768]{1,0:T(8,128)(2,1)}, f32[128,768]{1,0:T(8,128)}, f32[128,768]{1,0:T(8,128)}) custom-call(s32[4]{0:T(128)} %pad_add_fusion.where, bf16[288,512]{1,0:T(8,128)(2,1)} %get-tuple-element.87.refs_0_, bf16[288,1280]{1,0:T(8,128)(2,1)} %copy-done.4, bf16[288,1280]{1,0:T(8,128)(2,1)} %get-tuple-element.88.refs_2_), custom_call_target="tpu_custom_call" | custom-call | flops 452984832 | bytes 2949136 | tf_op jit(solution)/shard_map/pallas_call | solution.py:430
  103.0 1.6 collective-permute-start.18
  105.9 7.3 %shard_map.150 = (bf16[288,512]{1,0:T(8,128)(2,1)}, bf16[288,1280]{1,0:T(8,128)(2,1)}, bf16[288,768]{1,0:T(8,128)(2,1)}, bf16[288,768]{1,0:T(8,128)(2,1)}, f32[128,768]{1,0:T(8,128)}) custom-call(s32[4]{0:T(128)} %pad_add_fusion.where, bf16[288,1536]{1,0:T(8,128)(2,1)} %get-tuple-element.85.triple, ...), custom_call_target="tpu_custom_call", output_to_operand_aliasing={{4}: (3, {})} | custom-call | flops 1207959552 | bytes 8863760 | tf_op jit(solution)/shard_map/pallas_call | solution.py:430
  114.1 1.0 collective-permute-done.17.refs_6_.refs_5_.refs_2_
  115.1 5.8 %collective-permute-done.16.refs_3_ = bf16[288,1280]{1,0:T(8,128)(2,1)S(1)} collective-permute-done((bf16[288,1280]{1,0:T(8,128)(2,1)}, bf16[288,1280]{1,0:T(8,128)(2,1)S(1)}, u32[]{:S(2)}, u32[]{:S(2)}) %collective-permute-start.16) | collective-permute-done | bytes 737312 | tf_op jit(solution)/shard_map/ppermute | solution.py:454
  121.8 4.7 %shard_map.151 = (bf16[256,1280]{1,0:T(8,128)(2,1)}, f32[128,1280]{1,0:T(8,128)}, f32[128,1280]{1,0:T(8,128)}, bf16[288,512]{1,0:T(8,128)(2,1)}, bf16[256,768]{1,0:T(8,128)(2,1)}) custom-call(s32[4]{0:T(128)} %pad_add_fusion.where, bf16[288,512]{1,0:T(8,128)(2,1)} %get-tuple-element.87.refs_0_, ...), custom_call_target="tpu_custom_call", output_to_operand_aliasing={{3}: (8, {}), {4}: (9, {})} | custom-call | flops 754974720 | bytes 6340624 | tf_op jit(solution)/shard_map/pallas_call | solution.py:430
  126.6 1.6 collective-permute-start.21
  128.7 8.1 %collective-permute-done.20.refs_1_ = bf16[288,1280]{1,0:T(8,128)(2,1)S(1)} collective-permute-done((bf16[288,1280]{1,0:T(8,128)(2,1)}, bf16[288,1280]{1,0:T(8,128)(2,1)S(1)}, u32[]{:S(2)}, u32[]{:S(2)}) %collective-permute-start.20) | collective-permute-done | bytes 737312 | tf_op jit(solution)/shard_map/ppermute | solution.py:454
  137.6 4.3 %shard_map.152 = (bf16[256,1280]{1,0:T(8,128)(2,1)}, f32[128,1280]{1,0:T(8,128)}, f32[128,1280]{1,0:T(8,128)}, f32[128,1280]{1,0:T(8,128)}) custom-call(s32[4]{0:T(128)} %pad_add_fusion.where, bf16[288,512]{1,0:T(8,128)(2,1)} %get-tuple-element.104.refs_0_, bf16[288,1280]{1,0:T(8,128)(2,1)} %copy-done.14, ...), custom_call_target="tpu_custom_call", output_to_operand_aliasing={{3}: (8, {})} | custom-call | flops 754974720 | bytes 5570576 | tf_op jit(solution)/shard_map/pallas_call | solution.py:430
  142.0 1.6 collective-permute-start.24
  143.9 2.6 %collective-permute-start.19 = (bf16[128,768]{1,0:T(8,128)(2,1)S(1)}, bf16[128,768]{1,0:T(8,128)(2,1)S(1)}, u32[]{:S(2)}, u32[]{:S(2)}) collective-permute-start(bf16[128,768]{1,0:T(8,128)(2,1)S(1)} %add_convert_fusion.4), channel_id=1, source_target_pairs={{0,8},{4,12},{8,0},{12,4},{1,9},{5,13},{9,1},{13,5},{2,10},{6,14},... | collective-permute-start | bytes 589832 | tf_op jit(solution)/shard_map/ppermute | solution.py:521
  147.3 3.4 %shard_map.154 = (bf16[256,768]{1,0:T(8,128)(2,1)}, f32[128,768]{1,0:T(8,128)}, f32[128,768]{1,0:T(8,128)}, f32[128,1280]{1,0:T(8,128)}) custom-call(s32[4]{0:T(128)} %pad_add_fusion.where, bf16[288,512]{1,0:T(8,128)(2,1)} %get-tuple-element.107.refs_4_.refs_0_, ...), custom_call_target="tpu_custom_call", output_to_operand_aliasing={{3}: (6, {})} | custom-call | flops 452984832 | bytes 3899408 | tf_op jit(solution)/shard_map/pallas_call | solution.py:430
  151.2 1.9 collective-permute-start.22
  153.1 17.8 %collective-permute-done.24.refs_1_ = bf16[256,1280]{1,0:T(8,128)(2,1)S(1)} collective-permute-done((bf16[256,1280]{1,0:T(8,128)(2,1)}, bf16[256,1280]{1,0:T(8,128)(2,1)S(1)}, u32[]{:S(2)}, u32[]{:S(2)}) %collective-permute-start.24) | collective-permute-done | bytes 655392 | tf_op jit(solution)/shard_map/ppermute | solution.py:519
  171.1 7.6 %collective-permute-done.26.refs_4_ = bf16[256,768]{1,0:T(8,128)(2,1)S(1)} collective-permute-done((bf16[256,768]{1,0:T(8,128)(2,1)}, bf16[256,768]{1,0:T(8,128)(2,1)S(1)}, u32[]{:S(2)}, u32[]{:S(2)}) %collective-permute-start.26) | collective-permute-done | bytes 393248 | tf_op jit(solution)/shard_map/ppermute | solution.py:519
  179.3 0.9 copy.50
  181.0 3.0 %shard_map.153.kept = f32[128,4,512]{2,1,0:T(4,128)} custom-call(f32[128,768]{1,0:T(8,128)} %get-tuple-element.96.refs_0_, bf16[256,768]{1,0:T(8,128)(2,1)} %get-tuple-element.102.refs_1_, bf16[128,768]{1,0:T(8,128)(2,1)} %copy-done.32, f32[128,1280]{1,0:T(8,128)} %get-tuple-element.110.refs_3_, bf16[256,1280]{1,0:T(8,128)(2,1)} %copy-done.10, ...), custom_call_target="tpu_custom_call" | custom-call | bytes 3670016 | tf_op jit(solution)/shard_map/pallas_call | solution.py:430
  184.1 12.6 %collective-permute-done.27.refs_5_ = bf16[128,768]{1,0:T(8,128)(2,1)S(1)} collective-permute-done((bf16[128,768]{1,0:T(8,128)(2,1)S(1)}, bf16[128,768]{1,0:T(8,128)(2,1)S(1)}, u32[]{:S(2)}, u32[]{:S(2)}) %collective-permute-start.27) | collective-permute-done | bytes 196640 | tf_op jit(solution)/shard_map/ppermute | solution.py:521
  197.5 3.0 %shard_map.155 = (f32[128,4,512]{2,1,0:T(4,128)}, f32[128,4,512]{2,1,0:T(4,128)}) custom-call(f32[128,4,512]{2,1,0:T(4,128)} %shard_map.153.kept, f32[128,1280]{1,0:T(8,128)} %get-tuple-element.115.refs_0_, bf16[256,1280]{1,0:T(8,128)(2,1)} %copy-done.11, bf16[128,1280]{1,0:T(8,128)(2,1)} %copy-done.27, ...), custom_call_target="tpu_custom_call", output_to_operand_aliasing={{1}: (0, {})} | custom-call | bytes 4718592 | tf_op jit(solution)/shard_map/pallas_call | solution.py:430
  (119 shorter events, 15.9 us)
Async XLA Ops:
  2.7 7.8 %copy-start = (bf16[512,4,512]{2,0,1:T(8,128)(2,1)}, bf16[512,4,512]{2,0,1:T(8,128)(2,1)S(1)}, u32[]{:S(2)}) copy-start(bf16[512,4,512]{2,0,1:T(8,128)(2,1)S(1)} %copy.55) | copy-start | bytes 6291460
  3.9 15.9 %collective-permute-start = (bf16[4,128,512]{2,1,0:T(8,128)(2,1)}, bf16[4,128,512]{2,1,0:T(8,128)(2,1)S(1)}, u32[]{:S(2)}, u32[]{:S(2)}) collective-permute-start(bf16[4,128,512]{2,1,0:T(8,128)(2,1)} %get-tuple-element.125), channel_id=1, source_target_pairs={{0,2},{2,0},{1,3},{3,1},{4,6},{6,4},{5,7},{7,5},{8,10},{10,8},{9,1... | collective-permute-start | bytes 1572872 | tf_op jit(solution)/shard_map/ppermute | solution.py:454
  10.5 20.5 %collective-permute-start.3 = (bf16[4,128,512]{2,1,0:T(8,128)(2,1)}, bf16[4,128,512]{2,1,0:T(8,128)(2,1)S(1)}, u32[]{:S(2)}, u32[]{:S(2)}) collective-permute-start(bf16[4,128,512]{2,1,0:T(8,128)(2,1)} %get-tuple-element.69), channel_id=1, source_target_pairs={{0,2},{2,0},{1,3},{3,1},{4,6},{6,4},{5,7},{7,5},{8,10},{10,8},{9,1... | collective-permute-start | bytes 1572872 | tf_op jit(solution)/shard_map/ppermute | solution.py:454
  12.6 28.8 %copy-start.3 = (bf16[512,4,512]{2,0,1:T(8,128)(2,1)}, bf16[512,4,512]{2,0,1:T(8,128)(2,1)S(1)}, u32[]{:S(2)}) copy-start(bf16[512,4,512]{2,0,1:T(8,128)(2,1)S(1)} %copy.56) | copy-start | bytes 6291460
  19.8 13.6 %copy-start.8 = (bf16[4,128,512]{2,1,0:T(8,128)(2,1)}, bf16[4,128,512]{2,1,0:T(8,128)(2,1)S(1)}, u32[]{:S(2)}) copy-start(bf16[4,128,512]{2,1,0:T(8,128)(2,1)S(1)} %collective-permute-done.refs_3_) | copy-start | bytes 1572868
  19.8 12.4 %collective-permute-start.2 = (bf16[4,128,512]{2,1,0:T(8,128)(2,1)S(1)}, bf16[4,128,512]{2,1,0:T(8,128)(2,1)}, u32[]{:S(2)}, u32[]{:S(2)}) collective-permute-start(bf16[4,128,512]{2,1,0:T(8,128)(2,1)S(1)} %collective-permute-done.refs_3_), channel_id=1, source_target_pairs={{0,4},{4,0},{8,12},{12,8},{1,5},{5,1},{9,13},{13,9},{2,6},{6,2},{1... | collective-permute-start | bytes 1572872 | tf_op jit(solution)/shard_map/ppermute | solution.py:481
  22.0 11.5 %collective-permute-start.1 = (bf16[4,128,512]{2,1,0:T(8,128)(2,1)S(1)}, bf16[4,128,512]{2,1,0:T(8,128)(2,1)}, u32[]{:S(2)}, u32[]{:S(2)}) collective-permute-start(bf16[4,128,512]{2,1,0:T(8,128)(2,1)S(1)} %collective-permute-done.refs_3_), channel_id=1, source_target_pairs={{0,16},{16,0},{1,17},{17,1},{2,18},{18,2},{3,19},{19,3},{4,20},{20... | collective-permute-start | bytes 1572872 | tf_op jit(solution)/shard_map/ppermute | solution.py:454
  24.6 16.9 %collective-permute-start.5 = (bf16[4,128,512]{2,1,0:T(8,128)(2,1)}, bf16[4,128,512]{2,1,0:T(8,128)(2,1)S(1)}, u32[]{:S(2)}, u32[]{:S(2)}) collective-permute-start(bf16[4,128,512]{2,1,0:T(8,128)(2,1)} %get-tuple-element.71), channel_id=1, source_target_pairs={{0,2},{2,0},{1,3},{3,1},{4,6},{6,4},{5,7},{7,5},{8,10},{10,8},{9,1... | collective-permute-start | bytes 1572872 | tf_op jit(solution)/shard_map/ppermute | solution.py:454
  41.4 8.9 %copy-start.34 = (s32[1,12]{1,0:T(1,128)S(1)}, s32[1,12]{1,0:T(1,128)}, u32[]{:S(2)}) copy-start(s32[1,12]{1,0:T(1,128)} %cloud.1) | copy-start | bytes 148
  41.4 8.9 %copy-start.35 = (s32[1,12]{1,0:T(1,128)S(1)}, s32[1,12]{1,0:T(1,128)}, u32[]{:S(2)}) copy-start(s32[1,12]{1,0:T(1,128)} %drop.1) | copy-start | bytes 148
  41.4 8.9 %copy-start.36 = (bf16[144,1024]{1,0:T(8,128)(2,1)S(1)}, bf16[144,1024]{1,0:T(8,128)(2,1)}, u32[]{:S(2)}) copy-start(bf16[144,1024]{1,0:T(8,128)(2,1)} %get-tuple-element.70.refs_1_) | copy-start | bytes 884740
  42.3 4.8 %collective-permute-start.6 = (bf16[144,1024]{1,0:T(8,128)(2,1)}, bf16[144,1024]{1,0:T(8,128)(2,1)S(1)}, u32[]{:S(2)}, u32[]{:S(2)}) collective-permute-start(bf16[144,1024]{1,0:T(8,128)(2,1)} %get-tuple-element.73.here), channel_id=1, source_target_pairs={{0,1},{1,0},{2,3},{3,2},{4,5},{5,4},{6,7},{7,6},{8,9},{9,8},{10,11... | collective-permute-start | bytes 884744 | tf_op jit(solution)/shard_map/ppermute | solution.py:454
  42.3 14.9 %collective-permute-start.10 = (bf16[4,128,512]{2,1,0:T(8,128)(2,1)}, bf16[4,128,512]{2,1,0:T(8,128)(2,1)S(1)}, u32[]{:S(2)}, u32[]{:S(2)}) collective-permute-start(bf16[4,128,512]{2,1,0:T(8,128)(2,1)} %get-tuple-element.78), channel_id=1, source_target_pairs={{0,2},{2,0},{1,3},{3,1},{4,6},{6,4},{5,7},{7,5},{8,10},{10,8},{9,1... | collective-permute-start | bytes 1572872 | tf_op jit(solution)/shard_map/ppermute | solution.py:454
  44.0 14.3 %collective-permute-start.9 = (bf16[4,128,512]{2,1,0:T(8,128)(2,1)}, bf16[4,128,512]{2,1,0:T(8,128)(2,1)S(1)}, u32[]{:S(2)}, u32[]{:S(2)}) collective-permute-start(bf16[4,128,512]{2,1,0:T(8,128)(2,1)} %get-tuple-element.77.refs_5_), channel_id=1, source_target_pairs={{0,4},{4,0},{8,12},{12,8},{1,5},{5,1},{9,13},{13,9},{2,6},{6,2},{1... | collective-permute-start | bytes 1572872 | tf_op jit(solution)/shard_map/ppermute | solution.py:481
  45.6 14.0 %collective-permute-start.8 = (bf16[4,128,512]{2,1,0:T(8,128)(2,1)}, bf16[4,128,512]{2,1,0:T(8,128)(2,1)S(1)}, u32[]{:S(2)}, u32[]{:S(2)}) collective-permute-start(bf16[4,128,512]{2,1,0:T(8,128)(2,1)} %get-tuple-element.77.refs_5_), channel_id=1, source_target_pairs={{0,16},{16,0},{1,17},{17,1},{2,18},{18,2},{3,19},{19,3},{4,20},{20... | collective-permute-start | bytes 1572872 | tf_op jit(solution)/shard_map/ppermute | solution.py:454
  49.8 13.3 %collective-permute-start.7 = (bf16[144,1024]{1,0:T(8,128)(2,1)}, bf16[144,1024]{1,0:T(8,128)(2,1)S(1)}, u32[]{:S(2)}, u32[]{:S(2)}) collective-permute-start(bf16[144,1024]{1,0:T(8,128)(2,1)} %get-tuple-element.76), channel_id=1, source_target_pairs={{0,2},{2,0},{1,3},{3,1},{4,6},{6,4},{5,7},{7,5},{8,10},{10,8},{9,1... | collective-permute-start | bytes 884744 | tf_op jit(solution)/shard_map/ppermute | solution.py:454
  50.3 16.1 %collective-permute-start.4 = (bf16[144,1024]{1,0:T(8,128)(2,1)S(1)}, bf16[144,1024]{1,0:T(8,128)(2,1)S(1)}, u32[]{:S(2)}, u32[]{:S(2)}) collective-permute-start(bf16[144,1024]{1,0:T(8,128)(2,1)S(1)} %copy-done.36), channel_id=1, source_target_pairs={{0,1},{1,0},{2,3},{3,2},{4,5},{5,4},{6,7},{7,6},{8,9},{9,8},{10,11... | collective-permute-start | bytes 884744 | tf_op jit(solution)/shard_map/ppermute | solution.py:454
  57.2 5.9 %copy-start.19 = (bf16[4,128,512]{2,1,0:T(8,128)(2,1)}, bf16[4,128,512]{2,1,0:T(8,128)(2,1)S(1)}, u32[]{:S(2)}) copy-start(bf16[4,128,512]{2,1,0:T(8,128)(2,1)S(1)} %collective-permute-done.10.refs_4_) | copy-start | bytes 1572868
  63.8 15.7 %collective-permute-start.13 = (bf16[288,1024]{1,0:T(8,128)(2,1)}, bf16[288,1024]{1,0:T(8,128)(2,1)S(1)}, u32[]{:S(2)}, u32[]{:S(2)}) collective-permute-start(bf16[288,1024]{1,0:T(8,128)(2,1)} %get-tuple-element.91), channel_id=1, source_target_pairs={{0,2},{2,0},{1,3},{3,1},{4,6},{6,4},{5,7},{7,5},{8,10},{10,8},{9,1... | collective-permute-start | bytes 1769480 | tf_op jit(solution)/shard_map/ppermute | solution.py:454
  79.2 19.6 %collective-permute-start.12 = (bf16[288,1280]{1,0:T(8,128)(2,1)}, bf16[288,1280]{1,0:T(8,128)(2,1)S(1)}, u32[]{:S(2)}, u32[]{:S(2)}) collective-permute-start(bf16[288,1280]{1,0:T(8,128)(2,1)} %get-tuple-element.88.refs_2_), channel_id=1, source_target_pairs={{0,2},{2,0},{1,3},{3,1},{4,6},{6,4},{5,7},{7,5},{8,10},{10,8},{9,1... | collective-permute-start | bytes 2211848 | tf_op jit(solution)/shard_map/ppermute | solution.py:454
  80.3 2.2 %collective-permute-start.14 = (bf16[288,1024]{1,0:T(8,128)(2,1)}, bf16[288,1024]{1,0:T(8,128)(2,1)S(1)}, u32[]{:S(2)}, u32[]{:S(2)}) collective-permute-start(bf16[288,1024]{1,0:T(8,128)(2,1)} %get-tuple-element.92.here), channel_id=1, source_target_pairs={{0,1},{1,0},{2,3},{3,2},{4,5},{5,4},{6,7},{7,6},{8,9},{9,8},{10,11... | collective-permute-start | bytes 1769480 | tf_op jit(solution)/shard_map/ppermute | solution.py:454
  86.6 18.5 %collective-permute-start.15 = (bf16[144,1024]{1,0:T(8,128)(2,1)}, bf16[144,1024]{1,0:T(8,128)(2,1)S(1)}, u32[]{:S(2)}, u32[]{:S(2)}) collective-permute-start(bf16[144,1024]{1,0:T(8,128)(2,1)} %get-tuple-element.95), channel_id=1, source_target_pairs={{0,2},{2,0},{1,3},{3,1},{4,6},{6,4},{5,7},{7,5},{8,10},{10,8},{9,1... | collective-permute-start | bytes 884744 | tf_op jit(solution)/shard_map/ppermute | solution.py:454
  88.4 32.6 %collective-permute-start.16 = (bf16[288,1280]{1,0:T(8,128)(2,1)}, bf16[288,1280]{1,0:T(8,128)(2,1)S(1)}, u32[]{:S(2)}, u32[]{:S(2)}) collective-permute-start(bf16[288,1280]{1,0:T(8,128)(2,1)} %get-tuple-element.97.refs_2_), channel_id=1, source_target_pairs={{0,2},{2,0},{1,3},{3,1},{4,6},{6,4},{5,7},{7,5},{8,10},{10,8},{9,1... | collective-permute-start | bytes 2211848 | tf_op jit(solution)/shard_map/ppermute | solution.py:454
  103.0 11.1 %collective-permute-start.18 = (bf16[256,768]{1,0:T(8,128)(2,1)}, bf16[256,768]{1,0:T(8,128)(2,1)S(1)}, u32[]{:S(2)}, u32[]{:S(2)}) collective-permute-start(bf16[256,768]{1,0:T(8,128)(2,1)} %get-tuple-element.101), channel_id=1, source_target_pairs={{0,4},{4,0},{8,12},{12,8},{1,5},{5,1},{9,13},{13,9},{2,6},{6,2},{1... | collective-permute-start | bytes 1179656 | tf_op jit(solution)/shard_map/ppermute | solution.py:519
  105.9 7.5 %copy-start.2 = (bf16[288,1024]{1,0:T(8,128)(2,1)S(1)}, bf16[288,1024]{1,0:T(8,128)(2,1)}, u32[]{:S(2)}) copy-start(bf16[288,1024]{1,0:T(8,128)(2,1)} %get-tuple-element.99.refs_5_.refs_3_.refs_1_) | copy-start | bytes 1769476
  105.9 7.6 %copy-start.17 = (bf16[288,1024]{1,0:T(8,128)(2,1)S(1)}, bf16[288,1024]{1,0:T(8,128)(2,1)}, u32[]{:S(2)}) copy-start(bf16[288,1024]{1,0:T(8,128)(2,1)} %get-tuple-element.84) | copy-start | bytes 1769476
  105.9 8.2 %copy-start.25 = (f32[128,768]{1,0:T(8,128)S(1)}, f32[128,768]{1,0:T(8,128)}, u32[]{:S(2)}) copy-start(f32[128,768]{1,0:T(8,128)} %get-tuple-element.103) | copy-start | bytes 1179652
  113.2 23.6 %collective-permute-start.20 = (bf16[288,1280]{1,0:T(8,128)(2,1)}, bf16[288,1280]{1,0:T(8,128)(2,1)S(1)}, u32[]{:S(2)}, u32[]{:S(2)}) collective-permute-start(bf16[288,1280]{1,0:T(8,128)(2,1)} %get-tuple-element.105), channel_id=1, source_target_pairs={{0,2},{2,0},{1,3},{3,1},{4,6},{6,4},{5,7},{7,5},{8,10},{10,8},{9,1... | collective-permute-start | bytes 2211848 | tf_op jit(solution)/shard_map/ppermute | solution.py:454
  113.5 1.6 collective-permute-start.17
  113.6 30.0 %collective-permute-start.11 = (bf16[288,1024]{1,0:T(8,128)(2,1)S(1)}, bf16[288,1024]{1,0:T(8,128)(2,1)S(1)}, u32[]{:S(2)}, u32[]{:S(2)}) collective-permute-start(bf16[288,1024]{1,0:T(8,128)(2,1)S(1)} %copy-done.17), channel_id=1, source_target_pairs={{0,1},{1,0},{2,3},{3,2},{4,5},{5,4},{6,7},{7,6},{8,9},{9,8},{10,11... | collective-permute-start | bytes 1769480 | tf_op jit(solution)/shard_map/ppermute | solution.py:454
  114.0 6.9 %copy-start.6 = (bf16[256,768]{1,0:T(8,128)(2,1)}, bf16[256,768]{1,0:T(8,128)(2,1)S(1)}, u32[]{:S(2)}) copy-start(bf16[256,768]{1,0:T(8,128)(2,1)S(1)} %collective-permute-done.18.refs_8_) | copy-start | bytes 1179652
  115.1 5.9 %copy-start.5 = (bf16[288,512]{1,0:T(8,128)(2,1)}, bf16[288,512]{1,0:T(8,128)(2,1)S(1)}, u32[]{:S(2)}) copy-start(bf16[288,512]{1,0:T(8,128)(2,1)S(1)} %collective-permute-done.17.refs_6_.refs_5_.refs_2_) | copy-start | bytes 884740
  121.8 6.3 %copy-start.23 = (bf16[288,768]{1,0:T(8,128)(2,1)S(1)}, bf16[288,768]{1,0:T(8,128)(2,1)}, u32[]{:S(2)}) copy-start(bf16[288,768]{1,0:T(8,128)(2,1)} %get-tuple-element.113.refs_3_) | copy-start | bytes 1327108
  126.6 17.0 %copy-start.7 = (bf16[288,1024]{1,0:T(8,128)(2,1)S(1)}, bf16[288,1024]{1,0:T(8,128)(2,1)}, u32[]{:S(2)}) copy-start(bf16[288,1024]{1,0:T(8,128)(2,1)} %get-tuple-element.83.joined) | copy-start | bytes 1769476
  126.6 24.5 %collective-permute-start.21 = (bf16[256,1280]{1,0:T(8,128)(2,1)}, bf16[256,1280]{1,0:T(8,128)(2,1)S(1)}, u32[]{:S(2)}, u32[]{:S(2)}) collective-permute-start(bf16[256,1280]{1,0:T(8,128)(2,1)} %get-tuple-element.111), channel_id=1, source_target_pairs={{0,4},{4,0},{8,12},{12,8},{1,5},{5,1},{9,13},{13,9},{2,6},{6,2},{1... | collective-permute-start | bytes 1966088 | tf_op jit(solution)/shard_map/ppermute | solution.py:519
  128.1 18.4 %collective-permute-start.23 = (bf16[288,768]{1,0:T(8,128)(2,1)S(1)}, bf16[288,768]{1,0:T(8,128)(2,1)S(1)}, u32[]{:S(2)}, u32[]{:S(2)}) collective-permute-start(bf16[288,768]{1,0:T(8,128)(2,1)S(1)} %copy-done.23), channel_id=1, source_target_pairs={{0,2},{2,0},{1,3},{3,1},{4,6},{6,4},{5,7},{7,5},{8,10},{10,8},{9,1... | collective-permute-start | bytes 1327112 | tf_op jit(solution)/shard_map/ppermute | solution.py:454
  142.0 9.1 %copy-start.15 = (f32[128,1280]{1,0:T(8,128)S(1)}, f32[128,1280]{1,0:T(8,128)}, u32[]{:S(2)}) copy-start(f32[128,1280]{1,0:T(8,128)} %get-tuple-element.112) | copy-start | bytes 1966084
  142.0 29.0 %collective-permute-start.24 = (bf16[256,1280]{1,0:T(8,128)(2,1)}, bf16[256,1280]{1,0:T(8,128)(2,1)S(1)}, u32[]{:S(2)}, u32[]{:S(2)}) collective-permute-start(bf16[256,1280]{1,0:T(8,128)(2,1)} %get-tuple-element.116), channel_id=1, source_target_pairs={{0,4},{4,0},{8,12},{12,8},{1,5},{5,1},{9,13},{13,9},{2,6},{6,2},{1... | collective-permute-start | bytes 1966088 | tf_op jit(solution)/shard_map/ppermute | solution.py:519
  143.9 27.1 %copy-start.16 = (f32[128,1280]{1,0:T(8,128)S(1)}, f32[128,1280]{1,0:T(8,128)}, u32[]{:S(2)}) copy-start(f32[128,1280]{1,0:T(8,128)} %get-tuple-element.117) | copy-start | bytes 1966084
  143.9 36.3 %collective-permute-start.19 = (bf16[128,768]{1,0:T(8,128)(2,1)S(1)}, bf16[128,768]{1,0:T(8,128)(2,1)S(1)}, u32[]{:S(2)}, u32[]{:S(2)}) collective-permute-start(bf16[128,768]{1,0:T(8,128)(2,1)S(1)} %add_convert_fusion.4), channel_id=1, source_target_pairs={{0,8},{4,12},{8,0},{12,4},{1,9},{5,13},{9,1},{13,5},{2,10},{6,14},... | collective-permute-start | bytes 589832 | tf_op jit(solution)/shard_map/ppermute | solution.py:521
  150.7 28.0 %copy-start.26 = (f32[128,768]{1,0:T(8,128)S(1)}, f32[128,768]{1,0:T(8,128)}, u32[]{:S(2)}) copy-start(f32[128,768]{1,0:T(8,128)} %get-tuple-element.120) | copy-start | bytes 1179652
  150.7 28.0 %collective-permute-start.26 = (bf16[256,768]{1,0:T(8,128)(2,1)}, bf16[256,768]{1,0:T(8,128)(2,1)S(1)}, u32[]{:S(2)}, u32[]{:S(2)}) collective-permute-start(bf16[256,768]{1,0:T(8,128)(2,1)} %get-tuple-element.119), channel_id=1, source_target_pairs={{0,4},{4,0},{8,12},{12,8},{1,5},{5,1},{9,13},{13,9},{2,6},{6,2},{1... | collective-permute-start | bytes 1179656 | tf_op jit(solution)/shard_map/ppermute | solution.py:519
  151.1 28.2 %copy-start.10 = (bf16[256,1280]{1,0:T(8,128)(2,1)}, bf16[256,1280]{1,0:T(8,128)(2,1)S(1)}, u32[]{:S(2)}) copy-start(bf16[256,1280]{1,0:T(8,128)(2,1)S(1)} %collective-permute-done.21.refs_4_) | copy-start | bytes 1966084
  151.2 29.0 %collective-permute-start.22 = (bf16[128,1280]{1,0:T(8,128)(2,1)S(1)}, bf16[128,1280]{1,0:T(8,128)(2,1)S(1)}, u32[]{:S(2)}, u32[]{:S(2)}) collective-permute-start(bf16[128,1280]{1,0:T(8,128)(2,1)S(1)} %add_convert_fusion.2), channel_id=1, source_target_pairs={{0,8},{4,12},{8,0},{12,4},{1,9},{5,13},{9,1},{13,5},{2,10},{6,14},... | collective-permute-start | bytes 983048 | tf_op jit(solution)/shard_map/ppermute | solution.py:521
  170.9 9.3 %copy-start.11 = (bf16[256,1280]{1,0:T(8,128)(2,1)}, bf16[256,1280]{1,0:T(8,128)(2,1)S(1)}, u32[]{:S(2)}) copy-start(bf16[256,1280]{1,0:T(8,128)(2,1)S(1)} %collective-permute-done.24.refs_1_) | copy-start | bytes 1966084
  171.0 25.7 %collective-permute-start.25 = (bf16[128,1280]{1,0:T(8,128)(2,1)S(1)}, bf16[128,1280]{1,0:T(8,128)(2,1)S(1)}, u32[]{:S(2)}, u32[]{:S(2)}) collective-permute-start(bf16[128,1280]{1,0:T(8,128)(2,1)S(1)} %add_convert_fusion.1), channel_id=1, source_target_pairs={{0,8},{4,12},{8,0},{12,4},{1,9},{5,13},{9,1},{13,5},{2,10},{6,14},... | collective-permute-start | bytes 983048 | tf_op jit(solution)/shard_map/ppermute | solution.py:521
  178.7 5.4 %copy-start.12 = (bf16[256,768]{1,0:T(8,128)(2,1)}, bf16[256,768]{1,0:T(8,128)(2,1)S(1)}, u32[]{:S(2)}) copy-start(bf16[256,768]{1,0:T(8,128)(2,1)S(1)} %collective-permute-done.26.refs_4_) | copy-start | bytes 1179652
  178.7 18.0 %collective-permute-start.27 = (bf16[128,768]{1,0:T(8,128)(2,1)S(1)}, bf16[128,768]{1,0:T(8,128)(2,1)S(1)}, u32[]{:S(2)}, u32[]{:S(2)}) collective-permute-start(bf16[128,768]{1,0:T(8,128)(2,1)S(1)} %add_convert_fusion.3), channel_id=1, source_target_pairs={{0,8},{4,12},{8,0},{12,4},{1,9},{5,13},{9,1},{13,5},{2,10},{6,14},... | collective-permute-start | bytes 589832 | tf_op jit(solution)/shard_map/ppermute | solution.py:521
  (18 other events, 22.5 us)

commit v7 on v6

--- a/solution.py
+++ b/solution.py
@@ -824,6 +824,7 @@
         ),
         kept=(backward[0], intake[1]),
     )
+    sums[0], intake[2] = fence(sums[0], intake[2])
     outlet = [*summed_over_loc(sums)]
     half = model // 2
     backward_other = swap(backward[1], "date")

time: 201 us -> 197 us (0.980)
  waiting for transfers between devices: 93.3 us -> 88.6 us
    ppermute x4, waiting for transfers between devices: 25.4 us -> 23.2 us  [summed_over_loc(): beside = lax.ppermute(sent, 'loc', PAIRS)]
    ppermute x4, waiting for transfers between devices: 12.7 us -> 10.5 us  [summed_over_loc(): return (near, beside, lax.ppermute(far, 'loc', APART))]
  transfers between devices with their start and end apart: 28 -> 28, of which waited for: 17 -> 15; matrix products, arithmetic and copies ran while one was open for 3% -> 3% of each run, Pallas kernels for 27% -> 28%
where the time goes in v7:
time: 197 us
  waiting for transfers between devices  88.6 us (45%)
  Pallas kernels  57.3 us (29%)
  starting transfers between devices  29.8 us (15%)
  local copies, waits for them, and re-layouts  19 us (10%)
    pallas_call x12, Pallas kernels, call(): pl.pallas_call(body, out_shape=outs, in_specs=specs, out_specs=out_specs,...  57.3 us
    ppermute x18, waiting for transfers between devices, swap(): return lax.ppermute(array, axis, [(0, 1), (1, 0)])  52.7 us
    ppermute x4, waiting for transfers between devices, summed_over_loc(): beside = lax.ppermute(sent, 'loc', PAIRS)  23.2 us
    ppermute x18, starting transfers between devices, swap(): return lax.ppermute(array, axis, [(0, 1), (1, 0)])  16.5 us
    unnamed x78, local copies, waits for them, and re-layouts  15 us
    ppermute x4, waiting for transfers between devices, summed_over_loc(): return (near, beside, lax.ppermute(far, 'loc', APART))  10.5 us
    ppermute x4, starting transfers between devices, summed_over_loc(): return (near, beside, lax.ppermute(far, 'loc', APART))  5.5 us
    ppermute x4, starting transfers between devices, summed_over_loc(): beside = lax.ppermute(sent, 'loc', PAIRS)  4.05 us
  transfers between devices with their start and end apart: 28, of which 15 were waited for; matrix products, arithmetic and copies ran while one was open for 3% of the time, Pallas kernels for 28%

profile of v7, /device:TPU:0, one launch (start us, length us, event | category | flops | bytes accessed | tf_op | source)
XLA Modules:
  0.0 197.0 jit_solution(5123409319065592960)
XLA Ops:
  0.7 2.0 %copy.57 = bf16[512,4,512]{2,0,1:T(8,128)(2,1)S(1)} copy(bf16[512,4,512]{2,1,0:T(4,128)(2,1)} %param.20) | data formatting | bytes 4194304 | tf_op args[8]
  2.7 1.2 dynamic-slice_bitcast_fusion
  3.9 2.9 %collective-permute-start = (bf16[4,128,512]{2,1,0:T(8,128)(2,1)}, bf16[4,128,512]{2,1,0:T(8,128)(2,1)S(1)}, u32[]{:S(2)}, u32[]{:S(2)}) collective-permute-start(bf16[4,128,512]{2,1,0:T(8,128)(2,1)} %get-tuple-element.129), channel_id=1, source_target_pairs={{0,2},{2,0},{1,3},{3,1},{4,6},{6,4},{5,7},{7,5},{8,10},{10,8},{9,1... | collective-permute-start | bytes 1572872 | tf_op jit(solution)/shard_map/ppermute | solution.py:454
  7.5 3.1 %shard_map.139 = (bf16[144,1024]{1,0:T(8,128)(2,1)}, bf16[144,1024]{1,0:T(8,128)(2,1)}, bf16[288,1024]{1,0:T(8,128)(2,1)}, f32[12,1024]{1,0:T(8,128)}) custom-call(s32[1,12]{1,0:T(1,128)} %cloud.1, s32[1,12]{1,0:T(1,128)} %drop.1, s32[1,48]{1,0:T(1,128)} %keep.1, s32[4]{0:T(128)} %pad_add_fusion.where, bf16[6,48,1024]{2,1,0:T(8,128)(2,1)} %bitcast.47, ...), custom_call_target="tpu_custom_call" | custom-call | bytes 3424560 | tf_op jit(solution)/shard_map/pallas_call | solution.py:430
  10.7 2.0 %copy.58 = bf16[512,4,512]{2,0,1:T(8,128)(2,1)S(1)} copy(bf16[512,4,512]{2,1,0:T(4,128)(2,1)} %param.22) | data formatting | bytes 4194304 | tf_op args[10]
  12.7 7.1 %collective-permute-done.refs_3_ = bf16[4,128,512]{2,1,0:T(8,128)(2,1)S(1)} collective-permute-done((bf16[4,128,512]{2,1,0:T(8,128)(2,1)}, bf16[4,128,512]{2,1,0:T(8,128)(2,1)S(1)}, u32[]{:S(2)}, u32[]{:S(2)}) %collective-permute-start) | collective-permute-done | bytes 524320 | tf_op jit(solution)/shard_map/ppermute | solution.py:454
  19.8 2.1 %collective-permute-start.2 = (bf16[4,128,512]{2,1,0:T(8,128)(2,1)S(1)}, bf16[4,128,512]{2,1,0:T(8,128)(2,1)}, u32[]{:S(2)}, u32[]{:S(2)}) collective-permute-start(bf16[4,128,512]{2,1,0:T(8,128)(2,1)S(1)} %collective-permute-done.refs_3_), channel_id=1, source_target_pairs={{0,4},{4,0},{8,12},{12,8},{1,5},{5,1},{9,13},{13,9},{2,6},{6,2},{1... | collective-permute-start | bytes 1572872 | tf_op jit(solution)/shard_map/ppermute | solution.py:481
  21.9 1.5 collective-permute-start.1
  23.5 1.1 dynamic-slice_bitcast_fusion.2
  24.6 1.5 collective-permute-start.5
  26.1 5.0 %collective-permute-done.3.refs_6_ = bf16[4,128,512]{2,1,0:T(8,128)(2,1)S(1)} collective-permute-done((bf16[4,128,512]{2,1,0:T(8,128)(2,1)}, bf16[4,128,512]{2,1,0:T(8,128)(2,1)S(1)}, u32[]{:S(2)}, u32[]{:S(2)}) %collective-permute-start.3) | collective-permute-done | bytes 524320 | tf_op jit(solution)/shard_map/ppermute | solution.py:454
  31.0 1.2 collective-permute-done.2.refs_5_
  32.2 1.2 collective-permute-done.1.refs_4_
  33.4 8.0 %shard_map.142 = (bf16[144,1024]{1,0:T(8,128)(2,1)}, bf16[144,1024]{1,0:T(8,128)(2,1)}, bf16[288,512]{1,0:T(8,128)(2,1)}, bf16[288,512]{1,0:T(8,128)(2,1)}, bf16...) custom-call(s32[4]{0:T(128)} %pad_add_fusion.where, ...), custom_call_target="tpu_custom_call" | custom-call | flops 1207959552 | bytes 9211920 | tf_op jit(solution)/shard_map/pallas_call | solution.py:430
  42.2 1.7 collective-permute-start.10
  44.0 1.6 collective-permute-start.9
  45.6 1.5 collective-permute-start.8
  47.8 2.0 %shard_map.144 = (bf16[144,1024]{1,0:T(8,128)(2,1)}, bf16[288,1024]{1,0:T(8,128)(2,1)}) custom-call(bf16[144,1024]{1,0:T(8,128)(2,1)} %get-tuple-element.70.refs_1_.start, bf16[144,1024]{1,0:T(8,128)(2,1)} %get-tuple-element.75.here, bf16[144,1024]{1,0:T(8,128)(2,1)} %copy-done.32, ...), custom_call_target="tpu_custom_call", output_to_operand_aliasing={{1}: (3, {})} | custom-call | bytes 1769472 | tf_op jit(solution)/shard_map/pallas_call | solution.py:430
  50.4 6.8 %collective-permute-done.10.refs_4_ = bf16[4,128,512]{2,1,0:T(8,128)(2,1)S(1)} collective-permute-done((bf16[4,128,512]{2,1,0:T(8,128)(2,1)}, bf16[4,128,512]{2,1,0:T(8,128)(2,1)S(1)}, u32[]{:S(2)}, u32[]{:S(2)}) %collective-permute-start.10) | collective-permute-done | bytes 524320 | tf_op jit(solution)/shard_map/ppermute | solution.py:454
  57.2 1.1 collective-permute-done.9.refs_3_
  58.2 1.3 collective-permute-done.8.refs_2_
  59.5 3.6 %collective-permute-done.7.refs_1_ = bf16[144,1024]{1,0:T(8,128)(2,1)S(1)} collective-permute-done((bf16[144,1024]{1,0:T(8,128)(2,1)}, bf16[144,1024]{1,0:T(8,128)(2,1)S(1)}, u32[]{:S(2)}, u32[]{:S(2)}) %collective-permute-start.7) | collective-permute-done | bytes 294944 | tf_op jit(solution)/shard_map/ppermute | solution.py:454
  63.8 1.7 collective-permute-start.13
  67.2 12.0 %shard_map.146 = (bf16[288,512]{1,0:T(8,128)(2,1)}, bf16[288,1280]{1,0:T(8,128)(2,1)}, bf16[288,1280]{1,0:T(8,128)(2,1)}, bf16[288,1024]{1,0:T(8,128)(2,1)}, bf1...) custom-call(s32[4]{0:T(128)} %pad_add_fusion.where, f32[1,1024]{1,0:T(1,128)} %bitcast.52, ...), custom_call_target="tpu_custom_call" | custom-call | flops 2415919104 | bytes 9851280 | tf_op jit(solution)/shard_map/pallas_call | solution.py:430
  80.3 2.2 %collective-permute-done.14.there = bf16[288,1024]{1,0:T(8,128)(2,1)S(1)} collective-permute-done((bf16[288,1024]{1,0:T(8,128)(2,1)}, bf16[288,1024]{1,0:T(8,128)(2,1)S(1)}, u32[]{:S(2)}, u32[]{:S(2)}) %collective-permute-start.14) | collective-permute-done | bytes 589856 | tf_op jit(solution)/shard_map/ppermute | solution.py:454
  83.3 3.3 %shard_map.149 = (bf16[144,1024]{1,0:T(8,128)(2,1)}, bf16[144,1024]{1,0:T(8,128)(2,1)}, bf16[288,1280]{1,0:T(8,128)(2,1)}) custom-call(f32[1,1024]{1,0:T(1,128)} %bitcast.53, bf16[288,1024]{1,0:T(8,128)(2,1)} %get-tuple-element.94.here, bf16[288,1024]{1,0:T(8,128)(2,1)} %copy-done.19, ...), custom_call_target="tpu_custom_call", output_to_operand_aliasing={{2}: (5, {})} | custom-call | bytes 3690496 | tf_op jit(solution)/shard_map/pallas_call | solution.py:430
  86.6 1.7 collective-permute-start.15
  88.3 10.5 %collective-permute-done.12.refs_1_ = bf16[288,1280]{1,0:T(8,128)(2,1)S(1)} collective-permute-done((bf16[288,1280]{1,0:T(8,128)(2,1)}, bf16[288,1280]{1,0:T(8,128)(2,1)S(1)}, u32[]{:S(2)}, u32[]{:S(2)}) %collective-permute-start.12) | collective-permute-done | bytes 737312 | tf_op jit(solution)/shard_map/ppermute | solution.py:454
  98.8 0.9 copy-done.4
  99.7 3.3 %shard_map.147 = (bf16[256,768]{1,0:T(8,128)(2,1)}, f32[128,768]{1,0:T(8,128)}, f32[128,768]{1,0:T(8,128)}) custom-call(s32[4]{0:T(128)} %pad_add_fusion.where, bf16[288,512]{1,0:T(8,128)(2,1)} %get-tuple-element.89.refs_0_, bf16[288,1280]{1,0:T(8,128)(2,1)} %copy-done.4, bf16[288,1280]{1,0:T(8,128)(2,1)} %get-tuple-element.90.refs_2_), custom_call_target="tpu_custom_call" | custom-call | flops 452984832 | bytes 2949136 | tf_op jit(solution)/shard_map/pallas_call | solution.py:430
  102.9 1.6 collective-permute-start.18
  105.8 7.3 %shard_map.150 = (bf16[288,512]{1,0:T(8,128)(2,1)}, bf16[288,1280]{1,0:T(8,128)(2,1)}, bf16[288,768]{1,0:T(8,128)(2,1)}, bf16[288,768]{1,0:T(8,128)(2,1)}, f32[128,768]{1,0:T(8,128)}) custom-call(s32[4]{0:T(128)} %pad_add_fusion.where, bf16[288,1536]{1,0:T(8,128)(2,1)} %get-tuple-element.87.triple, ...), custom_call_target="tpu_custom_call", output_to_operand_aliasing={{4}: (3, {})} | custom-call | flops 1207959552 | bytes 8863760 | tf_op jit(solution)/shard_map/pallas_call | solution.py:430
  113.1 1.5 collective-permute-start.20
  115.2 2.7 %collective-permute-start.19 = (bf16[128,768]{1,0:T(8,128)(2,1)S(1)}, bf16[128,768]{1,0:T(8,128)(2,1)S(1)}, u32[]{:S(2)}, u32[]{:S(2)}) collective-permute-start(bf16[128,768]{1,0:T(8,128)(2,1)S(1)} %add_convert_fusion.4), channel_id=1, source_target_pairs={{0,8},{4,12},{8,0},{12,4},{1,9},{5,13},{9,1},{13,5},{2,10},{6,14},... | collective-permute-start | bytes 589832 | tf_op jit(solution)/shard_map/ppermute | solution.py:521
  117.9 6.3 %collective-permute-done.16.refs_3_ = bf16[288,1280]{1,0:T(8,128)(2,1)S(1)} collective-permute-done((bf16[288,1280]{1,0:T(8,128)(2,1)}, bf16[288,1280]{1,0:T(8,128)(2,1)S(1)}, u32[]{:S(2)}, u32[]{:S(2)}) %collective-permute-start.16) | collective-permute-done | bytes 737312 | tf_op jit(solution)/shard_map/ppermute | solution.py:454
  125.0 4.7 %shard_map.151 = (bf16[256,1280]{1,0:T(8,128)(2,1)}, f32[128,1280]{1,0:T(8,128)}, f32[128,1280]{1,0:T(8,128)}, bf16[288,512]{1,0:T(8,128)(2,1)}, bf16[256,768]{1,0:T(8,128)(2,1)}) custom-call(s32[4]{0:T(128)} %pad_add_fusion.where, bf16[288,512]{1,0:T(8,128)(2,1)} %get-tuple-element.89.refs_0_, ...), custom_call_target="tpu_custom_call", output_to_operand_aliasing={{3}: (8, {}), {4}: (9, {})} | custom-call | flops 754974720 | bytes 6340624 | tf_op jit(solution)/shard_map/pallas_call | solution.py:430
  131.2 8.7 %collective-permute-done.20.refs_1_ = bf16[288,1280]{1,0:T(8,128)(2,1)S(1)} collective-permute-done((bf16[288,1280]{1,0:T(8,128)(2,1)}, bf16[288,1280]{1,0:T(8,128)(2,1)S(1)}, u32[]{:S(2)}, u32[]{:S(2)}) %collective-permute-start.20) | collective-permute-done | bytes 737312 | tf_op jit(solution)/shard_map/ppermute | solution.py:454
  140.0 0.9 copy-done.15
  140.8 4.3 %shard_map.153 = (bf16[256,1280]{1,0:T(8,128)(2,1)}, f32[128,1280]{1,0:T(8,128)}, f32[128,1280]{1,0:T(8,128)}, f32[128,1280]{1,0:T(8,128)}) custom-call(s32[4]{0:T(128)} %pad_add_fusion.where, bf16[288,512]{1,0:T(8,128)(2,1)} %get-tuple-element.108.refs_0_, bf16[288,1280]{1,0:T(8,128)(2,1)} %copy-done.15, ...), custom_call_target="tpu_custom_call", output_to_operand_aliasing={{3}: (8, {})} | custom-call | flops 754974720 | bytes 5570576 | tf_op jit(solution)/shard_map/pallas_call | solution.py:430
  146.7 3.4 %shard_map.155 = (bf16[256,768]{1,0:T(8,128)(2,1)}, f32[128,768]{1,0:T(8,128)}, f32[128,768]{1,0:T(8,128)}, f32[128,1280]{1,0:T(8,128)}) custom-call(s32[4]{0:T(128)} %pad_add_fusion.where, bf16[288,512]{1,0:T(8,128)(2,1)} %get-tuple-element.111.refs_4_.refs_0_, ...), custom_call_target="tpu_custom_call", output_to_operand_aliasing={{3}: (6, {})} | custom-call | flops 452984832 | bytes 3899408 | tf_op jit(solution)/shard_map/pallas_call | solution.py:430
  150.1 1.6 collective-permute-start.26
  151.7 2.7 %collective-permute-start.22 = (bf16[128,1280]{1,0:T(8,128)(2,1)S(1)}, bf16[128,1280]{1,0:T(8,128)(2,1)S(1)}, u32[]{:S(2)}, u32[]{:S(2)}) collective-permute-start(bf16[128,1280]{1,0:T(8,128)(2,1)S(1)} %add_convert_fusion.2), channel_id=1, source_target_pairs={{0,8},{4,12},{8,0},{12,4},{1,9},{5,13},{9,1},{13,5},{2,10},{6,14},... | collective-permute-start | bytes 983048 | tf_op jit(solution)/shard_map/ppermute | solution.py:521
  154.4 19.1 %collective-permute-done.24.refs_1_ = bf16[256,1280]{1,0:T(8,128)(2,1)S(1)} collective-permute-done((bf16[256,1280]{1,0:T(8,128)(2,1)}, bf16[256,1280]{1,0:T(8,128)(2,1)S(1)}, u32[]{:S(2)}, u32[]{:S(2)}) %collective-permute-start.24) | collective-permute-done | bytes 655392 | tf_op jit(solution)/shard_map/ppermute | solution.py:519
  173.6 4.1 %collective-permute-done.26.refs_4_ = bf16[256,768]{1,0:T(8,128)(2,1)S(1)} collective-permute-done((bf16[256,768]{1,0:T(8,128)(2,1)}, bf16[256,768]{1,0:T(8,128)(2,1)S(1)}, u32[]{:S(2)}, u32[]{:S(2)}) %collective-permute-start.26) | collective-permute-done | bytes 393248 | tf_op jit(solution)/shard_map/ppermute | solution.py:519
  178.0 0.9 copy.52
  179.6 3.0 %shard_map.154.kept = f32[128,4,512]{2,1,0:T(4,128)} custom-call(f32[128,768]{1,0:T(8,128)} %get-tuple-element.98.refs_0_, bf16[256,768]{1,0:T(8,128)(2,1)} %get-tuple-element.104.refs_1_, bf16[128,768]{1,0:T(8,128)(2,1)} %get-tuple-element.107.refs_2_, f32[128,1280]{1,0:T(8,128)} %get-tuple-element.114.refs_3_, bf16[256,1280]{1,0:T(8,128)(2,1)} %copy-done.10, ...), custom_call_target="tpu_custom_call" | custom-call | bytes 3670016 | tf_op jit(solution)/shard_map/pallas_call | solution.py:430
  182.6 10.5 %collective-permute-done.27.refs_5_ = bf16[128,768]{1,0:T(8,128)(2,1)S(1)} collective-permute-done((bf16[128,768]{1,0:T(8,128)(2,1)S(1)}, bf16[128,768]{1,0:T(8,128)(2,1)S(1)}, u32[]{:S(2)}, u32[]{:S(2)}) %collective-permute-start.27) | collective-permute-done | bytes 196640 | tf_op jit(solution)/shard_map/ppermute | solution.py:521
  193.9 3.0 %shard_map.156 = (f32[128,4,512]{2,1,0:T(4,128)}, f32[128,4,512]{2,1,0:T(4,128)}) custom-call(f32[128,4,512]{2,1,0:T(4,128)} %shard_map.154.kept, f32[128,1280]{1,0:T(8,128)} %get-tuple-element.119.refs_0_, bf16[256,1280]{1,0:T(8,128)(2,1)} %copy-done.11, bf16[128,1280]{1,0:T(8,128)(2,1)} %copy-done.28, ...), custom_call_target="tpu_custom_call", output_to_operand_aliasing={{1}: (0, {})} | custom-call | bytes 4718592 | tf_op jit(solution)/shard_map/pallas_call | solution.py:430
  (120 shorter events, 14.9 us)
Async XLA Ops:
  2.7 7.9 %copy-start = (bf16[512,4,512]{2,0,1:T(8,128)(2,1)}, bf16[512,4,512]{2,0,1:T(8,128)(2,1)S(1)}, u32[]{:S(2)}) copy-start(bf16[512,4,512]{2,0,1:T(8,128)(2,1)S(1)} %copy.57) | copy-start | bytes 6291460
  3.9 15.9 %collective-permute-start = (bf16[4,128,512]{2,1,0:T(8,128)(2,1)}, bf16[4,128,512]{2,1,0:T(8,128)(2,1)S(1)}, u32[]{:S(2)}, u32[]{:S(2)}) collective-permute-start(bf16[4,128,512]{2,1,0:T(8,128)(2,1)} %get-tuple-element.129), channel_id=1, source_target_pairs={{0,2},{2,0},{1,3},{3,1},{4,6},{6,4},{5,7},{7,5},{8,10},{10,8},{9,1... | collective-permute-start | bytes 1572872 | tf_op jit(solution)/shard_map/ppermute | solution.py:454
  10.6 20.4 %collective-permute-start.3 = (bf16[4,128,512]{2,1,0:T(8,128)(2,1)}, bf16[4,128,512]{2,1,0:T(8,128)(2,1)S(1)}, u32[]{:S(2)}, u32[]{:S(2)}) collective-permute-start(bf16[4,128,512]{2,1,0:T(8,128)(2,1)} %get-tuple-element.71), channel_id=1, source_target_pairs={{0,2},{2,0},{1,3},{3,1},{4,6},{6,4},{5,7},{7,5},{8,10},{10,8},{9,1... | collective-permute-start | bytes 1572872 | tf_op jit(solution)/shard_map/ppermute | solution.py:454
  12.7 28.7 %copy-start.3 = (bf16[512,4,512]{2,0,1:T(8,128)(2,1)}, bf16[512,4,512]{2,0,1:T(8,128)(2,1)S(1)}, u32[]{:S(2)}) copy-start(bf16[512,4,512]{2,0,1:T(8,128)(2,1)S(1)} %copy.58) | copy-start | bytes 6291460
  19.8 13.6 %copy-start.8 = (bf16[4,128,512]{2,1,0:T(8,128)(2,1)}, bf16[4,128,512]{2,1,0:T(8,128)(2,1)S(1)}, u32[]{:S(2)}) copy-start(bf16[4,128,512]{2,1,0:T(8,128)(2,1)S(1)} %collective-permute-done.refs_3_) | copy-start | bytes 1572868
  19.8 12.4 %collective-permute-start.2 = (bf16[4,128,512]{2,1,0:T(8,128)(2,1)S(1)}, bf16[4,128,512]{2,1,0:T(8,128)(2,1)}, u32[]{:S(2)}, u32[]{:S(2)}) collective-permute-start(bf16[4,128,512]{2,1,0:T(8,128)(2,1)S(1)} %collective-permute-done.refs_3_), channel_id=1, source_target_pairs={{0,4},{4,0},{8,12},{12,8},{1,5},{5,1},{9,13},{13,9},{2,6},{6,2},{1... | collective-permute-start | bytes 1572872 | tf_op jit(solution)/shard_map/ppermute | solution.py:481
  21.9 11.5 %collective-permute-start.1 = (bf16[4,128,512]{2,1,0:T(8,128)(2,1)S(1)}, bf16[4,128,512]{2,1,0:T(8,128)(2,1)}, u32[]{:S(2)}, u32[]{:S(2)}) collective-permute-start(bf16[4,128,512]{2,1,0:T(8,128)(2,1)S(1)} %collective-permute-done.refs_3_), channel_id=1, source_target_pairs={{0,16},{16,0},{1,17},{17,1},{2,18},{18,2},{3,19},{19,3},{4,20},{20... | collective-permute-start | bytes 1572872 | tf_op jit(solution)/shard_map/ppermute | solution.py:454
  24.6 16.9 %collective-permute-start.5 = (bf16[4,128,512]{2,1,0:T(8,128)(2,1)}, bf16[4,128,512]{2,1,0:T(8,128)(2,1)S(1)}, u32[]{:S(2)}, u32[]{:S(2)}) collective-permute-start(bf16[4,128,512]{2,1,0:T(8,128)(2,1)} %get-tuple-element.73), channel_id=1, source_target_pairs={{0,2},{2,0},{1,3},{3,1},{4,6},{6,4},{5,7},{7,5},{8,10},{10,8},{9,1... | collective-permute-start | bytes 1572872 | tf_op jit(solution)/shard_map/ppermute | solution.py:454
  41.4 8.9 %copy-start.34 = (s32[1,12]{1,0:T(1,128)S(1)}, s32[1,12]{1,0:T(1,128)}, u32[]{:S(2)}) copy-start(s32[1,12]{1,0:T(1,128)} %cloud.1) | copy-start | bytes 148
  41.4 8.9 %copy-start.35 = (s32[1,12]{1,0:T(1,128)S(1)}, s32[1,12]{1,0:T(1,128)}, u32[]{:S(2)}) copy-start(s32[1,12]{1,0:T(1,128)} %drop.1) | copy-start | bytes 148
  41.4 8.9 %copy-start.36 = (bf16[144,1024]{1,0:T(8,128)(2,1)S(1)}, bf16[144,1024]{1,0:T(8,128)(2,1)}, u32[]{:S(2)}) copy-start(bf16[144,1024]{1,0:T(8,128)(2,1)} %get-tuple-element.72.refs_1_) | copy-start | bytes 884740
  42.2 4.8 %collective-permute-start.6 = (bf16[144,1024]{1,0:T(8,128)(2,1)}, bf16[144,1024]{1,0:T(8,128)(2,1)S(1)}, u32[]{:S(2)}, u32[]{:S(2)}) collective-permute-start(bf16[144,1024]{1,0:T(8,128)(2,1)} %get-tuple-element.75.here), channel_id=1, source_target_pairs={{0,1},{1,0},{2,3},{3,2},{4,5},{5,4},{6,7},{7,6},{8,9},{9,8},{10,11... | collective-permute-start | bytes 884744 | tf_op jit(solution)/shard_map/ppermute | solution.py:454
  42.2 14.9 %collective-permute-start.10 = (bf16[4,128,512]{2,1,0:T(8,128)(2,1)}, bf16[4,128,512]{2,1,0:T(8,128)(2,1)S(1)}, u32[]{:S(2)}, u32[]{:S(2)}) collective-permute-start(bf16[4,128,512]{2,1,0:T(8,128)(2,1)} %get-tuple-element.80), channel_id=1, source_target_pairs={{0,2},{2,0},{1,3},{3,1},{4,6},{6,4},{5,7},{7,5},{8,10},{10,8},{9,1... | collective-permute-start | bytes 1572872 | tf_op jit(solution)/shard_map/ppermute | solution.py:454
  44.0 14.3 %collective-permute-start.9 = (bf16[4,128,512]{2,1,0:T(8,128)(2,1)}, bf16[4,128,512]{2,1,0:T(8,128)(2,1)S(1)}, u32[]{:S(2)}, u32[]{:S(2)}) collective-permute-start(bf16[4,128,512]{2,1,0:T(8,128)(2,1)} %get-tuple-element.79.refs_5_), channel_id=1, source_target_pairs={{0,4},{4,0},{8,12},{12,8},{1,5},{5,1},{9,13},{13,9},{2,6},{6,2},{1... | collective-permute-start | bytes 1572872 | tf_op jit(solution)/shard_map/ppermute | solution.py:481
  45.6 14.0 %collective-permute-start.8 = (bf16[4,128,512]{2,1,0:T(8,128)(2,1)}, bf16[4,128,512]{2,1,0:T(8,128)(2,1)S(1)}, u32[]{:S(2)}, u32[]{:S(2)}) collective-permute-start(bf16[4,128,512]{2,1,0:T(8,128)(2,1)} %get-tuple-element.79.refs_5_), channel_id=1, source_target_pairs={{0,16},{16,0},{1,17},{17,1},{2,18},{18,2},{3,19},{19,3},{4,20},{20... | collective-permute-start | bytes 1572872 | tf_op jit(solution)/shard_map/ppermute | solution.py:454
  49.8 13.3 %collective-permute-start.7 = (bf16[144,1024]{1,0:T(8,128)(2,1)}, bf16[144,1024]{1,0:T(8,128)(2,1)S(1)}, u32[]{:S(2)}, u32[]{:S(2)}) collective-permute-start(bf16[144,1024]{1,0:T(8,128)(2,1)} %get-tuple-element.78), channel_id=1, source_target_pairs={{0,2},{2,0},{1,3},{3,1},{4,6},{6,4},{5,7},{7,5},{8,10},{10,8},{9,1... | collective-permute-start | bytes 884744 | tf_op jit(solution)/shard_map/ppermute | solution.py:454
  50.3 16.1 %collective-permute-start.4 = (bf16[144,1024]{1,0:T(8,128)(2,1)S(1)}, bf16[144,1024]{1,0:T(8,128)(2,1)S(1)}, u32[]{:S(2)}, u32[]{:S(2)}) collective-permute-start(bf16[144,1024]{1,0:T(8,128)(2,1)S(1)} %copy-done.36), channel_id=1, source_target_pairs={{0,1},{1,0},{2,3},{3,2},{4,5},{5,4},{6,7},{7,6},{8,9},{9,8},{10,11... | collective-permute-start | bytes 884744 | tf_op jit(solution)/shard_map/ppermute | solution.py:454
  57.2 5.9 %copy-start.20 = (bf16[4,128,512]{2,1,0:T(8,128)(2,1)}, bf16[4,128,512]{2,1,0:T(8,128)(2,1)S(1)}, u32[]{:S(2)}) copy-start(bf16[4,128,512]{2,1,0:T(8,128)(2,1)S(1)} %collective-permute-done.10.refs_4_) | copy-start | bytes 1572868
  63.8 15.6 %collective-permute-start.13 = (bf16[288,1024]{1,0:T(8,128)(2,1)}, bf16[288,1024]{1,0:T(8,128)(2,1)S(1)}, u32[]{:S(2)}, u32[]{:S(2)}) collective-permute-start(bf16[288,1024]{1,0:T(8,128)(2,1)} %get-tuple-element.93), channel_id=1, source_target_pairs={{0,2},{2,0},{1,3},{3,1},{4,6},{6,4},{5,7},{7,5},{8,10},{10,8},{9,1... | collective-permute-start | bytes 1769480 | tf_op jit(solution)/shard_map/ppermute | solution.py:454
  79.2 19.6 %collective-permute-start.12 = (bf16[288,1280]{1,0:T(8,128)(2,1)}, bf16[288,1280]{1,0:T(8,128)(2,1)S(1)}, u32[]{:S(2)}, u32[]{:S(2)}) collective-permute-start(bf16[288,1280]{1,0:T(8,128)(2,1)} %get-tuple-element.90.refs_2_), channel_id=1, source_target_pairs={{0,2},{2,0},{1,3},{3,1},{4,6},{6,4},{5,7},{7,5},{8,10},{10,8},{9,1... | collective-permute-start | bytes 2211848 | tf_op jit(solution)/shard_map/ppermute | solution.py:454
  80.3 2.2 %collective-permute-start.14 = (bf16[288,1024]{1,0:T(8,128)(2,1)}, bf16[288,1024]{1,0:T(8,128)(2,1)S(1)}, u32[]{:S(2)}, u32[]{:S(2)}) collective-permute-start(bf16[288,1024]{1,0:T(8,128)(2,1)} %get-tuple-element.94.here), channel_id=1, source_target_pairs={{0,1},{1,0},{2,3},{3,2},{4,5},{5,4},{6,7},{7,6},{8,9},{9,8},{10,11... | collective-permute-start | bytes 1769480 | tf_op jit(solution)/shard_map/ppermute | solution.py:454
  86.6 18.5 %collective-permute-start.15 = (bf16[144,1024]{1,0:T(8,128)(2,1)}, bf16[144,1024]{1,0:T(8,128)(2,1)S(1)}, u32[]{:S(2)}, u32[]{:S(2)}) collective-permute-start(bf16[144,1024]{1,0:T(8,128)(2,1)} %get-tuple-element.97), channel_id=1, source_target_pairs={{0,2},{2,0},{1,3},{3,1},{4,6},{6,4},{5,7},{7,5},{8,10},{10,8},{9,1... | collective-permute-start | bytes 884744 | tf_op jit(solution)/shard_map/ppermute | solution.py:454
  102.9 12.2 %collective-permute-start.18 = (bf16[256,768]{1,0:T(8,128)(2,1)}, bf16[256,768]{1,0:T(8,128)(2,1)S(1)}, u32[]{:S(2)}, u32[]{:S(2)}) collective-permute-start(bf16[256,768]{1,0:T(8,128)(2,1)} %get-tuple-element.103), channel_id=1, source_target_pairs={{0,4},{4,0},{8,12},{12,8},{1,5},{5,1},{9,13},{13,9},{2,6},{6,2},{1... | collective-permute-start | bytes 1179656 | tf_op jit(solution)/shard_map/ppermute | solution.py:519
  104.5 19.6 %collective-permute-start.16 = (bf16[288,1280]{1,0:T(8,128)(2,1)}, bf16[288,1280]{1,0:T(8,128)(2,1)S(1)}, u32[]{:S(2)}, u32[]{:S(2)}) collective-permute-start(bf16[288,1280]{1,0:T(8,128)(2,1)} %get-tuple-element.99.refs_2_), channel_id=1, source_target_pairs={{0,2},{2,0},{1,3},{3,1},{4,6},{6,4},{5,7},{7,5},{8,10},{10,8},{9,1... | collective-permute-start | bytes 2211848 | tf_op jit(solution)/shard_map/ppermute | solution.py:454
  105.8 8.7 %copy-start.18 = (bf16[288,1024]{1,0:T(8,128)(2,1)S(1)}, bf16[288,1024]{1,0:T(8,128)(2,1)}, u32[]{:S(2)}) copy-start(bf16[288,1024]{1,0:T(8,128)(2,1)} %get-tuple-element.86) | copy-start | bytes 1769476
  105.8 8.7 %copy-start.2 = (bf16[288,1024]{1,0:T(8,128)(2,1)S(1)}, bf16[288,1024]{1,0:T(8,128)(2,1)}, u32[]{:S(2)}) copy-start(bf16[288,1024]{1,0:T(8,128)(2,1)} %get-tuple-element.101.refs_5_.refs_3_.refs_1_) | copy-start | bytes 1769476
  105.8 9.3 %copy-start.26 = (f32[128,768]{1,0:T(8,128)S(1)}, f32[128,768]{1,0:T(8,128)}, u32[]{:S(2)}) copy-start(f32[128,768]{1,0:T(8,128)} %get-tuple-element.106) | copy-start | bytes 1179652
  113.1 26.9 %collective-permute-start.20 = (bf16[288,1280]{1,0:T(8,128)(2,1)}, bf16[288,1280]{1,0:T(8,128)(2,1)S(1)}, u32[]{:S(2)}, u32[]{:S(2)}) collective-permute-start(bf16[288,1280]{1,0:T(8,128)(2,1)} %get-tuple-element.109), channel_id=1, source_target_pairs={{0,2},{2,0},{1,3},{3,1},{4,6},{6,4},{5,7},{7,5},{8,10},{10,8},{9,1... | collective-permute-start | bytes 2211848 | tf_op jit(solution)/shard_map/ppermute | solution.py:454
  114.5 31.1 %collective-permute-start.11 = (bf16[288,1024]{1,0:T(8,128)(2,1)S(1)}, bf16[288,1024]{1,0:T(8,128)(2,1)S(1)}, u32[]{:S(2)}, u32[]{:S(2)}) collective-permute-start(bf16[288,1024]{1,0:T(8,128)(2,1)S(1)} %copy-done.18), channel_id=1, source_target_pairs={{0,1},{1,0},{2,3},{3,2},{4,5},{5,4},{6,7},{7,6},{8,9},{9,8},{10,11... | collective-permute-start | bytes 1769480 | tf_op jit(solution)/shard_map/ppermute | solution.py:454
  114.6 3.3 %collective-permute-start.17 = (bf16[288,512]{1,0:T(8,128)(2,1)S(1)}, bf16[288,512]{1,0:T(8,128)(2,1)S(1)}, u32[]{:S(2)}, u32[]{:S(2)}) collective-permute-start(bf16[288,512]{1,0:T(8,128)(2,1)S(1)} %slice.33), channel_id=1, source_target_pairs={{0,1},{1,0},{2,3},{3,2},{4,5},{5,4},{6,7},{7,6},{8,9},{9,8},{10,11... | collective-permute-start | bytes 884744 | tf_op jit(solution)/shard_map/ppermute | solution.py:454
  115.1 9.0 %copy-start.6 = (bf16[256,768]{1,0:T(8,128)(2,1)}, bf16[256,768]{1,0:T(8,128)(2,1)S(1)}, u32[]{:S(2)}) copy-start(bf16[256,768]{1,0:T(8,128)(2,1)S(1)} %collective-permute-done.18.refs_8_) | copy-start | bytes 1179652
  115.2 14.6 %collective-permute-start.19 = (bf16[128,768]{1,0:T(8,128)(2,1)S(1)}, bf16[128,768]{1,0:T(8,128)(2,1)S(1)}, u32[]{:S(2)}, u32[]{:S(2)}) collective-permute-start(bf16[128,768]{1,0:T(8,128)(2,1)S(1)} %add_convert_fusion.4), channel_id=1, source_target_pairs={{0,8},{4,12},{8,0},{12,4},{1,9},{5,13},{9,1},{13,5},{2,10},{6,14},... | collective-permute-start | bytes 589832 | tf_op jit(solution)/shard_map/ppermute | solution.py:521
  117.9 6.3 %copy-start.5 = (bf16[288,512]{1,0:T(8,128)(2,1)}, bf16[288,512]{1,0:T(8,128)(2,1)S(1)}, u32[]{:S(2)}) copy-start(bf16[288,512]{1,0:T(8,128)(2,1)S(1)} %collective-permute-done.17.refs_6_.refs_5_.refs_2_) | copy-start | bytes 884740
  125.0 5.9 %copy-start.24 = (bf16[288,768]{1,0:T(8,128)(2,1)S(1)}, bf16[288,768]{1,0:T(8,128)(2,1)}, u32[]{:S(2)}) copy-start(bf16[288,768]{1,0:T(8,128)(2,1)} %get-tuple-element.117.refs_3_) | copy-start | bytes 1327108
  130.5 15.1 %copy-start.7 = (bf16[288,1024]{1,0:T(8,128)(2,1)S(1)}, bf16[288,1024]{1,0:T(8,128)(2,1)}, u32[]{:S(2)}) copy-start(bf16[288,1024]{1,0:T(8,128)(2,1)} %get-tuple-element.85.joined) | copy-start | bytes 1769476
  130.5 21.2 %collective-permute-start.21 = (bf16[256,1280]{1,0:T(8,128)(2,1)}, bf16[256,1280]{1,0:T(8,128)(2,1)S(1)}, u32[]{:S(2)}, u32[]{:S(2)}) collective-permute-start(bf16[256,1280]{1,0:T(8,128)(2,1)} %get-tuple-element.115), channel_id=1, source_target_pairs={{0,4},{4,0},{8,12},{12,8},{1,5},{5,1},{9,13},{13,9},{2,6},{6,2},{1... | collective-permute-start | bytes 1966088 | tf_op jit(solution)/shard_map/ppermute | solution.py:519
  130.9 15.0 %collective-permute-start.23 = (bf16[288,768]{1,0:T(8,128)(2,1)S(1)}, bf16[288,768]{1,0:T(8,128)(2,1)S(1)}, u32[]{:S(2)}, u32[]{:S(2)}) collective-permute-start(bf16[288,768]{1,0:T(8,128)(2,1)S(1)} %copy-done.24), channel_id=1, source_target_pairs={{0,2},{2,0},{1,3},{3,1},{4,6},{6,4},{5,7},{7,5},{8,10},{10,8},{9,1... | collective-permute-start | bytes 1327112 | tf_op jit(solution)/shard_map/ppermute | solution.py:454
  145.1 6.5 %copy-start.16 = (f32[128,1280]{1,0:T(8,128)S(1)}, f32[128,1280]{1,0:T(8,128)}, u32[]{:S(2)}) copy-start(f32[128,1280]{1,0:T(8,128)} %get-tuple-element.116) | copy-start | bytes 1966084
  145.1 28.3 %collective-permute-start.24 = (bf16[256,1280]{1,0:T(8,128)(2,1)}, bf16[256,1280]{1,0:T(8,128)(2,1)S(1)}, u32[]{:S(2)}, u32[]{:S(2)}) collective-permute-start(bf16[256,1280]{1,0:T(8,128)(2,1)} %get-tuple-element.120), channel_id=1, source_target_pairs={{0,4},{4,0},{8,12},{12,8},{1,5},{5,1},{9,13},{13,9},{2,6},{6,2},{1... | collective-permute-start | bytes 1966088 | tf_op jit(solution)/shard_map/ppermute | solution.py:519
  145.9 27.5 %copy-start.17 = (f32[128,1280]{1,0:T(8,128)S(1)}, f32[128,1280]{1,0:T(8,128)}, u32[]{:S(2)}) copy-start(f32[128,1280]{1,0:T(8,128)} %get-tuple-element.121) | copy-start | bytes 1966084
  150.1 27.7 %copy-start.27 = (f32[128,768]{1,0:T(8,128)S(1)}, f32[128,768]{1,0:T(8,128)}, u32[]{:S(2)}) copy-start(f32[128,768]{1,0:T(8,128)} %get-tuple-element.124) | copy-start | bytes 1179652
  150.1 27.6 %collective-permute-start.26 = (bf16[256,768]{1,0:T(8,128)(2,1)}, bf16[256,768]{1,0:T(8,128)(2,1)S(1)}, u32[]{:S(2)}, u32[]{:S(2)}) collective-permute-start(bf16[256,768]{1,0:T(8,128)(2,1)} %get-tuple-element.123), channel_id=1, source_target_pairs={{0,4},{4,0},{8,12},{12,8},{1,5},{5,1},{9,13},{13,9},{2,6},{6,2},{1... | collective-permute-start | bytes 1179656 | tf_op jit(solution)/shard_map/ppermute | solution.py:519
  151.6 26.3 %copy-start.10 = (bf16[256,1280]{1,0:T(8,128)(2,1)}, bf16[256,1280]{1,0:T(8,128)(2,1)S(1)}, u32[]{:S(2)}) copy-start(bf16[256,1280]{1,0:T(8,128)(2,1)S(1)} %collective-permute-done.21.refs_4_) | copy-start | bytes 1966084
  151.7 27.2 %collective-permute-start.22 = (bf16[128,1280]{1,0:T(8,128)(2,1)S(1)}, bf16[128,1280]{1,0:T(8,128)(2,1)S(1)}, u32[]{:S(2)}, u32[]{:S(2)}) collective-permute-start(bf16[128,1280]{1,0:T(8,128)(2,1)S(1)} %add_convert_fusion.2), channel_id=1, source_target_pairs={{0,8},{4,12},{8,0},{12,4},{1,9},{5,13},{9,1},{13,5},{2,10},{6,14},... | collective-permute-start | bytes 983048 | tf_op jit(solution)/shard_map/ppermute | solution.py:521
  173.5 5.4 %copy-start.11 = (bf16[256,1280]{1,0:T(8,128)(2,1)}, bf16[256,1280]{1,0:T(8,128)(2,1)S(1)}, u32[]{:S(2)}) copy-start(bf16[256,1280]{1,0:T(8,128)(2,1)S(1)} %collective-permute-done.24.refs_1_) | copy-start | bytes 1966084
  173.5 19.6 %collective-permute-start.25 = (bf16[128,1280]{1,0:T(8,128)(2,1)S(1)}, bf16[128,1280]{1,0:T(8,128)(2,1)S(1)}, u32[]{:S(2)}, u32[]{:S(2)}) collective-permute-start(bf16[128,1280]{1,0:T(8,128)(2,1)S(1)} %add_convert_fusion.1), channel_id=1, source_target_pairs={{0,8},{4,12},{8,0},{12,4},{1,9},{5,13},{9,1},{13,5},{2,10},{6,14},... | collective-permute-start | bytes 983048 | tf_op jit(solution)/shard_map/ppermute | solution.py:521
  177.7 4.9 %copy-start.12 = (bf16[256,768]{1,0:T(8,128)(2,1)}, bf16[256,768]{1,0:T(8,128)(2,1)S(1)}, u32[]{:S(2)}) copy-start(bf16[256,768]{1,0:T(8,128)(2,1)S(1)} %collective-permute-done.26.refs_4_) | copy-start | bytes 1179652
  177.8 15.3 %collective-permute-start.27 = (bf16[128,768]{1,0:T(8,128)(2,1)S(1)}, bf16[128,768]{1,0:T(8,128)(2,1)S(1)}, u32[]{:S(2)}, u32[]{:S(2)}) collective-permute-start(bf16[128,768]{1,0:T(8,128)(2,1)S(1)} %add_convert_fusion.3), channel_id=1, source_target_pairs={{0,8},{4,12},{8,0},{12,4},{1,9},{5,13},{9,1},{13,5},{2,10},{6,14},... | collective-permute-start | bytes 589832 | tf_op jit(solution)/shard_map/ppermute | solution.py:521
  (18 other events, 22.5 us)

commit v8 on v7

--- a/solution.py
+++ b/solution.py
@@ -664,8 +664,8 @@
             shape(rows, model // 2 + 3 * width // 2),
             shape(rows, 3 * width // 2 + width),
         )
-        back_shapes = (shape(rows, 3 * width // 2), shape(rows, 3 * width // 2))
-        backward_grads = (own, shape(rows, model // 2 + 3 * width // 2))
+        back_shapes = (shape(rows, 2 * width), shape(rows, width))
+        backward_grads = (own, shape(rows, model // 2 + 2 * width))
     else:
         origins = (start,)
         spatial_moves = [(0, at * spatial_size, at * spatial_size, spatial_size) for at in range(spatial_blocks)]

time: 197 us -> 203 us (1.030)
  waiting for transfers between devices: 88.6 us -> 92.1 us
  starting transfers between devices: 29.8 us -> 32.4 us
    ppermute x18, starting transfers between devices: 16.5 us -> 18.9 us  [swap(): return lax.ppermute(array, axis, [(0, 1), (1, 0)])]
    ppermute x4, waiting for transfers between devices: 10.5 us -> 12.6 us  [summed_over_loc(): return (near, beside, lax.ppermute(far, 'loc', APART))]
  transfers between devices with their start and end apart: 28 -> 28, of which waited for: 15 -> 15; matrix products, arithmetic and copies ran while one was open for 3% -> 3% of each run, Pallas kernels for 28% -> 27%
where the time goes in v8:
time: 203 us
  waiting for transfers between devices  92.1 us (45%)
  Pallas kernels  57.2 us (28%)
  starting transfers between devices  32.4 us (16%)
  local copies, waits for them, and re-layouts  18.9 us (9%)
    pallas_call x12, Pallas kernels, call(): pl.pallas_call(body, out_shape=outs, in_specs=specs, out_specs=out_specs,...  57.2 us
    ppermute x18, waiting for transfers between devices, swap(): return lax.ppermute(array, axis, [(0, 1), (1, 0)])  54.2 us
    ppermute x4, waiting for transfers between devices, summed_over_loc(): beside = lax.ppermute(sent, 'loc', PAIRS)  23 us
    ppermute x18, starting transfers between devices, swap(): return lax.ppermute(array, axis, [(0, 1), (1, 0)])  18.9 us
    unnamed x78, local copies, waits for them, and re-layouts  15 us
    ppermute x4, waiting for transfers between devices, summed_over_loc(): return (near, beside, lax.ppermute(far, 'loc', APART))  12.6 us
    ppermute x4, starting transfers between devices, summed_over_loc(): return (near, beside, lax.ppermute(far, 'loc', APART))  5.7 us
  transfers between devices with their start and end apart: 28, of which 15 were waited for; matrix products, arithmetic and copies ran while one was open for 3% of the time, Pallas kernels for 27%

profile of v8, /device:TPU:0, one launch (start us, length us, event | category | flops | bytes accessed | tf_op | source)
XLA Modules:
  0.0 202.9 jit_solution(17560653289894890106)
XLA Ops:
  0.7 2.0 copy.57
  2.7 1.2 dynamic-slice_bitcast_fusion
  3.9 2.9 %collective-permute-start = (bf16[4,128,512]{2,1,0:T(8,128)(2,1)}, bf16[4,128,512]{2,1,0:T(8,128)(2,1)S(1)}, u32[]{:S(2)}, u32[]{:S(2)}) collective-permute-start(bf16[4,128,512]{2,1,0:T(8,128)(2,1)} %get-tuple-element.129), channel_id=1, source_target_pairs={{0,2},{2,0},{1,3},{3,1},{4,6},{6,4},{5,7},{7,5},{8,10},{10,8},{9,1... | collective-permute-start | bytes 1572872 | tf_op jit(solution)/shard_map/ppermute | solution.py:454
  7.5 3.1 %shard_map.139 = (bf16[144,1024]{1,0:T(8,128)(2,1)}, bf16[144,1024]{1,0:T(8,128)(2,1)}, bf16[288,1024]{1,0:T(8,128)(2,1)}, f32[12,1024]{1,0:T(8,128)}) custom-call(s32[1,12]{1,0:T(1,128)} %cloud.1, s32[1,12]{1,0:T(1,128)} %drop.1, s32[1,48]{1,0:T(1,128)} %keep.1, s32[4]{0:T(128)} %pad_add_fusion.where, bf16[6,48,1024]{2,1,0:T(8,128)(2,1)} %bitcast.47, ...), custom_call_target="tpu_custom_call" | custom-call | bytes 3424560 | tf_op jit(solution)/shard_map/pallas_call | solution.py:430
  10.7 2.0 copy.58
  12.7 7.1 %collective-permute-done.refs_3_ = bf16[4,128,512]{2,1,0:T(8,128)(2,1)S(1)} collective-permute-done((bf16[4,128,512]{2,1,0:T(8,128)(2,1)}, bf16[4,128,512]{2,1,0:T(8,128)(2,1)S(1)}, u32[]{:S(2)}, u32[]{:S(2)}) %collective-permute-start) | collective-permute-done | bytes 524320 | tf_op jit(solution)/shard_map/ppermute | solution.py:454
  19.8 2.1 %collective-permute-start.2 = (bf16[4,128,512]{2,1,0:T(8,128)(2,1)S(1)}, bf16[4,128,512]{2,1,0:T(8,128)(2,1)}, u32[]{:S(2)}, u32[]{:S(2)}) collective-permute-start(bf16[4,128,512]{2,1,0:T(8,128)(2,1)S(1)} %collective-permute-done.refs_3_), channel_id=1, source_target_pairs={{0,4},{4,0},{8,12},{12,8},{1,5},{5,1},{9,13},{13,9},{2,6},{6,2},{1... | collective-permute-start | bytes 1572872 | tf_op jit(solution)/shard_map/ppermute | solution.py:481
  21.9 1.5 collective-permute-start.1
  23.5 1.1 dynamic-slice_bitcast_fusion.2
  24.6 1.5 collective-permute-start.5
  26.1 5.0 %collective-permute-done.3.refs_6_ = bf16[4,128,512]{2,1,0:T(8,128)(2,1)S(1)} collective-permute-done((bf16[4,128,512]{2,1,0:T(8,128)(2,1)}, bf16[4,128,512]{2,1,0:T(8,128)(2,1)S(1)}, u32[]{:S(2)}, u32[]{:S(2)}) %collective-permute-start.3) | collective-permute-done | bytes 524320 | tf_op jit(solution)/shard_map/ppermute | solution.py:454
  31.0 1.2 collective-permute-done.2.refs_5_
  32.2 1.2 collective-permute-done.1.refs_4_
  33.4 8.0 %shard_map.142 = (bf16[144,1024]{1,0:T(8,128)(2,1)}, bf16[144,1024]{1,0:T(8,128)(2,1)}, bf16[288,512]{1,0:T(8,128)(2,1)}, bf16[288,512]{1,0:T(8,128)(2,1)}, bf16...) custom-call(s32[4]{0:T(128)} %pad_add_fusion.where, ...), custom_call_target="tpu_custom_call" | custom-call | flops 1207959552 | bytes 9211920 | tf_op jit(solution)/shard_map/pallas_call | solution.py:430
  42.2 1.7 collective-permute-start.10
  44.0 1.6 collective-permute-start.9
  45.6 1.5 collective-permute-start.8
  47.8 2.0 shard_map.144
  50.4 6.8 %collective-permute-done.10.refs_4_ = bf16[4,128,512]{2,1,0:T(8,128)(2,1)S(1)} collective-permute-done((bf16[4,128,512]{2,1,0:T(8,128)(2,1)}, bf16[4,128,512]{2,1,0:T(8,128)(2,1)S(1)}, u32[]{:S(2)}, u32[]{:S(2)}) %collective-permute-start.10) | collective-permute-done | bytes 524320 | tf_op jit(solution)/shard_map/ppermute | solution.py:454
  57.2 1.1 collective-permute-done.9.refs_3_
  58.2 1.3 collective-permute-done.8.refs_2_
  59.5 3.6 %collective-permute-done.7.refs_1_ = bf16[144,1024]{1,0:T(8,128)(2,1)S(1)} collective-permute-done((bf16[144,1024]{1,0:T(8,128)(2,1)}, bf16[144,1024]{1,0:T(8,128)(2,1)S(1)}, u32[]{:S(2)}, u32[]{:S(2)}) %collective-permute-start.7) | collective-permute-done | bytes 294944 | tf_op jit(solution)/shard_map/ppermute | solution.py:454
  63.8 1.7 collective-permute-start.13
  67.2 12.0 %shard_map.146 = (bf16[288,512]{1,0:T(8,128)(2,1)}, bf16[288,1280]{1,0:T(8,128)(2,1)}, bf16[288,1280]{1,0:T(8,128)(2,1)}, bf16[288,1024]{1,0:T(8,128)(2,1)}, bf1...) custom-call(s32[4]{0:T(128)} %pad_add_fusion.where, f32[1,1024]{1,0:T(1,128)} %bitcast.52, ...), custom_call_target="tpu_custom_call" | custom-call | flops 2415919104 | bytes 9851280 | tf_op jit(solution)/shard_map/pallas_call | solution.py:430
  80.0 1.6 collective-permute-start.12
  83.0 3.3 %shard_map.149 = (bf16[144,1024]{1,0:T(8,128)(2,1)}, bf16[144,1024]{1,0:T(8,128)(2,1)}, bf16[288,1280]{1,0:T(8,128)(2,1)}) custom-call(f32[1,1024]{1,0:T(1,128)} %bitcast.53, bf16[288,1024]{1,0:T(8,128)(2,1)} %get-tuple-element.94.here, bf16[288,1024]{1,0:T(8,128)(2,1)} %copy-done.19, ...), custom_call_target="tpu_custom_call", output_to_operand_aliasing={{2}: (5, {})} | custom-call | bytes 3690496 | tf_op jit(solution)/shard_map/pallas_call | solution.py:430
  86.3 1.6 collective-permute-start.15
  87.9 11.6 %collective-permute-done.12.refs_1_ = bf16[288,1280]{1,0:T(8,128)(2,1)S(1)} collective-permute-done((bf16[288,1280]{1,0:T(8,128)(2,1)}, bf16[288,1280]{1,0:T(8,128)(2,1)S(1)}, u32[]{:S(2)}, u32[]{:S(2)}) %collective-permute-start.12) | collective-permute-done | bytes 737312 | tf_op jit(solution)/shard_map/ppermute | solution.py:454
  99.5 0.9 copy-done.4
  100.4 3.3 %shard_map.147 = (bf16[256,768]{1,0:T(8,128)(2,1)}, f32[128,768]{1,0:T(8,128)}, f32[128,768]{1,0:T(8,128)}) custom-call(s32[4]{0:T(128)} %pad_add_fusion.where, bf16[288,512]{1,0:T(8,128)(2,1)} %get-tuple-element.89.refs_0_, bf16[288,1280]{1,0:T(8,128)(2,1)} %copy-done.4, bf16[288,1280]{1,0:T(8,128)(2,1)} %get-tuple-element.90.refs_2_), custom_call_target="tpu_custom_call" | custom-call | flops 452984832 | bytes 2949136 | tf_op jit(solution)/shard_map/pallas_call | solution.py:430
  103.6 1.6 collective-permute-start.18
  105.3 1.5 collective-permute-start.16
  107.5 7.3 %shard_map.150 = (bf16[288,512]{1,0:T(8,128)(2,1)}, bf16[288,1536]{1,0:T(8,128)(2,1)}, bf16[288,1024]{1,0:T(8,128)(2,1)}, bf16[288,512]{1,0:T(8,128)(2,1)}, f32[128,768]{1,0:T(8,128)}) custom-call(s32[4]{0:T(128)} %pad_add_fusion.where, bf16[288,1536]{1,0:T(8,128)(2,1)} %get-tuple-element.87.triple, ...), custom_call_target="tpu_custom_call", output_to_operand_aliasing={{4}: (3, {})} | custom-call | flops 1207959552 | bytes 9011216 | tf_op jit(solution)/shard_map/pallas_call | solution.py:430
  116.0 2.7 %collective-permute-start.19 = (bf16[128,768]{1,0:T(8,128)(2,1)S(1)}, bf16[128,768]{1,0:T(8,128)(2,1)S(1)}, u32[]{:S(2)}, u32[]{:S(2)}) collective-permute-start(bf16[128,768]{1,0:T(8,128)(2,1)S(1)} %add_convert_fusion.3), channel_id=1, source_target_pairs={{0,8},{4,12},{8,0},{12,4},{1,9},{5,13},{9,1},{13,5},{2,10},{6,14},... | collective-permute-start | bytes 589832 | tf_op jit(solution)/shard_map/ppermute | solution.py:521
  118.7 6.2 %collective-permute-done.16.refs_3_ = bf16[288,1280]{1,0:T(8,128)(2,1)S(1)} collective-permute-done((bf16[288,1280]{1,0:T(8,128)(2,1)}, bf16[288,1280]{1,0:T(8,128)(2,1)S(1)}, u32[]{:S(2)}, u32[]{:S(2)}) %collective-permute-start.16) | collective-permute-done | bytes 737312 | tf_op jit(solution)/shard_map/ppermute | solution.py:454
  125.8 4.7 %shard_map.151 = (bf16[256,1280]{1,0:T(8,128)(2,1)}, f32[128,1280]{1,0:T(8,128)}, f32[128,1280]{1,0:T(8,128)}, bf16[288,512]{1,0:T(8,128)(2,1)}, bf16[256,768]{1,0:T(8,128)(2,1)}) custom-call(s32[4]{0:T(128)} %pad_add_fusion.where, bf16[288,512]{1,0:T(8,128)(2,1)} %get-tuple-element.89.refs_0_, ...), custom_call_target="tpu_custom_call", output_to_operand_aliasing={{3}: (8, {}), {4}: (9, {})} | custom-call | flops 754974720 | bytes 6340624 | tf_op jit(solution)/shard_map/pallas_call | solution.py:430
  131.5 1.6 collective-permute-start.23
  133.1 10.8 %collective-permute-done.20.refs_1_ = bf16[288,1536]{1,0:T(8,128)(2,1)S(1)} collective-permute-done((bf16[288,1536]{1,0:T(8,128)(2,1)}, bf16[288,1536]{1,0:T(8,128)(2,1)S(1)}, u32[]{:S(2)}, u32[]{:S(2)}) %collective-permute-start.20) | collective-permute-done | bytes 884768 | tf_op jit(solution)/shard_map/ppermute | solution.py:454
  143.9 0.9 copy-done.12
  144.8 4.7 %shard_map.153 = (bf16[256,1536]{1,0:T(8,128)(2,1)}, f32[128,1536]{1,0:T(8,128)}, f32[128,1536]{1,0:T(8,128)}, f32[128,1280]{1,0:T(8,128)}) custom-call(s32[4]{0:T(128)} %pad_add_fusion.where, bf16[288,512]{1,0:T(8,128)(2,1)} %get-tuple-element.108.refs_0_, bf16[288,1536]{1,0:T(8,128)(2,1)} %copy-done.12, ...), custom_call_target="tpu_custom_call", output_to_operand_aliasing={{3}: (8, {})} | custom-call | flops 905969664 | bytes 6258704 | tf_op jit(solution)/shard_map/pallas_call | solution.py:430
  150.9 2.9 %shard_map.155 = (bf16[256,512]{1,0:T(8,128)(2,1)}, f32[128,512]{1,0:T(8,128)}, f32[128,512]{1,0:T(8,128)}, f32[128,1536]{1,0:T(8,128)}) custom-call(s32[4]{0:T(128)} %pad_add_fusion.where, bf16[288,512]{1,0:T(8,128)(2,1)} %get-tuple-element.111.refs_4_.refs_0_, ...), custom_call_target="tpu_custom_call", output_to_operand_aliasing={{3}: (6, {})} | custom-call | flops 301989888 | bytes 3342352 | tf_op jit(solution)/shard_map/pallas_call | solution.py:430
  153.8 1.6 collective-permute-start.26
  155.5 2.6 %collective-permute-start.22 = (bf16[128,1280]{1,0:T(8,128)(2,1)S(1)}, bf16[128,1280]{1,0:T(8,128)(2,1)S(1)}, u32[]{:S(2)}, u32[]{:S(2)}) collective-permute-start(bf16[128,1280]{1,0:T(8,128)(2,1)S(1)} %add_convert_fusion.2), channel_id=1, source_target_pairs={{0,8},{4,12},{8,0},{12,4},{1,9},{5,13},{9,1},{13,5},{2,10},{6,14},... | collective-permute-start | bytes 983048 | tf_op jit(solution)/shard_map/ppermute | solution.py:521
  158.2 20.4 %collective-permute-done.24.refs_1_ = bf16[256,1536]{1,0:T(8,128)(2,1)S(1)} collective-permute-done((bf16[256,1536]{1,0:T(8,128)(2,1)}, bf16[256,1536]{1,0:T(8,128)(2,1)S(1)}, u32[]{:S(2)}, u32[]{:S(2)}) %collective-permute-start.24) | collective-permute-done | bytes 786464 | tf_op jit(solution)/shard_map/ppermute | solution.py:519
  178.7 2.7 %collective-permute-done.26.refs_4_ = bf16[256,512]{1,0:T(8,128)(2,1)S(1)} collective-permute-done((bf16[256,512]{1,0:T(8,128)(2,1)}, bf16[256,512]{1,0:T(8,128)(2,1)S(1)}, u32[]{:S(2)}, u32[]{:S(2)}) %collective-permute-start.26) | collective-permute-done | bytes 262176 | tf_op jit(solution)/shard_map/ppermute | solution.py:519
  183.5 3.0 %shard_map.154.kept = f32[128,4,512]{2,1,0:T(4,128)} custom-call(f32[128,768]{1,0:T(8,128)} %get-tuple-element.98.refs_0_, bf16[256,768]{1,0:T(8,128)(2,1)} %get-tuple-element.104.refs_1_, bf16[128,768]{1,0:T(8,128)(2,1)} %get-tuple-element.107.refs_2_, f32[128,1280]{1,0:T(8,128)} %get-tuple-element.114.refs_3_, bf16[256,1280]{1,0:T(8,128)(2,1)} %copy-done.11, ...), custom_call_target="tpu_custom_call" | custom-call | bytes 3670016 | tf_op jit(solution)/shard_map/pallas_call | solution.py:430
  186.5 12.6 %collective-permute-done.27.refs_5_ = bf16[128,512]{1,0:T(8,128)(2,1)S(1)} collective-permute-done((bf16[128,512]{1,0:T(8,128)(2,1)S(1)}, bf16[128,512]{1,0:T(8,128)(2,1)S(1)}, u32[]{:S(2)}, u32[]{:S(2)}) %collective-permute-start.27) | collective-permute-done | bytes 131104 | tf_op jit(solution)/shard_map/ppermute | solution.py:521
  199.9 3.0 %shard_map.156 = (f32[128,4,512]{2,1,0:T(4,128)}, f32[128,4,512]{2,1,0:T(4,128)}) custom-call(f32[128,4,512]{2,1,0:T(4,128)} %shard_map.154.kept, f32[128,1536]{1,0:T(8,128)} %get-tuple-element.119.refs_0_, bf16[256,1536]{1,0:T(8,128)(2,1)} %copy-done.10, bf16[128,1536]{1,0:T(8,128)(2,1)} %copy-done.24, ...), custom_call_target="tpu_custom_call", output_to_operand_aliasing={{1}: (0, {})} | custom-call | bytes 4718592 | tf_op jit(solution)/shard_map/pallas_call | solution.py:430
  (120 shorter events, 15.9 us)
Async XLA Ops:
  2.7 7.9 %copy-start = (bf16[512,4,512]{2,0,1:T(8,128)(2,1)}, bf16[512,4,512]{2,0,1:T(8,128)(2,1)S(1)}, u32[]{:S(2)}) copy-start(bf16[512,4,512]{2,0,1:T(8,128)(2,1)S(1)} %copy.57) | copy-start | bytes 6291460
  3.9 15.9 %collective-permute-start = (bf16[4,128,512]{2,1,0:T(8,128)(2,1)}, bf16[4,128,512]{2,1,0:T(8,128)(2,1)S(1)}, u32[]{:S(2)}, u32[]{:S(2)}) collective-permute-start(bf16[4,128,512]{2,1,0:T(8,128)(2,1)} %get-tuple-element.129), channel_id=1, source_target_pairs={{0,2},{2,0},{1,3},{3,1},{4,6},{6,4},{5,7},{7,5},{8,10},{10,8},{9,1... | collective-permute-start | bytes 1572872 | tf_op jit(solution)/shard_map/ppermute | solution.py:454
  10.6 20.4 %collective-permute-start.3 = (bf16[4,128,512]{2,1,0:T(8,128)(2,1)}, bf16[4,128,512]{2,1,0:T(8,128)(2,1)S(1)}, u32[]{:S(2)}, u32[]{:S(2)}) collective-permute-start(bf16[4,128,512]{2,1,0:T(8,128)(2,1)} %get-tuple-element.71), channel_id=1, source_target_pairs={{0,2},{2,0},{1,3},{3,1},{4,6},{6,4},{5,7},{7,5},{8,10},{10,8},{9,1... | collective-permute-start | bytes 1572872 | tf_op jit(solution)/shard_map/ppermute | solution.py:454
  12.7 28.7 %copy-start.3 = (bf16[512,4,512]{2,0,1:T(8,128)(2,1)}, bf16[512,4,512]{2,0,1:T(8,128)(2,1)S(1)}, u32[]{:S(2)}) copy-start(bf16[512,4,512]{2,0,1:T(8,128)(2,1)S(1)} %copy.58) | copy-start | bytes 6291460
  19.8 13.6 %copy-start.8 = (bf16[4,128,512]{2,1,0:T(8,128)(2,1)}, bf16[4,128,512]{2,1,0:T(8,128)(2,1)S(1)}, u32[]{:S(2)}) copy-start(bf16[4,128,512]{2,1,0:T(8,128)(2,1)S(1)} %collective-permute-done.refs_3_) | copy-start | bytes 1572868
  19.8 12.4 %collective-permute-start.2 = (bf16[4,128,512]{2,1,0:T(8,128)(2,1)S(1)}, bf16[4,128,512]{2,1,0:T(8,128)(2,1)}, u32[]{:S(2)}, u32[]{:S(2)}) collective-permute-start(bf16[4,128,512]{2,1,0:T(8,128)(2,1)S(1)} %collective-permute-done.refs_3_), channel_id=1, source_target_pairs={{0,4},{4,0},{8,12},{12,8},{1,5},{5,1},{9,13},{13,9},{2,6},{6,2},{1... | collective-permute-start | bytes 1572872 | tf_op jit(solution)/shard_map/ppermute | solution.py:481
  21.9 11.5 %collective-permute-start.1 = (bf16[4,128,512]{2,1,0:T(8,128)(2,1)S(1)}, bf16[4,128,512]{2,1,0:T(8,128)(2,1)}, u32[]{:S(2)}, u32[]{:S(2)}) collective-permute-start(bf16[4,128,512]{2,1,0:T(8,128)(2,1)S(1)} %collective-permute-done.refs_3_), channel_id=1, source_target_pairs={{0,16},{16,0},{1,17},{17,1},{2,18},{18,2},{3,19},{19,3},{4,20},{20... | collective-permute-start | bytes 1572872 | tf_op jit(solution)/shard_map/ppermute | solution.py:454
  24.6 16.9 %collective-permute-start.5 = (bf16[4,128,512]{2,1,0:T(8,128)(2,1)}, bf16[4,128,512]{2,1,0:T(8,128)(2,1)S(1)}, u32[]{:S(2)}, u32[]{:S(2)}) collective-permute-start(bf16[4,128,512]{2,1,0:T(8,128)(2,1)} %get-tuple-element.73), channel_id=1, source_target_pairs={{0,2},{2,0},{1,3},{3,1},{4,6},{6,4},{5,7},{7,5},{8,10},{10,8},{9,1... | collective-permute-start | bytes 1572872 | tf_op jit(solution)/shard_map/ppermute | solution.py:454
  41.4 8.9 %copy-start.34 = (s32[1,12]{1,0:T(1,128)S(1)}, s32[1,12]{1,0:T(1,128)}, u32[]{:S(2)}) copy-start(s32[1,12]{1,0:T(1,128)} %cloud.1) | copy-start | bytes 148
  41.4 8.9 %copy-start.35 = (s32[1,12]{1,0:T(1,128)S(1)}, s32[1,12]{1,0:T(1,128)}, u32[]{:S(2)}) copy-start(s32[1,12]{1,0:T(1,128)} %drop.1) | copy-start | bytes 148
  41.4 8.9 %copy-start.36 = (bf16[144,1024]{1,0:T(8,128)(2,1)S(1)}, bf16[144,1024]{1,0:T(8,128)(2,1)}, u32[]{:S(2)}) copy-start(bf16[144,1024]{1,0:T(8,128)(2,1)} %get-tuple-element.72.refs_1_) | copy-start | bytes 884740
  42.2 4.8 %collective-permute-start.6 = (bf16[144,1024]{1,0:T(8,128)(2,1)}, bf16[144,1024]{1,0:T(8,128)(2,1)S(1)}, u32[]{:S(2)}, u32[]{:S(2)}) collective-permute-start(bf16[144,1024]{1,0:T(8,128)(2,1)} %get-tuple-element.75.here), channel_id=1, source_target_pairs={{0,1},{1,0},{2,3},{3,2},{4,5},{5,4},{6,7},{7,6},{8,9},{9,8},{10,11... | collective-permute-start | bytes 884744 | tf_op jit(solution)/shard_map/ppermute | solution.py:454
  42.2 14.9 %collective-permute-start.10 = (bf16[4,128,512]{2,1,0:T(8,128)(2,1)}, bf16[4,128,512]{2,1,0:T(8,128)(2,1)S(1)}, u32[]{:S(2)}, u32[]{:S(2)}) collective-permute-start(bf16[4,128,512]{2,1,0:T(8,128)(2,1)} %get-tuple-element.80), channel_id=1, source_target_pairs={{0,2},{2,0},{1,3},{3,1},{4,6},{6,4},{5,7},{7,5},{8,10},{10,8},{9,1... | collective-permute-start | bytes 1572872 | tf_op jit(solution)/shard_map/ppermute | solution.py:454
  44.0 14.3 %collective-permute-start.9 = (bf16[4,128,512]{2,1,0:T(8,128)(2,1)}, bf16[4,128,512]{2,1,0:T(8,128)(2,1)S(1)}, u32[]{:S(2)}, u32[]{:S(2)}) collective-permute-start(bf16[4,128,512]{2,1,0:T(8,128)(2,1)} %get-tuple-element.79.refs_5_), channel_id=1, source_target_pairs={{0,4},{4,0},{8,12},{12,8},{1,5},{5,1},{9,13},{13,9},{2,6},{6,2},{1... | collective-permute-start | bytes 1572872 | tf_op jit(solution)/shard_map/ppermute | solution.py:481
  45.6 14.0 %collective-permute-start.8 = (bf16[4,128,512]{2,1,0:T(8,128)(2,1)}, bf16[4,128,512]{2,1,0:T(8,128)(2,1)S(1)}, u32[]{:S(2)}, u32[]{:S(2)}) collective-permute-start(bf16[4,128,512]{2,1,0:T(8,128)(2,1)} %get-tuple-element.79.refs_5_), channel_id=1, source_target_pairs={{0,16},{16,0},{1,17},{17,1},{2,18},{18,2},{3,19},{19,3},{4,20},{20... | collective-permute-start | bytes 1572872 | tf_op jit(solution)/shard_map/ppermute | solution.py:454
  49.8 13.3 %collective-permute-start.7 = (bf16[144,1024]{1,0:T(8,128)(2,1)}, bf16[144,1024]{1,0:T(8,128)(2,1)S(1)}, u32[]{:S(2)}, u32[]{:S(2)}) collective-permute-start(bf16[144,1024]{1,0:T(8,128)(2,1)} %get-tuple-element.78), channel_id=1, source_target_pairs={{0,2},{2,0},{1,3},{3,1},{4,6},{6,4},{5,7},{7,5},{8,10},{10,8},{9,1... | collective-permute-start | bytes 884744 | tf_op jit(solution)/shard_map/ppermute | solution.py:454
  50.3 16.1 %collective-permute-start.4 = (bf16[144,1024]{1,0:T(8,128)(2,1)S(1)}, bf16[144,1024]{1,0:T(8,128)(2,1)S(1)}, u32[]{:S(2)}, u32[]{:S(2)}) collective-permute-start(bf16[144,1024]{1,0:T(8,128)(2,1)S(1)} %copy-done.36), channel_id=1, source_target_pairs={{0,1},{1,0},{2,3},{3,2},{4,5},{5,4},{6,7},{7,6},{8,9},{9,8},{10,11... | collective-permute-start | bytes 884744 | tf_op jit(solution)/shard_map/ppermute | solution.py:454
  57.2 5.9 %copy-start.20 = (bf16[4,128,512]{2,1,0:T(8,128)(2,1)}, bf16[4,128,512]{2,1,0:T(8,128)(2,1)S(1)}, u32[]{:S(2)}) copy-start(bf16[4,128,512]{2,1,0:T(8,128)(2,1)S(1)} %collective-permute-done.10.refs_4_) | copy-start | bytes 1572868
  58.2 4.9 %copy-start.21 = (bf16[4,128,512]{2,1,0:T(8,128)(2,1)}, bf16[4,128,512]{2,1,0:T(8,128)(2,1)S(1)}, u32[]{:S(2)}) copy-start(bf16[4,128,512]{2,1,0:T(8,128)(2,1)S(1)} %collective-permute-done.9.refs_3_) | copy-start | bytes 1572868
  63.8 15.3 %collective-permute-start.13 = (bf16[288,1024]{1,0:T(8,128)(2,1)}, bf16[288,1024]{1,0:T(8,128)(2,1)S(1)}, u32[]{:S(2)}, u32[]{:S(2)}) collective-permute-start(bf16[288,1024]{1,0:T(8,128)(2,1)} %get-tuple-element.93), channel_id=1, source_target_pairs={{0,2},{2,0},{1,3},{3,1},{4,6},{6,4},{5,7},{7,5},{8,10},{10,8},{9,1... | collective-permute-start | bytes 1769480 | tf_op jit(solution)/shard_map/ppermute | solution.py:454
  80.0 2.2 %collective-permute-start.14 = (bf16[288,1024]{1,0:T(8,128)(2,1)}, bf16[288,1024]{1,0:T(8,128)(2,1)S(1)}, u32[]{:S(2)}, u32[]{:S(2)}) collective-permute-start(bf16[288,1024]{1,0:T(8,128)(2,1)} %get-tuple-element.94.here), channel_id=1, source_target_pairs={{0,1},{1,0},{2,3},{3,2},{4,5},{5,4},{6,7},{7,6},{8,9},{9,8},{10,11... | collective-permute-start | bytes 1769480 | tf_op jit(solution)/shard_map/ppermute | solution.py:454
  80.0 19.5 %collective-permute-start.12 = (bf16[288,1280]{1,0:T(8,128)(2,1)}, bf16[288,1280]{1,0:T(8,128)(2,1)S(1)}, u32[]{:S(2)}, u32[]{:S(2)}) collective-permute-start(bf16[288,1280]{1,0:T(8,128)(2,1)} %get-tuple-element.90.refs_2_), channel_id=1, source_target_pairs={{0,2},{2,0},{1,3},{3,1},{4,6},{6,4},{5,7},{7,5},{8,10},{10,8},{9,1... | collective-permute-start | bytes 2211848 | tf_op jit(solution)/shard_map/ppermute | solution.py:454
  86.3 20.5 %collective-permute-start.15 = (bf16[144,1024]{1,0:T(8,128)(2,1)}, bf16[144,1024]{1,0:T(8,128)(2,1)S(1)}, u32[]{:S(2)}, u32[]{:S(2)}) collective-permute-start(bf16[144,1024]{1,0:T(8,128)(2,1)} %get-tuple-element.97), channel_id=1, source_target_pairs={{0,2},{2,0},{1,3},{3,1},{4,6},{6,4},{5,7},{7,5},{8,10},{10,8},{9,1... | collective-permute-start | bytes 884744 | tf_op jit(solution)/shard_map/ppermute | solution.py:454
  103.6 12.4 %collective-permute-start.18 = (bf16[256,768]{1,0:T(8,128)(2,1)}, bf16[256,768]{1,0:T(8,128)(2,1)S(1)}, u32[]{:S(2)}, u32[]{:S(2)}) collective-permute-start(bf16[256,768]{1,0:T(8,128)(2,1)} %get-tuple-element.103), channel_id=1, source_target_pairs={{0,4},{4,0},{8,12},{12,8},{1,5},{5,1},{9,13},{13,9},{2,6},{6,2},{1... | collective-permute-start | bytes 1179656 | tf_op jit(solution)/shard_map/ppermute | solution.py:519
  105.3 19.6 %collective-permute-start.16 = (bf16[288,1280]{1,0:T(8,128)(2,1)}, bf16[288,1280]{1,0:T(8,128)(2,1)S(1)}, u32[]{:S(2)}, u32[]{:S(2)}) collective-permute-start(bf16[288,1280]{1,0:T(8,128)(2,1)} %get-tuple-element.99.refs_2_), channel_id=1, source_target_pairs={{0,2},{2,0},{1,3},{3,1},{4,6},{6,4},{5,7},{7,5},{8,10},{10,8},{9,1... | collective-permute-start | bytes 2211848 | tf_op jit(solution)/shard_map/ppermute | solution.py:454
  107.5 7.9 %copy-start.18 = (bf16[288,1024]{1,0:T(8,128)(2,1)S(1)}, bf16[288,1024]{1,0:T(8,128)(2,1)}, u32[]{:S(2)}) copy-start(bf16[288,1024]{1,0:T(8,128)(2,1)} %get-tuple-element.86) | copy-start | bytes 1769476
  107.5 7.9 %copy-start.2 = (bf16[288,1024]{1,0:T(8,128)(2,1)S(1)}, bf16[288,1024]{1,0:T(8,128)(2,1)}, u32[]{:S(2)}) copy-start(bf16[288,1024]{1,0:T(8,128)(2,1)} %get-tuple-element.101.refs_5_.refs_3_.refs_1_) | copy-start | bytes 1769476
  107.5 8.5 %copy-start.25 = (f32[128,768]{1,0:T(8,128)S(1)}, f32[128,768]{1,0:T(8,128)}, u32[]{:S(2)}) copy-start(f32[128,768]{1,0:T(8,128)} %get-tuple-element.106) | copy-start | bytes 1179652
  114.9 29.0 %collective-permute-start.20 = (bf16[288,1536]{1,0:T(8,128)(2,1)}, bf16[288,1536]{1,0:T(8,128)(2,1)S(1)}, u32[]{:S(2)}, u32[]{:S(2)}) collective-permute-start(bf16[288,1536]{1,0:T(8,128)(2,1)} %get-tuple-element.109), channel_id=1, source_target_pairs={{0,2},{2,0},{1,3},{3,1},{4,6},{6,4},{5,7},{7,5},{8,10},{10,8},{9,1... | collective-permute-start | bytes 2654216 | tf_op jit(solution)/shard_map/ppermute | solution.py:454
  115.4 34.5 %collective-permute-start.11 = (bf16[288,1024]{1,0:T(8,128)(2,1)S(1)}, bf16[288,1024]{1,0:T(8,128)(2,1)S(1)}, u32[]{:S(2)}, u32[]{:S(2)}) collective-permute-start(bf16[288,1024]{1,0:T(8,128)(2,1)S(1)} %copy-done.18), channel_id=1, source_target_pairs={{0,1},{1,0},{2,3},{3,2},{4,5},{5,4},{6,7},{7,6},{8,9},{9,8},{10,11... | collective-permute-start | bytes 1769480 | tf_op jit(solution)/shard_map/ppermute | solution.py:454
  115.4 3.3 %collective-permute-start.17 = (bf16[288,512]{1,0:T(8,128)(2,1)S(1)}, bf16[288,512]{1,0:T(8,128)(2,1)S(1)}, u32[]{:S(2)}, u32[]{:S(2)}) collective-permute-start(bf16[288,512]{1,0:T(8,128)(2,1)S(1)} %slice.33), channel_id=1, source_target_pairs={{0,1},{1,0},{2,3},{3,2},{4,5},{5,4},{6,7},{7,6},{8,9},{9,8},{10,11... | collective-permute-start | bytes 884744 | tf_op jit(solution)/shard_map/ppermute | solution.py:454
  116.0 8.9 %copy-start.6 = (bf16[256,768]{1,0:T(8,128)(2,1)}, bf16[256,768]{1,0:T(8,128)(2,1)S(1)}, u32[]{:S(2)}) copy-start(bf16[256,768]{1,0:T(8,128)(2,1)S(1)} %collective-permute-done.18.refs_8_) | copy-start | bytes 1179652
  116.0 14.4 %collective-permute-start.19 = (bf16[128,768]{1,0:T(8,128)(2,1)S(1)}, bf16[128,768]{1,0:T(8,128)(2,1)S(1)}, u32[]{:S(2)}, u32[]{:S(2)}) collective-permute-start(bf16[128,768]{1,0:T(8,128)(2,1)S(1)} %add_convert_fusion.3), channel_id=1, source_target_pairs={{0,8},{4,12},{8,0},{12,4},{1,9},{5,13},{9,1},{13,5},{2,10},{6,14},... | collective-permute-start | bytes 589832 | tf_op jit(solution)/shard_map/ppermute | solution.py:521
  118.7 6.2 %copy-start.5 = (bf16[288,512]{1,0:T(8,128)(2,1)}, bf16[288,512]{1,0:T(8,128)(2,1)S(1)}, u32[]{:S(2)}) copy-start(bf16[288,512]{1,0:T(8,128)(2,1)S(1)} %collective-permute-done.17.refs_6_.refs_5_.refs_2_) | copy-start | bytes 884740
  125.8 5.7 %copy-start.29 = (bf16[288,512]{1,0:T(8,128)(2,1)S(1)}, bf16[288,512]{1,0:T(8,128)(2,1)}, u32[]{:S(2)}) copy-start(bf16[288,512]{1,0:T(8,128)(2,1)} %get-tuple-element.117.refs_3_) | copy-start | bytes 884740
  131.1 18.7 %copy-start.7 = (bf16[288,1024]{1,0:T(8,128)(2,1)S(1)}, bf16[288,1024]{1,0:T(8,128)(2,1)}, u32[]{:S(2)}) copy-start(bf16[288,1024]{1,0:T(8,128)(2,1)} %get-tuple-element.85.joined) | copy-start | bytes 1769476
  131.1 24.3 %collective-permute-start.21 = (bf16[256,1280]{1,0:T(8,128)(2,1)}, bf16[256,1280]{1,0:T(8,128)(2,1)S(1)}, u32[]{:S(2)}, u32[]{:S(2)}) collective-permute-start(bf16[256,1280]{1,0:T(8,128)(2,1)} %get-tuple-element.115), channel_id=1, source_target_pairs={{0,4},{4,0},{8,12},{12,8},{1,5},{5,1},{9,13},{13,9},{2,6},{6,2},{1... | collective-permute-start | bytes 1966088 | tf_op jit(solution)/shard_map/ppermute | solution.py:519
  131.5 18.7 %collective-permute-start.23 = (bf16[288,512]{1,0:T(8,128)(2,1)S(1)}, bf16[288,512]{1,0:T(8,128)(2,1)S(1)}, u32[]{:S(2)}, u32[]{:S(2)}) collective-permute-start(bf16[288,512]{1,0:T(8,128)(2,1)S(1)} %copy-done.29), channel_id=1, source_target_pairs={{0,2},{2,0},{1,3},{3,1},{4,6},{6,4},{5,7},{7,5},{8,10},{10,8},{9,1... | collective-permute-start | bytes 884744 | tf_op jit(solution)/shard_map/ppermute | solution.py:454
  149.5 6.0 %copy-start.16 = (f32[128,1280]{1,0:T(8,128)S(1)}, f32[128,1280]{1,0:T(8,128)}, u32[]{:S(2)}) copy-start(f32[128,1280]{1,0:T(8,128)} %get-tuple-element.116) | copy-start | bytes 1966084
  149.5 29.1 %collective-permute-start.24 = (bf16[256,1536]{1,0:T(8,128)(2,1)}, bf16[256,1536]{1,0:T(8,128)(2,1)S(1)}, u32[]{:S(2)}, u32[]{:S(2)}) collective-permute-start(bf16[256,1536]{1,0:T(8,128)(2,1)} %get-tuple-element.120), channel_id=1, source_target_pairs={{0,4},{4,0},{8,12},{12,8},{1,5},{5,1},{9,13},{13,9},{2,6},{6,2},{1... | collective-permute-start | bytes 2359304 | tf_op jit(solution)/shard_map/ppermute | solution.py:519
  150.2 28.4 %copy-start.14 = (f32[128,1536]{1,0:T(8,128)S(1)}, f32[128,1536]{1,0:T(8,128)}, u32[]{:S(2)}) copy-start(f32[128,1536]{1,0:T(8,128)} %get-tuple-element.121) | copy-start | bytes 2359300
  153.8 27.5 %copy-start.32 = (f32[128,512]{1,0:T(8,128)S(1)}, f32[128,512]{1,0:T(8,128)}, u32[]{:S(2)}) copy-start(f32[128,512]{1,0:T(8,128)} %get-tuple-element.124) | copy-start | bytes 786436
  153.8 27.5 %collective-permute-start.26 = (bf16[256,512]{1,0:T(8,128)(2,1)}, bf16[256,512]{1,0:T(8,128)(2,1)S(1)}, u32[]{:S(2)}, u32[]{:S(2)}) collective-permute-start(bf16[256,512]{1,0:T(8,128)(2,1)} %get-tuple-element.123), channel_id=1, source_target_pairs={{0,4},{4,0},{8,12},{12,8},{1,5},{5,1},{9,13},{13,9},{2,6},{6,2},{1... | collective-permute-start | bytes 786440 | tf_op jit(solution)/shard_map/ppermute | solution.py:519
  155.5 26.4 %copy-start.11 = (bf16[256,1280]{1,0:T(8,128)(2,1)}, bf16[256,1280]{1,0:T(8,128)(2,1)S(1)}, u32[]{:S(2)}) copy-start(bf16[256,1280]{1,0:T(8,128)(2,1)S(1)} %collective-permute-done.21.refs_4_) | copy-start | bytes 1966084
  155.5 27.2 %collective-permute-start.22 = (bf16[128,1280]{1,0:T(8,128)(2,1)S(1)}, bf16[128,1280]{1,0:T(8,128)(2,1)S(1)}, u32[]{:S(2)}, u32[]{:S(2)}) collective-permute-start(bf16[128,1280]{1,0:T(8,128)(2,1)S(1)} %add_convert_fusion.2), channel_id=1, source_target_pairs={{0,8},{4,12},{8,0},{12,4},{1,9},{5,13},{9,1},{13,5},{2,10},{6,14},... | collective-permute-start | bytes 983048 | tf_op jit(solution)/shard_map/ppermute | solution.py:521
  178.6 20.5 %collective-permute-start.25 = (bf16[128,1536]{1,0:T(8,128)(2,1)S(1)}, bf16[128,1536]{1,0:T(8,128)(2,1)S(1)}, u32[]{:S(2)}, u32[]{:S(2)}) collective-permute-start(bf16[128,1536]{1,0:T(8,128)(2,1)S(1)} %add_convert_fusion.1), channel_id=1, source_target_pairs={{0,8},{4,12},{8,0},{12,4},{1,9},{5,13},{9,1},{13,5},{2,10},{6,14},... | collective-permute-start | bytes 1179656 | tf_op jit(solution)/shard_map/ppermute | solution.py:521
  181.3 5.2 %copy-start.17 = (bf16[256,512]{1,0:T(8,128)(2,1)}, bf16[256,512]{1,0:T(8,128)(2,1)S(1)}, u32[]{:S(2)}) copy-start(bf16[256,512]{1,0:T(8,128)(2,1)S(1)} %collective-permute-done.26.refs_4_) | copy-start | bytes 786436
  181.4 17.7 %collective-permute-start.27 = (bf16[128,512]{1,0:T(8,128)(2,1)S(1)}, bf16[128,512]{1,0:T(8,128)(2,1)S(1)}, u32[]{:S(2)}, u32[]{:S(2)}) collective-permute-start(bf16[128,512]{1,0:T(8,128)(2,1)S(1)} %add_convert_fusion.4), channel_id=1, source_target_pairs={{0,8},{4,12},{8,0},{12,4},{1,9},{5,13},{9,1},{13,5},{2,10},{6,14},... | collective-permute-start | bytes 393224 | tf_op jit(solution)/shard_map/ppermute | solution.py:521
  (18 other events, 21.7 us)

commit v9 on v8

--- a/solution.py
+++ b/solution.py
@@ -664,8 +664,8 @@
             shape(rows, model // 2 + 3 * width // 2),
             shape(rows, 3 * width // 2 + width),
         )
-        back_shapes = (shape(rows, 2 * width), shape(rows, width))
-        backward_grads = (own, shape(rows, model // 2 + 2 * width))
+        back_shapes = (shape(rows, width), shape(rows, 2 * width))
+        backward_grads = (own, shape(rows, model // 2 + width))
     else:
         origins = (start,)
         spatial_moves = [(0, at * spatial_size, at * spatial_size, spatial_size) for at in range(spatial_blocks)]

time: 203 us -> 214 us (1.054)
  waiting for transfers between devices: 92.1 us -> 106 us
  starting transfers between devices: 32.4 us -> 29.4 us
    ppermute x18, waiting for transfers between devices: 54.2 us -> 69.5 us  [swap(): return lax.ppermute(array, axis, [(0, 1), (1, 0)])]
    ppermute x18, starting transfers between devices: 18.9 us -> 16.2 us  [swap(): return lax.ppermute(array, axis, [(0, 1), (1, 0)])]
  transfers between devices with their start and end apart: 28 -> 28, of which waited for: 15 -> 17; matrix products, arithmetic and copies ran while one was open for 3% -> 3% of each run, Pallas kernels for 27% -> 25%
where the time goes in v9:
time: 214 us
  waiting for transfers between devices  106 us (50%)
  Pallas kernels  57.3 us (27%)
  starting transfers between devices  29.4 us (14%)
  local copies, waits for them, and re-layouts  18.9 us (9%)
    ppermute x18, waiting for transfers between devices, swap(): return lax.ppermute(array, axis, [(0, 1), (1, 0)])  69.5 us
    pallas_call x12, Pallas kernels, call(): pl.pallas_call(body, out_shape=outs, in_specs=specs, out_specs=out_specs,...  57.3 us
    ppermute x4, waiting for transfers between devices, summed_over_loc(): beside = lax.ppermute(sent, 'loc', PAIRS)  21.1 us
    ppermute x18, starting transfers between devices, swap(): return lax.ppermute(array, axis, [(0, 1), (1, 0)])  16.2 us
    unnamed x78, local copies, waits for them, and re-layouts  14.9 us
    ppermute x4, waiting for transfers between devices, summed_over_loc(): return (near, beside, lax.ppermute(far, 'loc', APART))  12.9 us
    ppermute x4, starting transfers between devices, summed_over_loc(): return (near, beside, lax.ppermute(far, 'loc', APART))  6.74 us
  transfers between devices with their start and end apart: 28, of which 17 were waited for; matrix products, arithmetic and copies ran while one was open for 3% of the time, Pallas kernels for 25%

profile of v9, /device:TPU:0, one launch (start us, length us, event | category | flops | bytes accessed | tf_op | source)
XLA Modules:
  0.0 213.7 jit_solution(16845463219659555890)
XLA Ops:
  0.7 2.0 copy.57
  2.7 1.2 dynamic-slice_bitcast_fusion
  3.9 2.9 %collective-permute-start = (bf16[4,128,512]{2,1,0:T(8,128)(2,1)}, bf16[4,128,512]{2,1,0:T(8,128)(2,1)S(1)}, u32[]{:S(2)}, u32[]{:S(2)}) collective-permute-start(bf16[4,128,512]{2,1,0:T(8,128)(2,1)} %get-tuple-element.129), channel_id=1, source_target_pairs={{0,2},{2,0},{1,3},{3,1},{4,6},{6,4},{5,7},{7,5},{8,10},{10,8},{9,1... | collective-permute-start | bytes 1572872 | tf_op jit(solution)/shard_map/ppermute | solution.py:454
  7.5 3.1 %shard_map.139 = (bf16[144,1024]{1,0:T(8,128)(2,1)}, bf16[144,1024]{1,0:T(8,128)(2,1)}, bf16[288,1024]{1,0:T(8,128)(2,1)}, f32[12,1024]{1,0:T(8,128)}) custom-call(s32[1,12]{1,0:T(1,128)} %cloud.1, s32[1,12]{1,0:T(1,128)} %drop.1, s32[1,48]{1,0:T(1,128)} %keep.1, s32[4]{0:T(128)} %pad_add_fusion.where, bf16[6,48,1024]{2,1,0:T(8,128)(2,1)} %bitcast.47, ...), custom_call_target="tpu_custom_call" | custom-call | bytes 3424560 | tf_op jit(solution)/shard_map/pallas_call | solution.py:430
  10.7 2.0 copy.58
  12.7 7.1 %collective-permute-done.refs_3_ = bf16[4,128,512]{2,1,0:T(8,128)(2,1)S(1)} collective-permute-done((bf16[4,128,512]{2,1,0:T(8,128)(2,1)}, bf16[4,128,512]{2,1,0:T(8,128)(2,1)S(1)}, u32[]{:S(2)}, u32[]{:S(2)}) %collective-permute-start) | collective-permute-done | bytes 524320 | tf_op jit(solution)/shard_map/ppermute | solution.py:454
  19.8 2.1 %collective-permute-start.2 = (bf16[4,128,512]{2,1,0:T(8,128)(2,1)S(1)}, bf16[4,128,512]{2,1,0:T(8,128)(2,1)}, u32[]{:S(2)}, u32[]{:S(2)}) collective-permute-start(bf16[4,128,512]{2,1,0:T(8,128)(2,1)S(1)} %collective-permute-done.refs_3_), channel_id=1, source_target_pairs={{0,4},{4,0},{8,12},{12,8},{1,5},{5,1},{9,13},{13,9},{2,6},{6,2},{1... | collective-permute-start | bytes 1572872 | tf_op jit(solution)/shard_map/ppermute | solution.py:481
  21.9 1.5 collective-permute-start.1
  23.5 1.1 dynamic-slice_bitcast_fusion.2
  24.6 1.5 collective-permute-start.5
  26.1 5.0 %collective-permute-done.3.refs_6_ = bf16[4,128,512]{2,1,0:T(8,128)(2,1)S(1)} collective-permute-done((bf16[4,128,512]{2,1,0:T(8,128)(2,1)}, bf16[4,128,512]{2,1,0:T(8,128)(2,1)S(1)}, u32[]{:S(2)}, u32[]{:S(2)}) %collective-permute-start.3) | collective-permute-done | bytes 524320 | tf_op jit(solution)/shard_map/ppermute | solution.py:454
  31.0 1.2 collective-permute-done.2.refs_5_
  32.2 1.2 collective-permute-done.1.refs_4_
  33.4 8.0 %shard_map.142 = (bf16[144,1024]{1,0:T(8,128)(2,1)}, bf16[144,1024]{1,0:T(8,128)(2,1)}, bf16[288,512]{1,0:T(8,128)(2,1)}, bf16[288,512]{1,0:T(8,128)(2,1)}, bf16...) custom-call(s32[4]{0:T(128)} %pad_add_fusion.where, ...), custom_call_target="tpu_custom_call" | custom-call | flops 1207959552 | bytes 9211920 | tf_op jit(solution)/shard_map/pallas_call | solution.py:430
  42.2 1.7 collective-permute-start.10
  44.0 1.6 collective-permute-start.9
  45.6 1.5 collective-permute-start.8
  47.8 2.0 shard_map.144
  50.5 6.7 %collective-permute-done.10.refs_4_ = bf16[4,128,512]{2,1,0:T(8,128)(2,1)S(1)} collective-permute-done((bf16[4,128,512]{2,1,0:T(8,128)(2,1)}, bf16[4,128,512]{2,1,0:T(8,128)(2,1)S(1)}, u32[]{:S(2)}, u32[]{:S(2)}) %collective-permute-start.10) | collective-permute-done | bytes 524320 | tf_op jit(solution)/shard_map/ppermute | solution.py:454
  57.2 1.1 collective-permute-done.9.refs_3_
  58.2 1.3 collective-permute-done.8.refs_2_
  59.5 3.6 %collective-permute-done.7.refs_1_ = bf16[144,1024]{1,0:T(8,128)(2,1)S(1)} collective-permute-done((bf16[144,1024]{1,0:T(8,128)(2,1)}, bf16[144,1024]{1,0:T(8,128)(2,1)S(1)}, u32[]{:S(2)}, u32[]{:S(2)}) %collective-permute-start.7) | collective-permute-done | bytes 294944 | tf_op jit(solution)/shard_map/ppermute | solution.py:454
  63.8 1.7 collective-permute-start.13
  67.1 12.0 %shard_map.146 = (bf16[288,512]{1,0:T(8,128)(2,1)}, bf16[288,1280]{1,0:T(8,128)(2,1)}, bf16[288,1280]{1,0:T(8,128)(2,1)}, bf16[288,1024]{1,0:T(8,128)(2,1)}, bf1...) custom-call(s32[4]{0:T(128)} %pad_add_fusion.where, f32[1,1024]{1,0:T(1,128)} %bitcast.52, ...), custom_call_target="tpu_custom_call" | custom-call | flops 2415919104 | bytes 9851280 | tf_op jit(solution)/shard_map/pallas_call | solution.py:430
  80.2 16.9 %collective-permute-done.12.refs_1_ = bf16[288,1280]{1,0:T(8,128)(2,1)S(1)} collective-permute-done((bf16[288,1280]{1,0:T(8,128)(2,1)}, bf16[288,1280]{1,0:T(8,128)(2,1)S(1)}, u32[]{:S(2)}, u32[]{:S(2)}) %collective-permute-start.12) | collective-permute-done | bytes 737312 | tf_op jit(solution)/shard_map/ppermute | solution.py:454
  97.2 0.9 copy-done.4
  98.0 3.3 %shard_map.147 = (bf16[256,768]{1,0:T(8,128)(2,1)}, f32[128,768]{1,0:T(8,128)}, f32[128,768]{1,0:T(8,128)}) custom-call(s32[4]{0:T(128)} %pad_add_fusion.where, bf16[288,512]{1,0:T(8,128)(2,1)} %get-tuple-element.89.refs_0_, bf16[288,1280]{1,0:T(8,128)(2,1)} %copy-done.4, bf16[288,1280]{1,0:T(8,128)(2,1)} %get-tuple-element.90.refs_2_), custom_call_target="tpu_custom_call" | custom-call | flops 452984832 | bytes 2949136 | tf_op jit(solution)/shard_map/pallas_call | solution.py:430
  101.4 1.6 collective-permute-start.18
  103.8 3.3 %shard_map.149 = (bf16[144,1024]{1,0:T(8,128)(2,1)}, bf16[144,1024]{1,0:T(8,128)(2,1)}, bf16[288,1280]{1,0:T(8,128)(2,1)}) custom-call(f32[1,1024]{1,0:T(1,128)} %bitcast.53, bf16[288,1024]{1,0:T(8,128)(2,1)} %get-tuple-element.94.here, bf16[288,1024]{1,0:T(8,128)(2,1)} %copy-done.20, ...), custom_call_target="tpu_custom_call", output_to_operand_aliasing={{2}: (5, {})} | custom-call | bytes 3690496 | tf_op jit(solution)/shard_map/pallas_call | solution.py:430
  107.6 1.5 collective-permute-start.15
  109.2 1.9 collective-permute-done.18.refs_8_
  111.2 2.7 %collective-permute-start.19 = (bf16[128,768]{1,0:T(8,128)(2,1)S(1)}, bf16[128,768]{1,0:T(8,128)(2,1)S(1)}, u32[]{:S(2)}, u32[]{:S(2)}) collective-permute-start(bf16[128,768]{1,0:T(8,128)(2,1)S(1)} %add_convert_fusion.4), channel_id=1, source_target_pairs={{0,8},{4,12},{8,0},{12,4},{1,9},{5,13},{9,1},{13,5},{2,10},{6,14},... | collective-permute-start | bytes 589832 | tf_op jit(solution)/shard_map/ppermute | solution.py:521
  113.8 16.4 %collective-permute-done.15.refs_1_ = bf16[144,1024]{1,0:T(8,128)(2,1)S(1)} collective-permute-done((bf16[144,1024]{1,0:T(8,128)(2,1)}, bf16[144,1024]{1,0:T(8,128)(2,1)S(1)}, u32[]{:S(2)}, u32[]{:S(2)}) %collective-permute-start.15) | collective-permute-done | bytes 294944 | tf_op jit(solution)/shard_map/ppermute | solution.py:454
  130.9 7.1 %shard_map.150 = (bf16[288,512]{1,0:T(8,128)(2,1)}, bf16[288,1024]{1,0:T(8,128)(2,1)}, bf16[288,512]{1,0:T(8,128)(2,1)}, bf16[288,1024]{1,0:T(8,128)(2,1)}, f32[128,768]{1,0:T(8,128)}) custom-call(s32[4]{0:T(128)} %pad_add_fusion.where, bf16[288,1536]{1,0:T(8,128)(2,1)} %get-tuple-element.87.triple, ...), custom_call_target="tpu_custom_call", output_to_operand_aliasing={{4}: (3, {})} | custom-call | flops 1207959552 | bytes 8716304 | tf_op jit(solution)/shard_map/pallas_call | solution.py:430
  139.5 4.7 %shard_map.151 = (bf16[256,1280]{1,0:T(8,128)(2,1)}, f32[128,1280]{1,0:T(8,128)}, f32[128,1280]{1,0:T(8,128)}, bf16[288,512]{1,0:T(8,128)(2,1)}, bf16[256,768]{1,0:T(8,128)(2,1)}) custom-call(s32[4]{0:T(128)} %pad_add_fusion.where, bf16[288,512]{1,0:T(8,128)(2,1)} %get-tuple-element.89.refs_0_, ...), custom_call_target="tpu_custom_call", output_to_operand_aliasing={{3}: (8, {}), {4}: (9, {})} | custom-call | flops 754974720 | bytes 6340624 | tf_op jit(solution)/shard_map/pallas_call | solution.py:430
  145.2 1.6 collective-permute-start.23
  146.9 7.6 %collective-permute-done.20.refs_1_ = bf16[288,1024]{1,0:T(8,128)(2,1)S(1)} collective-permute-done((bf16[288,1024]{1,0:T(8,128)(2,1)}, bf16[288,1024]{1,0:T(8,128)(2,1)S(1)}, u32[]{:S(2)}, u32[]{:S(2)}) %collective-permute-start.20) | collective-permute-done | bytes 589856 | tf_op jit(solution)/shard_map/ppermute | solution.py:454
  155.3 3.9 %shard_map.153 = (bf16[256,1024]{1,0:T(8,128)(2,1)}, f32[128,1024]{1,0:T(8,128)}, f32[128,1024]{1,0:T(8,128)}, f32[128,1280]{1,0:T(8,128)}) custom-call(s32[4]{0:T(128)} %pad_add_fusion.where, bf16[288,512]{1,0:T(8,128)(2,1)} %get-tuple-element.108.refs_0_, bf16[288,1024]{1,0:T(8,128)(2,1)} %copy-done.18, ...), custom_call_target="tpu_custom_call", output_to_operand_aliasing={{3}: (8, {})} | custom-call | flops 603979776 | bytes 4882448 | tf_op jit(solution)/shard_map/pallas_call | solution.py:430
  159.7 3.7 %collective-permute-done.23.refs_4_ = bf16[288,1024]{1,0:T(8,128)(2,1)S(1)} collective-permute-done((bf16[288,1024]{1,0:T(8,128)(2,1)S(1)}, bf16[288,1024]{1,0:T(8,128)(2,1)S(1)}, u32[]{:S(2)}, u32[]{:S(2)}) %collective-permute-start.23) | collective-permute-done | bytes 589856 | tf_op jit(solution)/shard_map/ppermute | solution.py:454
  164.2 3.8 %shard_map.155 = (bf16[256,1024]{1,0:T(8,128)(2,1)}, f32[128,1024]{1,0:T(8,128)}, f32[128,1024]{1,0:T(8,128)}, f32[128,1024]{1,0:T(8,128)}) custom-call(s32[4]{0:T(128)} %pad_add_fusion.where, bf16[288,512]{1,0:T(8,128)(2,1)} %get-tuple-element.111.refs_4_.refs_0_, ...), custom_call_target="tpu_custom_call", output_to_operand_aliasing={{3}: (6, {})} | custom-call | flops 603979776 | bytes 4456464 | tf_op jit(solution)/shard_map/pallas_call | solution.py:430
  168.6 2.7 %collective-permute-start.22 = (bf16[128,1280]{1,0:T(8,128)(2,1)S(1)}, bf16[128,1280]{1,0:T(8,128)(2,1)S(1)}, u32[]{:S(2)}, u32[]{:S(2)}) collective-permute-start(bf16[128,1280]{1,0:T(8,128)(2,1)S(1)} %add_convert_fusion.1), channel_id=1, source_target_pairs={{0,8},{4,12},{8,0},{12,4},{1,9},{5,13},{9,1},{13,5},{2,10},{6,14},... | collective-permute-start | bytes 983048 | tf_op jit(solution)/shard_map/ppermute | solution.py:521
  171.2 11.4 %collective-permute-done.24.refs_1_ = bf16[256,1024]{1,0:T(8,128)(2,1)S(1)} collective-permute-done((bf16[256,1024]{1,0:T(8,128)(2,1)}, bf16[256,1024]{1,0:T(8,128)(2,1)S(1)}, u32[]{:S(2)}, u32[]{:S(2)}) %collective-permute-start.24) | collective-permute-done | bytes 524320 | tf_op jit(solution)/shard_map/ppermute | solution.py:519
  183.4 7.8 %collective-permute-done.26.refs_4_ = bf16[256,1024]{1,0:T(8,128)(2,1)S(1)} collective-permute-done((bf16[256,1024]{1,0:T(8,128)(2,1)}, bf16[256,1024]{1,0:T(8,128)(2,1)S(1)}, u32[]{:S(2)}, u32[]{:S(2)}) %collective-permute-start.26) | collective-permute-done | bytes 524320 | tf_op jit(solution)/shard_map/ppermute | solution.py:519
  192.5 0.9 copy.52
  194.1 3.0 %shard_map.154.kept = f32[128,4,512]{2,1,0:T(4,128)} custom-call(f32[128,768]{1,0:T(8,128)} %get-tuple-element.98.refs_0_, bf16[256,768]{1,0:T(8,128)(2,1)} %get-tuple-element.104.refs_1_, bf16[128,768]{1,0:T(8,128)(2,1)} %get-tuple-element.107.refs_2_, f32[128,1280]{1,0:T(8,128)} %get-tuple-element.114.refs_3_, bf16[256,1280]{1,0:T(8,128)(2,1)} %copy-done.10, ...), custom_call_target="tpu_custom_call" | custom-call | bytes 3670016 | tf_op jit(solution)/shard_map/pallas_call | solution.py:430
  197.1 10.0 %collective-permute-done.25.refs_2_ = bf16[128,1024]{1,0:T(8,128)(2,1)S(1)} collective-permute-done((bf16[128,1024]{1,0:T(8,128)(2,1)S(1)}, bf16[128,1024]{1,0:T(8,128)(2,1)S(1)}, u32[]{:S(2)}, u32[]{:S(2)}) %collective-permute-start.25) | collective-permute-done | bytes 262176 | tf_op jit(solution)/shard_map/ppermute | solution.py:521
  207.1 2.9 %collective-permute-done.27.refs_5_ = bf16[128,1024]{1,0:T(8,128)(2,1)S(1)} collective-permute-done((bf16[128,1024]{1,0:T(8,128)(2,1)S(1)}, bf16[128,1024]{1,0:T(8,128)(2,1)S(1)}, u32[]{:S(2)}, u32[]{:S(2)}) %collective-permute-start.27) | collective-permute-done | bytes 262176 | tf_op jit(solution)/shard_map/ppermute | solution.py:521
  210.7 3.0 %shard_map.156 = (f32[128,4,512]{2,1,0:T(4,128)}, f32[128,4,512]{2,1,0:T(4,128)}) custom-call(f32[128,4,512]{2,1,0:T(4,128)} %shard_map.154.kept, f32[128,1024]{1,0:T(8,128)} %get-tuple-element.119.refs_0_, bf16[256,1024]{1,0:T(8,128)(2,1)} %copy-done.11, bf16[128,1024]{1,0:T(8,128)(2,1)} %copy-done.32, ...), custom_call_target="tpu_custom_call", output_to_operand_aliasing={{1}: (0, {})} | custom-call | bytes 4718592 | tf_op jit(solution)/shard_map/pallas_call | solution.py:430
  (120 shorter events, 17.0 us)
Async XLA Ops:
  2.7 7.9 %copy-start = (bf16[512,4,512]{2,0,1:T(8,128)(2,1)}, bf16[512,4,512]{2,0,1:T(8,128)(2,1)S(1)}, u32[]{:S(2)}) copy-start(bf16[512,4,512]{2,0,1:T(8,128)(2,1)S(1)} %copy.57) | copy-start | bytes 6291460
  3.9 15.9 %collective-permute-start = (bf16[4,128,512]{2,1,0:T(8,128)(2,1)}, bf16[4,128,512]{2,1,0:T(8,128)(2,1)S(1)}, u32[]{:S(2)}, u32[]{:S(2)}) collective-permute-start(bf16[4,128,512]{2,1,0:T(8,128)(2,1)} %get-tuple-element.129), channel_id=1, source_target_pairs={{0,2},{2,0},{1,3},{3,1},{4,6},{6,4},{5,7},{7,5},{8,10},{10,8},{9,1... | collective-permute-start | bytes 1572872 | tf_op jit(solution)/shard_map/ppermute | solution.py:454
  10.6 20.4 %collective-permute-start.3 = (bf16[4,128,512]{2,1,0:T(8,128)(2,1)}, bf16[4,128,512]{2,1,0:T(8,128)(2,1)S(1)}, u32[]{:S(2)}, u32[]{:S(2)}) collective-permute-start(bf16[4,128,512]{2,1,0:T(8,128)(2,1)} %get-tuple-element.71), channel_id=1, source_target_pairs={{0,2},{2,0},{1,3},{3,1},{4,6},{6,4},{5,7},{7,5},{8,10},{10,8},{9,1... | collective-permute-start | bytes 1572872 | tf_op jit(solution)/shard_map/ppermute | solution.py:454
  12.7 28.7 %copy-start.3 = (bf16[512,4,512]{2,0,1:T(8,128)(2,1)}, bf16[512,4,512]{2,0,1:T(8,128)(2,1)S(1)}, u32[]{:S(2)}) copy-start(bf16[512,4,512]{2,0,1:T(8,128)(2,1)S(1)} %copy.58) | copy-start | bytes 6291460
  19.8 13.6 %copy-start.8 = (bf16[4,128,512]{2,1,0:T(8,128)(2,1)}, bf16[4,128,512]{2,1,0:T(8,128)(2,1)S(1)}, u32[]{:S(2)}) copy-start(bf16[4,128,512]{2,1,0:T(8,128)(2,1)S(1)} %collective-permute-done.refs_3_) | copy-start | bytes 1572868
  19.8 12.4 %collective-permute-start.2 = (bf16[4,128,512]{2,1,0:T(8,128)(2,1)S(1)}, bf16[4,128,512]{2,1,0:T(8,128)(2,1)}, u32[]{:S(2)}, u32[]{:S(2)}) collective-permute-start(bf16[4,128,512]{2,1,0:T(8,128)(2,1)S(1)} %collective-permute-done.refs_3_), channel_id=1, source_target_pairs={{0,4},{4,0},{8,12},{12,8},{1,5},{5,1},{9,13},{13,9},{2,6},{6,2},{1... | collective-permute-start | bytes 1572872 | tf_op jit(solution)/shard_map/ppermute | solution.py:481
  21.9 11.5 %collective-permute-start.1 = (bf16[4,128,512]{2,1,0:T(8,128)(2,1)S(1)}, bf16[4,128,512]{2,1,0:T(8,128)(2,1)}, u32[]{:S(2)}, u32[]{:S(2)}) collective-permute-start(bf16[4,128,512]{2,1,0:T(8,128)(2,1)S(1)} %collective-permute-done.refs_3_), channel_id=1, source_target_pairs={{0,16},{16,0},{1,17},{17,1},{2,18},{18,2},{3,19},{19,3},{4,20},{20... | collective-permute-start | bytes 1572872 | tf_op jit(solution)/shard_map/ppermute | solution.py:454
  24.6 16.9 %collective-permute-start.5 = (bf16[4,128,512]{2,1,0:T(8,128)(2,1)}, bf16[4,128,512]{2,1,0:T(8,128)(2,1)S(1)}, u32[]{:S(2)}, u32[]{:S(2)}) collective-permute-start(bf16[4,128,512]{2,1,0:T(8,128)(2,1)} %get-tuple-element.73), channel_id=1, source_target_pairs={{0,2},{2,0},{1,3},{3,1},{4,6},{6,4},{5,7},{7,5},{8,10},{10,8},{9,1... | collective-permute-start | bytes 1572872 | tf_op jit(solution)/shard_map/ppermute | solution.py:454
  41.4 8.9 %copy-start.34 = (s32[1,12]{1,0:T(1,128)S(1)}, s32[1,12]{1,0:T(1,128)}, u32[]{:S(2)}) copy-start(s32[1,12]{1,0:T(1,128)} %cloud.1) | copy-start | bytes 148
  41.4 8.9 %copy-start.35 = (s32[1,12]{1,0:T(1,128)S(1)}, s32[1,12]{1,0:T(1,128)}, u32[]{:S(2)}) copy-start(s32[1,12]{1,0:T(1,128)} %drop.1) | copy-start | bytes 148
  41.4 8.9 %copy-start.36 = (bf16[144,1024]{1,0:T(8,128)(2,1)S(1)}, bf16[144,1024]{1,0:T(8,128)(2,1)}, u32[]{:S(2)}) copy-start(bf16[144,1024]{1,0:T(8,128)(2,1)} %get-tuple-element.72.refs_1_) | copy-start | bytes 884740
  42.2 4.8 %collective-permute-start.6 = (bf16[144,1024]{1,0:T(8,128)(2,1)}, bf16[144,1024]{1,0:T(8,128)(2,1)S(1)}, u32[]{:S(2)}, u32[]{:S(2)}) collective-permute-start(bf16[144,1024]{1,0:T(8,128)(2,1)} %get-tuple-element.75.here), channel_id=1, source_target_pairs={{0,1},{1,0},{2,3},{3,2},{4,5},{5,4},{6,7},{7,6},{8,9},{9,8},{10,11... | collective-permute-start | bytes 884744 | tf_op jit(solution)/shard_map/ppermute | solution.py:454
  42.2 14.9 %collective-permute-start.10 = (bf16[4,128,512]{2,1,0:T(8,128)(2,1)}, bf16[4,128,512]{2,1,0:T(8,128)(2,1)S(1)}, u32[]{:S(2)}, u32[]{:S(2)}) collective-permute-start(bf16[4,128,512]{2,1,0:T(8,128)(2,1)} %get-tuple-element.80), channel_id=1, source_target_pairs={{0,2},{2,0},{1,3},{3,1},{4,6},{6,4},{5,7},{7,5},{8,10},{10,8},{9,1... | collective-permute-start | bytes 1572872 | tf_op jit(solution)/shard_map/ppermute | solution.py:454
  44.0 14.3 %collective-permute-start.9 = (bf16[4,128,512]{2,1,0:T(8,128)(2,1)}, bf16[4,128,512]{2,1,0:T(8,128)(2,1)S(1)}, u32[]{:S(2)}, u32[]{:S(2)}) collective-permute-start(bf16[4,128,512]{2,1,0:T(8,128)(2,1)} %get-tuple-element.79.refs_5_), channel_id=1, source_target_pairs={{0,4},{4,0},{8,12},{12,8},{1,5},{5,1},{9,13},{13,9},{2,6},{6,2},{1... | collective-permute-start | bytes 1572872 | tf_op jit(solution)/shard_map/ppermute | solution.py:481
  45.6 14.0 %collective-permute-start.8 = (bf16[4,128,512]{2,1,0:T(8,128)(2,1)}, bf16[4,128,512]{2,1,0:T(8,128)(2,1)S(1)}, u32[]{:S(2)}, u32[]{:S(2)}) collective-permute-start(bf16[4,128,512]{2,1,0:T(8,128)(2,1)} %get-tuple-element.79.refs_5_), channel_id=1, source_target_pairs={{0,16},{16,0},{1,17},{17,1},{2,18},{18,2},{3,19},{19,3},{4,20},{20... | collective-permute-start | bytes 1572872 | tf_op jit(solution)/shard_map/ppermute | solution.py:454
  49.8 13.3 %collective-permute-start.7 = (bf16[144,1024]{1,0:T(8,128)(2,1)}, bf16[144,1024]{1,0:T(8,128)(2,1)S(1)}, u32[]{:S(2)}, u32[]{:S(2)}) collective-permute-start(bf16[144,1024]{1,0:T(8,128)(2,1)} %get-tuple-element.78), channel_id=1, source_target_pairs={{0,2},{2,0},{1,3},{3,1},{4,6},{6,4},{5,7},{7,5},{8,10},{10,8},{9,1... | collective-permute-start | bytes 884744 | tf_op jit(solution)/shard_map/ppermute | solution.py:454
  50.3 16.0 %collective-permute-start.4 = (bf16[144,1024]{1,0:T(8,128)(2,1)S(1)}, bf16[144,1024]{1,0:T(8,128)(2,1)S(1)}, u32[]{:S(2)}, u32[]{:S(2)}) collective-permute-start(bf16[144,1024]{1,0:T(8,128)(2,1)S(1)} %copy-done.36), channel_id=1, source_target_pairs={{0,1},{1,0},{2,3},{3,2},{4,5},{5,4},{6,7},{7,6},{8,9},{9,8},{10,11... | collective-permute-start | bytes 884744 | tf_op jit(solution)/shard_map/ppermute | solution.py:454
  57.2 5.9 %copy-start.21 = (bf16[4,128,512]{2,1,0:T(8,128)(2,1)}, bf16[4,128,512]{2,1,0:T(8,128)(2,1)S(1)}, u32[]{:S(2)}) copy-start(bf16[4,128,512]{2,1,0:T(8,128)(2,1)S(1)} %collective-permute-done.10.refs_4_) | copy-start | bytes 1572868
  58.2 4.9 %copy-start.22 = (bf16[4,128,512]{2,1,0:T(8,128)(2,1)}, bf16[4,128,512]{2,1,0:T(8,128)(2,1)S(1)}, u32[]{:S(2)}) copy-start(bf16[4,128,512]{2,1,0:T(8,128)(2,1)S(1)} %collective-permute-done.9.refs_3_) | copy-start | bytes 1572868
  59.5 3.6 %copy-start.23 = (bf16[4,128,512]{2,1,0:T(8,128)(2,1)}, bf16[4,128,512]{2,1,0:T(8,128)(2,1)S(1)}, u32[]{:S(2)}) copy-start(bf16[4,128,512]{2,1,0:T(8,128)(2,1)S(1)} %collective-permute-done.8.refs_2_) | copy-start | bytes 1572868
  63.8 15.6 %collective-permute-start.13 = (bf16[288,1024]{1,0:T(8,128)(2,1)}, bf16[288,1024]{1,0:T(8,128)(2,1)S(1)}, u32[]{:S(2)}, u32[]{:S(2)}) collective-permute-start(bf16[288,1024]{1,0:T(8,128)(2,1)} %get-tuple-element.93), channel_id=1, source_target_pairs={{0,2},{2,0},{1,3},{3,1},{4,6},{6,4},{5,7},{7,5},{8,10},{10,8},{9,1... | collective-permute-start | bytes 1769480 | tf_op jit(solution)/shard_map/ppermute | solution.py:454
  79.1 18.0 %collective-permute-start.12 = (bf16[288,1280]{1,0:T(8,128)(2,1)}, bf16[288,1280]{1,0:T(8,128)(2,1)S(1)}, u32[]{:S(2)}, u32[]{:S(2)}) collective-permute-start(bf16[288,1280]{1,0:T(8,128)(2,1)} %get-tuple-element.90.refs_2_), channel_id=1, source_target_pairs={{0,2},{2,0},{1,3},{3,1},{4,6},{6,4},{5,7},{7,5},{8,10},{10,8},{9,1... | collective-permute-start | bytes 2211848 | tf_op jit(solution)/shard_map/ppermute | solution.py:454
  80.2 22.7 %collective-permute-start.14 = (bf16[288,1024]{1,0:T(8,128)(2,1)}, bf16[288,1024]{1,0:T(8,128)(2,1)S(1)}, u32[]{:S(2)}, u32[]{:S(2)}) collective-permute-start(bf16[288,1024]{1,0:T(8,128)(2,1)} %get-tuple-element.94.here), channel_id=1, source_target_pairs={{0,1},{1,0},{2,3},{3,2},{4,5},{5,4},{6,7},{7,6},{8,9},{9,8},{10,11... | collective-permute-start | bytes 1769480 | tf_op jit(solution)/shard_map/ppermute | solution.py:454
  98.0 11.1 %copy-start.2 = (bf16[288,1024]{1,0:T(8,128)(2,1)S(1)}, bf16[288,1024]{1,0:T(8,128)(2,1)}, u32[]{:S(2)}) copy-start(bf16[288,1024]{1,0:T(8,128)(2,1)} %get-tuple-element.101.refs_5_.refs_3_.refs_1_) | copy-start | bytes 1769476
  101.4 9.8 %copy-start.27 = (f32[128,768]{1,0:T(8,128)S(1)}, f32[128,768]{1,0:T(8,128)}, u32[]{:S(2)}) copy-start(f32[128,768]{1,0:T(8,128)} %get-tuple-element.106) | copy-start | bytes 1179652
  101.4 9.7 %collective-permute-start.18 = (bf16[256,768]{1,0:T(8,128)(2,1)}, bf16[256,768]{1,0:T(8,128)(2,1)S(1)}, u32[]{:S(2)}, u32[]{:S(2)}) collective-permute-start(bf16[256,768]{1,0:T(8,128)(2,1)} %get-tuple-element.103), channel_id=1, source_target_pairs={{0,4},{4,0},{8,12},{12,8},{1,5},{5,1},{9,13},{13,9},{2,6},{6,2},{1... | collective-permute-start | bytes 1179656 | tf_op jit(solution)/shard_map/ppermute | solution.py:519
  107.1 31.5 %collective-permute-start.16 = (bf16[288,1280]{1,0:T(8,128)(2,1)}, bf16[288,1280]{1,0:T(8,128)(2,1)S(1)}, u32[]{:S(2)}, u32[]{:S(2)}) collective-permute-start(bf16[288,1280]{1,0:T(8,128)(2,1)} %get-tuple-element.99.refs_2_), channel_id=1, source_target_pairs={{0,2},{2,0},{1,3},{3,1},{4,6},{6,4},{5,7},{7,5},{8,10},{10,8},{9,1... | collective-permute-start | bytes 2211848 | tf_op jit(solution)/shard_map/ppermute | solution.py:454
  107.6 22.6 %collective-permute-start.15 = (bf16[144,1024]{1,0:T(8,128)(2,1)}, bf16[144,1024]{1,0:T(8,128)(2,1)S(1)}, u32[]{:S(2)}, u32[]{:S(2)}) collective-permute-start(bf16[144,1024]{1,0:T(8,128)(2,1)} %get-tuple-element.97), channel_id=1, source_target_pairs={{0,2},{2,0},{1,3},{3,1},{4,6},{6,4},{5,7},{7,5},{8,10},{10,8},{9,1... | collective-permute-start | bytes 884744 | tf_op jit(solution)/shard_map/ppermute | solution.py:454
  109.1 29.4 %collective-permute-start.17 = (bf16[288,512]{1,0:T(8,128)(2,1)S(1)}, bf16[288,512]{1,0:T(8,128)(2,1)S(1)}, u32[]{:S(2)}, u32[]{:S(2)}) collective-permute-start(bf16[288,512]{1,0:T(8,128)(2,1)S(1)} %slice.33), channel_id=1, source_target_pairs={{0,1},{1,0},{2,3},{3,2},{4,5},{5,4},{6,7},{7,6},{8,9},{9,8},{10,11... | collective-permute-start | bytes 884744 | tf_op jit(solution)/shard_map/ppermute | solution.py:454
  111.1 26.9 %copy-start.6 = (bf16[256,768]{1,0:T(8,128)(2,1)}, bf16[256,768]{1,0:T(8,128)(2,1)S(1)}, u32[]{:S(2)}) copy-start(bf16[256,768]{1,0:T(8,128)(2,1)S(1)} %collective-permute-done.18.refs_8_) | copy-start | bytes 1179652
  111.2 33.1 %collective-permute-start.19 = (bf16[128,768]{1,0:T(8,128)(2,1)S(1)}, bf16[128,768]{1,0:T(8,128)(2,1)S(1)}, u32[]{:S(2)}, u32[]{:S(2)}) collective-permute-start(bf16[128,768]{1,0:T(8,128)(2,1)S(1)} %add_convert_fusion.4), channel_id=1, source_target_pairs={{0,8},{4,12},{8,0},{12,4},{1,9},{5,13},{9,1},{13,5},{2,10},{6,14},... | collective-permute-start | bytes 589832 | tf_op jit(solution)/shard_map/ppermute | solution.py:521
  138.0 16.5 %collective-permute-start.20 = (bf16[288,1024]{1,0:T(8,128)(2,1)}, bf16[288,1024]{1,0:T(8,128)(2,1)S(1)}, u32[]{:S(2)}, u32[]{:S(2)}) collective-permute-start(bf16[288,1024]{1,0:T(8,128)(2,1)} %get-tuple-element.109), channel_id=1, source_target_pairs={{0,2},{2,0},{1,3},{3,1},{4,6},{6,4},{5,7},{7,5},{8,10},{10,8},{9,1... | collective-permute-start | bytes 1769480 | tf_op jit(solution)/shard_map/ppermute | solution.py:454
  139.5 5.7 %copy-start.17 = (bf16[288,1024]{1,0:T(8,128)(2,1)S(1)}, bf16[288,1024]{1,0:T(8,128)(2,1)}, u32[]{:S(2)}) copy-start(bf16[288,1024]{1,0:T(8,128)(2,1)} %get-tuple-element.117.refs_3_) | copy-start | bytes 1769476
  139.5 7.4 %copy-start.16 = (bf16[288,1024]{1,0:T(8,128)(2,1)S(1)}, bf16[288,1024]{1,0:T(8,128)(2,1)}, u32[]{:S(2)}) copy-start(bf16[288,1024]{1,0:T(8,128)(2,1)} %get-tuple-element.86) | copy-start | bytes 1769476
  144.9 23.6 %collective-permute-start.21 = (bf16[256,1280]{1,0:T(8,128)(2,1)}, bf16[256,1280]{1,0:T(8,128)(2,1)S(1)}, u32[]{:S(2)}, u32[]{:S(2)}) collective-permute-start(bf16[256,1280]{1,0:T(8,128)(2,1)} %get-tuple-element.115), channel_id=1, source_target_pairs={{0,4},{4,0},{8,12},{12,8},{1,5},{5,1},{9,13},{13,9},{2,6},{6,2},{1... | collective-permute-start | bytes 1966088 | tf_op jit(solution)/shard_map/ppermute | solution.py:519
  145.2 18.2 %collective-permute-start.23 = (bf16[288,1024]{1,0:T(8,128)(2,1)S(1)}, bf16[288,1024]{1,0:T(8,128)(2,1)S(1)}, u32[]{:S(2)}, u32[]{:S(2)}) collective-permute-start(bf16[288,1024]{1,0:T(8,128)(2,1)S(1)} %copy-done.17), channel_id=1, source_target_pairs={{0,2},{2,0},{1,3},{3,1},{4,6},{6,4},{5,7},{7,5},{8,10},{10,8},{9,1... | collective-permute-start | bytes 1769480 | tf_op jit(solution)/shard_map/ppermute | solution.py:454
  146.9 45.1 %collective-permute-start.11 = (bf16[288,1024]{1,0:T(8,128)(2,1)S(1)}, bf16[288,1024]{1,0:T(8,128)(2,1)S(1)}, u32[]{:S(2)}, u32[]{:S(2)}) collective-permute-start(bf16[288,1024]{1,0:T(8,128)(2,1)S(1)} %copy-done.16), channel_id=1, source_target_pairs={{0,1},{1,0},{2,3},{3,2},{4,5},{5,4},{6,7},{7,6},{8,9},{9,8},{10,11... | collective-permute-start | bytes 1769480 | tf_op jit(solution)/shard_map/ppermute | solution.py:454
  159.2 9.3 %copy-start.15 = (f32[128,1280]{1,0:T(8,128)S(1)}, f32[128,1280]{1,0:T(8,128)}, u32[]{:S(2)}) copy-start(f32[128,1280]{1,0:T(8,128)} %get-tuple-element.116) | copy-start | bytes 1966084
  159.2 23.4 %collective-permute-start.24 = (bf16[256,1024]{1,0:T(8,128)(2,1)}, bf16[256,1024]{1,0:T(8,128)(2,1)S(1)}, u32[]{:S(2)}, u32[]{:S(2)}) collective-permute-start(bf16[256,1024]{1,0:T(8,128)(2,1)} %get-tuple-element.120), channel_id=1, source_target_pairs={{0,4},{4,0},{8,12},{12,8},{1,5},{5,1},{9,13},{13,9},{2,6},{6,2},{1... | collective-permute-start | bytes 1572872 | tf_op jit(solution)/shard_map/ppermute | solution.py:519
  164.2 18.4 %copy-start.24 = (f32[128,1024]{1,0:T(8,128)S(1)}, f32[128,1024]{1,0:T(8,128)}, u32[]{:S(2)}) copy-start(f32[128,1024]{1,0:T(8,128)} %get-tuple-element.121) | copy-start | bytes 1572868
  168.0 23.2 %copy-start.25 = (f32[128,1024]{1,0:T(8,128)S(1)}, f32[128,1024]{1,0:T(8,128)}, u32[]{:S(2)}) copy-start(f32[128,1024]{1,0:T(8,128)} %get-tuple-element.124) | copy-start | bytes 1572868
  168.0 23.9 %copy-start.7 = (bf16[288,1024]{1,0:T(8,128)(2,1)S(1)}, bf16[288,1024]{1,0:T(8,128)(2,1)}, u32[]{:S(2)}) copy-start(bf16[288,1024]{1,0:T(8,128)(2,1)} %get-tuple-element.85.joined) | copy-start | bytes 1769476
  168.0 23.2 %collective-permute-start.26 = (bf16[256,1024]{1,0:T(8,128)(2,1)}, bf16[256,1024]{1,0:T(8,128)(2,1)S(1)}, u32[]{:S(2)}, u32[]{:S(2)}) collective-permute-start(bf16[256,1024]{1,0:T(8,128)(2,1)} %get-tuple-element.123), channel_id=1, source_target_pairs={{0,4},{4,0},{8,12},{12,8},{1,5},{5,1},{9,13},{13,9},{2,6},{6,2},{1... | collective-permute-start | bytes 1572872 | tf_op jit(solution)/shard_map/ppermute | solution.py:519
  168.5 23.8 %copy-start.10 = (bf16[256,1280]{1,0:T(8,128)(2,1)}, bf16[256,1280]{1,0:T(8,128)(2,1)S(1)}, u32[]{:S(2)}) copy-start(bf16[256,1280]{1,0:T(8,128)(2,1)S(1)} %collective-permute-done.21.refs_4_) | copy-start | bytes 1966084
  168.6 24.8 %collective-permute-start.22 = (bf16[128,1280]{1,0:T(8,128)(2,1)S(1)}, bf16[128,1280]{1,0:T(8,128)(2,1)S(1)}, u32[]{:S(2)}, u32[]{:S(2)}) collective-permute-start(bf16[128,1280]{1,0:T(8,128)(2,1)S(1)} %add_convert_fusion.1), channel_id=1, source_target_pairs={{0,8},{4,12},{8,0},{12,4},{1,9},{5,13},{9,1},{13,5},{2,10},{6,14},... | collective-permute-start | bytes 983048 | tf_op jit(solution)/shard_map/ppermute | solution.py:521
  182.6 9.7 %copy-start.11 = (bf16[256,1024]{1,0:T(8,128)(2,1)}, bf16[256,1024]{1,0:T(8,128)(2,1)S(1)}, u32[]{:S(2)}) copy-start(bf16[256,1024]{1,0:T(8,128)(2,1)S(1)} %collective-permute-done.24.refs_1_) | copy-start | bytes 1572868
  182.7 24.4 %collective-permute-start.25 = (bf16[128,1024]{1,0:T(8,128)(2,1)S(1)}, bf16[128,1024]{1,0:T(8,128)(2,1)S(1)}, u32[]{:S(2)}, u32[]{:S(2)}) collective-permute-start(bf16[128,1024]{1,0:T(8,128)(2,1)S(1)} %add_convert_fusion.3), channel_id=1, source_target_pairs={{0,8},{4,12},{8,0},{12,4},{1,9},{5,13},{9,1},{13,5},{2,10},{6,14},... | collective-permute-start | bytes 786440 | tf_op jit(solution)/shard_map/ppermute | solution.py:521
  191.3 18.7 %collective-permute-start.27 = (bf16[128,1024]{1,0:T(8,128)(2,1)S(1)}, bf16[128,1024]{1,0:T(8,128)(2,1)S(1)}, u32[]{:S(2)}, u32[]{:S(2)}) collective-permute-start(bf16[128,1024]{1,0:T(8,128)(2,1)S(1)} %add_convert_fusion.2), channel_id=1, source_target_pairs={{0,8},{4,12},{8,0},{12,4},{1,9},{5,13},{9,1},{13,5},{2,10},{6,14},... | collective-permute-start | bytes 786440 | tf_op jit(solution)/shard_map/ppermute | solution.py:521
  (18 other events, 18.2 us)

commit v10 on v7

--- a/solution.py
+++ b/solution.py
@@ -81,13 +81,23 @@
     return found
 
 
+def joint(parts):
+    small = [entry for entry in parts if entry[0].shape[0] < 256]
+    pairs = [small[at : at + 2] for at in range(0, len(small), 2)]
+    return [[entry] for entry in parts if entry[0].shape[0] >= 256] + pairs
+
+
 def rows_times(rows_ref, parts, out_ref, column):
     width = parts[0][0].shape[1]
     step = min(width, 256)
     for at in range(0, width, step):
         total = None
-        for part, columns in parts:
-            term = dot(rows_ref[:, columns], part[:, at : at + step], NN)
+        for group in joint(parts):
+            left = [rows_ref[:, columns] for _, columns in group]
+            right = [part[:, at : at + step] for part, _ in group]
+            if len(group) > 1:
+                left, right = [jnp.concatenate(left, axis=1)], [jnp.concatenate(right, axis=0)]
+            term = dot(left[0], right[0], NN)
             total = term if total is None else total + term
         out_ref[:, column + at : column + at + step] = total.astype(out_ref.dtype)
 

time: 197 us -> 197 us (level)
  transfers between devices with their start and end apart: 28 -> 28, of which waited for: 15 -> 17; matrix products, arithmetic and copies ran while one was open for 3% -> 3% of each run, Pallas kernels for 28% -> 27%
where the time goes in v10:
time: 197 us; the launch traced here: 196 us
  waiting for transfers between devices  89.1 us (45%)
  Pallas kernels  56 us (28%)
  starting transfers between devices  29.8 us (15%)
  local copies, waits for them, and re-layouts  19 us (10%)
    pallas_call x12, Pallas kernels, call(): pl.pallas_call(body, out_shape=outs, in_specs=specs, out_specs=out_specs,...  55.9 us
    ppermute x18, waiting for transfers between devices, swap(): return lax.ppermute(array, axis, [(0, 1), (1, 0)])  53.3 us
    ppermute x4, waiting for transfers between devices, summed_over_loc(): beside = lax.ppermute(sent, 'loc', PAIRS)  23.1 us
    ppermute x18, starting transfers between devices, swap(): return lax.ppermute(array, axis, [(0, 1), (1, 0)])  16.6 us
    unnamed x78, local copies, waits for them, and re-layouts  15 us
    ppermute x4, waiting for transfers between devices, summed_over_loc(): return (near, beside, lax.ppermute(far, 'loc', APART))  10.5 us
    ppermute x4, starting transfers between devices, summed_over_loc(): return (near, beside, lax.ppermute(far, 'loc', APART))  5.44 us
    ppermute x4, starting transfers between devices, summed_over_loc(): beside = lax.ppermute(sent, 'loc', PAIRS)  4.04 us
  transfers between devices with their start and end apart: 28, of which 17 were waited for; matrix products, arithmetic and copies ran while one was open for 3% of the time, Pallas kernels for 27%

profile of v10, /device:TPU:0, one launch (start us, length us, event | category | flops | bytes accessed | tf_op | source)
XLA Modules:
  0.0 196.1 jit_solution(190504106196358901)
XLA Ops:
  0.7 2.0 %copy.57 = bf16[512,4,512]{2,0,1:T(8,128)(2,1)S(1)} copy(bf16[512,4,512]{2,1,0:T(4,128)(2,1)} %param.20) | data formatting | bytes 4194304 | tf_op args[8]
  2.7 1.2 dynamic-slice_bitcast_fusion
  3.9 2.9 %collective-permute-start = (bf16[4,128,512]{2,1,0:T(8,128)(2,1)}, bf16[4,128,512]{2,1,0:T(8,128)(2,1)S(1)}, u32[]{:S(2)}, u32[]{:S(2)}) collective-permute-start(bf16[4,128,512]{2,1,0:T(8,128)(2,1)} %get-tuple-element.129), channel_id=1, source_target_pairs={{0,2},{2,0},{1,3},{3,1},{4,6},{6,4},{5,7},{7,5},{8,10},{10,8},{9,1... | collective-permute-start | bytes 1572872 | tf_op jit(solution)/shard_map/ppermute | solution.py:464
  7.5 3.1 %shard_map.139 = (bf16[144,1024]{1,0:T(8,128)(2,1)}, bf16[144,1024]{1,0:T(8,128)(2,1)}, bf16[288,1024]{1,0:T(8,128)(2,1)}, f32[12,1024]{1,0:T(8,128)}) custom-call(s32[1,12]{1,0:T(1,128)} %cloud.1, s32[1,12]{1,0:T(1,128)} %drop.1, s32[1,48]{1,0:T(1,128)} %keep.1, s32[4]{0:T(128)} %pad_add_fusion.where, bf16[6,48,1024]{2,1,0:T(8,128)(2,1)} %bitcast.47, ...), custom_call_target="tpu_custom_call" | custom-call | bytes 3424560 | tf_op jit(solution)/shard_map/pallas_call | solution.py:440
  10.7 2.0 %copy.58 = bf16[512,4,512]{2,0,1:T(8,128)(2,1)S(1)} copy(bf16[512,4,512]{2,1,0:T(4,128)(2,1)} %param.22) | data formatting | bytes 4194304 | tf_op args[10]
  12.7 7.1 %collective-permute-done.refs_3_ = bf16[4,128,512]{2,1,0:T(8,128)(2,1)S(1)} collective-permute-done((bf16[4,128,512]{2,1,0:T(8,128)(2,1)}, bf16[4,128,512]{2,1,0:T(8,128)(2,1)S(1)}, u32[]{:S(2)}, u32[]{:S(2)}) %collective-permute-start) | collective-permute-done | bytes 524320 | tf_op jit(solution)/shard_map/ppermute | solution.py:464
  19.8 2.1 %collective-permute-start.2 = (bf16[4,128,512]{2,1,0:T(8,128)(2,1)S(1)}, bf16[4,128,512]{2,1,0:T(8,128)(2,1)}, u32[]{:S(2)}, u32[]{:S(2)}) collective-permute-start(bf16[4,128,512]{2,1,0:T(8,128)(2,1)S(1)} %collective-permute-done.refs_3_), channel_id=1, source_target_pairs={{0,4},{4,0},{8,12},{12,8},{1,5},{5,1},{9,13},{13,9},{2,6},{6,2},{1... | collective-permute-start | bytes 1572872 | tf_op jit(solution)/shard_map/ppermute | solution.py:491
  21.9 1.5 collective-permute-start.1
  23.5 1.1 dynamic-slice_bitcast_fusion.2
  24.6 1.5 collective-permute-start.5
  26.1 5.0 %collective-permute-done.3.refs_6_ = bf16[4,128,512]{2,1,0:T(8,128)(2,1)S(1)} collective-permute-done((bf16[4,128,512]{2,1,0:T(8,128)(2,1)}, bf16[4,128,512]{2,1,0:T(8,128)(2,1)S(1)}, u32[]{:S(2)}, u32[]{:S(2)}) %collective-permute-start.3) | collective-permute-done | bytes 524320 | tf_op jit(solution)/shard_map/ppermute | solution.py:464
  31.0 1.2 collective-permute-done.2.refs_5_
  32.2 1.2 collective-permute-done.1.refs_4_
  33.4 7.5 %shard_map.142 = (bf16[144,1024]{1,0:T(8,128)(2,1)}, bf16[144,1024]{1,0:T(8,128)(2,1)}, bf16[288,512]{1,0:T(8,128)(2,1)}, bf16[288,512]{1,0:T(8,128)(2,1)}, bf16...) custom-call(s32[4]{0:T(128)} %pad_add_fusion.where, ...), custom_call_target="tpu_custom_call" | custom-call | flops 1207959552 | bytes 9211920 | tf_op jit(solution)/shard_map/pallas_call | solution.py:440
  42.2 1.7 collective-permute-start.10
  44.0 1.6 collective-permute-start.9
  45.6 1.5 collective-permute-start.8
  47.8 2.0 %shard_map.144 = (bf16[144,1024]{1,0:T(8,128)(2,1)}, bf16[288,1024]{1,0:T(8,128)(2,1)}) custom-call(bf16[144,1024]{1,0:T(8,128)(2,1)} %get-tuple-element.70.refs_1_.start, bf16[144,1024]{1,0:T(8,128)(2,1)} %get-tuple-element.75.here, bf16[144,1024]{1,0:T(8,128)(2,1)} %copy-done.32, ...), custom_call_target="tpu_custom_call", output_to_operand_aliasing={{1}: (3, {})} | custom-call | bytes 1769472 | tf_op jit(solution)/shard_map/pallas_call | solution.py:440
  50.4 6.8 %collective-permute-done.10.refs_4_ = bf16[4,128,512]{2,1,0:T(8,128)(2,1)S(1)} collective-permute-done((bf16[4,128,512]{2,1,0:T(8,128)(2,1)}, bf16[4,128,512]{2,1,0:T(8,128)(2,1)S(1)}, u32[]{:S(2)}, u32[]{:S(2)}) %collective-permute-start.10) | collective-permute-done | bytes 524320 | tf_op jit(solution)/shard_map/ppermute | solution.py:464
  57.2 1.1 collective-permute-done.9.refs_3_
  58.2 1.3 collective-permute-done.8.refs_2_
  59.5 3.6 %collective-permute-done.7.refs_1_ = bf16[144,1024]{1,0:T(8,128)(2,1)S(1)} collective-permute-done((bf16[144,1024]{1,0:T(8,128)(2,1)}, bf16[144,1024]{1,0:T(8,128)(2,1)S(1)}, u32[]{:S(2)}, u32[]{:S(2)}) %collective-permute-start.7) | collective-permute-done | bytes 294944 | tf_op jit(solution)/shard_map/ppermute | solution.py:464
  63.8 1.7 collective-permute-start.13
  67.2 11.3 %shard_map.146 = (bf16[288,512]{1,0:T(8,128)(2,1)}, bf16[288,1280]{1,0:T(8,128)(2,1)}, bf16[288,1280]{1,0:T(8,128)(2,1)}, bf16[288,1024]{1,0:T(8,128)(2,1)}, bf1...) custom-call(s32[4]{0:T(128)} %pad_add_fusion.where, f32[1,1024]{1,0:T(1,128)} %bitcast.52, ...), custom_call_target="tpu_custom_call" | custom-call | flops 2415919104 | bytes 9851280 | tf_op jit(solution)/shard_map/pallas_call | solution.py:440
  79.8 2.2 %collective-permute-done.14.there = bf16[288,1024]{1,0:T(8,128)(2,1)S(1)} collective-permute-done((bf16[288,1024]{1,0:T(8,128)(2,1)}, bf16[288,1024]{1,0:T(8,128)(2,1)S(1)}, u32[]{:S(2)}, u32[]{:S(2)}) %collective-permute-start.14) | collective-permute-done | bytes 589856 | tf_op jit(solution)/shard_map/ppermute | solution.py:464
  82.9 3.3 %shard_map.149 = (bf16[144,1024]{1,0:T(8,128)(2,1)}, bf16[144,1024]{1,0:T(8,128)(2,1)}, bf16[288,1280]{1,0:T(8,128)(2,1)}) custom-call(f32[1,1024]{1,0:T(1,128)} %bitcast.53, bf16[288,1024]{1,0:T(8,128)(2,1)} %get-tuple-element.94.here, bf16[288,1024]{1,0:T(8,128)(2,1)} %copy-done.19, ...), custom_call_target="tpu_custom_call", output_to_operand_aliasing={{2}: (5, {})} | custom-call | bytes 3690496 | tf_op jit(solution)/shard_map/pallas_call | solution.py:440
  86.1 1.7 collective-permute-start.15
  87.8 10.2 %collective-permute-done.12.refs_1_ = bf16[288,1280]{1,0:T(8,128)(2,1)S(1)} collective-permute-done((bf16[288,1280]{1,0:T(8,128)(2,1)}, bf16[288,1280]{1,0:T(8,128)(2,1)S(1)}, u32[]{:S(2)}, u32[]{:S(2)}) %collective-permute-start.12) | collective-permute-done | bytes 737312 | tf_op jit(solution)/shard_map/ppermute | solution.py:464
  98.1 0.9 copy-done.4
  99.0 3.3 %shard_map.147 = (bf16[256,768]{1,0:T(8,128)(2,1)}, f32[128,768]{1,0:T(8,128)}, f32[128,768]{1,0:T(8,128)}) custom-call(s32[4]{0:T(128)} %pad_add_fusion.where, bf16[288,512]{1,0:T(8,128)(2,1)} %get-tuple-element.89.refs_0_, bf16[288,1280]{1,0:T(8,128)(2,1)} %copy-done.4, bf16[288,1280]{1,0:T(8,128)(2,1)} %get-tuple-element.90.refs_2_), custom_call_target="tpu_custom_call" | custom-call | flops 452984832 | bytes 2949136 | tf_op jit(solution)/shard_map/pallas_call | solution.py:440
  102.2 1.6 collective-permute-start.18
  105.1 7.1 %shard_map.150 = (bf16[288,512]{1,0:T(8,128)(2,1)}, bf16[288,1280]{1,0:T(8,128)(2,1)}, bf16[288,768]{1,0:T(8,128)(2,1)}, bf16[288,768]{1,0:T(8,128)(2,1)}, f32[128,768]{1,0:T(8,128)}) custom-call(s32[4]{0:T(128)} %pad_add_fusion.where, bf16[288,1536]{1,0:T(8,128)(2,1)} %get-tuple-element.87.triple, ...), custom_call_target="tpu_custom_call", output_to_operand_aliasing={{4}: (3, {})} | custom-call | flops 1207959552 | bytes 8863760 | tf_op jit(solution)/shard_map/pallas_call | solution.py:440
  112.1 1.5 collective-permute-start.20
  114.3 2.6 %collective-permute-start.19 = (bf16[128,768]{1,0:T(8,128)(2,1)S(1)}, bf16[128,768]{1,0:T(8,128)(2,1)S(1)}, u32[]{:S(2)}, u32[]{:S(2)}) collective-permute-start(bf16[128,768]{1,0:T(8,128)(2,1)S(1)} %add_convert_fusion.4), channel_id=1, source_target_pairs={{0,8},{4,12},{8,0},{12,4},{1,9},{5,13},{9,1},{13,5},{2,10},{6,14},... | collective-permute-start | bytes 589832 | tf_op jit(solution)/shard_map/ppermute | solution.py:531
  116.9 6.5 %collective-permute-done.16.refs_3_ = bf16[288,1280]{1,0:T(8,128)(2,1)S(1)} collective-permute-done((bf16[288,1280]{1,0:T(8,128)(2,1)}, bf16[288,1280]{1,0:T(8,128)(2,1)S(1)}, u32[]{:S(2)}, u32[]{:S(2)}) %collective-permute-start.16) | collective-permute-done | bytes 737312 | tf_op jit(solution)/shard_map/ppermute | solution.py:464
  124.3 4.7 %shard_map.151 = (bf16[256,1280]{1,0:T(8,128)(2,1)}, f32[128,1280]{1,0:T(8,128)}, f32[128,1280]{1,0:T(8,128)}, bf16[288,512]{1,0:T(8,128)(2,1)}, bf16[256,768]{1,0:T(8,128)(2,1)}) custom-call(s32[4]{0:T(128)} %pad_add_fusion.where, bf16[288,512]{1,0:T(8,128)(2,1)} %get-tuple-element.89.refs_0_, ...), custom_call_target="tpu_custom_call", output_to_operand_aliasing={{3}: (8, {}), {4}: (9, {})} | custom-call | flops 754974720 | bytes 6340624 | tf_op jit(solution)/shard_map/pallas_call | solution.py:440
  130.5 8.7 %collective-permute-done.20.refs_1_ = bf16[288,1280]{1,0:T(8,128)(2,1)S(1)} collective-permute-done((bf16[288,1280]{1,0:T(8,128)(2,1)}, bf16[288,1280]{1,0:T(8,128)(2,1)S(1)}, u32[]{:S(2)}, u32[]{:S(2)}) %collective-permute-start.20) | collective-permute-done | bytes 737312 | tf_op jit(solution)/shard_map/ppermute | solution.py:464
  139.2 0.9 copy-done.15
  140.1 4.3 %shard_map.153 = (bf16[256,1280]{1,0:T(8,128)(2,1)}, f32[128,1280]{1,0:T(8,128)}, f32[128,1280]{1,0:T(8,128)}, f32[128,1280]{1,0:T(8,128)}) custom-call(s32[4]{0:T(128)} %pad_add_fusion.where, bf16[288,512]{1,0:T(8,128)(2,1)} %get-tuple-element.108.refs_0_, bf16[288,1280]{1,0:T(8,128)(2,1)} %copy-done.15, ...), custom_call_target="tpu_custom_call", output_to_operand_aliasing={{3}: (8, {})} | custom-call | flops 754974720 | bytes 5570576 | tf_op jit(solution)/shard_map/pallas_call | solution.py:440
  146.0 3.4 %shard_map.155 = (bf16[256,768]{1,0:T(8,128)(2,1)}, f32[128,768]{1,0:T(8,128)}, f32[128,768]{1,0:T(8,128)}, f32[128,1280]{1,0:T(8,128)}) custom-call(s32[4]{0:T(128)} %pad_add_fusion.where, bf16[288,512]{1,0:T(8,128)(2,1)} %get-tuple-element.111.refs_4_.refs_0_, ...), custom_call_target="tpu_custom_call", output_to_operand_aliasing={{3}: (6, {})} | custom-call | flops 452984832 | bytes 3899408 | tf_op jit(solution)/shard_map/pallas_call | solution.py:440
  149.4 1.5 collective-permute-start.26
  151.0 2.7 %collective-permute-start.22 = (bf16[128,1280]{1,0:T(8,128)(2,1)S(1)}, bf16[128,1280]{1,0:T(8,128)(2,1)S(1)}, u32[]{:S(2)}, u32[]{:S(2)}) collective-permute-start(bf16[128,1280]{1,0:T(8,128)(2,1)S(1)} %add_convert_fusion.2), channel_id=1, source_target_pairs={{0,8},{4,12},{8,0},{12,4},{1,9},{5,13},{9,1},{13,5},{2,10},{6,14},... | collective-permute-start | bytes 983048 | tf_op jit(solution)/shard_map/ppermute | solution.py:531
  153.6 19.0 %collective-permute-done.24.refs_1_ = bf16[256,1280]{1,0:T(8,128)(2,1)S(1)} collective-permute-done((bf16[256,1280]{1,0:T(8,128)(2,1)}, bf16[256,1280]{1,0:T(8,128)(2,1)S(1)}, u32[]{:S(2)}, u32[]{:S(2)}) %collective-permute-start.24) | collective-permute-done | bytes 655392 | tf_op jit(solution)/shard_map/ppermute | solution.py:529
  172.7 4.1 %collective-permute-done.26.refs_4_ = bf16[256,768]{1,0:T(8,128)(2,1)S(1)} collective-permute-done((bf16[256,768]{1,0:T(8,128)(2,1)}, bf16[256,768]{1,0:T(8,128)(2,1)S(1)}, u32[]{:S(2)}, u32[]{:S(2)}) %collective-permute-start.26) | collective-permute-done | bytes 393248 | tf_op jit(solution)/shard_map/ppermute | solution.py:529
  177.1 0.9 copy.52
  178.7 3.0 %shard_map.154.kept = f32[128,4,512]{2,1,0:T(4,128)} custom-call(f32[128,768]{1,0:T(8,128)} %get-tuple-element.98.refs_0_, bf16[256,768]{1,0:T(8,128)(2,1)} %get-tuple-element.104.refs_1_, bf16[128,768]{1,0:T(8,128)(2,1)} %get-tuple-element.107.refs_2_, f32[128,1280]{1,0:T(8,128)} %get-tuple-element.114.refs_3_, bf16[256,1280]{1,0:T(8,128)(2,1)} %copy-done.10, ...), custom_call_target="tpu_custom_call" | custom-call | bytes 3670016 | tf_op jit(solution)/shard_map/pallas_call | solution.py:440
  181.8 10.5 %collective-permute-done.27.refs_5_ = bf16[128,768]{1,0:T(8,128)(2,1)S(1)} collective-permute-done((bf16[128,768]{1,0:T(8,128)(2,1)S(1)}, bf16[128,768]{1,0:T(8,128)(2,1)S(1)}, u32[]{:S(2)}, u32[]{:S(2)}) %collective-permute-start.27) | collective-permute-done | bytes 196640 | tf_op jit(solution)/shard_map/ppermute | solution.py:531
  193.1 3.0 %shard_map.156 = (f32[128,4,512]{2,1,0:T(4,128)}, f32[128,4,512]{2,1,0:T(4,128)}) custom-call(f32[128,4,512]{2,1,0:T(4,128)} %shard_map.154.kept, f32[128,1280]{1,0:T(8,128)} %get-tuple-element.119.refs_0_, bf16[256,1280]{1,0:T(8,128)(2,1)} %copy-done.11, bf16[128,1280]{1,0:T(8,128)(2,1)} %copy-done.28, ...), custom_call_target="tpu_custom_call", output_to_operand_aliasing={{1}: (0, {})} | custom-call | bytes 4718592 | tf_op jit(solution)/shard_map/pallas_call | solution.py:440
  (120 shorter events, 15.6 us)
Async XLA Ops:
  2.7 7.9 %copy-start = (bf16[512,4,512]{2,0,1:T(8,128)(2,1)}, bf16[512,4,512]{2,0,1:T(8,128)(2,1)S(1)}, u32[]{:S(2)}) copy-start(bf16[512,4,512]{2,0,1:T(8,128)(2,1)S(1)} %copy.57) | copy-start | bytes 6291460
  3.9 15.9 %collective-permute-start = (bf16[4,128,512]{2,1,0:T(8,128)(2,1)}, bf16[4,128,512]{2,1,0:T(8,128)(2,1)S(1)}, u32[]{:S(2)}, u32[]{:S(2)}) collective-permute-start(bf16[4,128,512]{2,1,0:T(8,128)(2,1)} %get-tuple-element.129), channel_id=1, source_target_pairs={{0,2},{2,0},{1,3},{3,1},{4,6},{6,4},{5,7},{7,5},{8,10},{10,8},{9,1... | collective-permute-start | bytes 1572872 | tf_op jit(solution)/shard_map/ppermute | solution.py:464
  10.6 20.4 %collective-permute-start.3 = (bf16[4,128,512]{2,1,0:T(8,128)(2,1)}, bf16[4,128,512]{2,1,0:T(8,128)(2,1)S(1)}, u32[]{:S(2)}, u32[]{:S(2)}) collective-permute-start(bf16[4,128,512]{2,1,0:T(8,128)(2,1)} %get-tuple-element.71), channel_id=1, source_target_pairs={{0,2},{2,0},{1,3},{3,1},{4,6},{6,4},{5,7},{7,5},{8,10},{10,8},{9,1... | collective-permute-start | bytes 1572872 | tf_op jit(solution)/shard_map/ppermute | solution.py:464
  12.7 28.3 %copy-start.3 = (bf16[512,4,512]{2,0,1:T(8,128)(2,1)}, bf16[512,4,512]{2,0,1:T(8,128)(2,1)S(1)}, u32[]{:S(2)}) copy-start(bf16[512,4,512]{2,0,1:T(8,128)(2,1)S(1)} %copy.58) | copy-start | bytes 6291460
  19.8 13.6 %copy-start.8 = (bf16[4,128,512]{2,1,0:T(8,128)(2,1)}, bf16[4,128,512]{2,1,0:T(8,128)(2,1)S(1)}, u32[]{:S(2)}) copy-start(bf16[4,128,512]{2,1,0:T(8,128)(2,1)S(1)} %collective-permute-done.refs_3_) | copy-start | bytes 1572868
  19.8 12.4 %collective-permute-start.2 = (bf16[4,128,512]{2,1,0:T(8,128)(2,1)S(1)}, bf16[4,128,512]{2,1,0:T(8,128)(2,1)}, u32[]{:S(2)}, u32[]{:S(2)}) collective-permute-start(bf16[4,128,512]{2,1,0:T(8,128)(2,1)S(1)} %collective-permute-done.refs_3_), channel_id=1, source_target_pairs={{0,4},{4,0},{8,12},{12,8},{1,5},{5,1},{9,13},{13,9},{2,6},{6,2},{1... | collective-permute-start | bytes 1572872 | tf_op jit(solution)/shard_map/ppermute | solution.py:491
  21.9 11.5 %collective-permute-start.1 = (bf16[4,128,512]{2,1,0:T(8,128)(2,1)S(1)}, bf16[4,128,512]{2,1,0:T(8,128)(2,1)}, u32[]{:S(2)}, u32[]{:S(2)}) collective-permute-start(bf16[4,128,512]{2,1,0:T(8,128)(2,1)S(1)} %collective-permute-done.refs_3_), channel_id=1, source_target_pairs={{0,16},{16,0},{1,17},{17,1},{2,18},{18,2},{3,19},{19,3},{4,20},{20... | collective-permute-start | bytes 1572872 | tf_op jit(solution)/shard_map/ppermute | solution.py:464
  24.6 16.9 %collective-permute-start.5 = (bf16[4,128,512]{2,1,0:T(8,128)(2,1)}, bf16[4,128,512]{2,1,0:T(8,128)(2,1)S(1)}, u32[]{:S(2)}, u32[]{:S(2)}) collective-permute-start(bf16[4,128,512]{2,1,0:T(8,128)(2,1)} %get-tuple-element.73), channel_id=1, source_target_pairs={{0,2},{2,0},{1,3},{3,1},{4,6},{6,4},{5,7},{7,5},{8,10},{10,8},{9,1... | collective-permute-start | bytes 1572872 | tf_op jit(solution)/shard_map/ppermute | solution.py:464
  41.0 9.3 %copy-start.34 = (s32[1,12]{1,0:T(1,128)S(1)}, s32[1,12]{1,0:T(1,128)}, u32[]{:S(2)}) copy-start(s32[1,12]{1,0:T(1,128)} %cloud.1) | copy-start | bytes 148
  41.0 9.3 %copy-start.35 = (s32[1,12]{1,0:T(1,128)S(1)}, s32[1,12]{1,0:T(1,128)}, u32[]{:S(2)}) copy-start(s32[1,12]{1,0:T(1,128)} %drop.1) | copy-start | bytes 148
  41.0 9.3 %copy-start.36 = (bf16[144,1024]{1,0:T(8,128)(2,1)S(1)}, bf16[144,1024]{1,0:T(8,128)(2,1)}, u32[]{:S(2)}) copy-start(bf16[144,1024]{1,0:T(8,128)(2,1)} %get-tuple-element.72.refs_1_) | copy-start | bytes 884740
  42.2 4.8 %collective-permute-start.6 = (bf16[144,1024]{1,0:T(8,128)(2,1)}, bf16[144,1024]{1,0:T(8,128)(2,1)S(1)}, u32[]{:S(2)}, u32[]{:S(2)}) collective-permute-start(bf16[144,1024]{1,0:T(8,128)(2,1)} %get-tuple-element.75.here), channel_id=1, source_target_pairs={{0,1},{1,0},{2,3},{3,2},{4,5},{5,4},{6,7},{7,6},{8,9},{9,8},{10,11... | collective-permute-start | bytes 884744 | tf_op jit(solution)/shard_map/ppermute | solution.py:464
  42.2 14.9 %collective-permute-start.10 = (bf16[4,128,512]{2,1,0:T(8,128)(2,1)}, bf16[4,128,512]{2,1,0:T(8,128)(2,1)S(1)}, u32[]{:S(2)}, u32[]{:S(2)}) collective-permute-start(bf16[4,128,512]{2,1,0:T(8,128)(2,1)} %get-tuple-element.80), channel_id=1, source_target_pairs={{0,2},{2,0},{1,3},{3,1},{4,6},{6,4},{5,7},{7,5},{8,10},{10,8},{9,1... | collective-permute-start | bytes 1572872 | tf_op jit(solution)/shard_map/ppermute | solution.py:464
  44.0 14.3 %collective-permute-start.9 = (bf16[4,128,512]{2,1,0:T(8,128)(2,1)}, bf16[4,128,512]{2,1,0:T(8,128)(2,1)S(1)}, u32[]{:S(2)}, u32[]{:S(2)}) collective-permute-start(bf16[4,128,512]{2,1,0:T(8,128)(2,1)} %get-tuple-element.79.refs_5_), channel_id=1, source_target_pairs={{0,4},{4,0},{8,12},{12,8},{1,5},{5,1},{9,13},{13,9},{2,6},{6,2},{1... | collective-permute-start | bytes 1572872 | tf_op jit(solution)/shard_map/ppermute | solution.py:491
  45.6 14.0 %collective-permute-start.8 = (bf16[4,128,512]{2,1,0:T(8,128)(2,1)}, bf16[4,128,512]{2,1,0:T(8,128)(2,1)S(1)}, u32[]{:S(2)}, u32[]{:S(2)}) collective-permute-start(bf16[4,128,512]{2,1,0:T(8,128)(2,1)} %get-tuple-element.79.refs_5_), channel_id=1, source_target_pairs={{0,16},{16,0},{1,17},{17,1},{2,18},{18,2},{3,19},{19,3},{4,20},{20... | collective-permute-start | bytes 1572872 | tf_op jit(solution)/shard_map/ppermute | solution.py:464
  49.8 13.3 %collective-permute-start.7 = (bf16[144,1024]{1,0:T(8,128)(2,1)}, bf16[144,1024]{1,0:T(8,128)(2,1)S(1)}, u32[]{:S(2)}, u32[]{:S(2)}) collective-permute-start(bf16[144,1024]{1,0:T(8,128)(2,1)} %get-tuple-element.78), channel_id=1, source_target_pairs={{0,2},{2,0},{1,3},{3,1},{4,6},{6,4},{5,7},{7,5},{8,10},{10,8},{9,1... | collective-permute-start | bytes 884744 | tf_op jit(solution)/shard_map/ppermute | solution.py:464
  50.3 16.1 %collective-permute-start.4 = (bf16[144,1024]{1,0:T(8,128)(2,1)S(1)}, bf16[144,1024]{1,0:T(8,128)(2,1)S(1)}, u32[]{:S(2)}, u32[]{:S(2)}) collective-permute-start(bf16[144,1024]{1,0:T(8,128)(2,1)S(1)} %copy-done.36), channel_id=1, source_target_pairs={{0,1},{1,0},{2,3},{3,2},{4,5},{5,4},{6,7},{7,6},{8,9},{9,8},{10,11... | collective-permute-start | bytes 884744 | tf_op jit(solution)/shard_map/ppermute | solution.py:464
  57.2 5.9 %copy-start.20 = (bf16[4,128,512]{2,1,0:T(8,128)(2,1)}, bf16[4,128,512]{2,1,0:T(8,128)(2,1)S(1)}, u32[]{:S(2)}) copy-start(bf16[4,128,512]{2,1,0:T(8,128)(2,1)S(1)} %collective-permute-done.10.refs_4_) | copy-start | bytes 1572868
  63.8 15.2 %collective-permute-start.13 = (bf16[288,1024]{1,0:T(8,128)(2,1)}, bf16[288,1024]{1,0:T(8,128)(2,1)S(1)}, u32[]{:S(2)}, u32[]{:S(2)}) collective-permute-start(bf16[288,1024]{1,0:T(8,128)(2,1)} %get-tuple-element.93), channel_id=1, source_target_pairs={{0,2},{2,0},{1,3},{3,1},{4,6},{6,4},{5,7},{7,5},{8,10},{10,8},{9,1... | collective-permute-start | bytes 1769480 | tf_op jit(solution)/shard_map/ppermute | solution.py:464
  78.4 19.6 %collective-permute-start.12 = (bf16[288,1280]{1,0:T(8,128)(2,1)}, bf16[288,1280]{1,0:T(8,128)(2,1)S(1)}, u32[]{:S(2)}, u32[]{:S(2)}) collective-permute-start(bf16[288,1280]{1,0:T(8,128)(2,1)} %get-tuple-element.90.refs_2_), channel_id=1, source_target_pairs={{0,2},{2,0},{1,3},{3,1},{4,6},{6,4},{5,7},{7,5},{8,10},{10,8},{9,1... | collective-permute-start | bytes 2211848 | tf_op jit(solution)/shard_map/ppermute | solution.py:464
  79.8 2.2 %collective-permute-start.14 = (bf16[288,1024]{1,0:T(8,128)(2,1)}, bf16[288,1024]{1,0:T(8,128)(2,1)S(1)}, u32[]{:S(2)}, u32[]{:S(2)}) collective-permute-start(bf16[288,1024]{1,0:T(8,128)(2,1)} %get-tuple-element.94.here), channel_id=1, source_target_pairs={{0,1},{1,0},{2,3},{3,2},{4,5},{5,4},{6,7},{7,6},{8,9},{9,8},{10,11... | collective-permute-start | bytes 1769480 | tf_op jit(solution)/shard_map/ppermute | solution.py:464
  86.1 18.2 %collective-permute-start.15 = (bf16[144,1024]{1,0:T(8,128)(2,1)}, bf16[144,1024]{1,0:T(8,128)(2,1)S(1)}, u32[]{:S(2)}, u32[]{:S(2)}) collective-permute-start(bf16[144,1024]{1,0:T(8,128)(2,1)} %get-tuple-element.97), channel_id=1, source_target_pairs={{0,2},{2,0},{1,3},{3,1},{4,6},{6,4},{5,7},{7,5},{8,10},{10,8},{9,1... | collective-permute-start | bytes 884744 | tf_op jit(solution)/shard_map/ppermute | solution.py:464
  102.2 12.0 %collective-permute-start.18 = (bf16[256,768]{1,0:T(8,128)(2,1)}, bf16[256,768]{1,0:T(8,128)(2,1)S(1)}, u32[]{:S(2)}, u32[]{:S(2)}) collective-permute-start(bf16[256,768]{1,0:T(8,128)(2,1)} %get-tuple-element.103), channel_id=1, source_target_pairs={{0,4},{4,0},{8,12},{12,8},{1,5},{5,1},{9,13},{13,9},{2,6},{6,2},{1... | collective-permute-start | bytes 1179656 | tf_op jit(solution)/shard_map/ppermute | solution.py:529
  103.8 19.6 %collective-permute-start.16 = (bf16[288,1280]{1,0:T(8,128)(2,1)}, bf16[288,1280]{1,0:T(8,128)(2,1)S(1)}, u32[]{:S(2)}, u32[]{:S(2)}) collective-permute-start(bf16[288,1280]{1,0:T(8,128)(2,1)} %get-tuple-element.99.refs_2_), channel_id=1, source_target_pairs={{0,2},{2,0},{1,3},{3,1},{4,6},{6,4},{5,7},{7,5},{8,10},{10,8},{9,1... | collective-permute-start | bytes 2211848 | tf_op jit(solution)/shard_map/ppermute | solution.py:464
  105.1 8.6 %copy-start.18 = (bf16[288,1024]{1,0:T(8,128)(2,1)S(1)}, bf16[288,1024]{1,0:T(8,128)(2,1)}, u32[]{:S(2)}) copy-start(bf16[288,1024]{1,0:T(8,128)(2,1)} %get-tuple-element.86) | copy-start | bytes 1769476
  105.1 8.6 %copy-start.2 = (bf16[288,1024]{1,0:T(8,128)(2,1)S(1)}, bf16[288,1024]{1,0:T(8,128)(2,1)}, u32[]{:S(2)}) copy-start(bf16[288,1024]{1,0:T(8,128)(2,1)} %get-tuple-element.101.refs_5_.refs_3_.refs_1_) | copy-start | bytes 1769476
  105.1 9.2 %copy-start.26 = (f32[128,768]{1,0:T(8,128)S(1)}, f32[128,768]{1,0:T(8,128)}, u32[]{:S(2)}) copy-start(f32[128,768]{1,0:T(8,128)} %get-tuple-element.106) | copy-start | bytes 1179652
  112.1 27.1 %collective-permute-start.20 = (bf16[288,1280]{1,0:T(8,128)(2,1)}, bf16[288,1280]{1,0:T(8,128)(2,1)S(1)}, u32[]{:S(2)}, u32[]{:S(2)}) collective-permute-start(bf16[288,1280]{1,0:T(8,128)(2,1)} %get-tuple-element.109), channel_id=1, source_target_pairs={{0,2},{2,0},{1,3},{3,1},{4,6},{6,4},{5,7},{7,5},{8,10},{10,8},{9,1... | collective-permute-start | bytes 2211848 | tf_op jit(solution)/shard_map/ppermute | solution.py:464
  113.6 31.2 %collective-permute-start.11 = (bf16[288,1024]{1,0:T(8,128)(2,1)S(1)}, bf16[288,1024]{1,0:T(8,128)(2,1)S(1)}, u32[]{:S(2)}, u32[]{:S(2)}) collective-permute-start(bf16[288,1024]{1,0:T(8,128)(2,1)S(1)} %copy-done.18), channel_id=1, source_target_pairs={{0,1},{1,0},{2,3},{3,2},{4,5},{5,4},{6,7},{7,6},{8,9},{9,8},{10,11... | collective-permute-start | bytes 1769480 | tf_op jit(solution)/shard_map/ppermute | solution.py:464
  113.7 3.3 %collective-permute-start.17 = (bf16[288,512]{1,0:T(8,128)(2,1)S(1)}, bf16[288,512]{1,0:T(8,128)(2,1)S(1)}, u32[]{:S(2)}, u32[]{:S(2)}) collective-permute-start(bf16[288,512]{1,0:T(8,128)(2,1)S(1)} %slice.33), channel_id=1, source_target_pairs={{0,1},{1,0},{2,3},{3,2},{4,5},{5,4},{6,7},{7,6},{8,9},{9,8},{10,11... | collective-permute-start | bytes 884744 | tf_op jit(solution)/shard_map/ppermute | solution.py:464
  114.2 9.2 %copy-start.6 = (bf16[256,768]{1,0:T(8,128)(2,1)}, bf16[256,768]{1,0:T(8,128)(2,1)S(1)}, u32[]{:S(2)}) copy-start(bf16[256,768]{1,0:T(8,128)(2,1)S(1)} %collective-permute-done.18.refs_8_) | copy-start | bytes 1179652
  114.3 14.8 %collective-permute-start.19 = (bf16[128,768]{1,0:T(8,128)(2,1)S(1)}, bf16[128,768]{1,0:T(8,128)(2,1)S(1)}, u32[]{:S(2)}, u32[]{:S(2)}) collective-permute-start(bf16[128,768]{1,0:T(8,128)(2,1)S(1)} %add_convert_fusion.4), channel_id=1, source_target_pairs={{0,8},{4,12},{8,0},{12,4},{1,9},{5,13},{9,1},{13,5},{2,10},{6,14},... | collective-permute-start | bytes 589832 | tf_op jit(solution)/shard_map/ppermute | solution.py:531
  116.9 6.5 %copy-start.5 = (bf16[288,512]{1,0:T(8,128)(2,1)}, bf16[288,512]{1,0:T(8,128)(2,1)S(1)}, u32[]{:S(2)}) copy-start(bf16[288,512]{1,0:T(8,128)(2,1)S(1)} %collective-permute-done.17.refs_6_.refs_5_.refs_2_) | copy-start | bytes 884740
  124.3 5.9 %copy-start.24 = (bf16[288,768]{1,0:T(8,128)(2,1)S(1)}, bf16[288,768]{1,0:T(8,128)(2,1)}, u32[]{:S(2)}) copy-start(bf16[288,768]{1,0:T(8,128)(2,1)} %get-tuple-element.117.refs_3_) | copy-start | bytes 1327108
  129.7 15.2 %copy-start.7 = (bf16[288,1024]{1,0:T(8,128)(2,1)S(1)}, bf16[288,1024]{1,0:T(8,128)(2,1)}, u32[]{:S(2)}) copy-start(bf16[288,1024]{1,0:T(8,128)(2,1)} %get-tuple-element.85.joined) | copy-start | bytes 1769476
  129.7 21.2 %collective-permute-start.21 = (bf16[256,1280]{1,0:T(8,128)(2,1)}, bf16[256,1280]{1,0:T(8,128)(2,1)S(1)}, u32[]{:S(2)}, u32[]{:S(2)}) collective-permute-start(bf16[256,1280]{1,0:T(8,128)(2,1)} %get-tuple-element.115), channel_id=1, source_target_pairs={{0,4},{4,0},{8,12},{12,8},{1,5},{5,1},{9,13},{13,9},{2,6},{6,2},{1... | collective-permute-start | bytes 1966088 | tf_op jit(solution)/shard_map/ppermute | solution.py:529
  130.2 15.0 %collective-permute-start.23 = (bf16[288,768]{1,0:T(8,128)(2,1)S(1)}, bf16[288,768]{1,0:T(8,128)(2,1)S(1)}, u32[]{:S(2)}, u32[]{:S(2)}) collective-permute-start(bf16[288,768]{1,0:T(8,128)(2,1)S(1)} %copy-done.24), channel_id=1, source_target_pairs={{0,2},{2,0},{1,3},{3,1},{4,6},{6,4},{5,7},{7,5},{8,10},{10,8},{9,1... | collective-permute-start | bytes 1327112 | tf_op jit(solution)/shard_map/ppermute | solution.py:464
  144.4 6.5 %copy-start.16 = (f32[128,1280]{1,0:T(8,128)S(1)}, f32[128,1280]{1,0:T(8,128)}, u32[]{:S(2)}) copy-start(f32[128,1280]{1,0:T(8,128)} %get-tuple-element.116) | copy-start | bytes 1966084
  144.4 28.2 %collective-permute-start.24 = (bf16[256,1280]{1,0:T(8,128)(2,1)}, bf16[256,1280]{1,0:T(8,128)(2,1)S(1)}, u32[]{:S(2)}, u32[]{:S(2)}) collective-permute-start(bf16[256,1280]{1,0:T(8,128)(2,1)} %get-tuple-element.120), channel_id=1, source_target_pairs={{0,4},{4,0},{8,12},{12,8},{1,5},{5,1},{9,13},{13,9},{2,6},{6,2},{1... | collective-permute-start | bytes 1966088 | tf_op jit(solution)/shard_map/ppermute | solution.py:529
  145.2 27.4 %copy-start.17 = (f32[128,1280]{1,0:T(8,128)S(1)}, f32[128,1280]{1,0:T(8,128)}, u32[]{:S(2)}) copy-start(f32[128,1280]{1,0:T(8,128)} %get-tuple-element.121) | copy-start | bytes 1966084
  149.4 27.5 %copy-start.27 = (f32[128,768]{1,0:T(8,128)S(1)}, f32[128,768]{1,0:T(8,128)}, u32[]{:S(2)}) copy-start(f32[128,768]{1,0:T(8,128)} %get-tuple-element.124) | copy-start | bytes 1179652
  149.4 27.5 %collective-permute-start.26 = (bf16[256,768]{1,0:T(8,128)(2,1)}, bf16[256,768]{1,0:T(8,128)(2,1)S(1)}, u32[]{:S(2)}, u32[]{:S(2)}) collective-permute-start(bf16[256,768]{1,0:T(8,128)(2,1)} %get-tuple-element.123), channel_id=1, source_target_pairs={{0,4},{4,0},{8,12},{12,8},{1,5},{5,1},{9,13},{13,9},{2,6},{6,2},{1... | collective-permute-start | bytes 1179656 | tf_op jit(solution)/shard_map/ppermute | solution.py:529
  150.9 26.2 %copy-start.10 = (bf16[256,1280]{1,0:T(8,128)(2,1)}, bf16[256,1280]{1,0:T(8,128)(2,1)S(1)}, u32[]{:S(2)}) copy-start(bf16[256,1280]{1,0:T(8,128)(2,1)S(1)} %collective-permute-done.21.refs_4_) | copy-start | bytes 1966084
  151.0 27.0 %collective-permute-start.22 = (bf16[128,1280]{1,0:T(8,128)(2,1)S(1)}, bf16[128,1280]{1,0:T(8,128)(2,1)S(1)}, u32[]{:S(2)}, u32[]{:S(2)}) collective-permute-start(bf16[128,1280]{1,0:T(8,128)(2,1)S(1)} %add_convert_fusion.2), channel_id=1, source_target_pairs={{0,8},{4,12},{8,0},{12,4},{1,9},{5,13},{9,1},{13,5},{2,10},{6,14},... | collective-permute-start | bytes 983048 | tf_op jit(solution)/shard_map/ppermute | solution.py:531
  172.6 5.4 %copy-start.11 = (bf16[256,1280]{1,0:T(8,128)(2,1)}, bf16[256,1280]{1,0:T(8,128)(2,1)S(1)}, u32[]{:S(2)}) copy-start(bf16[256,1280]{1,0:T(8,128)(2,1)S(1)} %collective-permute-done.24.refs_1_) | copy-start | bytes 1966084
  172.6 19.6 %collective-permute-start.25 = (bf16[128,1280]{1,0:T(8,128)(2,1)S(1)}, bf16[128,1280]{1,0:T(8,128)(2,1)S(1)}, u32[]{:S(2)}, u32[]{:S(2)}) collective-permute-start(bf16[128,1280]{1,0:T(8,128)(2,1)S(1)} %add_convert_fusion.1), channel_id=1, source_target_pairs={{0,8},{4,12},{8,0},{12,4},{1,9},{5,13},{9,1},{13,5},{2,10},{6,14},... | collective-permute-start | bytes 983048 | tf_op jit(solution)/shard_map/ppermute | solution.py:531
  176.9 4.9 %copy-start.12 = (bf16[256,768]{1,0:T(8,128)(2,1)}, bf16[256,768]{1,0:T(8,128)(2,1)S(1)}, u32[]{:S(2)}) copy-start(bf16[256,768]{1,0:T(8,128)(2,1)S(1)} %collective-permute-done.26.refs_4_) | copy-start | bytes 1179652
  176.9 15.3 %collective-permute-start.27 = (bf16[128,768]{1,0:T(8,128)(2,1)S(1)}, bf16[128,768]{1,0:T(8,128)(2,1)S(1)}, u32[]{:S(2)}, u32[]{:S(2)}) collective-permute-start(bf16[128,768]{1,0:T(8,128)(2,1)S(1)} %add_convert_fusion.3), channel_id=1, source_target_pairs={{0,8},{4,12},{8,0},{12,4},{1,9},{5,13},{9,1},{13,5},{2,10},{6,14},... | collective-permute-start | bytes 589832 | tf_op jit(solution)/shard_map/ppermute | solution.py:531
  (18 other events, 22.4 us)
